TPU v7x, 128 devices: a whole 4x4x4 slice. The times are simulated.
128 devices in a mesh: row: 16 (over y_lo, z, core), col: 8 (over x, y_hi).
Axes of the slice: x: 4, y: 4 (y_hi: 2, y_lo: 2; y = y_hi * 2 + y_lo), z: 4, core: 2. Of those that a mesh axis runs over, the one named last changes fastest.
Arguments:
- out_grad: bfloat16 [65536, 256], P(('row', 'col')), may hold values from -6 to 6
- out_bits: int32 [65536, 16], P(('row', 'col')), may hold values from 0 to 65535
- agg_saved: bfloat16 [65536, 256], P(('row', 'col')), may hold values from -6 to 6
- weight: bfloat16 [256, 256], replicated, may hold values from -0.375 to 0.375
- tiles: bfloat16 [16, 8, 512, 128, 128], P('row', 'col'), may hold values from -0.0625 to 0.0625
- tile_coords: int32 [16, 8, 512, 2], P('row', 'col'), may hold values from 0 to 63, as said below
- tile_count: int32 [16, 8], P('row', 'col'), may hold values from 64 to 512, as said below
- in_bits: int32 [65536, 16], P(('row', 'col')), may hold values from 0 to 65535
Outputs:
- weight_grad: float32 [256, 256], replicated
- prev_grad: bfloat16 [65536, 256], P(('row', 'col'))
Inputs may be any that keep to these rules, and one draw needn't show every extreme that they name: `tile_coords`: within one block, all 512 slots name distinct tile positions; tile rows are below 32 and tile columns below 64. `tile_count`: slots at or beyond a block's count are ignored; some block uses all 512 slots.
All inputs are finite; a program needn't handle non-finite values.
Results may differ from a plain program's by a relative error of at most 0.0049.
Values may be sent and summed in bfloat16 or wider, within the bound.
No kernel may reach another device: no remote copies, remote signals or barrier semaphores. Data moves between devices by JAX's collectives and lax.ppermute only.
A program may use at most 128 MiB of HBM per device.

v0:
```python
import math

import jax
import jax.numpy as jnp
from jax import lax
from jax.sharding import PartitionSpec as P

TILE = 128


def unpack(packed):
    shift_list = jnp.arange(16, dtype=jnp.int32)
    bit_values = jnp.right_shift(packed[:, :, None], shift_list[None, None, :]) & 1
    return bit_values.reshape(packed.shape[0], packed.shape[1] * 16)


def total_weight(weight_part, norm_scale):
    return lax.psum(weight_part, ("row", "col")) * norm_scale


def shards(out_grad, out_bits, agg_saved, weight, tiles, tile_coords, tile_count, in_bits):
    row_total = lax.axis_size("row")
    col_total = lax.axis_size("col")
    rows_dev, features = out_grad.shape
    node_total = rows_dev * row_total * col_total
    masked_grad = jnp.where(unpack(out_bits) == 1, out_grad, jnp.zeros_like(out_grad))
    weight_part = lax.dot_general(
        agg_saved, masked_grad, (((0,), (0,)), ((), ())), preferred_element_type=jnp.float32
    )
    hidden_grad = lax.dot_general(
        masked_grad, weight, (((1,), (1,)), ((), ())), preferred_element_type=jnp.float32
    ).astype(jnp.bfloat16)
    gathered = lax.all_gather(hidden_grad, "col", axis=0, tiled=True)
    row_count = gathered.shape[0] // TILE
    row_flat = gathered.reshape(row_count, TILE * features)
    own_tiles = tiles[0, 0]
    own_coords = tile_coords[0, 0]
    tile_total = tile_count[0, 0]
    slot_total = own_tiles.shape[0]
    group_size = min(64, slot_total)
    col_tiles = row_total * rows_dev // TILE
    group_starts = jnp.arange(slot_total // group_size, dtype=jnp.int32) * group_size
    row_ids = jnp.arange(row_count, dtype=jnp.int32)
    norm_scale = 1.0 / math.sqrt(node_total)
    window_ids = jnp.arange(col_tiles, dtype=jnp.int32)

    def scan_group(partial_value, first_slot):
        tile_block = lax.dynamic_slice_in_dim(own_tiles, first_slot, group_size, 0)
        block_coords = lax.dynamic_slice_in_dim(own_coords, first_slot, group_size, 0)
        select = (block_coords[:, 0][:, None] == row_ids[None, :]).astype(jnp.bfloat16)
        picked = jnp.dot(select, row_flat, preferred_element_type=jnp.float32).astype(jnp.bfloat16)
        picked = picked.reshape(group_size, TILE, features)
        products = jnp.einsum(
            "kij,kih->kjh", tile_block, picked, preferred_element_type=jnp.float32
        )
        target = block_coords[:, 1] - 0
        alive_mask = first_slot + jnp.arange(group_size, dtype=jnp.int32) < tile_total
        placing = (window_ids[:, None] == target[None, :]) & alive_mask[None, :]
        placing = placing.astype(jnp.float32)
        added = jnp.dot(
            placing,
            products.reshape(group_size, TILE * features),
            precision=lax.Precision.HIGHEST,
            preferred_element_type=jnp.float32,
        )
        return (partial_value + added, None)

    zero_sums = jnp.zeros((col_tiles, TILE * features), jnp.float32)
    partial_value, unused = lax.scan(scan_group, zero_sums, group_starts)
    flat_sums = partial_value.reshape(col_tiles * TILE, features)
    summed = lax.psum_scatter(flat_sums, "row", scatter_dimension=0, tiled=True)
    weight_grad = total_weight(weight_part, norm_scale)
    prev_grad = jnp.where(unpack(in_bits) == 1, summed, jnp.zeros_like(summed)).astype(jnp.bfloat16)
    return (weight_grad, prev_grad)


def solution(mesh):
    return jax.shard_map(
        shards,
        mesh=mesh,
        in_specs=(
            P(("row", "col"), None),
            P(("row", "col"), None),
            P(("row", "col"), None),
            P(),
            P("row", "col", None, None, None),
            P("row", "col", None, None),
            P("row", "col"),
            P(("row", "col"), None),
        ),
        out_specs=(P(), P(("row", "col"), None)),
        check_vma=False,
    )
```

profile of v0, /device:TPU:0, one launch (start us, length us, event | category | flops | bytes accessed | tf_op | source)
XLA Modules:
  0.0 365.1 jit_solution(10695797896538475142)
XLA Ops:
  10.2 1.9 convolution_convert_fusion.1
  13.2 22.5 %copy.19 = bf16[1,1,512,128,128]{3,4,2,1,0:T(8,128)(2,1)} copy(bf16[1,1,512,128,128]{4,3,2,1,0:T(8,128)(2,1)} %param.14) | data formatting | bytes 33554432 | tf_op args[4]
  35.6 34.1 %all-gather.2.cloned.1.call-done = bf16[4096,256]{1,0:T(8,128)(2,1)} async-done(((bf16[512,256]{1,0:T(8,128)(2,1)}), bf16[4096,256]{1,0:T(8,128)(2,1)}) %all-gather.2.cloned.1.call-update) | async-done | bytes 2097168 | tf_op jit(solution)/shard_map/all_gather | solution.py:33
  69.8 2.9 reshape.32
  72.7 190.7 %while.11 = (s32[]{:T(128)}, f32[64,32768]{1,0:T(8,128)}, s32[8]{0:T(128)S(1)}, s32[512,2]{0,1:T(2,128)}, s32[]{:T(128)}, /*index=5*/bf16[512,128,128]{1,2,0:T(8...) while((s32[]{:T(128)}, f32[64,32768]{1,0:T(8,128)}, s32[8]{0:T(128)S(1)}, ...), condition=%wide.region_2.3_spmd.clone, body=%wide.region_1.2_spmd.clone.sunk | while | flops 2288003072 | bytes 71306032 | solution.py:69
  75.2 1.3 add_compare_fusion.2
  77.3 1.3 convolution_convert_fusion.3
  79.7 2.9 fusion.35
  82.5 4.7 %copy.28 = f32[8,8,128,256]{3,1,2,0:T(8,128)S(1)} copy(f32[8,8,128,256]{3,2,1,0:T(8,128)S(1)} %bitcast.55) | data formatting | bytes 16777216 | tf_op jit(solution)/shard_map/while
  87.3 7.4 %convolution_add_fusion.2 = f32[64,32768]{1,0:T(8,128)} fusion(f32[64,32768]{1,0:T(8,128)S(1)} %bitcast.56, f32[64,32768]{1,0:T(8,128)} %get-tuple-element.158, pred[]{:T(512)S(6)} %compare.3, s32[64]{0:T(128)S(1)} %get-tuple-element.146, pred[64]{0:T(512)(128)(4,1)S(1)} %add_compare_fusion.2), kind=kOutput, calls=%fused_computation.2.clone.1 | convolution fusion | flops 1614815232 | bytes 25166144 | tf_op jit(solution)/shard_map/while/body/eval_jaxpr/dot_general | solution.py:60
  97.2 1.3 add_compare_fusion.2
  99.2 1.3 convolution_convert_fusion.3
  101.6 2.9 fusion.35
  104.5 4.7 %copy.28 = f32[8,8,128,256]{3,1,2,0:T(8,128)S(1)} copy(f32[8,8,128,256]{3,2,1,0:T(8,128)S(1)} %bitcast.55) | data formatting | bytes 16777216 | tf_op jit(solution)/shard_map/while
  109.2 9.5 %convolution_add_fusion.2 = f32[64,32768]{1,0:T(8,128)} fusion(f32[64,32768]{1,0:T(8,128)S(1)} %bitcast.56, f32[64,32768]{1,0:T(8,128)} %get-tuple-element.158, pred[]{:T(512)S(6)} %compare.3, s32[64]{0:T(128)S(1)} %get-tuple-element.146, pred[64]{0:T(512)(128)(4,1)S(1)} %add_compare_fusion.2), kind=kOutput, calls=%fused_computation.2.clone.1 | convolution fusion | flops 1614815232 | bytes 25166144 | tf_op jit(solution)/shard_map/while/body/eval_jaxpr/dot_general | solution.py:60
  121.3 1.3 add_compare_fusion.2
  123.3 1.3 convolution_convert_fusion.3
  125.7 2.9 fusion.35
  128.6 4.7 %copy.28 = f32[8,8,128,256]{3,1,2,0:T(8,128)S(1)} copy(f32[8,8,128,256]{3,2,1,0:T(8,128)S(1)} %bitcast.55) | data formatting | bytes 16777216 | tf_op jit(solution)/shard_map/while
  133.3 9.5 %convolution_add_fusion.2 = f32[64,32768]{1,0:T(8,128)} fusion(f32[64,32768]{1,0:T(8,128)S(1)} %bitcast.56, f32[64,32768]{1,0:T(8,128)} %get-tuple-element.158, pred[]{:T(512)S(6)} %compare.3, s32[64]{0:T(128)S(1)} %get-tuple-element.146, pred[64]{0:T(512)(128)(4,1)S(1)} %add_compare_fusion.2), kind=kOutput, calls=%fused_computation.2.clone.1 | convolution fusion | flops 1614815232 | bytes 25166144 | tf_op jit(solution)/shard_map/while/body/eval_jaxpr/dot_general | solution.py:60
  145.4 1.3 add_compare_fusion.2
  147.4 1.3 convolution_convert_fusion.3
  149.8 2.9 fusion.35
  152.7 4.7 %copy.28 = f32[8,8,128,256]{3,1,2,0:T(8,128)S(1)} copy(f32[8,8,128,256]{3,2,1,0:T(8,128)S(1)} %bitcast.55) | data formatting | bytes 16777216 | tf_op jit(solution)/shard_map/while
  157.4 9.5 %convolution_add_fusion.2 = f32[64,32768]{1,0:T(8,128)} fusion(f32[64,32768]{1,0:T(8,128)S(1)} %bitcast.56, f32[64,32768]{1,0:T(8,128)} %get-tuple-element.158, pred[]{:T(512)S(6)} %compare.3, s32[64]{0:T(128)S(1)} %get-tuple-element.146, pred[64]{0:T(512)(128)(4,1)S(1)} %add_compare_fusion.2), kind=kOutput, calls=%fused_computation.2.clone.1 | convolution fusion | flops 1614815232 | bytes 25166144 | tf_op jit(solution)/shard_map/while/body/eval_jaxpr/dot_general | solution.py:60
  169.5 1.3 add_compare_fusion.2
  171.6 1.3 convolution_convert_fusion.3
  174.0 2.9 fusion.35
  176.8 4.7 %copy.28 = f32[8,8,128,256]{3,1,2,0:T(8,128)S(1)} copy(f32[8,8,128,256]{3,2,1,0:T(8,128)S(1)} %bitcast.55) | data formatting | bytes 16777216 | tf_op jit(solution)/shard_map/while
  181.6 9.5 %convolution_add_fusion.2 = f32[64,32768]{1,0:T(8,128)} fusion(f32[64,32768]{1,0:T(8,128)S(1)} %bitcast.56, f32[64,32768]{1,0:T(8,128)} %get-tuple-element.158, pred[]{:T(512)S(6)} %compare.3, s32[64]{0:T(128)S(1)} %get-tuple-element.146, pred[64]{0:T(512)(128)(4,1)S(1)} %add_compare_fusion.2), kind=kOutput, calls=%fused_computation.2.clone.1 | convolution fusion | flops 1614815232 | bytes 25166144 | tf_op jit(solution)/shard_map/while/body/eval_jaxpr/dot_general | solution.py:60
  193.6 1.3 add_compare_fusion.2
  195.7 1.3 convolution_convert_fusion.3
  198.1 2.9 fusion.35
  200.9 4.7 %copy.28 = f32[8,8,128,256]{3,1,2,0:T(8,128)S(1)} copy(f32[8,8,128,256]{3,2,1,0:T(8,128)S(1)} %bitcast.55) | data formatting | bytes 16777216 | tf_op jit(solution)/shard_map/while
  205.7 9.5 %convolution_add_fusion.2 = f32[64,32768]{1,0:T(8,128)} fusion(f32[64,32768]{1,0:T(8,128)S(1)} %bitcast.56, f32[64,32768]{1,0:T(8,128)} %get-tuple-element.158, pred[]{:T(512)S(6)} %compare.3, s32[64]{0:T(128)S(1)} %get-tuple-element.146, pred[64]{0:T(512)(128)(4,1)S(1)} %add_compare_fusion.2), kind=kOutput, calls=%fused_computation.2.clone.1 | convolution fusion | flops 1614815232 | bytes 25166144 | tf_op jit(solution)/shard_map/while/body/eval_jaxpr/dot_general | solution.py:60
  217.7 1.3 add_compare_fusion.2
  219.8 1.3 convolution_convert_fusion.3
  222.2 2.9 fusion.35
  225.0 4.7 %copy.28 = f32[8,8,128,256]{3,1,2,0:T(8,128)S(1)} copy(f32[8,8,128,256]{3,2,1,0:T(8,128)S(1)} %bitcast.55) | data formatting | bytes 16777216 | tf_op jit(solution)/shard_map/while
  229.8 9.5 %convolution_add_fusion.2 = f32[64,32768]{1,0:T(8,128)} fusion(f32[64,32768]{1,0:T(8,128)S(1)} %bitcast.56, f32[64,32768]{1,0:T(8,128)} %get-tuple-element.158, pred[]{:T(512)S(6)} %compare.3, s32[64]{0:T(128)S(1)} %get-tuple-element.146, pred[64]{0:T(512)(128)(4,1)S(1)} %add_compare_fusion.2), kind=kOutput, calls=%fused_computation.2.clone.1 | convolution fusion | flops 1614815232 | bytes 25166144 | tf_op jit(solution)/shard_map/while/body/eval_jaxpr/dot_general | solution.py:60
  241.8 1.3 add_compare_fusion.2
  243.9 1.3 convolution_convert_fusion.3
  246.3 2.9 fusion.35
  249.1 4.7 %copy.28 = f32[8,8,128,256]{3,1,2,0:T(8,128)S(1)} copy(f32[8,8,128,256]{3,2,1,0:T(8,128)S(1)} %bitcast.55) | data formatting | bytes 16777216 | tf_op jit(solution)/shard_map/while
  253.9 9.5 %convolution_add_fusion.2 = f32[64,32768]{1,0:T(8,128)} fusion(f32[64,32768]{1,0:T(8,128)S(1)} %bitcast.56, f32[64,32768]{1,0:T(8,128)} %get-tuple-element.158, pred[]{:T(512)S(6)} %compare.3, s32[64]{0:T(128)S(1)} %get-tuple-element.146, pred[64]{0:T(512)(128)(4,1)S(1)} %add_compare_fusion.2), kind=kOutput, calls=%fused_computation.2.clone.1 | convolution fusion | flops 1614815232 | bytes 25166144 | tf_op jit(solution)/shard_map/while/body/eval_jaxpr/dot_general | solution.py:60
  263.4 9.2 %reshape.33 = f32[8192,256]{1,0:T(8,128)} reshape(f32[64,32768]{1,0:T(8,128)} %get-tuple-element.49) | data formatting | bytes 16777216 | tf_op jit(solution)/shard_map/reshape | solution.py:70
  272.6 8.9 %copy.20 = f32[8192,256]{0,1:T(8,128)} copy(f32[8192,256]{1,0:T(8,128)} %reshape.33) | data formatting | bytes 16777216 | tf_op jit(solution)/shard_map/reshape | solution.py:70
  283.5 72.1 %reduce-scatter.2.cloned.1.call-done = f32[512,256]{0,1:T(8,128)} async-done(((f32[8192,256]{0,1:T(8,128)}), f32[512,256]{0,1:T(8,128)}) %reduce-scatter.2.cloned.1.call-update) | async-done | bytes 524304 | tf_op jit(solution)/shard_map/reduce_scatter | solution.py:71
  (56 shorter events, 26.7 us)
Async XLA Ops:
  8.0 4.1 %copy-start = (bf16[512,256]{1,0:T(8,128)(2,1)S(1)}, bf16[512,256]{1,0:T(8,128)(2,1)}, u32[]{:S(2)}) copy-start(bf16[512,256]{1,0:T(8,128)(2,1)} %param.12) | copy-start | bytes 786436
  8.0 61.8 %all-gather.2.cloned.1.call-start = ((), (), s32[]{:S(2)}) async-start(), calls=%async_computation.2 | async-start | bytes 2359296 | tf_op jit(solution)/shard_map/all_gather | solution.py:33
  12.1 269.6 %all-reduce.2.cloned.1.call-start = ((), (), s32[]{:S(2)}) async-start(), calls=%async_computation.1 | async-start | bytes 524288 | tf_op jit(solution)/shard_map/psum | solution.py:18
  13.1 342.5 %reduce-scatter.2.cloned.1.call-start = ((), (), s32[]{:S(2)}) async-start(), calls=%async_computation.3 | async-start | bytes 8912896 | tf_op jit(solution)/shard_map/reduce_scatter | solution.py:71
  272.6 85.0 %copy-start.1 = (bf16[512,256]{1,0:T(8,128)(2,1)S(1)}, bf16[512,256]{1,0:T(8,128)(2,1)}, u32[]{:S(2)}) copy-start(bf16[512,256]{1,0:T(8,128)(2,1)} %param.12) | copy-start | bytes 786436
  281.6 74.0 %copy-start.2 = (s32[512,16]{0,1:T(8,128)S(1)}, s32[512,16]{0,1:T(8,128)}, u32[]{:S(2)}) copy-start(s32[512,16]{0,1:T(8,128)} %param.17) | copy-start | bytes 98308
Sparse Core Ops, SparseCore 0:
  12.2 57.5 all-gather.1
  281.7 73.8 reduce-scatter.1
Sparse Core Ops, SparseCore 1:
  17.9 154.3 all-reduce.1
where the time goes:
time: 367 us; the launch traced here: 365 us
  matrix products  110 us (30%)
  waiting for transfers between devices  106 us (29%)
  local copies, waits for them, and re-layouts  104 us (28%)
  loops' own time  15.8 us (4%)
  between operations  15.6 us (4%)
  other arithmetic  13.5 us (4%)
    dot_general x8, matrix products, scan_group(): jnp.dot(placing, products.reshape(group_size, TILE * features), precision...  73.9 us
    reduce_scatter x1, waiting for transfers between devices, shards(): summed = lax.psum_scatter(flat_sums, 'row', scatter_dimension=0, tiled=True)  72.1 us
    while x16, local copies, waits for them, and re-layouts  46.7 us
    all_gather x1, waiting for transfers between devices, shards(): gathered = lax.all_gather(hidden_grad, 'col', axis=0, tiled=True)  34.1 us
    unnamed x10, local copies, waits for them, and re-layouts  25.2 us
    dot_general x8, matrix products, scan_group(): jnp.einsum('kij,kih->kjh', tile_block, picked, preferred_element_type=jnp...  22.8 us
    reshape x2, local copies, waits for them, and re-layouts, shards(): flat_sums = partial_value.reshape(col_tiles * TILE, features)  18.2 us
    another operation x1, loops' own time, shards(): partial_value, unused = lax.scan(scan_group, zero_sums, group_starts)  15.8 us
  transfers between devices with their start and end apart: 3, of which 2 were waited for; matrix products, arithmetic and copies ran while one was open for 61% of the time, Pallas kernels for 0%

commit v1 on v0

v1 whole, which is shorter than its diff:
```python
import functools

import jax
import jax.numpy as jnp
from jax import lax
from jax.experimental import pallas as pl
from jax.experimental.pallas import tpu as pltpu
from jax.sharding import PartitionSpec as P

T = 128
N_STEP = 384
UNROLL = 16
LIMIT = 40
AHEAD = 3
ZERO_ROW = 32
bf16 = jnp.bfloat16
f32 = jnp.float32
tie = lambda *values: lax.optimization_barrier(values)
VMEM = pl.BlockSpec(memory_space=pltpu.VMEM)
SMEM = pl.BlockSpec(memory_space=pltpu.SMEM)


def call(body, outs, ins, name, limit=8, scratch=(), flops=0, touched=0):
    return pl.pallas_call(
        body,
        in_specs=ins,
        out_specs=[VMEM] * len(outs),
        out_shape=[jax.ShapeDtypeStruct(s, d) for s, d in outs],
        scratch_shapes=list(scratch),
        compiler_params=pltpu.CompilerParams(vmem_limit_bytes=limit * 2**20),
        cost_estimate=pl.CostEstimate(flops=flops, bytes_accessed=touched, transcendentals=0),
        name=name,
    )


def contract(a, b, da, db):
    return lax.dot_general(a, b, (((da,), (db,)), ((), ())), preferred_element_type=f32)


def mask_of(words):
    low = (words & 255).astype(f32)
    high = ((words >> 8) & 255).astype(f32)
    pieces = jnp.concatenate([low, high], 0).astype(bf16)
    w = lax.broadcasted_iota(jnp.int32, (32, 256), 0)
    f = lax.broadcasted_iota(jnp.int32, (32, 256), 1)
    spread = ((f >> 4) + 16 * ((f >> 3) & 1) == w).astype(f32).astype(bf16)
    byte = contract(pieces, spread, 0, 0).astype(jnp.int32)
    lane = lax.broadcasted_iota(jnp.int32, byte.shape, 1)
    return ((byte >> (lane & 7)) & 1) == 1


def prep(grad_ref, words_ref, agg_ref, weight_ref, ha_ref, hb_ref, wp_ref):
    masked = jnp.where(mask_of(words_ref[...]), grad_ref[...], jnp.zeros((), bf16))
    hidden = contract(weight_ref[...], masked, 1, 1).astype(bf16)
    for t in range(4):
        ref = ha_ref if t < 2 else hb_ref
        ref[t & 1] = hidden[:, t * T : (t + 1) * T]
    wp_ref[...] = contract(agg_ref[...], masked, 0, 0) * (1.0 / 256.0)


def in_mask(words_ref, out_ref):
    out_ref[...] = mask_of(words_ref[...]).astype(f32).astype(bf16)


def order_slots(count_ref, coords_ref, sib_ref, own_ref):
    device_row, device_col = lax.axis_index("row"), lax.axis_index("col")
    x, y_hi = device_col >> 1, device_col & 1
    y_lo, z, core = device_row >> 3, (device_row >> 1) & 3, device_row & 1
    slots = coords_ref.shape[1]
    slot = lax.broadcasted_iota(jnp.int32, (1, slots), 1)
    i, j = coords_ref[0:1, :], coords_ref[1:2, :]
    t, src = i & 3, i >> 2
    dx, dyh = ((src >> 1) - x) & 3, (src & 1) ^ y_hi
    row = jnp.where(t < 2, dx * 4 + dyh * 2 + t, 16 + dyh * 8 + dx * 2 + (t & 1))
    u, q = j & 3, j >> 2
    dc, dz, dy = (q & 1) ^ core ^ 1, ((q >> 1) - z) & 3, (q >> 3) ^ y_lo
    key = dc * 32 + jnp.where(u < 2, (dy * 4 + dz) * 2 + u, 16 + (dz * 2 + dy) * 2 + (u & 1))
    key = jnp.where(slot < count_ref[0], key, 64)
    word = slot | (row << 9)
    both = jnp.concatenate([key, word, jnp.zeros((6, slots), jnp.int32)], 0).T
    key_c, word_c = both[:, 0:1], both[:, 1:2]
    s_id = lax.broadcasted_iota(jnp.int32, (slots, slots), 0)
    t_id = lax.broadcasted_iota(jnp.int32, (slots, slots), 1)
    rank = jnp.sum(jnp.where((key == key_c) & (t_id < s_id), 1, 0), 1, keepdims=True)
    k_id = lax.broadcasted_iota(jnp.int32, (slots, T), 1)
    held = jnp.sum(jnp.where(key_c == k_id, 1, 0), 0, keepdims=True)
    pairs = jnp.where(k_id[0:1] < 64, (held + 1) >> 1, 0)
    ahead = (k_id < key_c) & ((k_id >> 5) == (key_c >> 5))
    step = jnp.sum(jnp.where(ahead, pairs, 0), 1, keepdims=True) + (rank >> 1)
    kind = jnp.where(key_c < 64, (key_c >> 5) * 2 + (rank & 1), 4)
    p_id = lax.broadcasted_iota(jnp.int32, (slots, N_STEP), 1)
    here = step == p_id
    none = ZERO_ROW << 9
    for half, ref in ((0, sib_ref), (1, own_ref)):
        first = here & (kind == half * 2)
        second = here & (kind == half * 2 + 1)
        total = jnp.sum(jnp.where((k_id[0:1] >> 5) == half, pairs, 0), 1, keepdims=True)
        ref[0:1, :] = jnp.sum(jnp.where(first, (key_c & 31) - 32, 0), 0, keepdims=True) + 32
        ref[1:2, :] = jnp.sum(jnp.where(first, word_c - none, 0), 0, keepdims=True) + none
        ref[2:3, :] = jnp.sum(jnp.where(second, word_c - none, 0), 0, keepdims=True) + none
        ref[3:4, :] = jnp.broadcast_to(total, (1, N_STEP))
        ref[4:8, :] = jnp.zeros((4, N_STEP), jnp.int32)


def products(steps_ref, h_ref, tiles_ref, acc_ref, buf, sems):
    groups = (steps_ref[3, 0] + UNROLL - 1) // UNROLL

    def fetch(g):
        slot = lax.rem(g, AHEAD + 1)
        for u in range(UNROLL):
            for side in range(2):
                word = steps_ref[1 + side, g * UNROLL + u]
                pltpu.make_async_copy(
                    tiles_ref.at[word & 511], buf.at[slot * 2 * UNROLL + 2 * u + side], sems.at[slot]
                ).start()

    for g in range(AHEAD):
        pl.when(g < groups)(lambda g=g: fetch(g))

    def clear(k, carry):
        acc_ref[k] = jnp.zeros((256, T), f32)
        return carry

    lax.fori_loop(0, 33, clear, 0)

    def some(g, carry):
        slot = lax.rem(g, AHEAD + 1)
        part = pl.ds(pl.multiple_of(slot * 2 * UNROLL, 2 * UNROLL), 2 * UNROLL)
        pl.when(g + AHEAD < groups)(lambda: fetch(g + AHEAD))
        pltpu.make_async_copy(tiles_ref.at[pl.ds(0, 2 * UNROLL)], buf.at[part], sems.at[slot]).wait()
        results = []
        for u in range(UNROLL):
            s = g * UNROLL + u
            left = jnp.concatenate([h_ref[steps_ref[1 + side, s] >> 9] for side in range(2)], 1)
            right = jnp.concatenate([buf[slot * 2 * UNROLL + 2 * u + side] for side in range(2)], 0)
            results.append((steps_ref[0, s], jnp.dot(left, right, preferred_element_type=f32)))
        for k, result in results:
            acc_ref[k] += result
        return carry

    lax.fori_loop(0, groups, some, 0)


def for_partner(steps_ref, a0, a3, a1, a2, b0, b1, tiles_ref, out_ref, h_ref, acc_ref, buf, sems):
    h_ref[0:4], h_ref[4:8], h_ref[8:12], h_ref[12:16] = a0[...], a1[...], a2[...], a3[...]
    h_ref[16:24], h_ref[24:32] = b0[...], b1[...]
    h_ref[ZERO_ROW] = jnp.zeros((256, T), bf16)
    products(steps_ref, h_ref, tiles_ref, acc_ref, buf, sems)

    def narrow(k, carry):
        out_ref[k] = acc_ref[k].astype(bf16)
        return carry

    lax.fori_loop(0, 32, narrow, 0)


def for_self(steps_ref, h_ref, tiles_ref, acc_ref, buf, sems):
    products(steps_ref, h_ref, tiles_ref, acc_ref, buf, sems)


def join_cores(acc_ref, got_ref, a_keep, a_y, b_keep, b_z1, b_z2, b_z3):
    def add(k):
        return acc_ref[k] + got_ref[k].astype(f32)

    for k in range(8):
        a_keep[k] = add(k)
        a_y[k] = add(8 + k).astype(bf16)
    for k in range(4):
        b_keep[k] = add(16 + k)
        b_z1[k] = add(20 + k).astype(bf16)
        b_z2[k] = add(24 + k).astype(bf16)
        b_z3[k] = add(28 + k).astype(bf16)


def join_a(keep_ref, got_ref, a_keep, a_z1, a_z2, a_z3):
    for t in range(2):
        a_keep[t] = keep_ref[t] + got_ref[t].astype(f32)
        for dz, ref in ((1, a_z1), (2, a_z2), (3, a_z3)):
            ref[t] = (keep_ref[2 * dz + t] + got_ref[2 * dz + t].astype(f32)).astype(bf16)


def join_b(keep_ref, g1, g2, g3, b_keep, b_y):
    for k in range(4):
        total = keep_ref[k] + g1[k].astype(f32) + g2[k].astype(f32) + g3[k].astype(f32)
        if k < 2:
            b_keep[k] = total
        else:
            b_y[k - 2] = total.astype(bf16)


def finish(a_keep, g1, g2, g3, b_keep, gy, mask_ref, out_ref):
    for t in range(4):
        if t < 2:
            total = a_keep[t] + g1[t].astype(f32) + g2[t].astype(f32) + g3[t].astype(f32)
        else:
            total = b_keep[t - 2] + gy[t - 2].astype(f32)
        rows = slice(t * T, (t + 1) * T)
        out_ref[rows] = jnp.where(mask_ref[rows] == 1, total.T, 0.0).astype(bf16)


def shards(out_grad, out_bits, agg_saved, weight, tiles, tile_coords, tile_count, in_bits):
    def over_x(v, s):
        return lax.ppermute(v, "col", [(c, (((c >> 1) + s) & 3) * 2 + (c & 1)) for c in range(8)])

    def over_y_hi(v):
        return lax.ppermute(v, "col", [(c, c ^ 1) for c in range(8)])

    def over_z(v, s):
        return lax.ppermute(v, "row", [(r, (r & 9) | ((((r >> 1) + s) & 3) << 1)) for r in range(16)])

    def over_y_lo(v):
        return lax.ppermute(v, "row", [(r, r ^ 8) for r in range(16)])

    def over_core(v):
        return lax.ppermute(v, "row", [(r, r ^ 1) for r in range(16)])

    half = (2, 256, T)
    ha, hb, part = call(
        prep, [(half, bf16), (half, bf16), ((256, 256), f32)], [VMEM] * 4, "prep", flops=2 * 10**8
    )(out_grad, out_bits.T, agg_saved, weight)

    ha_y = over_y_hi(ha)
    hb_1, hb_2, hb_3 = over_x(hb, -1), over_x(hb, 2), over_x(hb, 1)
    pieces = lax.all_to_all(part.reshape(16, 16, 256), "row", 0, 0)

    count, coords, words, own_tiles, ha = tie(
        tile_count.reshape(1), tile_coords[0, 0].T, in_bits.T, tiles[0, 0], ha
    )
    sib_steps, own_steps = call(
        order_slots,
        [((8, N_STEP), jnp.int32)] * 2,
        [SMEM, VMEM],
        "order_slots",
        flops=10**7,
    )(count, coords)
    (mask,) = call(in_mask, [((512, 256), bf16)], [VMEM], "in_mask", flops=10**7)(words)

    ha, ha_y, hb, hb_1, hb_2, hb_3, sib_steps, own_steps, mask = tie(
        ha, ha_y, hb, hb_1, hb_2, hb_3, sib_steps, own_steps, mask
    )
    a0 = jnp.concatenate([ha, ha_y], 0)
    b0 = jnp.concatenate([hb, hb_1, hb_2, hb_3], 0)
    a3, a1, a2 = over_x(a0, 1), over_x(a0, -1), over_x(a0, 2)
    b1 = over_y_hi(b0)

    piece = jnp.sum(pieces, 0)
    pieces = lax.all_to_all(jnp.broadcast_to(piece[None], (8, 16, 256)), "col", 0, 0)
    piece = jnp.sum(pieces, 0)
    a0, a1, a2, a3, b0, b1, piece = tie(a0, a1, a2, a3, b0, b1, piece)
    fetching = [pltpu.VMEM(((AHEAD + 1) * 2 * UNROLL, T, T), bf16), pltpu.SemaphoreType.DMA((AHEAD + 1,))]
    to_partner, hidden = call(
        for_partner,
        [((32, 256, T), bf16), ((33, 256, T), bf16)],
        [SMEM] + [VMEM] * 6 + [pl.BlockSpec(memory_space=pl.ANY)],
        "for_partner",
        limit=LIMIT,
        scratch=[pltpu.VMEM((33, 256, T), f32)] + fetching,
        flops=4 * 10**9,
        touched=2**23,
    )(sib_steps, a0, a3, a1, a2, b0, b1, own_tiles)
    from_partner = over_core(to_partner)
    (acc,) = call(
        for_self,
        [((33, 256, T), f32)],
        [SMEM, VMEM, pl.BlockSpec(memory_space=pl.ANY)],
        "for_self",
        limit=LIMIT,
        scratch=fetching,
        flops=4 * 10**9,
        touched=2**23,
    )(own_steps, hidden, own_tiles)
    quad = (4, 256, T)
    a_keep, a_y, b_keep, b_z1, b_z2, b_z3 = call(
        join_cores,
        [((8, 256, T), f32), ((8, 256, T), bf16), (quad, f32)] + [(quad, bf16)] * 3,
        [VMEM] * 2,
        "join_cores",
        flops=10**6,
    )(acc, from_partner)

    a_keep, a_y, b_keep, b_z1, b_z2, b_z3, piece = tie(a_keep, a_y, b_keep, b_z1, b_z2, b_z3, piece)
    a_got = over_y_lo(a_y)
    b_got = [over_z(b_z1, 1), over_z(b_z2, 2), over_z(b_z3, -1)]
    a_keep, a_z1, a_z2, a_z3 = call(
        join_a, [(half, f32)] + [(half, bf16)] * 3, [VMEM] * 2, "join_a", flops=10**6
    )(a_keep, a_got)
    a_got = [over_z(a_z1, 1), over_z(a_z2, 2), over_z(a_z3, -1)]
    b_keep, b_y = call(join_b, [(half, f32), (half, bf16)], [VMEM] * 4, "join_b", flops=10**6)(b_keep, *b_got)
    b_got = over_y_lo(b_y)
    pieces = lax.all_to_all(jnp.broadcast_to(piece[None], (16, 16, 256)), "row", 0, 0)
    weight_grad = pieces.reshape(256, 256)
    a_keep, b_keep, weight_grad = tie(a_keep, b_keep, weight_grad)
    (prev_grad,) = call(finish, [((512, 256), bf16)], [VMEM] * 7, "finish", flops=10**6)(
        a_keep, *a_got, b_keep, b_got, mask
    )
    return weight_grad, prev_grad


def solution(mesh):
    nodes = P(("row", "col"), None)
    return jax.shard_map(
        shards,
        mesh=mesh,
        in_specs=(nodes, nodes, nodes, P(), P("row", "col"), P("row", "col"), P("row", "col"), nodes),
        out_specs=(P(), nodes),
        check_vma=False,
    )
```

time: 367 us -> 99.3 us (0.27)
  matrix products: 110 us -> 0 us
  local copies, waits for them, and re-layouts: 104 us -> 7.5 us
  waiting for transfers between devices: 106 us -> 17.8 us
  starting transfers between devices: 0.12 us -> 39.8 us
  Pallas kernels: 0 us -> 16.9 us
  loops' own time: 15.8 us -> 0 us
  blocking collectives: 0 us -> 14.2 us
  between operations: 15.6 us -> 1.5 us
  other arithmetic: 13.5 us -> 0.03 us
    dot_general x26 -> x0, matrix products: 110 us -> none  [the longest x8 73.9 us: scan_group(): jnp.dot(placing, products.reshape(group_size, TILE * features), precision...]
    reduce_scatter x1 -> x0, waiting for transfers between devices: 72.1 us -> none  [shards(): summed = lax.psum_scatter(flat_sums, 'row', scatter_dimension=0, tiled=True)]
    while x16 -> x0, local copies, waits for them, and re-layouts: 46.7 us -> none
    all_gather x1 -> x0, waiting for transfers between devices: 34.1 us -> none  [shards(): gathered = lax.all_gather(hidden_grad, 'col', axis=0, tiled=True)]
    ppermute x0 -> x17, starting transfers between devices: none -> 29.2 us  [the longest x6 11.8 us: over_z(): lax.ppermute(v, 'row', [(r, r & 9 | ((r >> 1) + s & 3) << 1) for r in ran...]
    reshape x3 -> x0, local copies, waits for them, and re-layouts: 21.1 us -> none  [the longest x2 18.2 us: shards(): flat_sums = partial_value.reshape(col_tiles * TILE, features)]
    unnamed x10 -> x17, local copies, waits for them, and re-layouts: 25.2 us -> 6.72 us
    pallas_call x0 -> x9, Pallas kernels: none -> 16.9 us  [the longest x1 6.45 us: shards(): call(for_self, [((33, 256, T), f32)], [SMEM, VMEM, pl.BlockSpec(memory_sp...]
  transfers between devices with their start and end apart: 3 -> 19, of which waited for: 2 -> 7; matrix products, arithmetic and copies ran while one was open for 61% -> 1% of each run, Pallas kernels for 0% -> 9%
where the time goes in v1:
time: 99.3 us; the launch traced here: 97.8 us
  starting transfers between devices  39.8 us (40%)
  waiting for transfers between devices  17.8 us (18%)
  Pallas kernels  16.9 us (17%)
  blocking collectives  14.2 us (14%)
  local copies, waits for them, and re-layouts  7.5 us (8%)
  between operations  1.5 us (2%)
    all_to_all x1, blocking collectives, shards(): lax.all_to_all(jnp.broadcast_to(piece[None], (8, 16, 256)), 'col', 0, 0)  14.2 us
    ppermute x6, starting transfers between devices, over_z(): lax.ppermute(v, 'row', [(r, r & 9 | ((r >> 1) + s & 3) << 1) for r in ran...  11.8 us
    ppermute x6, starting transfers between devices, over_x(): lax.ppermute(v, 'col', [(c, ((c >> 1) + s & 3) * 2 + (c & 1)) for c in ra...  11 us
    ppermute x6, waiting for transfers between devices, over_z(): lax.ppermute(v, 'row', [(r, r & 9 | ((r >> 1) + s & 3) << 1) for r in ran...  10.8 us
    unnamed x17, local copies, waits for them, and re-layouts  6.72 us
    all_to_all x1, waiting for transfers between devices, shards(): pieces = lax.all_to_all(part.reshape(16, 16, 256), 'row', 0, 0)  6.58 us
    pallas_call x1, Pallas kernels, shards(): call(for_self, [((33, 256, T), f32)], [SMEM, VMEM, pl.BlockSpec(memory_sp...  6.45 us
    all_to_all x1, starting transfers between devices, shards(): pieces = lax.all_to_all(part.reshape(16, 16, 256), 'row', 0, 0)  6.43 us
  transfers between devices with their start and end apart: 19, of which 7 were waited for; matrix products, arithmetic and copies ran while one was open for 1% of the time, Pallas kernels for 9%

profile of v1, /device:TPU:0, one launch (start us, length us, event | category | flops | bytes accessed | tf_op | source)
XLA Modules:
  0.0 97.8 jit_solution(5259073363504389910)
XLA Ops:
  0.6 0.9 copy-done.1
  1.6 0.9 copy-done.2
  2.5 0.9 copy-done.3
  3.4 0.8 copy-done.4
  4.2 1.2 %prep.1 = (bf16[2,256,128]{2,1,0:T(8,128)(2,1)S(1)}, bf16[2,256,128]{2,1,0:T(8,128)(2,1)S(1)}, f32[256,256]{1,0:T(8,128)}) custom-call(bf16[512,256]{1,0:T(8,128)(2,1)S(1)} %copy-done.1, s32[16,512]{1,0:T(8,128)S(1)} %bitcast.11, bf16[512,256]{1,0:T(8,128)(2,1)S(1)} %copy-done.2, bf16[256,256]{1,0:T(8,128)(2,1)S(1)} %copy-done.3), custom_call_target="tpu_custom_call" | custom-call | flops 200000000 | tf_op jit(solution)/shard_map/prep/pallas_call | solution.py:218
  5.4 3.3 %collective-permute-start = (bf16[2,256,128]{2,1,0:T(8,128)(2,1)S(1)}, bf16[2,256,128]{2,1,0:T(8,128)(2,1)S(1)}, u32[]{:S(2)}, u32[]{:S(2)}) collective-permute-start(bf16[2,256,128]{2,1,0:T(8,128)(2,1)S(1)} %get-tuple-element.62), channel_id=1, source_target_pairs={{0,1},{1,0},{2,3},{3,2},{4,5},{5,4},{6,7},{7,6},{8,9},{9,8},{10,11... | collective-permute-start | bytes 393224 | tf_op jit(solution)/shard_map/ppermute | solution.py:206
  8.7 1.5 %collective-permute-start.3 = (bf16[2,256,128]{2,1,0:T(8,128)(2,1)S(1)}, bf16[2,256,128]{2,1,0:T(8,128)(2,1)S(1)}, u32[]{:S(2)}, u32[]{:S(2)}) collective-permute-start(bf16[2,256,128]{2,1,0:T(8,128)(2,1)S(1)} %get-tuple-element.64), channel_id=1, source_target_pairs={{0,2},{1,3},{2,4},{3,5},{4,6},{5,7},{6,0},{7,1},{8,10},{9,11},{10,... | collective-permute-start | bytes 393224 | tf_op jit(solution)/shard_map/ppermute | solution.py:203
  10.2 2.7 %collective-permute-start.2 = (bf16[2,256,128]{2,1,0:T(8,128)(2,1)S(1)}, bf16[2,256,128]{2,1,0:T(8,128)(2,1)S(1)}, u32[]{:S(2)}, u32[]{:S(2)}) collective-permute-start(bf16[2,256,128]{2,1,0:T(8,128)(2,1)S(1)} %get-tuple-element.64), channel_id=1, source_target_pairs={{0,4},{1,5},{2,6},{3,7},{4,0},{5,1},{6,2},{7,3},{8,12},{9,13},{10,... | collective-permute-start | bytes 393224 | tf_op jit(solution)/shard_map/ppermute | solution.py:203
  12.9 1.4 %collective-permute-start.1 = (bf16[2,256,128]{2,1,0:T(8,128)(2,1)S(1)}, bf16[2,256,128]{2,1,0:T(8,128)(2,1)S(1)}, u32[]{:S(2)}, u32[]{:S(2)}) collective-permute-start(bf16[2,256,128]{2,1,0:T(8,128)(2,1)S(1)} %get-tuple-element.64), channel_id=1, source_target_pairs={{0,6},{1,7},{2,0},{3,1},{4,2},{5,3},{6,4},{7,5},{8,14},{9,15},{10,... | collective-permute-start | bytes 393224 | tf_op jit(solution)/shard_map/ppermute | solution.py:203
  15.0 0.0 copy-start
  15.0 0.7 copy-done
  15.8 0.3 in_mask.1.mask_ref
  16.1 0.0 copy-start.5
  16.1 0.7 copy-done.5
  16.8 1.4 %order_slots.1 = (s32[8,384]{1,0:T(8,128)S(1)}, s32[8,384]{1,0:T(8,128)S(1)}) custom-call(s32[1]{0:T(128)} %bitcast.9.count_ref, s32[2,512]{1,0:T(2,128)S(1)} %bitcast.12), custom_call_target="tpu_custom_call" | custom-call | flops 10000000 | tf_op jit(solution)/shard_map/order_slots/pallas_call | solution.py:229
  18.2 0.0 collective-permute-done
  18.2 0.0 collective-permute-done.3
  18.2 0.5 collective-permute-done.2
  18.7 0.0 collective-permute-done.1
  18.8 0.4 collective-permute-start.7
  19.2 6.4 %all-to-all-start = ((f32[16,16,256]{2,1,0:T(8,128)}), f32[16,16,256]{2,1,0:T(8,128)S(1)}, u32[]{:S(2)}, u32[]{:S(2)}) async-start(f32[16,16,256]{2,1,0:T(8,128)} %bitcast.6), calls=%async_computation | async-start | bytes 524288 | tf_op jit(solution)/shard_map/all_to_all | solution.py:224
  25.7 1.4 %collective-permute-start.6 = (bf16[4,256,128]{2,1,0:T(8,128)(2,1)S(1)}, bf16[4,256,128]{2,1,0:T(8,128)(2,1)S(1)}, u32[]{:S(2)}, u32[]{:S(2)}) collective-permute-start(bf16[4,256,128]{2,1,0:T(8,128)(2,1)S(1)} %constant_dynamic-update-slice_fusion.a0), channel_id=1, source_target_pairs={{0,2},{1,3},{2,4},{3,5},{4,6},{5,7},{6,0},{7,1},{8,10},{9,11},{10,... | collective-permute-start | bytes 786440 | tf_op jit(solution)/shard_map/ppermute | solution.py:203
  27.1 2.7 %collective-permute-start.5 = (bf16[4,256,128]{2,1,0:T(8,128)(2,1)S(1)}, bf16[4,256,128]{2,1,0:T(8,128)(2,1)S(1)}, u32[]{:S(2)}, u32[]{:S(2)}) collective-permute-start(bf16[4,256,128]{2,1,0:T(8,128)(2,1)S(1)} %constant_dynamic-update-slice_fusion.a0), channel_id=1, source_target_pairs={{0,4},{1,5},{2,6},{3,7},{4,0},{5,1},{6,2},{7,3},{8,12},{9,13},{10,... | collective-permute-start | bytes 786440 | tf_op jit(solution)/shard_map/ppermute | solution.py:203
  29.8 1.3 %collective-permute-start.4 = (bf16[4,256,128]{2,1,0:T(8,128)(2,1)S(1)}, bf16[4,256,128]{2,1,0:T(8,128)(2,1)S(1)}, u32[]{:S(2)}, u32[]{:S(2)}) collective-permute-start(bf16[4,256,128]{2,1,0:T(8,128)(2,1)S(1)} %constant_dynamic-update-slice_fusion.a0), channel_id=1, source_target_pairs={{0,6},{1,7},{2,0},{3,1},{4,2},{5,3},{6,4},{7,5},{8,14},{9,15},{10,... | collective-permute-start | bytes 786440 | tf_op jit(solution)/shard_map/ppermute | solution.py:203
  31.0 6.6 %all-to-all-done = f32[16,16,256]{2,1,0:T(8,128)S(1)} async-done(((f32[16,16,256]{2,1,0:T(8,128)}), f32[16,16,256]{2,1,0:T(8,128)S(1)}, u32[]{:S(2)}, u32[]{:S(2)}) %all-to-all-start) | async-done | bytes 262176 | tf_op jit(solution)/shard_map/all_to_all | solution.py:224
  37.7 14.2 %all_to_all.15 = f32[8,16,256]{2,1,0:T(8,128)S(1)} all-to-all(f32[8,16,256]{2,1,0:T(8,128)S(1)} %broadcast_in_dim.4), channel_id=1, replica_groups=mesh['row'=16,'col'=8] {'col'}, dimensions={0} | all-to-all | bytes 262144 | tf_op jit(solution)/shard_map/all_to_all | solution.py:247
  51.9 0.0 collective-permute-done.6.a3
  51.9 5.3 %for_partner.1 = (bf16[32,256,128]{2,1,0:T(8,128)(2,1)S(1)}, bf16[33,256,128]{2,1,0:T(8,128)(2,1)S(1)}) custom-call(s32[8,384]{1,0:T(8,128)S(1)} %get-tuple-element.61.steps_ref, bf16[4,256,128]{2,1,0:T(8,128)(2,1)S(1)} %constant_dynamic-update-slice_fusion.a0, bf16[4,256,128]{2,1,0:T(8,128)(2,1)S(1)} %collective-permute-done.6.a3, ...), custom_call_target="tpu_custom_call" | custom-call | flops 4000000000 | bytes 8388608 | tf_op jit(solution)/shard_map/for_partner/pallas_call | solution.py:251
  57.2 0.1 collective-permute-start.8
  57.3 6.5 %for_self.1.acc_ref = f32[33,256,128]{2,1,0:T(8,128)S(1)} custom-call(s32[8,384]{1,0:T(8,128)S(1)} %get-tuple-element.60.steps_ref, bf16[33,256,128]{2,1,0:T(8,128)(2,1)S(1)} %get-tuple-element.76.h_ref, bf16[512,128,128]{2,1,0:T(8,128)(2,1)} %bitcast.14), custom_call_target="tpu_custom_call" | custom-call | flops 4000000000 | bytes 8388608 | tf_op jit(solution)/shard_map/for_self/pallas_call | solution.py:262
  63.8 1.2 %join_cores.1 = (f32[8,256,128]{2,1,0:T(8,128)S(1)}, bf16[8,256,128]{2,1,0:T(8,128)(2,1)}, f32[4,256,128]{2,1,0:T(8,128)S(1)}, bf16[4,256,128]{2,1,0:T(8,128)(2,...) custom-call(f32[33,256,128]{2,1,0:T(8,128)S(1)} %for_self.1.acc_ref, ...), custom_call_target="tpu_custom_call" | custom-call | flops 1000000 | tf_op jit(solution)/shard_map/join_cores/pallas_call | solution.py:273
  64.9 3.9 %collective-permute-start.11 = (bf16[4,256,128]{2,1,0:T(8,128)(2,1)}, bf16[4,256,128]{2,1,0:T(8,128)(2,1)S(1)}, u32[]{:S(2)}, u32[]{:S(2)}) collective-permute-start(bf16[4,256,128]{2,1,0:T(8,128)(2,1)} %get-tuple-element.90), channel_id=1, source_target_pairs={{0,32},{8,40},{16,48},{24,56},{32,0},{40,8},{48,16},{56,24},{64,96... | collective-permute-start | bytes 786440 | tf_op jit(solution)/shard_map/ppermute | solution.py:209
  68.9 2.6 %collective-permute-start.12 = (bf16[4,256,128]{2,1,0:T(8,128)(2,1)S(1)}, bf16[4,256,128]{2,1,0:T(8,128)(2,1)S(1)}, u32[]{:S(2)}, u32[]{:S(2)}) collective-permute-start(bf16[4,256,128]{2,1,0:T(8,128)(2,1)S(1)} %get-tuple-element.91), channel_id=1, source_target_pairs={{0,48},{8,56},{16,0},{24,8},{32,16},{40,24},{48,32},{56,40},{64,11... | collective-permute-start | bytes 786440 | tf_op jit(solution)/shard_map/ppermute | solution.py:209
  71.5 0.7 broadcast_in_dim.5
  72.2 4.2 %all-to-all-start.2 = ((f32[16,16,256]{2,1,0:T(8,128)}), f32[16,16,256]{2,1,0:T(8,128)}, u32[]{:S(2)}, u32[]{:S(2)}) async-start(f32[16,16,256]{2,1,0:T(8,128)} %broadcast_in_dim.5), calls=%async_computation.2 | async-start | bytes 524288 | tf_op jit(solution)/shard_map/all_to_all | solution.py:290
  76.4 5.4 %collective-permute-done.11.g2 = bf16[4,256,128]{2,1,0:T(8,128)(2,1)S(1)} collective-permute-done((bf16[4,256,128]{2,1,0:T(8,128)(2,1)}, bf16[4,256,128]{2,1,0:T(8,128)(2,1)S(1)}, u32[]{:S(2)}, u32[]{:S(2)}) %collective-permute-start.11) | collective-permute-done | bytes 262176 | tf_op jit(solution)/shard_map/ppermute | solution.py:209
  81.8 0.8 collective-permute-done.12.g3
  82.6 0.1 join_b.1
  82.7 2.6 %collective-permute-start.16 = (bf16[2,256,128]{2,1,0:T(8,128)(2,1)S(1)}, bf16[2,256,128]{2,1,0:T(8,128)(2,1)S(1)}, u32[]{:S(2)}, u32[]{:S(2)}) collective-permute-start(bf16[2,256,128]{2,1,0:T(8,128)(2,1)S(1)} %get-tuple-element.100), channel_id=1, source_target_pairs={{0,64},{8,72},{16,80},{24,88},{32,96},{40,104},{48,112},{56,120},{... | collective-permute-start | bytes 393224 | tf_op jit(solution)/shard_map/ppermute | solution.py:212
  85.3 0.1 join_a.1
  85.4 1.6 %collective-permute-start.13 = (bf16[2,256,128]{2,1,0:T(8,128)(2,1)S(1)}, bf16[2,256,128]{2,1,0:T(8,128)(2,1)S(1)}, u32[]{:S(2)}, u32[]{:S(2)}) collective-permute-start(bf16[2,256,128]{2,1,0:T(8,128)(2,1)S(1)} %get-tuple-element.96), channel_id=1, source_target_pairs={{0,16},{8,24},{16,32},{24,40},{32,48},{40,56},{48,0},{56,8},{64,80... | collective-permute-start | bytes 393224 | tf_op jit(solution)/shard_map/ppermute | solution.py:209
  87.0 2.3 %collective-permute-start.14 = (bf16[2,256,128]{2,1,0:T(8,128)(2,1)S(1)}, bf16[2,256,128]{2,1,0:T(8,128)(2,1)S(1)}, u32[]{:S(2)}, u32[]{:S(2)}) collective-permute-start(bf16[2,256,128]{2,1,0:T(8,128)(2,1)S(1)} %get-tuple-element.97), channel_id=1, source_target_pairs={{0,32},{8,40},{16,48},{24,56},{32,0},{40,8},{48,16},{56,24},{64,96... | collective-permute-start | bytes 393224 | tf_op jit(solution)/shard_map/ppermute | solution.py:209
  89.3 1.3 %collective-permute-start.15 = (bf16[2,256,128]{2,1,0:T(8,128)(2,1)S(1)}, bf16[2,256,128]{2,1,0:T(8,128)(2,1)S(1)}, u32[]{:S(2)}, u32[]{:S(2)}) collective-permute-start(bf16[2,256,128]{2,1,0:T(8,128)(2,1)S(1)} %get-tuple-element.98), channel_id=1, source_target_pairs={{0,48},{8,56},{16,0},{24,8},{32,16},{40,24},{48,32},{56,40},{64,11... | collective-permute-start | bytes 393224 | tf_op jit(solution)/shard_map/ppermute | solution.py:209
  90.7 1.7 %collective-permute-done.13.g1 = bf16[2,256,128]{2,1,0:T(8,128)(2,1)S(1)} collective-permute-done((bf16[2,256,128]{2,1,0:T(8,128)(2,1)S(1)}, bf16[2,256,128]{2,1,0:T(8,128)(2,1)S(1)}, u32[]{:S(2)}, u32[]{:S(2)}) %collective-permute-start.13) | collective-permute-done | bytes 131104 | tf_op jit(solution)/shard_map/ppermute | solution.py:209
  92.4 2.8 %collective-permute-done.14.g2 = bf16[2,256,128]{2,1,0:T(8,128)(2,1)S(1)} collective-permute-done((bf16[2,256,128]{2,1,0:T(8,128)(2,1)S(1)}, bf16[2,256,128]{2,1,0:T(8,128)(2,1)S(1)}, u32[]{:S(2)}, u32[]{:S(2)}) %collective-permute-start.14) | collective-permute-done | bytes 131104 | tf_op jit(solution)/shard_map/ppermute | solution.py:209
  95.2 0.1 collective-permute-done.15.g3
  95.2 0.9 finish.1
  96.1 1.7 %copy.16 = f32[256,256]{1,0:T(8,128)} copy(f32[256,256]{1,0:T(8,128)} %bitcast.7) | data formatting | bytes 524288
  (23 shorter events, 0.2 us)
Async XLA Ops:
  0.6 1.0 copy-start.1
  1.6 0.9 copy-start.2
  2.5 0.9 copy-start.3
  3.4 0.8 copy-start.4
  5.4 12.8 %collective-permute-start = (bf16[2,256,128]{2,1,0:T(8,128)(2,1)S(1)}, bf16[2,256,128]{2,1,0:T(8,128)(2,1)S(1)}, u32[]{:S(2)}, u32[]{:S(2)}) collective-permute-start(bf16[2,256,128]{2,1,0:T(8,128)(2,1)S(1)} %get-tuple-element.62), channel_id=1, source_target_pairs={{0,1},{1,0},{2,3},{3,2},{4,5},{5,4},{6,7},{7,6},{8,9},{9,8},{10,11... | collective-permute-start | bytes 393224 | tf_op jit(solution)/shard_map/ppermute | solution.py:206
  8.7 9.5 %collective-permute-start.3 = (bf16[2,256,128]{2,1,0:T(8,128)(2,1)S(1)}, bf16[2,256,128]{2,1,0:T(8,128)(2,1)S(1)}, u32[]{:S(2)}, u32[]{:S(2)}) collective-permute-start(bf16[2,256,128]{2,1,0:T(8,128)(2,1)S(1)} %get-tuple-element.64), channel_id=1, source_target_pairs={{0,2},{1,3},{2,4},{3,5},{4,6},{5,7},{6,0},{7,1},{8,10},{9,11},{10,... | collective-permute-start | bytes 393224 | tf_op jit(solution)/shard_map/ppermute | solution.py:203
  10.2 8.5 %collective-permute-start.2 = (bf16[2,256,128]{2,1,0:T(8,128)(2,1)S(1)}, bf16[2,256,128]{2,1,0:T(8,128)(2,1)S(1)}, u32[]{:S(2)}, u32[]{:S(2)}) collective-permute-start(bf16[2,256,128]{2,1,0:T(8,128)(2,1)S(1)} %get-tuple-element.64), channel_id=1, source_target_pairs={{0,4},{1,5},{2,6},{3,7},{4,0},{5,1},{6,2},{7,3},{8,12},{9,13},{10,... | collective-permute-start | bytes 393224 | tf_op jit(solution)/shard_map/ppermute | solution.py:203
  12.9 5.7 %collective-permute-start.1 = (bf16[2,256,128]{2,1,0:T(8,128)(2,1)S(1)}, bf16[2,256,128]{2,1,0:T(8,128)(2,1)S(1)}, u32[]{:S(2)}, u32[]{:S(2)}) collective-permute-start(bf16[2,256,128]{2,1,0:T(8,128)(2,1)S(1)} %get-tuple-element.64), channel_id=1, source_target_pairs={{0,6},{1,7},{2,0},{3,1},{4,2},{5,3},{6,4},{7,5},{8,14},{9,15},{10,... | collective-permute-start | bytes 393224 | tf_op jit(solution)/shard_map/ppermute | solution.py:203
  15.0 0.8 copy-start
  16.1 0.7 copy-start.5
  18.8 33.1 %collective-permute-start.7 = (bf16[8,256,128]{2,1,0:T(8,128)(2,1)S(1)}, bf16[8,256,128]{2,1,0:T(8,128)(2,1)S(1)}, u32[]{:S(2)}, u32[]{:S(2)}) collective-permute-start(bf16[8,256,128]{2,1,0:T(8,128)(2,1)S(1)} %constant_dynamic-update-slice_fusion.2.b0), channel_id=1, source_target_pairs={{0,1},{1,0},{2,3},{3,2},{4,5},{5,4},{6,7},{7,6},{8,9},{9,8},{10,11... | collective-permute-start | bytes 1572872 | tf_op jit(solution)/shard_map/ppermute | solution.py:206
  19.2 18.4 %all-to-all-start = ((f32[16,16,256]{2,1,0:T(8,128)}), f32[16,16,256]{2,1,0:T(8,128)S(1)}, u32[]{:S(2)}, u32[]{:S(2)}) async-start(f32[16,16,256]{2,1,0:T(8,128)} %bitcast.6), calls=%async_computation | async-start | bytes 524288 | tf_op jit(solution)/shard_map/all_to_all | solution.py:224
  25.7 26.2 %collective-permute-start.6 = (bf16[4,256,128]{2,1,0:T(8,128)(2,1)S(1)}, bf16[4,256,128]{2,1,0:T(8,128)(2,1)S(1)}, u32[]{:S(2)}, u32[]{:S(2)}) collective-permute-start(bf16[4,256,128]{2,1,0:T(8,128)(2,1)S(1)} %constant_dynamic-update-slice_fusion.a0), channel_id=1, source_target_pairs={{0,2},{1,3},{2,4},{3,5},{4,6},{5,7},{6,0},{7,1},{8,10},{9,11},{10,... | collective-permute-start | bytes 786440 | tf_op jit(solution)/shard_map/ppermute | solution.py:203
  27.1 24.8 %collective-permute-start.5 = (bf16[4,256,128]{2,1,0:T(8,128)(2,1)S(1)}, bf16[4,256,128]{2,1,0:T(8,128)(2,1)S(1)}, u32[]{:S(2)}, u32[]{:S(2)}) collective-permute-start(bf16[4,256,128]{2,1,0:T(8,128)(2,1)S(1)} %constant_dynamic-update-slice_fusion.a0), channel_id=1, source_target_pairs={{0,4},{1,5},{2,6},{3,7},{4,0},{5,1},{6,2},{7,3},{8,12},{9,13},{10,... | collective-permute-start | bytes 786440 | tf_op jit(solution)/shard_map/ppermute | solution.py:203
  29.8 22.1 %collective-permute-start.4 = (bf16[4,256,128]{2,1,0:T(8,128)(2,1)S(1)}, bf16[4,256,128]{2,1,0:T(8,128)(2,1)S(1)}, u32[]{:S(2)}, u32[]{:S(2)}) collective-permute-start(bf16[4,256,128]{2,1,0:T(8,128)(2,1)S(1)} %constant_dynamic-update-slice_fusion.a0), channel_id=1, source_target_pairs={{0,6},{1,7},{2,0},{3,1},{4,2},{5,3},{6,4},{7,5},{8,14},{9,15},{10,... | collective-permute-start | bytes 786440 | tf_op jit(solution)/shard_map/ppermute | solution.py:203
  57.2 6.6 %collective-permute-start.8 = (bf16[32,256,128]{2,1,0:T(8,128)(2,1)S(1)}, bf16[32,256,128]{2,1,0:T(8,128)(2,1)S(1)}, u32[]{:S(2)}, u32[]{:S(2)}) collective-permute-start(bf16[32,256,128]{2,1,0:T(8,128)(2,1)S(1)} %get-tuple-element.77), channel_id=1, source_target_pairs={{0,8},{8,0},{16,24},{24,16},{32,40},{40,32},{48,56},{56,48},{64,72... | collective-permute-start | bytes 6291464 | tf_op jit(solution)/shard_map/ppermute | solution.py:215
  64.9 20.4 %collective-permute-start.9 = (bf16[8,256,128]{2,1,0:T(8,128)(2,1)}, bf16[8,256,128]{2,1,0:T(8,128)(2,1)S(1)}, u32[]{:S(2)}, u32[]{:S(2)}) collective-permute-start(bf16[8,256,128]{2,1,0:T(8,128)(2,1)} %get-tuple-element.86), channel_id=1, source_target_pairs={{0,64},{8,72},{16,80},{24,88},{32,96},{40,104},{48,112},{56,120},{... | collective-permute-start | bytes 1572872 | tf_op jit(solution)/shard_map/ppermute | solution.py:212
  64.9 11.5 %collective-permute-start.10 = (bf16[4,256,128]{2,1,0:T(8,128)(2,1)}, bf16[4,256,128]{2,1,0:T(8,128)(2,1)S(1)}, u32[]{:S(2)}, u32[]{:S(2)}) collective-permute-start(bf16[4,256,128]{2,1,0:T(8,128)(2,1)} %get-tuple-element.89), channel_id=1, source_target_pairs={{0,16},{8,24},{16,32},{24,40},{32,48},{40,56},{48,0},{56,8},{64,80... | collective-permute-start | bytes 786440 | tf_op jit(solution)/shard_map/ppermute | solution.py:209
  64.9 16.9 %collective-permute-start.11 = (bf16[4,256,128]{2,1,0:T(8,128)(2,1)}, bf16[4,256,128]{2,1,0:T(8,128)(2,1)S(1)}, u32[]{:S(2)}, u32[]{:S(2)}) collective-permute-start(bf16[4,256,128]{2,1,0:T(8,128)(2,1)} %get-tuple-element.90), channel_id=1, source_target_pairs={{0,32},{8,40},{16,48},{24,56},{32,0},{40,8},{48,16},{56,24},{64,96... | collective-permute-start | bytes 786440 | tf_op jit(solution)/shard_map/ppermute | solution.py:209
  68.9 13.7 %collective-permute-start.12 = (bf16[4,256,128]{2,1,0:T(8,128)(2,1)S(1)}, bf16[4,256,128]{2,1,0:T(8,128)(2,1)S(1)}, u32[]{:S(2)}, u32[]{:S(2)}) collective-permute-start(bf16[4,256,128]{2,1,0:T(8,128)(2,1)S(1)} %get-tuple-element.91), channel_id=1, source_target_pairs={{0,48},{8,56},{16,0},{24,8},{32,16},{40,24},{48,32},{56,40},{64,11... | collective-permute-start | bytes 786440 | tf_op jit(solution)/shard_map/ppermute | solution.py:209
  72.2 18.5 %all-to-all-start.2 = ((f32[16,16,256]{2,1,0:T(8,128)}), f32[16,16,256]{2,1,0:T(8,128)}, u32[]{:S(2)}, u32[]{:S(2)}) async-start(f32[16,16,256]{2,1,0:T(8,128)} %broadcast_in_dim.5), calls=%async_computation.2 | async-start | bytes 524288 | tf_op jit(solution)/shard_map/all_to_all | solution.py:290
  82.7 7.9 %collective-permute-start.16 = (bf16[2,256,128]{2,1,0:T(8,128)(2,1)S(1)}, bf16[2,256,128]{2,1,0:T(8,128)(2,1)S(1)}, u32[]{:S(2)}, u32[]{:S(2)}) collective-permute-start(bf16[2,256,128]{2,1,0:T(8,128)(2,1)S(1)} %get-tuple-element.100), channel_id=1, source_target_pairs={{0,64},{8,72},{16,80},{24,88},{32,96},{40,104},{48,112},{56,120},{... | collective-permute-start | bytes 393224 | tf_op jit(solution)/shard_map/ppermute | solution.py:212
  85.4 6.9 %collective-permute-start.13 = (bf16[2,256,128]{2,1,0:T(8,128)(2,1)S(1)}, bf16[2,256,128]{2,1,0:T(8,128)(2,1)S(1)}, u32[]{:S(2)}, u32[]{:S(2)}) collective-permute-start(bf16[2,256,128]{2,1,0:T(8,128)(2,1)S(1)} %get-tuple-element.96), channel_id=1, source_target_pairs={{0,16},{8,24},{16,32},{24,40},{32,48},{40,56},{48,0},{56,8},{64,80... | collective-permute-start | bytes 393224 | tf_op jit(solution)/shard_map/ppermute | solution.py:209
  87.0 8.2 %collective-permute-start.14 = (bf16[2,256,128]{2,1,0:T(8,128)(2,1)S(1)}, bf16[2,256,128]{2,1,0:T(8,128)(2,1)S(1)}, u32[]{:S(2)}, u32[]{:S(2)}) collective-permute-start(bf16[2,256,128]{2,1,0:T(8,128)(2,1)S(1)} %get-tuple-element.97), channel_id=1, source_target_pairs={{0,32},{8,40},{16,48},{24,56},{32,0},{40,8},{48,16},{56,24},{64,96... | collective-permute-start | bytes 393224 | tf_op jit(solution)/shard_map/ppermute | solution.py:209
  89.3 5.9 %collective-permute-start.15 = (bf16[2,256,128]{2,1,0:T(8,128)(2,1)S(1)}, bf16[2,256,128]{2,1,0:T(8,128)(2,1)S(1)}, u32[]{:S(2)}, u32[]{:S(2)}) collective-permute-start(bf16[2,256,128]{2,1,0:T(8,128)(2,1)S(1)} %get-tuple-element.98), channel_id=1, source_target_pairs={{0,48},{8,56},{16,0},{24,8},{32,16},{40,24},{48,32},{56,40},{64,11... | collective-permute-start | bytes 393224 | tf_op jit(solution)/shard_map/ppermute | solution.py:209

commit v2 on v1

--- a/solution.py
+++ b/solution.py
@@ -10,13 +10,15 @@
 T = 128
 N_STEP = 384
 UNROLL = 16
-LIMIT = 40
-AHEAD = 3
+LIMIT = 28
+PREP_LIMIT = 61
+STAGE_LIMIT = 24
 ZERO_ROW = 32
 bf16 = jnp.bfloat16
 f32 = jnp.float32
 tie = lambda *values: lax.optimization_barrier(values)
 VMEM = pl.BlockSpec(memory_space=pltpu.VMEM)
+ANY = pl.BlockSpec(memory_space=pl.ANY)
 SMEM = pl.BlockSpec(memory_space=pltpu.SMEM)
 
 
@@ -49,13 +51,35 @@
     return ((byte >> (lane & 7)) & 1) == 1
 
 
-def prep(grad_ref, words_ref, agg_ref, weight_ref, ha_ref, hb_ref, wp_ref):
-    masked = jnp.where(mask_of(words_ref[...]), grad_ref[...], jnp.zeros((), bf16))
-    hidden = contract(weight_ref[...], masked, 1, 1).astype(bf16)
+def prep(grad_hbm, words_hbm, agg_hbm, weight_hbm, ha_ref, hb_ref, keep_ref, send_ref, grad, words, agg, weight, part, sems):
+    copies = [
+        pltpu.make_async_copy(src, dst, sems.at[i])
+        for i, (src, dst) in enumerate(((words_hbm, words), (grad_hbm, grad), (weight_hbm, weight), (agg_hbm, agg)))
+    ]
+    for copy in copies:
+        copy.start()
+    copies[0].wait()
+    mask = mask_of(words[...])
+    copies[1].wait()
+    masked = jnp.where(mask, grad[...], jnp.zeros((), bf16))
+    copies[2].wait()
+    hidden = contract(weight[...], masked, 1, 1).astype(bf16)
     for t in range(4):
         ref = ha_ref if t < 2 else hb_ref
         ref[t & 1] = hidden[:, t * T : (t + 1) * T]
-    wp_ref[...] = contract(agg_ref[...], masked, 0, 0) * (1.0 / 256.0)
+    copies[3].wait()
+    part[...] = contract(agg[...], masked, 0, 0) * (1.0 / 256.0)
+    core = lax.axis_index("row") & 1
+    keep_ref[...] = part[pl.ds(pl.multiple_of(core * T, T), T)]
+    send_ref[...] = part[pl.ds(pl.multiple_of((1 - core) * T, T), T)]
+
+
+def add_two(a, b, out):
+    out[...] = a[...] + b[...]
+
+
+def add_ring(own, left, across, right, out):
+    out[...] = (own[...] + across[...]) + (left[...] + right[...])
 
 
 def in_mask(words_ref, out_ref):
@@ -102,21 +126,21 @@
         ref[4:8, :] = jnp.zeros((4, N_STEP), jnp.int32)
 
 
-def products(steps_ref, h_ref, tiles_ref, acc_ref, buf, sems):
-    groups = (steps_ref[3, 0] + UNROLL - 1) // UNROLL
-
-    def fetch(g):
-        slot = lax.rem(g, AHEAD + 1)
-        for u in range(UNROLL):
-            for side in range(2):
-                word = steps_ref[1 + side, g * UNROLL + u]
-                pltpu.make_async_copy(
-                    tiles_ref.at[word & 511], buf.at[slot * 2 * UNROLL + 2 * u + side], sems.at[slot]
-                ).start()
-
-    for g in range(AHEAD):
-        pl.when(g < groups)(lambda g=g: fetch(g))
-
+def stage(count_ref, tiles_ref, out_ref, sems):
+    chunk = tiles_ref.shape[0] // 8
+
+    def copy(i):
+        part = pl.ds(i * chunk, chunk)
+        return pltpu.make_async_copy(tiles_ref.at[part], out_ref.at[part], sems.at[i])
+
+    used = (count_ref[0] + chunk - 1) // chunk
+    for i in range(8):
+        pl.when(i < used)(lambda i=i: copy(i).start())
+    for i in range(8):
+        pl.when(i < used)(lambda i=i: copy(i).wait())
+
+
+def products(steps_ref, h_ref, tiles_ref, acc_ref):
     def clear(k, carry):
         acc_ref[k] = jnp.zeros((256, T), f32)
         return carry
@@ -124,28 +148,25 @@
     lax.fori_loop(0, 33, clear, 0)
 
     def some(g, carry):
-        slot = lax.rem(g, AHEAD + 1)
-        part = pl.ds(pl.multiple_of(slot * 2 * UNROLL, 2 * UNROLL), 2 * UNROLL)
-        pl.when(g + AHEAD < groups)(lambda: fetch(g + AHEAD))
-        pltpu.make_async_copy(tiles_ref.at[pl.ds(0, 2 * UNROLL)], buf.at[part], sems.at[slot]).wait()
         results = []
         for u in range(UNROLL):
             s = g * UNROLL + u
-            left = jnp.concatenate([h_ref[steps_ref[1 + side, s] >> 9] for side in range(2)], 1)
-            right = jnp.concatenate([buf[slot * 2 * UNROLL + 2 * u + side] for side in range(2)], 0)
+            a, b = steps_ref[1, s], steps_ref[2, s]
+            left = jnp.concatenate([h_ref[a >> 9], h_ref[b >> 9]], 1)
+            right = jnp.concatenate([tiles_ref[a & 511], tiles_ref[b & 511]], 0)
             results.append((steps_ref[0, s], jnp.dot(left, right, preferred_element_type=f32)))
         for k, result in results:
             acc_ref[k] += result
         return carry
 
-    lax.fori_loop(0, groups, some, 0)
-
-
-def for_partner(steps_ref, a0, a3, a1, a2, b0, b1, tiles_ref, out_ref, h_ref, acc_ref, buf, sems):
+    lax.fori_loop(0, (steps_ref[3, 0] + UNROLL - 1) // UNROLL, some, 0)
+
+
+def for_partner(steps_ref, a0, a3, a1, a2, b0, b1, tiles_ref, out_ref, h_ref, acc_ref):
     h_ref[0:4], h_ref[4:8], h_ref[8:12], h_ref[12:16] = a0[...], a1[...], a2[...], a3[...]
     h_ref[16:24], h_ref[24:32] = b0[...], b1[...]
     h_ref[ZERO_ROW] = jnp.zeros((256, T), bf16)
-    products(steps_ref, h_ref, tiles_ref, acc_ref, buf, sems)
+    products(steps_ref, h_ref, tiles_ref, acc_ref)
 
     def narrow(k, carry):
         out_ref[k] = acc_ref[k].astype(bf16)
@@ -154,11 +175,11 @@
     lax.fori_loop(0, 32, narrow, 0)
 
 
-def for_self(steps_ref, h_ref, tiles_ref, acc_ref, buf, sems):
-    products(steps_ref, h_ref, tiles_ref, acc_ref, buf, sems)
-
-
-def join_cores(acc_ref, got_ref, a_keep, a_y, b_keep, b_z1, b_z2, b_z3):
+def for_self(steps_ref, h_ref, tiles_ref, acc_ref):
+    products(steps_ref, h_ref, tiles_ref, acc_ref)
+
+
+def join_cores(acc_ref, got_ref, w, wl, wx, wr, a_keep, a_y, b_keep, b_z1, b_z2, b_z3, w_out):
     def add(k):
         return acc_ref[k] + got_ref[k].astype(f32)
 
@@ -170,13 +191,15 @@
         b_z1[k] = add(20 + k).astype(bf16)
         b_z2[k] = add(24 + k).astype(bf16)
         b_z3[k] = add(28 + k).astype(bf16)
-
-
-def join_a(keep_ref, got_ref, a_keep, a_z1, a_z2, a_z3):
+    add_ring(w, wl, wx, wr, w_out)
+
+
+def join_a(keep_ref, got_ref, w, w_got, a_keep, a_z1, a_z2, a_z3, w_out):
     for t in range(2):
         a_keep[t] = keep_ref[t] + got_ref[t].astype(f32)
         for dz, ref in ((1, a_z1), (2, a_z2), (3, a_z3)):
             ref[t] = (keep_ref[2 * dz + t] + got_ref[2 * dz + t].astype(f32)).astype(bf16)
+    add_two(w, w_got, w_out)
 
 
 def join_b(keep_ref, g1, g2, g3, b_keep, b_y):
@@ -188,7 +211,10 @@
             b_y[k - 2] = total.astype(bf16)
 
 
-def finish(a_keep, g1, g2, g3, b_keep, gy, mask_ref, out_ref):
+def finish(a_keep, g1, g2, g3, b_keep, gy, mask_ref, w, w_got, out_ref, weight_ref):
+    core = lax.axis_index("row") & 1
+    weight_ref[pl.ds(pl.multiple_of(core * T, T), T)] = w[...]
+    weight_ref[pl.ds(pl.multiple_of((1 - core) * T, T), T)] = w_got[...]
     for t in range(4):
         if t < 2:
             total = a_keep[t] + g1[t].astype(f32) + g2[t].astype(f32) + g3[t].astype(f32)
@@ -214,85 +240,105 @@
     def over_core(v):
         return lax.ppermute(v, "row", [(r, r ^ 1) for r in range(16)])
 
-    half = (2, 256, T)
-    ha, hb, part = call(
-        prep, [(half, bf16), (half, bf16), ((256, 256), f32)], [VMEM] * 4, "prep", flops=2 * 10**8
+    half, quad, part = (2, 256, T), (4, 256, T), (T, 256)
+    ha, hb, w, w_send = call(
+        prep,
+        [(half, bf16), (half, bf16), (part, f32), (part, f32)],
+        [ANY] * 4,
+        "prep",
+        limit=PREP_LIMIT,
+        scratch=[
+            pltpu.VMEM((512, 256), bf16),
+            pltpu.VMEM((16, 512), jnp.int32),
+            pltpu.VMEM((512, 256), bf16),
+            pltpu.VMEM((256, 256), bf16),
+            pltpu.VMEM((256, 256), f32),
+            pltpu.SemaphoreType.DMA((4,)),
+        ],
+        flops=2 * 10**8,
     )(out_grad, out_bits.T, agg_saved, weight)
 
     ha_y = over_y_hi(ha)
     hb_1, hb_2, hb_3 = over_x(hb, -1), over_x(hb, 2), over_x(hb, 1)
-    pieces = lax.all_to_all(part.reshape(16, 16, 256), "row", 0, 0)
-
+    w_got = over_core(w_send)
     count, coords, words, own_tiles, ha = tie(
         tile_count.reshape(1), tile_coords[0, 0].T, in_bits.T, tiles[0, 0], ha
     )
     sib_steps, own_steps = call(
-        order_slots,
-        [((8, N_STEP), jnp.int32)] * 2,
-        [SMEM, VMEM],
-        "order_slots",
-        flops=10**7,
+        order_slots, [((8, N_STEP), jnp.int32)] * 2, [SMEM, VMEM], "order_slots", flops=10**7
     )(count, coords)
     (mask,) = call(in_mask, [((512, 256), bf16)], [VMEM], "in_mask", flops=10**7)(words)
-
-    ha, ha_y, hb, hb_1, hb_2, hb_3, sib_steps, own_steps, mask = tie(
-        ha, ha_y, hb, hb_1, hb_2, hb_3, sib_steps, own_steps, mask
+    ha, ha_y, hb, hb_1, hb_2, hb_3, sib_steps, own_steps, mask, w_got = tie(
+        ha, ha_y, hb, hb_1, hb_2, hb_3, sib_steps, own_steps, mask, w_got
     )
+
     a0 = jnp.concatenate([ha, ha_y], 0)
     b0 = jnp.concatenate([hb, hb_1, hb_2, hb_3], 0)
     a3, a1, a2 = over_x(a0, 1), over_x(a0, -1), over_x(a0, 2)
     b1 = over_y_hi(b0)
-
-    piece = jnp.sum(pieces, 0)
-    pieces = lax.all_to_all(jnp.broadcast_to(piece[None], (8, 16, 256)), "col", 0, 0)
-    piece = jnp.sum(pieces, 0)
-    a0, a1, a2, a3, b0, b1, piece = tie(a0, a1, a2, a3, b0, b1, piece)
-    fetching = [pltpu.VMEM(((AHEAD + 1) * 2 * UNROLL, T, T), bf16), pltpu.SemaphoreType.DMA((AHEAD + 1,))]
+    add = functools.partial(call, outs=[(part, f32)], limit=2)
+    (w,) = add(add_two, ins=[VMEM] * 2, name="w_core")(w, w_got)
+    w_got = over_y_hi(w)
+    count, own_tiles, w = tie(count, own_tiles, w)
+    (own_tiles,) = call(
+        stage,
+        [(own_tiles.shape, bf16)],
+        [SMEM, ANY],
+        "stage",
+        limit=STAGE_LIMIT,
+        scratch=[pltpu.SemaphoreType.DMA((8,))],
+        flops=10**9,
+    )(count, own_tiles)
+    (w,) = add(add_two, ins=[VMEM] * 2, name="w_y")(w, w_got)
+    a0, a1, a2, a3, b0, b1, own_tiles, w = tie(a0, a1, a2, a3, b0, b1, own_tiles, w)
+
+    w_3, w_1, w_2 = over_x(w, 1), over_x(w, -1), over_x(w, 2)
     to_partner, hidden = call(
         for_partner,
         [((32, 256, T), bf16), ((33, 256, T), bf16)],
-        [SMEM] + [VMEM] * 6 + [pl.BlockSpec(memory_space=pl.ANY)],
+        [SMEM] + [VMEM] * 7,
         "for_partner",
         limit=LIMIT,
-        scratch=[pltpu.VMEM((33, 256, T), f32)] + fetching,
+        scratch=[pltpu.VMEM((33, 256, T), f32)],
         flops=4 * 10**9,
         touched=2**23,
     )(sib_steps, a0, a3, a1, a2, b0, b1, own_tiles)
+    to_partner, hidden, w, w_1, w_2, w_3 = tie(to_partner, hidden, w, w_1, w_2, w_3)
     from_partner = over_core(to_partner)
+    (w,) = add(add_ring, ins=[VMEM] * 4, name="w_x")(w, w_1, w_2, w_3)
+    hidden, w = tie(hidden, w)
+    w_3, w_1, w_2 = over_z(w, 1), over_z(w, -1), over_z(w, 2)
     (acc,) = call(
         for_self,
         [((33, 256, T), f32)],
-        [SMEM, VMEM, pl.BlockSpec(memory_space=pl.ANY)],
+        [SMEM, VMEM, VMEM],
         "for_self",
         limit=LIMIT,
-        scratch=fetching,
         flops=4 * 10**9,
         touched=2**23,
     )(own_steps, hidden, own_tiles)
-    quad = (4, 256, T)
-    a_keep, a_y, b_keep, b_z1, b_z2, b_z3 = call(
+    a_keep, a_y, b_keep, b_z1, b_z2, b_z3, w = call(
         join_cores,
-        [((8, 256, T), f32), ((8, 256, T), bf16), (quad, f32)] + [(quad, bf16)] * 3,
-        [VMEM] * 2,
+        [((8, 256, T), f32), ((8, 256, T), bf16), (quad, f32)] + [(quad, bf16)] * 3 + [(part, f32)],
+        [VMEM] * 6,
         "join_cores",
         flops=10**6,
-    )(acc, from_partner)
-
-    a_keep, a_y, b_keep, b_z1, b_z2, b_z3, piece = tie(a_keep, a_y, b_keep, b_z1, b_z2, b_z3, piece)
+    )(acc, from_partner, w, w_1, w_2, w_3)
+
     a_got = over_y_lo(a_y)
     b_got = [over_z(b_z1, 1), over_z(b_z2, 2), over_z(b_z3, -1)]
-    a_keep, a_z1, a_z2, a_z3 = call(
-        join_a, [(half, f32)] + [(half, bf16)] * 3, [VMEM] * 2, "join_a", flops=10**6
-    )(a_keep, a_got)
+    w_got = over_y_lo(w)
+    a_got, w_got, b_got[0], b_got[1], b_got[2] = tie(a_got, w_got, *b_got)
+    a_keep, a_z1, a_z2, a_z3, w = call(
+        join_a, [(half, f32)] + [(half, bf16)] * 3 + [(part, f32)], [VMEM] * 4, "join_a", flops=10**6
+    )(a_keep, a_got, w, w_got)
     a_got = [over_z(a_z1, 1), over_z(a_z2, 2), over_z(a_z3, -1)]
     b_keep, b_y = call(join_b, [(half, f32), (half, bf16)], [VMEM] * 4, "join_b", flops=10**6)(b_keep, *b_got)
     b_got = over_y_lo(b_y)
-    pieces = lax.all_to_all(jnp.broadcast_to(piece[None], (16, 16, 256)), "row", 0, 0)
-    weight_grad = pieces.reshape(256, 256)
-    a_keep, b_keep, weight_grad = tie(a_keep, b_keep, weight_grad)
-    (prev_grad,) = call(finish, [((512, 256), bf16)], [VMEM] * 7, "finish", flops=10**6)(
-        a_keep, *a_got, b_keep, b_got, mask
-    )
+    w_got = over_core(w)
+    prev_grad, weight_grad = call(
+        finish, [((512, 256), bf16), ((256, 256), f32)], [VMEM] * 9, "finish", flops=10**6
+    )(a_keep, *a_got, b_keep, b_got, mask, w, w_got)
     return weight_grad, prev_grad
 
 

time: 99.3 us -> 88.2 us (0.89)
  blocking collectives: 14.2 us -> 0 us
  Pallas kernels: 16.9 us -> 20.4 us
  local copies, waits for them, and re-layouts: 7.5 us -> 4.25 us
  waiting for transfers between devices: 17.8 us -> 20.8 us
    all_to_all x1 -> x0, blocking collectives: 14.2 us -> none  [shards(): lax.all_to_all(jnp.broadcast_to(piece[None], (8, 16, 256)), 'col', 0, 0)]
    ppermute x2 -> x3, waiting for transfers between devices: 0.01 us -> 10.8 us  [over_y_lo(): return lax.ppermute(v, 'row', [(r, r ^ 8) for r in range(16)])]
    all_to_all x2 -> x0, starting transfers between devices: 10.6 us -> none  [the longest x1 6.43 us: shards(): pieces = lax.all_to_all(part.reshape(16, 16, 256), 'row', 0, 0)]
    all_to_all x2 -> x0, waiting for transfers between devices: 6.59 us -> none  [the longest x1 6.58 us: shards(): pieces = lax.all_to_all(part.reshape(16, 16, 256), 'row', 0, 0)]
    ppermute x6 -> x9, starting transfers between devices: 11 us -> 16.1 us  [over_x(): lax.ppermute(v, 'col', [(c, ((c >> 1) + s & 3) * 2 + (c & 1)) for c in ra...]
    ppermute x6 -> x9, waiting for transfers between devices: 10.8 us -> 6.23 us  [over_z(): lax.ppermute(v, 'row', [(r, r & 9 | ((r >> 1) + s & 3) << 1) for r in ran...]
    pallas_call x4 -> x8, Pallas kernels: 8.65 us -> 13 us  [the longest x1 5.36 us: shards(): call(for_self, [((33, 256, T), f32)], [SMEM, VMEM, VMEM], 'for_self', lim...]
    ppermute x2 -> x3, starting transfers between devices: 3.69 us -> 7.04 us  [over_y_hi(): return lax.ppermute(v, 'col', [(c, c ^ 1) for c in range(8)])]
  transfers between devices with their start and end apart: 19 -> 27, of which waited for: 7 -> 9; matrix products, arithmetic and copies ran while one was open for 1% -> 1% of each run, Pallas kernels for 9% -> 19%
where the time goes in v2:
time: 88.2 us; the launch traced here: 86.9 us
  starting transfers between devices  39.9 us (45%)
  waiting for transfers between devices  20.8 us (24%)
  Pallas kernels  20.4 us (23%)
  local copies, waits for them, and re-layouts  4.25 us (5%)
  between operations  1.53 us (2%)
    ppermute x9, starting transfers between devices, over_x(): lax.ppermute(v, 'col', [(c, ((c >> 1) + s & 3) * 2 + (c & 1)) for c in ra...  16.1 us
    ppermute x9, starting transfers between devices, over_z(): lax.ppermute(v, 'row', [(r, r & 9 | ((r >> 1) + s & 3) << 1) for r in ran...  13.8 us
    ppermute x3, waiting for transfers between devices, over_y_lo(): return lax.ppermute(v, 'row', [(r, r ^ 8) for r in range(16)])  10.8 us
    ppermute x3, starting transfers between devices, over_y_hi(): return lax.ppermute(v, 'col', [(c, c ^ 1) for c in range(8)])  7.04 us
    ppermute x9, waiting for transfers between devices, over_z(): lax.ppermute(v, 'row', [(r, r & 9 | ((r >> 1) + s & 3) << 1) for r in ran...  6.23 us
    pallas_call x1, Pallas kernels, shards(): call(for_self, [((33, 256, T), f32)], [SMEM, VMEM, VMEM], 'for_self', lim...  5.36 us
    pallas_call x1, Pallas kernels, shards(): call(for_partner, [((32, 256, T), bf16), ((33, 256, T), bf16)], [SMEM] +...  5.17 us
    unnamed x10, local copies, waits for them, and re-layouts  4.21 us
  transfers between devices with their start and end apart: 27, of which 9 were waited for; matrix products, arithmetic and copies ran while one was open for 1% of the time, Pallas kernels for 19%

profile of v2, /device:TPU:0, one launch (start us, length us, event | category | flops | bytes accessed | tf_op | source)
XLA Modules:
  0.0 86.9 jit_solution(4469543385603701322)
XLA Ops:
  0.6 2.5 %prep.1 = (bf16[2,256,128]{2,1,0:T(8,128)(2,1)}, bf16[2,256,128]{2,1,0:T(8,128)(2,1)}, f32[128,256]{1,0:T(8,128)}, f32[128,256]{1,0:T(8,128)}) custom-call(bf16[512,256]{1,0:T(8,128)(2,1)} %grad_hbm.1, s32[16,512]{1,0:T(8,128)} %bitcast.12, bf16[512,256]{1,0:T(8,128)(2,1)} %agg_hbm.1, bf16[256,256]{1,0:T(8,128)(2,1)} %weight_hbm.1), custom_call_target="tpu_custom_call" | custom-call | flops 200000000 | tf_op jit(solution)/shard_map/prep/pallas_call | solution.py:244
  3.1 0.1 collective-permute-start.4
  3.2 3.4 %collective-permute-start = (bf16[2,256,128]{2,1,0:T(8,128)(2,1)}, bf16[2,256,128]{2,1,0:T(8,128)(2,1)S(1)}, u32[]{:S(2)}, u32[]{:S(2)}) collective-permute-start(bf16[2,256,128]{2,1,0:T(8,128)(2,1)} %get-tuple-element.76), channel_id=1, source_target_pairs={{0,1},{1,0},{2,3},{3,2},{4,5},{5,4},{6,7},{7,6},{8,9},{9,8},{10,11... | collective-permute-start | bytes 393224 | tf_op jit(solution)/shard_map/ppermute | solution.py:232
  6.5 1.5 %collective-permute-start.3 = (bf16[2,256,128]{2,1,0:T(8,128)(2,1)}, bf16[2,256,128]{2,1,0:T(8,128)(2,1)S(1)}, u32[]{:S(2)}, u32[]{:S(2)}) collective-permute-start(bf16[2,256,128]{2,1,0:T(8,128)(2,1)} %get-tuple-element.78), channel_id=1, source_target_pairs={{0,2},{1,3},{2,4},{3,5},{4,6},{5,7},{6,0},{7,1},{8,10},{9,11},{10,... | collective-permute-start | bytes 393224 | tf_op jit(solution)/shard_map/ppermute | solution.py:229
  8.0 2.7 %collective-permute-start.2 = (bf16[2,256,128]{2,1,0:T(8,128)(2,1)}, bf16[2,256,128]{2,1,0:T(8,128)(2,1)S(1)}, u32[]{:S(2)}, u32[]{:S(2)}) collective-permute-start(bf16[2,256,128]{2,1,0:T(8,128)(2,1)} %get-tuple-element.78), channel_id=1, source_target_pairs={{0,4},{1,5},{2,6},{3,7},{4,0},{5,1},{6,2},{7,3},{8,12},{9,13},{10,... | collective-permute-start | bytes 393224 | tf_op jit(solution)/shard_map/ppermute | solution.py:229
  10.8 1.4 %collective-permute-start.1 = (bf16[2,256,128]{2,1,0:T(8,128)(2,1)}, bf16[2,256,128]{2,1,0:T(8,128)(2,1)S(1)}, u32[]{:S(2)}, u32[]{:S(2)}) collective-permute-start(bf16[2,256,128]{2,1,0:T(8,128)(2,1)} %get-tuple-element.78), channel_id=1, source_target_pairs={{0,6},{1,7},{2,0},{3,1},{4,2},{5,3},{6,4},{7,5},{8,14},{9,15},{10,... | collective-permute-start | bytes 393224 | tf_op jit(solution)/shard_map/ppermute | solution.py:229
  12.9 0.7 copy-done.1
  13.6 0.3 in_mask.1.mask_ref
  13.9 0.7 copy-done.2
  14.6 1.4 %order_slots.1 = (s32[8,384]{1,0:T(8,128)S(1)}, s32[8,384]{1,0:T(8,128)S(1)}) custom-call(s32[1]{0:T(128)} %bitcast.7.count_ref, s32[2,512]{1,0:T(2,128)S(1)} %bitcast.10), custom_call_target="tpu_custom_call" | custom-call | flops 10000000 | tf_op jit(solution)/shard_map/order_slots/pallas_call | solution.py:267
  16.1 1.3 %collective-permute-done.2 = bf16[2,256,128]{2,1,0:T(8,128)(2,1)S(1)} collective-permute-done((bf16[2,256,128]{2,1,0:T(8,128)(2,1)}, bf16[2,256,128]{2,1,0:T(8,128)(2,1)S(1)}, u32[]{:S(2)}, u32[]{:S(2)}) %collective-permute-start.2) | collective-permute-done | bytes 131104 | tf_op jit(solution)/shard_map/ppermute | solution.py:229
  17.3 0.9 %constant_dynamic-update-slice_fusion.5 = bf16[8,256,128]{2,1,0:T(8,128)(2,1)S(1)} fusion(bf16[2,256,128]{2,1,0:T(8,128)(2,1)} %get-tuple-element.78), kind=kLoop, calls=%fused_computation.5 | loop fusion | bytes 262144
  18.3 0.4 collective-permute-start.8
  18.7 0.9 %constant_dynamic-update-slice_fusion.1 = bf16[4,256,128]{2,1,0:T(8,128)(2,1)S(1)} fusion(bf16[2,256,128]{2,1,0:T(8,128)(2,1)} %get-tuple-element.76), kind=kLoop, calls=%fused_computation.1 | loop fusion | bytes 262144
  19.7 1.3 %collective-permute-start.7 = (bf16[4,256,128]{2,1,0:T(8,128)(2,1)S(1)}, bf16[4,256,128]{2,1,0:T(8,128)(2,1)S(1)}, u32[]{:S(2)}, u32[]{:S(2)}) collective-permute-start(bf16[4,256,128]{2,1,0:T(8,128)(2,1)S(1)} %constant_dynamic-update-slice_fusion.a0), channel_id=1, source_target_pairs={{0,2},{1,3},{2,4},{3,5},{4,6},{5,7},{6,0},{7,1},{8,10},{9,11},{10,... | collective-permute-start | bytes 786440 | tf_op jit(solution)/shard_map/ppermute | solution.py:229
  21.0 2.4 %collective-permute-start.6 = (bf16[4,256,128]{2,1,0:T(8,128)(2,1)S(1)}, bf16[4,256,128]{2,1,0:T(8,128)(2,1)S(1)}, u32[]{:S(2)}, u32[]{:S(2)}) collective-permute-start(bf16[4,256,128]{2,1,0:T(8,128)(2,1)S(1)} %constant_dynamic-update-slice_fusion.a0), channel_id=1, source_target_pairs={{0,4},{1,5},{2,6},{3,7},{4,0},{5,1},{6,2},{7,3},{8,12},{9,13},{10,... | collective-permute-start | bytes 786440 | tf_op jit(solution)/shard_map/ppermute | solution.py:229
  23.4 1.6 %collective-permute-start.5 = (bf16[4,256,128]{2,1,0:T(8,128)(2,1)S(1)}, bf16[4,256,128]{2,1,0:T(8,128)(2,1)S(1)}, u32[]{:S(2)}, u32[]{:S(2)}) collective-permute-start(bf16[4,256,128]{2,1,0:T(8,128)(2,1)S(1)} %constant_dynamic-update-slice_fusion.a0), channel_id=1, source_target_pairs={{0,6},{1,7},{2,0},{3,1},{4,2},{5,3},{6,4},{7,5},{8,14},{9,15},{10,... | collective-permute-start | bytes 786440 | tf_op jit(solution)/shard_map/ppermute | solution.py:229
  25.0 0.9 %copy-done = f32[128,256]{1,0:T(8,128)S(1)} copy-done((f32[128,256]{1,0:T(8,128)S(1)}, f32[128,256]{1,0:T(8,128)}, u32[]{:S(2)}) %copy-start) | copy-done | bytes 131096
  26.0 3.3 %collective-permute-start.9 = (f32[128,256]{1,0:T(8,128)S(1)}, f32[128,256]{1,0:T(8,128)S(1)}, u32[]{:S(2)}, u32[]{:S(2)}) collective-permute-start(f32[128,256]{1,0:T(8,128)S(1)} %w_core.1.a), channel_id=1, source_target_pairs={{0,1},{1,0},{2,3},{3,2},{4,5},{5,4},{6,7},{7,6},{8,9},{9,8},{10,11... | collective-permute-start | bytes 393224 | tf_op jit(solution)/shard_map/ppermute | solution.py:232
  29.2 4.1 %stage.1.tiles_ref = bf16[512,128,128]{2,1,0:T(8,128)(2,1)S(1)} custom-call(s32[1]{0:T(128)} %bitcast.8.count_ref, bf16[512,128,128]{2,1,0:T(8,128)(2,1)} %bitcast.11), custom_call_target="tpu_custom_call" | custom-call | flops 1000000000 | tf_op jit(solution)/shard_map/stage/pallas_call | solution.py:283
  33.4 2.5 %collective-permute-done.9.b = f32[128,256]{1,0:T(8,128)S(1)} collective-permute-done((f32[128,256]{1,0:T(8,128)S(1)}, f32[128,256]{1,0:T(8,128)S(1)}, u32[]{:S(2)}, u32[]{:S(2)}) %collective-permute-start.9) | collective-permute-done | bytes 131104 | tf_op jit(solution)/shard_map/ppermute | solution.py:232
  35.9 1.4 %collective-permute-start.12 = (f32[128,256]{1,0:T(8,128)S(1)}, f32[128,256]{1,0:T(8,128)S(1)}, u32[]{:S(2)}, u32[]{:S(2)}) collective-permute-start(f32[128,256]{1,0:T(8,128)S(1)} %w_y.1.own), channel_id=1, source_target_pairs={{0,2},{1,3},{2,4},{3,5},{4,6},{5,7},{6,0},{7,1},{8,10},{9,11},{10,... | collective-permute-start | bytes 393224 | tf_op jit(solution)/shard_map/ppermute | solution.py:229
  37.3 2.5 %collective-permute-start.11 = (f32[128,256]{1,0:T(8,128)S(1)}, f32[128,256]{1,0:T(8,128)S(1)}, u32[]{:S(2)}, u32[]{:S(2)}) collective-permute-start(f32[128,256]{1,0:T(8,128)S(1)} %w_y.1.own), channel_id=1, source_target_pairs={{0,4},{1,5},{2,6},{3,7},{4,0},{5,1},{6,2},{7,3},{8,12},{9,13},{10,... | collective-permute-start | bytes 393224 | tf_op jit(solution)/shard_map/ppermute | solution.py:229
  39.8 1.2 %collective-permute-start.10 = (f32[128,256]{1,0:T(8,128)S(1)}, f32[128,256]{1,0:T(8,128)S(1)}, u32[]{:S(2)}, u32[]{:S(2)}) collective-permute-start(f32[128,256]{1,0:T(8,128)S(1)} %w_y.1.own), channel_id=1, source_target_pairs={{0,6},{1,7},{2,0},{3,1},{4,2},{5,3},{6,4},{7,5},{8,14},{9,15},{10,... | collective-permute-start | bytes 393224 | tf_op jit(solution)/shard_map/ppermute | solution.py:229
  41.0 5.2 %for_partner.1 = (bf16[32,256,128]{2,1,0:T(8,128)(2,1)S(1)}, bf16[33,256,128]{2,1,0:T(8,128)(2,1)S(1)}) custom-call(s32[8,384]{1,0:T(8,128)S(1)} %get-tuple-element.75.steps_ref, bf16[4,256,128]{2,1,0:T(8,128)(2,1)S(1)} %constant_dynamic-update-slice_fusion.a0, bf16[4,256,128]{2,1,0:T(8,128)(2,1)S(1)} %collective-permute-done.7.a3, ...), custom_call_target="tpu_custom_call" | custom-call | flops 4000000000 | bytes 8388608 | tf_op jit(solution)/shard_map/for_partner/pallas_call | solution.py:296
  46.2 0.1 collective-permute-start.13
  46.3 0.5 collective-permute-start.16
  46.9 5.0 %collective-permute-start.15 = (f32[128,256]{1,0:T(8,128)S(1)}, f32[128,256]{1,0:T(8,128)S(1)}, u32[]{:S(2)}, u32[]{:S(2)}) collective-permute-start(f32[128,256]{1,0:T(8,128)S(1)} %w_x.1.w), channel_id=1, source_target_pairs={{0,32},{8,40},{16,48},{24,56},{32,0},{40,8},{48,16},{56,24},{64,96... | collective-permute-start | bytes 393224 | tf_op jit(solution)/shard_map/ppermute | solution.py:235
  51.9 5.4 %for_self.1.acc_ref = f32[33,256,128]{2,1,0:T(8,128)S(1)} custom-call(s32[8,384]{1,0:T(8,128)S(1)} %get-tuple-element.74.steps_ref, bf16[33,256,128]{2,1,0:T(8,128)(2,1)S(1)} %get-tuple-element.103.h_ref, bf16[512,128,128]{2,1,0:T(8,128)(2,1)S(1)} %stage.1.tiles_ref), custom_call_target="tpu_custom_call" | custom-call | flops 4000000000 | bytes 8388608 | tf_op jit(solution)/shard_map/for_self/pallas_call | solution.py:311
  57.3 1.3 %collective-permute-done.15.wx = f32[128,256]{1,0:T(8,128)S(1)} collective-permute-done((f32[128,256]{1,0:T(8,128)S(1)}, f32[128,256]{1,0:T(8,128)S(1)}, u32[]{:S(2)}, u32[]{:S(2)}) %collective-permute-start.15) | collective-permute-done | bytes 131104 | tf_op jit(solution)/shard_map/ppermute | solution.py:235
  58.6 0.3 join_cores.1
  59.0 1.2 %collective-permute-start.17 = (bf16[8,256,128]{2,1,0:T(8,128)(2,1)S(1)}, bf16[8,256,128]{2,1,0:T(8,128)(2,1)S(1)}, u32[]{:S(2)}, u32[]{:S(2)}) collective-permute-start(bf16[8,256,128]{2,1,0:T(8,128)(2,1)S(1)} %get-tuple-element.107), channel_id=1, source_target_pairs={{0,64},{8,72},{16,80},{24,88},{32,96},{40,104},{48,112},{56,120},{... | collective-permute-start | bytes 1572872 | tf_op jit(solution)/shard_map/ppermute | solution.py:238
  60.2 1.1 %collective-permute-start.19 = (bf16[4,256,128]{2,1,0:T(8,128)(2,1)S(1)}, bf16[4,256,128]{2,1,0:T(8,128)(2,1)S(1)}, u32[]{:S(2)}, u32[]{:S(2)}) collective-permute-start(bf16[4,256,128]{2,1,0:T(8,128)(2,1)S(1)} %get-tuple-element.109), channel_id=1, source_target_pairs={{0,16},{8,24},{16,32},{24,40},{32,48},{40,56},{48,0},{56,8},{64,80... | collective-permute-start | bytes 786440 | tf_op jit(solution)/shard_map/ppermute | solution.py:235
  61.3 3.0 %collective-permute-start.20 = (bf16[4,256,128]{2,1,0:T(8,128)(2,1)S(1)}, bf16[4,256,128]{2,1,0:T(8,128)(2,1)S(1)}, u32[]{:S(2)}, u32[]{:S(2)}) collective-permute-start(bf16[4,256,128]{2,1,0:T(8,128)(2,1)S(1)} %get-tuple-element.110), channel_id=1, source_target_pairs={{0,32},{8,40},{16,48},{24,56},{32,0},{40,8},{48,16},{56,24},{64,96... | collective-permute-start | bytes 786440 | tf_op jit(solution)/shard_map/ppermute | solution.py:235
  64.3 0.2 collective-permute-start.21
  64.5 0.2 collective-permute-start.18
  64.7 10.7 %collective-permute-done.18.w_got = f32[128,256]{1,0:T(8,128)S(1)} collective-permute-done((f32[128,256]{1,0:T(8,128)S(1)}, f32[128,256]{1,0:T(8,128)S(1)}, u32[]{:S(2)}, u32[]{:S(2)}) %collective-permute-start.18) | collective-permute-done | bytes 131104 | tf_op jit(solution)/shard_map/ppermute | solution.py:238
  75.4 0.5 collective-permute-done.20.g2
  75.9 0.1 join_a.1
  76.0 0.6 collective-permute-start.22
  76.5 3.0 %collective-permute-start.23 = (bf16[2,256,128]{2,1,0:T(8,128)(2,1)S(1)}, bf16[2,256,128]{2,1,0:T(8,128)(2,1)S(1)}, u32[]{:S(2)}, u32[]{:S(2)}) collective-permute-start(bf16[2,256,128]{2,1,0:T(8,128)(2,1)S(1)} %get-tuple-element.116), channel_id=1, source_target_pairs={{0,32},{8,40},{16,48},{24,56},{32,0},{40,8},{48,16},{56,24},{64,96... | collective-permute-start | bytes 393224 | tf_op jit(solution)/shard_map/ppermute | solution.py:235
  79.6 0.2 collective-permute-start.24
  79.8 0.1 join_b.1
  79.9 1.4 %collective-permute-start.25 = (bf16[2,256,128]{2,1,0:T(8,128)(2,1)S(1)}, bf16[2,256,128]{2,1,0:T(8,128)(2,1)S(1)}, u32[]{:S(2)}, u32[]{:S(2)}) collective-permute-start(bf16[2,256,128]{2,1,0:T(8,128)(2,1)S(1)} %get-tuple-element.123), channel_id=1, source_target_pairs={{0,64},{8,72},{16,80},{24,88},{32,96},{40,104},{48,112},{56,120},{... | collective-permute-start | bytes 393224 | tf_op jit(solution)/shard_map/ppermute | solution.py:238
  81.4 1.0 %collective-permute-done.22.g1 = bf16[2,256,128]{2,1,0:T(8,128)(2,1)S(1)} collective-permute-done((bf16[2,256,128]{2,1,0:T(8,128)(2,1)S(1)}, bf16[2,256,128]{2,1,0:T(8,128)(2,1)S(1)}, u32[]{:S(2)}, u32[]{:S(2)}) %collective-permute-start.22) | collective-permute-done | bytes 131104 | tf_op jit(solution)/shard_map/ppermute | solution.py:235
  82.4 3.4 %collective-permute-done.23.g2 = bf16[2,256,128]{2,1,0:T(8,128)(2,1)S(1)} collective-permute-done((bf16[2,256,128]{2,1,0:T(8,128)(2,1)S(1)}, bf16[2,256,128]{2,1,0:T(8,128)(2,1)S(1)}, u32[]{:S(2)}, u32[]{:S(2)}) %collective-permute-start.23) | collective-permute-done | bytes 131104 | tf_op jit(solution)/shard_map/ppermute | solution.py:235
  85.8 0.1 collective-permute-done.25.gy
  85.9 0.9 %finish.1 = (bf16[512,256]{1,0:T(8,128)(2,1)}, f32[256,256]{1,0:T(8,128)}) custom-call(f32[2,256,128]{2,1,0:T(8,128)S(1)} %get-tuple-element.114.a_keep, bf16[2,256,128]{2,1,0:T(8,128)(2,1)S(1)} %collective-permute-done.22.g1, bf16[2,256,128]{2,1,0:T(8,128)(2,1)S(1)} %collective-permute-done.23.g2, bf16[2,256,128]{2,1,0:T(8,128)(2,1)S(1)} %collective-permute-done.24.g3, ...), custom_call_target="tpu_custom_call" | custom-call | flops 1000000 | tf_op jit(solution)/shard_map/finish/pallas_call | solution.py:339
  (31 shorter events, 0.3 us)
Async XLA Ops:
  3.1 12.9 %collective-permute-start.4 = (f32[128,256]{1,0:T(8,128)}, f32[128,256]{1,0:T(8,128)S(1)}, u32[]{:S(2)}, u32[]{:S(2)}) collective-permute-start(f32[128,256]{1,0:T(8,128)} %get-tuple-element.73), channel_id=1, source_target_pairs={{0,8},{8,0},{16,24},{24,16},{32,40},{40,32},{48,56},{56,48},{64,72... | collective-permute-start | bytes 393224 | tf_op jit(solution)/shard_map/ppermute | solution.py:241
  3.2 12.8 %collective-permute-start = (bf16[2,256,128]{2,1,0:T(8,128)(2,1)}, bf16[2,256,128]{2,1,0:T(8,128)(2,1)S(1)}, u32[]{:S(2)}, u32[]{:S(2)}) collective-permute-start(bf16[2,256,128]{2,1,0:T(8,128)(2,1)} %get-tuple-element.76), channel_id=1, source_target_pairs={{0,1},{1,0},{2,3},{3,2},{4,5},{5,4},{6,7},{7,6},{8,9},{9,8},{10,11... | collective-permute-start | bytes 393224 | tf_op jit(solution)/shard_map/ppermute | solution.py:232
  6.5 9.5 %collective-permute-start.3 = (bf16[2,256,128]{2,1,0:T(8,128)(2,1)}, bf16[2,256,128]{2,1,0:T(8,128)(2,1)S(1)}, u32[]{:S(2)}, u32[]{:S(2)}) collective-permute-start(bf16[2,256,128]{2,1,0:T(8,128)(2,1)} %get-tuple-element.78), channel_id=1, source_target_pairs={{0,2},{1,3},{2,4},{3,5},{4,6},{5,7},{6,0},{7,1},{8,10},{9,11},{10,... | collective-permute-start | bytes 393224 | tf_op jit(solution)/shard_map/ppermute | solution.py:229
  8.0 9.3 %collective-permute-start.2 = (bf16[2,256,128]{2,1,0:T(8,128)(2,1)}, bf16[2,256,128]{2,1,0:T(8,128)(2,1)S(1)}, u32[]{:S(2)}, u32[]{:S(2)}) collective-permute-start(bf16[2,256,128]{2,1,0:T(8,128)(2,1)} %get-tuple-element.78), channel_id=1, source_target_pairs={{0,4},{1,5},{2,6},{3,7},{4,0},{5,1},{6,2},{7,3},{8,12},{9,13},{10,... | collective-permute-start | bytes 393224 | tf_op jit(solution)/shard_map/ppermute | solution.py:229
  10.8 6.5 %collective-permute-start.1 = (bf16[2,256,128]{2,1,0:T(8,128)(2,1)}, bf16[2,256,128]{2,1,0:T(8,128)(2,1)S(1)}, u32[]{:S(2)}, u32[]{:S(2)}) collective-permute-start(bf16[2,256,128]{2,1,0:T(8,128)(2,1)} %get-tuple-element.78), channel_id=1, source_target_pairs={{0,6},{1,7},{2,0},{3,1},{4,2},{5,3},{6,4},{7,5},{8,14},{9,15},{10,... | collective-permute-start | bytes 393224 | tf_op jit(solution)/shard_map/ppermute | solution.py:229
  12.8 0.8 copy-start.1
  13.9 0.7 copy-start.2
  18.3 17.6 %collective-permute-start.8 = (bf16[8,256,128]{2,1,0:T(8,128)(2,1)S(1)}, bf16[8,256,128]{2,1,0:T(8,128)(2,1)S(1)}, u32[]{:S(2)}, u32[]{:S(2)}) collective-permute-start(bf16[8,256,128]{2,1,0:T(8,128)(2,1)S(1)} %constant_dynamic-update-slice_fusion.2.b0), channel_id=1, source_target_pairs={{0,1},{1,0},{2,3},{3,2},{4,5},{5,4},{6,7},{7,6},{8,9},{9,8},{10,11... | collective-permute-start | bytes 1572872 | tf_op jit(solution)/shard_map/ppermute | solution.py:232
  19.7 16.2 %collective-permute-start.7 = (bf16[4,256,128]{2,1,0:T(8,128)(2,1)S(1)}, bf16[4,256,128]{2,1,0:T(8,128)(2,1)S(1)}, u32[]{:S(2)}, u32[]{:S(2)}) collective-permute-start(bf16[4,256,128]{2,1,0:T(8,128)(2,1)S(1)} %constant_dynamic-update-slice_fusion.a0), channel_id=1, source_target_pairs={{0,2},{1,3},{2,4},{3,5},{4,6},{5,7},{6,0},{7,1},{8,10},{9,11},{10,... | collective-permute-start | bytes 786440 | tf_op jit(solution)/shard_map/ppermute | solution.py:229
  21.0 14.9 %collective-permute-start.6 = (bf16[4,256,128]{2,1,0:T(8,128)(2,1)S(1)}, bf16[4,256,128]{2,1,0:T(8,128)(2,1)S(1)}, u32[]{:S(2)}, u32[]{:S(2)}) collective-permute-start(bf16[4,256,128]{2,1,0:T(8,128)(2,1)S(1)} %constant_dynamic-update-slice_fusion.a0), channel_id=1, source_target_pairs={{0,4},{1,5},{2,6},{3,7},{4,0},{5,1},{6,2},{7,3},{8,12},{9,13},{10,... | collective-permute-start | bytes 786440 | tf_op jit(solution)/shard_map/ppermute | solution.py:229
  23.4 12.5 %collective-permute-start.5 = (bf16[4,256,128]{2,1,0:T(8,128)(2,1)S(1)}, bf16[4,256,128]{2,1,0:T(8,128)(2,1)S(1)}, u32[]{:S(2)}, u32[]{:S(2)}) collective-permute-start(bf16[4,256,128]{2,1,0:T(8,128)(2,1)S(1)} %constant_dynamic-update-slice_fusion.a0), channel_id=1, source_target_pairs={{0,6},{1,7},{2,0},{3,1},{4,2},{5,3},{6,4},{7,5},{8,14},{9,15},{10,... | collective-permute-start | bytes 786440 | tf_op jit(solution)/shard_map/ppermute | solution.py:229
  25.0 0.9 %copy-start = (f32[128,256]{1,0:T(8,128)S(1)}, f32[128,256]{1,0:T(8,128)}, u32[]{:S(2)}) copy-start(f32[128,256]{1,0:T(8,128)} %get-tuple-element.83.a) | copy-start | bytes 393220
  26.0 9.9 %collective-permute-start.9 = (f32[128,256]{1,0:T(8,128)S(1)}, f32[128,256]{1,0:T(8,128)S(1)}, u32[]{:S(2)}, u32[]{:S(2)}) collective-permute-start(f32[128,256]{1,0:T(8,128)S(1)} %w_core.1.a), channel_id=1, source_target_pairs={{0,1},{1,0},{2,3},{3,2},{4,5},{5,4},{6,7},{7,6},{8,9},{9,8},{10,11... | collective-permute-start | bytes 393224 | tf_op jit(solution)/shard_map/ppermute | solution.py:232
  35.9 10.3 %collective-permute-start.12 = (f32[128,256]{1,0:T(8,128)S(1)}, f32[128,256]{1,0:T(8,128)S(1)}, u32[]{:S(2)}, u32[]{:S(2)}) collective-permute-start(f32[128,256]{1,0:T(8,128)S(1)} %w_y.1.own), channel_id=1, source_target_pairs={{0,2},{1,3},{2,4},{3,5},{4,6},{5,7},{6,0},{7,1},{8,10},{9,11},{10,... | collective-permute-start | bytes 393224 | tf_op jit(solution)/shard_map/ppermute | solution.py:229
  37.3 8.9 %collective-permute-start.11 = (f32[128,256]{1,0:T(8,128)S(1)}, f32[128,256]{1,0:T(8,128)S(1)}, u32[]{:S(2)}, u32[]{:S(2)}) collective-permute-start(f32[128,256]{1,0:T(8,128)S(1)} %w_y.1.own), channel_id=1, source_target_pairs={{0,4},{1,5},{2,6},{3,7},{4,0},{5,1},{6,2},{7,3},{8,12},{9,13},{10,... | collective-permute-start | bytes 393224 | tf_op jit(solution)/shard_map/ppermute | solution.py:229
  39.8 6.4 %collective-permute-start.10 = (f32[128,256]{1,0:T(8,128)S(1)}, f32[128,256]{1,0:T(8,128)S(1)}, u32[]{:S(2)}, u32[]{:S(2)}) collective-permute-start(f32[128,256]{1,0:T(8,128)S(1)} %w_y.1.own), channel_id=1, source_target_pairs={{0,6},{1,7},{2,0},{3,1},{4,2},{5,3},{6,4},{7,5},{8,14},{9,15},{10,... | collective-permute-start | bytes 393224 | tf_op jit(solution)/shard_map/ppermute | solution.py:229
  46.2 12.4 %collective-permute-start.13 = (bf16[32,256,128]{2,1,0:T(8,128)(2,1)S(1)}, bf16[32,256,128]{2,1,0:T(8,128)(2,1)S(1)}, u32[]{:S(2)}, u32[]{:S(2)}) collective-permute-start(bf16[32,256,128]{2,1,0:T(8,128)(2,1)S(1)} %get-tuple-element.104), channel_id=1, source_target_pairs={{0,8},{8,0},{16,24},{24,16},{32,40},{40,32},{48,56},{56,48},{64,72... | collective-permute-start | bytes 6291464 | tf_op jit(solution)/shard_map/ppermute | solution.py:241
  46.3 11.0 %collective-permute-start.16 = (f32[128,256]{1,0:T(8,128)S(1)}, f32[128,256]{1,0:T(8,128)S(1)}, u32[]{:S(2)}, u32[]{:S(2)}) collective-permute-start(f32[128,256]{1,0:T(8,128)S(1)} %w_x.1.w), channel_id=1, source_target_pairs={{0,16},{8,24},{16,32},{24,40},{32,48},{40,56},{48,0},{56,8},{64,80... | collective-permute-start | bytes 393224 | tf_op jit(solution)/shard_map/ppermute | solution.py:235
  46.9 11.7 %collective-permute-start.15 = (f32[128,256]{1,0:T(8,128)S(1)}, f32[128,256]{1,0:T(8,128)S(1)}, u32[]{:S(2)}, u32[]{:S(2)}) collective-permute-start(f32[128,256]{1,0:T(8,128)S(1)} %w_x.1.w), channel_id=1, source_target_pairs={{0,32},{8,40},{16,48},{24,56},{32,0},{40,8},{48,16},{56,24},{64,96... | collective-permute-start | bytes 393224 | tf_op jit(solution)/shard_map/ppermute | solution.py:235
  51.9 6.7 %collective-permute-start.14 = (f32[128,256]{1,0:T(8,128)S(1)}, f32[128,256]{1,0:T(8,128)S(1)}, u32[]{:S(2)}, u32[]{:S(2)}) collective-permute-start(f32[128,256]{1,0:T(8,128)S(1)} %w_x.1.w), channel_id=1, source_target_pairs={{0,48},{8,56},{16,0},{24,8},{32,16},{40,24},{48,32},{56,40},{64,11... | collective-permute-start | bytes 393224 | tf_op jit(solution)/shard_map/ppermute | solution.py:235
  59.0 16.9 %collective-permute-start.17 = (bf16[8,256,128]{2,1,0:T(8,128)(2,1)S(1)}, bf16[8,256,128]{2,1,0:T(8,128)(2,1)S(1)}, u32[]{:S(2)}, u32[]{:S(2)}) collective-permute-start(bf16[8,256,128]{2,1,0:T(8,128)(2,1)S(1)} %get-tuple-element.107), channel_id=1, source_target_pairs={{0,64},{8,72},{16,80},{24,88},{32,96},{40,104},{48,112},{56,120},{... | collective-permute-start | bytes 1572872 | tf_op jit(solution)/shard_map/ppermute | solution.py:238
  60.2 15.2 %collective-permute-start.19 = (bf16[4,256,128]{2,1,0:T(8,128)(2,1)S(1)}, bf16[4,256,128]{2,1,0:T(8,128)(2,1)S(1)}, u32[]{:S(2)}, u32[]{:S(2)}) collective-permute-start(bf16[4,256,128]{2,1,0:T(8,128)(2,1)S(1)} %get-tuple-element.109), channel_id=1, source_target_pairs={{0,16},{8,24},{16,32},{24,40},{32,48},{40,56},{48,0},{56,8},{64,80... | collective-permute-start | bytes 786440 | tf_op jit(solution)/shard_map/ppermute | solution.py:235
  61.3 14.6 %collective-permute-start.20 = (bf16[4,256,128]{2,1,0:T(8,128)(2,1)S(1)}, bf16[4,256,128]{2,1,0:T(8,128)(2,1)S(1)}, u32[]{:S(2)}, u32[]{:S(2)}) collective-permute-start(bf16[4,256,128]{2,1,0:T(8,128)(2,1)S(1)} %get-tuple-element.110), channel_id=1, source_target_pairs={{0,32},{8,40},{16,48},{24,56},{32,0},{40,8},{48,16},{56,24},{64,96... | collective-permute-start | bytes 786440 | tf_op jit(solution)/shard_map/ppermute | solution.py:235
  64.3 11.5 %collective-permute-start.21 = (bf16[4,256,128]{2,1,0:T(8,128)(2,1)S(1)}, bf16[4,256,128]{2,1,0:T(8,128)(2,1)S(1)}, u32[]{:S(2)}, u32[]{:S(2)}) collective-permute-start(bf16[4,256,128]{2,1,0:T(8,128)(2,1)S(1)} %get-tuple-element.111), channel_id=1, source_target_pairs={{0,48},{8,56},{16,0},{24,8},{32,16},{40,24},{48,32},{56,40},{64,11... | collective-permute-start | bytes 786440 | tf_op jit(solution)/shard_map/ppermute | solution.py:235
  64.5 10.9 %collective-permute-start.18 = (f32[128,256]{1,0:T(8,128)S(1)}, f32[128,256]{1,0:T(8,128)S(1)}, u32[]{:S(2)}, u32[]{:S(2)}) collective-permute-start(f32[128,256]{1,0:T(8,128)S(1)} %get-tuple-element.108.w), channel_id=1, source_target_pairs={{0,64},{8,72},{16,80},{24,88},{32,96},{40,104},{48,112},{56,120},{... | collective-permute-start | bytes 393224 | tf_op jit(solution)/shard_map/ppermute | solution.py:238
  76.0 6.4 %collective-permute-start.22 = (bf16[2,256,128]{2,1,0:T(8,128)(2,1)S(1)}, bf16[2,256,128]{2,1,0:T(8,128)(2,1)S(1)}, u32[]{:S(2)}, u32[]{:S(2)}) collective-permute-start(bf16[2,256,128]{2,1,0:T(8,128)(2,1)S(1)} %get-tuple-element.115), channel_id=1, source_target_pairs={{0,16},{8,24},{16,32},{24,40},{32,48},{40,56},{48,0},{56,8},{64,80... | collective-permute-start | bytes 393224 | tf_op jit(solution)/shard_map/ppermute | solution.py:235
  76.5 9.2 %collective-permute-start.23 = (bf16[2,256,128]{2,1,0:T(8,128)(2,1)S(1)}, bf16[2,256,128]{2,1,0:T(8,128)(2,1)S(1)}, u32[]{:S(2)}, u32[]{:S(2)}) collective-permute-start(bf16[2,256,128]{2,1,0:T(8,128)(2,1)S(1)} %get-tuple-element.116), channel_id=1, source_target_pairs={{0,32},{8,40},{16,48},{24,56},{32,0},{40,8},{48,16},{56,24},{64,96... | collective-permute-start | bytes 393224 | tf_op jit(solution)/shard_map/ppermute | solution.py:235
  79.6 6.3 %collective-permute-start.24 = (bf16[2,256,128]{2,1,0:T(8,128)(2,1)S(1)}, bf16[2,256,128]{2,1,0:T(8,128)(2,1)S(1)}, u32[]{:S(2)}, u32[]{:S(2)}) collective-permute-start(bf16[2,256,128]{2,1,0:T(8,128)(2,1)S(1)} %get-tuple-element.117), channel_id=1, source_target_pairs={{0,48},{8,56},{16,0},{24,8},{32,16},{40,24},{48,32},{56,40},{64,11... | collective-permute-start | bytes 393224 | tf_op jit(solution)/shard_map/ppermute | solution.py:235
  79.8 6.0 %collective-permute-start.26 = (f32[128,256]{1,0:T(8,128)S(1)}, f32[128,256]{1,0:T(8,128)S(1)}, u32[]{:S(2)}, u32[]{:S(2)}) collective-permute-start(f32[128,256]{1,0:T(8,128)S(1)} %get-tuple-element.125.w), channel_id=1, source_target_pairs={{0,8},{8,0},{16,24},{24,16},{32,40},{40,32},{48,56},{56,48},{64,72... | collective-permute-start | bytes 393224 | tf_op jit(solution)/shard_map/ppermute | solution.py:241
  79.9 6.0 %collective-permute-start.25 = (bf16[2,256,128]{2,1,0:T(8,128)(2,1)S(1)}, bf16[2,256,128]{2,1,0:T(8,128)(2,1)S(1)}, u32[]{:S(2)}, u32[]{:S(2)}) collective-permute-start(bf16[2,256,128]{2,1,0:T(8,128)(2,1)S(1)} %get-tuple-element.123), channel_id=1, source_target_pairs={{0,64},{8,72},{16,80},{24,88},{32,96},{40,104},{48,112},{56,120},{... | collective-permute-start | bytes 393224 | tf_op jit(solution)/shard_map/ppermute | solution.py:238

commit v3 on v2

v3 whole, which is shorter than its diff:
```python
import functools

import jax
import jax.numpy as jnp
from jax import lax
from jax.experimental import pallas as pl
from jax.experimental.pallas import tpu as pltpu
from jax.sharding import PartitionSpec as P

T = 128
N_STEP = 512
UNROLL = 16
LIMIT = 16
PREP_LIMIT = 61
STAGE_LIMIT = 24
ZERO_ROW = 32
bf16 = jnp.bfloat16
f32 = jnp.float32
tie = lambda *values: lax.optimization_barrier(values)
VMEM = pl.BlockSpec(memory_space=pltpu.VMEM)
ANY = pl.BlockSpec(memory_space=pl.ANY)
SMEM = pl.BlockSpec(memory_space=pltpu.SMEM)


def call(body, outs, ins, name, limit=8, scratch=(), flops=0, touched=0):
    return pl.pallas_call(
        body,
        in_specs=ins,
        out_specs=[VMEM] * len(outs),
        out_shape=[jax.ShapeDtypeStruct(s, d) for s, d in outs],
        scratch_shapes=list(scratch),
        compiler_params=pltpu.CompilerParams(vmem_limit_bytes=limit * 2**20),
        cost_estimate=pl.CostEstimate(flops=flops, bytes_accessed=touched, transcendentals=0),
        name=name,
    )


def contract(a, b, da, db):
    return lax.dot_general(a, b, (((da,), (db,)), ((), ())), preferred_element_type=f32)


def mask_of(words):
    low = (words & 255).astype(f32)
    high = ((words >> 8) & 255).astype(f32)
    pieces = jnp.concatenate([low, high], 0).astype(bf16)
    w = lax.broadcasted_iota(jnp.int32, (32, 256), 0)
    f = lax.broadcasted_iota(jnp.int32, (32, 256), 1)
    spread = ((f >> 4) + 16 * ((f >> 3) & 1) == w).astype(f32).astype(bf16)
    byte = contract(pieces, spread, 0, 0).astype(jnp.int32)
    lane = lax.broadcasted_iota(jnp.int32, byte.shape, 1)
    return ((byte >> (lane & 7)) & 1) == 1


def prep(grad_hbm, words_hbm, agg_hbm, weight_hbm, ha_ref, hb_ref, keep_ref, send_ref, grad, words, agg, weight, part, sems):
    copies = [
        pltpu.make_async_copy(src, dst, sems.at[i])
        for i, (src, dst) in enumerate(((words_hbm, words), (grad_hbm, grad), (weight_hbm, weight), (agg_hbm, agg)))
    ]
    for copy in copies:
        copy.start()
    copies[0].wait()
    mask = mask_of(words[...])
    copies[1].wait()
    masked = jnp.where(mask, grad[...], jnp.zeros((), bf16))
    copies[2].wait()
    hidden = contract(weight[...], masked, 1, 1).astype(bf16)
    for t in range(4):
        ref = ha_ref if t < 2 else hb_ref
        ref[t & 1] = hidden[:, t * T : (t + 1) * T]
    copies[3].wait()
    part[...] = contract(agg[...], masked, 0, 0) * (1.0 / 256.0)
    core = lax.axis_index("row") & 1
    keep_ref[...] = part[pl.ds(pl.multiple_of(core * T, T), T)]
    send_ref[...] = part[pl.ds(pl.multiple_of((1 - core) * T, T), T)]


def add_two(a, b, out):
    out[...] = a[...] + b[...]


def in_mask(words_ref, out_ref):
    out_ref[...] = mask_of(words_ref[...]).astype(f32).astype(bf16)


def order_slots(count_ref, coords_ref, out_ref):
    device_row, device_col = lax.axis_index("row"), lax.axis_index("col")
    x, y_hi = device_col >> 1, device_col & 1
    y_lo, z, core = device_row >> 3, (device_row >> 1) & 3, device_row & 1
    slots = coords_ref.shape[1]
    slot = lax.broadcasted_iota(jnp.int32, (1, slots), 1)
    i, j = coords_ref[0:1, :], coords_ref[1:2, :]
    t, src = i & 3, i >> 2
    dx, dyh = ((src >> 1) - x) & 3, (src & 1) ^ y_hi
    row = jnp.where(t < 2, dx * 4 + dyh * 2 + t, 16 + dyh * 8 + dx * 2 + (t & 1))
    late = jnp.where(jnp.where(t < 2, dx, dyh) == 0, 0, 64)
    u, q = j & 3, j >> 2
    dc, dz, dy = (q & 1) ^ core ^ 1, ((q >> 1) - z) & 3, (q >> 3) ^ y_lo
    column = (u >> 1) * 32 + dc * 16 + dz * 4 + dy * 2 + (u & 1)
    key = jnp.where(slot < count_ref[0], column + late, T)
    both = jnp.concatenate([key, slot | (row << 9), column << 15, jnp.zeros((5, slots), jnp.int32)], 0).T
    key_c, word_c, high_c = both[:, 0:1], both[:, 1:2], both[:, 2:3]
    s_id = lax.broadcasted_iota(jnp.int32, (slots, slots), 0)
    t_id = lax.broadcasted_iota(jnp.int32, (slots, slots), 1)
    rank = jnp.sum(jnp.where((key == key_c) & (t_id < s_id), 1, 0), 1, keepdims=True)
    k_id = lax.broadcasted_iota(jnp.int32, (slots, T), 1)
    lane = k_id[0:1]
    held = jnp.sum(jnp.where(key_c == k_id, 1, 0), 0, keepdims=True)
    pairs = (held + 1) >> 1

    def list_of(k):
        return jnp.where(k < 64, 0, (k >> 4) - 3)

    start = jnp.zeros((1, 1), jnp.int32)
    starts, counts, base = (jnp.zeros((1, T), jnp.int32) for _ in range(3))
    for number in range(5):
        total = jnp.sum(jnp.where(list_of(lane) == number, pairs, 0), 1, keepdims=True)
        groups = (total + UNROLL - 1) // UNROLL
        starts = jnp.where(lane == number, start, starts)
        counts = jnp.where(lane == number, groups, counts)
        base = jnp.where(list_of(lane) == number, start * UNROLL, base)
        start = start + groups
    ahead = (k_id < key_c) & (list_of(k_id) == list_of(key_c))
    step = jnp.sum(jnp.where(ahead, pairs, 0) + jnp.where(k_id == key_c, base, 0), 1, keepdims=True) + (rank >> 1)
    step = jnp.where(key_c < T, step, -1)
    first = jnp.where((rank & 1) == 0, step, -1)
    second = jnp.where((rank & 1) == 1, step, -1)
    p_id = lax.broadcasted_iota(jnp.int32, (slots, N_STEP), 1)
    none = ZERO_ROW << 9
    none_high = 64 << 15
    out_ref[0:1, :] = (
        jnp.sum(jnp.where(first == p_id, word_c + high_c - none - none_high, 0), 0, keepdims=True) + none + none_high
    )
    out_ref[1:2, :] = jnp.sum(jnp.where(second == p_id, word_c - none, 0), 0, keepdims=True) + none
    out_ref[2:8, :] = jnp.zeros((6, N_STEP), jnp.int32)
    out_ref[2:3, 0:T] = starts
    out_ref[3:4, 0:T] = counts


def stage(count_ref, tiles_ref, out_ref, sems):
    chunk = tiles_ref.shape[0] // 8

    def copy(i):
        part = pl.ds(i * chunk, chunk)
        return pltpu.make_async_copy(tiles_ref.at[part], out_ref.at[part], sems.at[i])

    used = (count_ref[0] + chunk - 1) // chunk
    for i in range(8):
        pl.when(i < used)(lambda i=i: copy(i).start())
    for i in range(8):
        pl.when(i < used)(lambda i=i: copy(i).wait())


def products(number, steps_ref, h_ref, tiles_ref, acc_ref):
    lowest = 0 if number == 0 else (number - 1) * 16
    spare = acc_ref.shape[0] - 1

    def some(g, carry):
        results = []
        for u in range(UNROLL):
            s = g * UNROLL + u
            a, b = steps_ref[0, s], steps_ref[1, s]
            left = jnp.concatenate([h_ref[(a >> 9) & 63], h_ref[b >> 9]], 1)
            right = jnp.concatenate([tiles_ref[a & 511], tiles_ref[b & 511]], 0)
            column = jnp.minimum((a >> 15) - lowest, spare)
            results.append((column, jnp.dot(left, right, preferred_element_type=f32)))
        for column, result in results:
            acc_ref[column] += result
        return carry

    first = steps_ref[2, number]
    lax.fori_loop(first, first + steps_ref[3, number], some, 0)


def early(steps_ref, a0, b0, tiles_ref, acc_ref, h_ref):
    h_ref[0:4], h_ref[16:24] = a0[...], b0[...]
    h_ref[ZERO_ROW] = jnp.zeros((256, T), bf16)

    def clear(k, carry):
        acc_ref[k] = jnp.zeros((256, T), f32)
        return carry

    lax.fori_loop(0, 65, clear, 0)
    products(0, steps_ref, h_ref, tiles_ref, acc_ref)


def late(number, steps_ref, h_ref, tiles_ref, so_far_ref, out_ref, acc_ref):
    base = (number - 1) * 16

    def take(k, carry):
        acc_ref[k] = so_far_ref[base + k]
        return carry

    lax.fori_loop(0, 16, take, 0)
    acc_ref[16] = jnp.zeros((256, T), f32)
    products(number, steps_ref, h_ref, tiles_ref, acc_ref)

    def give(k, carry):
        out_ref[k] = acc_ref[k].astype(out_ref.dtype)
        return carry

    lax.fori_loop(0, 16, give, 0)


def late_first(steps_ref, a0, a3, a1, a2, b0, b1, tiles_ref, so_far_ref, p_ref, q_ref, h_ref, acc_ref):
    h_ref[0:4], h_ref[4:8], h_ref[8:12], h_ref[12:16] = a0[...], a1[...], a2[...], a3[...]
    h_ref[16:24], h_ref[24:32] = b0[...], b1[...]
    h_ref[ZERO_ROW] = jnp.zeros((256, T), bf16)
    late(1, steps_ref, h_ref, tiles_ref, so_far_ref, p_ref, acc_ref)
    late(3, steps_ref, h_ref, tiles_ref, so_far_ref, q_ref, acc_ref)


def join_cores(acc_ref, got_ref, keep, z1, z2, z3):
    for k in range(4):
        keep[k] = acc_ref[k] + got_ref[k].astype(f32)
        for dz, ref in ((1, z1), (2, z2), (3, z3)):
            ref[k] = (acc_ref[4 * dz + k] + got_ref[4 * dz + k].astype(f32)).astype(bf16)


def join_z(keep_ref, g1, g2, g3, keep, y):
    for k in range(4):
        total = keep_ref[k] + g1[k].astype(f32) + g2[k].astype(f32) + g3[k].astype(f32)
        if k < 2:
            keep[k] = total
        else:
            y[k - 2] = total.astype(bf16)


def finish(p_keep, p_got, q_keep, q_got, mask_ref, w, w_got, out_ref, weight_ref):
    core = lax.axis_index("row") & 1
    weight_ref[pl.ds(pl.multiple_of(core * T, T), T)] = w[...]
    weight_ref[pl.ds(pl.multiple_of((1 - core) * T, T), T)] = w_got[...]
    for t in range(4):
        keep, got = (p_keep, p_got) if t < 2 else (q_keep, q_got)
        total = keep[t & 1] + got[t & 1].astype(f32)
        rows = slice(t * T, (t + 1) * T)
        out_ref[rows] = jnp.where(mask_ref[rows] == 1, total.T, 0.0).astype(bf16)


def shards(out_grad, out_bits, agg_saved, weight, tiles, tile_coords, tile_count, in_bits):
    def over_x(v, s):
        return lax.ppermute(v, "col", [(c, (((c >> 1) + s) & 3) * 2 + (c & 1)) for c in range(8)])

    def over_y_hi(v):
        return lax.ppermute(v, "col", [(c, c ^ 1) for c in range(8)])

    def over_z(v, s):
        return lax.ppermute(v, "row", [(r, (r & 9) | ((((r >> 1) + s) & 3) << 1)) for r in range(16)])

    def swap_x(v, bit):
        return lax.ppermute(v, "col", [(c, c ^ (2 << bit)) for c in range(8)])

    def swap_z(v, bit):
        return lax.ppermute(v, "row", [(r, r ^ (2 << bit)) for r in range(16)])

    def over_y_lo(v):
        return lax.ppermute(v, "row", [(r, r ^ 8) for r in range(16)])

    def over_core(v):
        return lax.ppermute(v, "row", [(r, r ^ 1) for r in range(16)])

    half, quad, part = (2, 256, T), (4, 256, T), (T, 256)
    ha, hb, w, w_send = call(
        prep,
        [(half, bf16), (half, bf16), (part, f32), (part, f32)],
        [ANY] * 4,
        "prep",
        limit=PREP_LIMIT,
        scratch=[
            pltpu.VMEM((512, 256), bf16),
            pltpu.VMEM((16, 512), jnp.int32),
            pltpu.VMEM((512, 256), bf16),
            pltpu.VMEM((256, 256), bf16),
            pltpu.VMEM((256, 256), f32),
            pltpu.SemaphoreType.DMA((4,)),
        ],
        flops=2 * 10**8,
    )(out_grad, out_bits.T, agg_saved, weight)

    w_got = over_core(w_send)
    ha_y = over_y_hi(ha)
    hb_1, hb_2, hb_3 = over_x(hb, -1), over_x(hb, 2), over_x(hb, 1)
    count, own_tiles, ha = tie(tile_count.reshape(1), tiles[0, 0], ha)
    (own_tiles,) = call(
        stage,
        [(own_tiles.shape, bf16)],
        [SMEM, ANY],
        "stage",
        limit=STAGE_LIMIT,
        scratch=[pltpu.SemaphoreType.DMA((8,))],
        flops=10**9,
    )(count, own_tiles)
    ha, ha_y, hb, hb_1, hb_2, hb_3, own_tiles, w_got, coords, count = tie(
        ha, ha_y, hb, hb_1, hb_2, hb_3, own_tiles, w_got, tile_coords[0, 0].T, count
    )

    a0 = jnp.concatenate([ha, ha_y], 0)
    b0 = jnp.concatenate([hb, hb_1, hb_2, hb_3], 0)
    a3, a1, a2 = over_x(a0, 1), over_x(a0, -1), over_x(a0, 2)
    b1 = over_y_hi(b0)
    add_w = call(add_two, [(part, f32)], [VMEM] * 2, "add_w", limit=2)
    (steps,) = call(order_slots, [((8, N_STEP), jnp.int32)], [SMEM, VMEM], "order_slots", flops=10**7)(count, coords)
    (w,) = add_w(w, w_got)
    w_got = swap_z(w, 0)
    (acc,) = call(
        early,
        [((65, 256, T), f32)],
        [SMEM] + [VMEM] * 3,
        "early",
        limit=LIMIT,
        scratch=[pltpu.VMEM((33, 256, T), bf16)],
        flops=4 * 10**9,
    )(steps, a0, b0, own_tiles)
    acc, w, w_got = tie(acc, w, w_got)
    (w,) = add_w(w, w_got)
    a0, a1, a2, a3, b0, b1, acc, w = tie(a0, a1, a2, a3, b0, b1, acc, w)
    w_got = swap_z(w, 1)

    cost = dict(flops=2 * 10**9)
    group = [pltpu.VMEM((17, 256, T), f32)]
    sixteen = (16, 256, T)

    def later(number, kind):
        body = functools.partial(late, number)
        name = "late_" + str(number)
        outs = [(sixteen, kind)]
        return call(body, outs, [SMEM] + [VMEM] * 3, name, limit=LIMIT, scratch=group, **cost)

    def split(own, got, name):
        outs = [(quad, f32)] + [(quad, bf16)] * 3
        return call(join_cores, outs, [VMEM] * 2, name, flops=10**6)(own, got)

    def around_z(z1, z2, z3):
        return over_z(z1, 1), over_z(z2, 2), over_z(z3, -1)

    def gather_z(keep, got, name):
        return call(join_z, [(half, f32), (half, bf16)], [VMEM] * 4, name, flops=10**6)(keep, *got)

    p_partner, q_partner, hidden = call(
        late_first,
        [(sixteen, bf16), (sixteen, bf16), ((33, 256, T), bf16)],
        [SMEM] + [VMEM] * 8,
        "late_first",
        limit=LIMIT,
        scratch=group,
        **cost,
    )(steps, a0, a3, a1, a2, b0, b1, own_tiles, acc)
    p_partner, q_partner, hidden, w, w_got = tie(p_partner, q_partner, hidden, w, w_got)
    p_partner, q_partner = over_core(p_partner), over_core(q_partner)
    (w,) = add_w(w, w_got)
    hidden, w = tie(hidden, w)
    w_got = over_y_lo(w)
    (own,) = later(2, f32)(steps, hidden, own_tiles, acc)
    p_keep, *p_z = split(own, p_partner, "split_p")
    p_z = around_z(*p_z)
    p_keep, hidden, w, w_got, q_partner = tie(p_keep, hidden, w, w_got, q_partner)
    (w,) = add_w(w, w_got)
    hidden, w = tie(hidden, w)
    w_got = over_y_hi(w)
    (own,) = later(4, f32)(steps, hidden, own_tiles, acc)
    q_keep, *q_z = split(own, q_partner, "split_q")
    q_z = around_z(*q_z)
    q_keep, w, w_got, words = tie(q_keep, w, w_got, in_bits.T)
    (w,) = add_w(w, w_got)
    w_got = swap_x(w, 0)
    (mask,) = call(in_mask, [((512, 256), bf16)], [VMEM], "in_mask", flops=10**7)(words)
    p_keep, p_y = gather_z(p_keep, p_z, "gather_p")
    p_got = over_y_lo(p_y)
    p_keep, w, w_got, mask = tie(p_keep, w, w_got, mask)
    (w,) = add_w(w, w_got)
    w_got = swap_x(w, 1)
    (w,) = add_w(w, w_got)
    w_got = over_core(w)
    q_keep, p_got = tie(q_keep, p_got)
    q_keep, q_y = gather_z(q_keep, q_z, "gather_q")
    q_got = over_y_lo(q_y)
    prev_grad, weight_grad = call(
        finish, [((512, 256), bf16), ((256, 256), f32)], [VMEM] * 7, "finish", flops=10**6
    )(p_keep, p_got, q_keep, q_got, mask, w, w_got)
    return weight_grad, prev_grad


def solution(mesh):
    nodes = P(("row", "col"), None)
    return jax.shard_map(
        shards,
        mesh=mesh,
        in_specs=(nodes, nodes, nodes, P(), P("row", "col"), P("row", "col"), P("row", "col"), nodes),
        out_specs=(P(), nodes),
        check_vma=False,
    )
```

time: 88.2 us -> 81.6 us (0.925)
  local copies, waits for them, and re-layouts: 4.25 us -> 0.13 us
  waiting for transfers between devices: 20.8 us -> 24.5 us
  starting transfers between devices: 39.9 us -> 36.2 us
  Pallas kernels: 20.4 us -> 17.7 us
    ppermute x9 -> x6, starting transfers between devices: 16.1 us -> 7.41 us  [over_x(): lax.ppermute(v, 'col', [(c, ((c >> 1) + s & 3) * 2 + (c & 1)) for c in ra...]
    ppermute x0 -> x4, starting transfers between devices: none -> 6.47 us  [the longest x2 5.88 us: swap_z(): return lax.ppermute(v, 'row', [(r, r ^ 2 << bit) for r in range(16)])]
    ppermute x9 -> x6, waiting for transfers between devices: 1.29 us -> 7.55 us  [over_x(): lax.ppermute(v, 'col', [(c, ((c >> 1) + s & 3) * 2 + (c & 1)) for c in ra...]
    unnamed x10 -> x14, local copies, waits for them, and re-layouts: 4.21 us -> 0.09 us
    ppermute x9 -> x6, starting transfers between devices: 13.8 us -> 10.1 us  [over_z(): lax.ppermute(v, 'row', [(r, r & 9 | ((r >> 1) + s & 3) << 1) for r in ran...]
    ppermute x3, waiting for transfers between devices: 10.8 us -> 7.67 us  [over_y_lo(): return lax.ppermute(v, 'row', [(r, r ^ 8) for r in range(16)])]
    ppermute x9 -> x6, waiting for transfers between devices: 6.23 us -> 8.8 us  [over_z(): lax.ppermute(v, 'row', [(r, r & 9 | ((r >> 1) + s & 3) << 1) for r in ran...]
    ppermute x3, starting transfers between devices: 7.04 us -> 9.57 us  [over_y_hi(): return lax.ppermute(v, 'col', [(c, c ^ 1) for c in range(8)])]
  transfers between devices with their start and end apart: 27 -> 26, of which waited for: 9 -> 12; matrix products, arithmetic and copies ran while one was open for 1% -> 0% of each run, Pallas kernels for 19% -> 18%
where the time goes in v3:
time: 81.6 us; the launch traced here: 80.1 us
  starting transfers between devices  36.2 us (44%)
  waiting for transfers between devices  24.5 us (30%)
  Pallas kernels  17.7 us (22%)
  between operations  1.54 us (2%)
    ppermute x6, starting transfers between devices, over_z(): lax.ppermute(v, 'row', [(r, r & 9 | ((r >> 1) + s & 3) << 1) for r in ran...  10.1 us
    ppermute x3, starting transfers between devices, over_y_hi(): return lax.ppermute(v, 'col', [(c, c ^ 1) for c in range(8)])  9.57 us
    ppermute x6, waiting for transfers between devices, over_z(): lax.ppermute(v, 'row', [(r, r & 9 | ((r >> 1) + s & 3) << 1) for r in ran...  8.8 us
    ppermute x3, waiting for transfers between devices, over_y_lo(): return lax.ppermute(v, 'row', [(r, r ^ 8) for r in range(16)])  7.67 us
    ppermute x6, waiting for transfers between devices, over_x(): lax.ppermute(v, 'col', [(c, ((c >> 1) + s & 3) * 2 + (c & 1)) for c in ra...  7.55 us
    ppermute x6, starting transfers between devices, over_x(): lax.ppermute(v, 'col', [(c, ((c >> 1) + s & 3) * 2 + (c & 1)) for c in ra...  7.41 us
    ppermute x2, starting transfers between devices, swap_z(): return lax.ppermute(v, 'row', [(r, r ^ 2 << bit) for r in range(16)])  5.88 us
    pallas_call x1, Pallas kernels, shards(): call(late_first, [(sixteen, bf16), (sixteen, bf16), ((33, 256, T), bf16)]...  3.11 us
  transfers between devices with their start and end apart: 26, of which 12 were waited for; matrix products, arithmetic and copies ran while one was open for 0% of the time, Pallas kernels for 18%

profile of v3, /device:TPU:0, one launch (start us, length us, event | category | flops | bytes accessed | tf_op | source)
XLA Modules:
  0.0 80.1 jit_solution(8399709911108095600)
XLA Ops:
  0.6 2.4 %prep.1 = (bf16[2,256,128]{2,1,0:T(8,128)(2,1)}, bf16[2,256,128]{2,1,0:T(8,128)(2,1)}, f32[128,256]{1,0:T(8,128)}, f32[128,256]{1,0:T(8,128)}) custom-call(bf16[512,256]{1,0:T(8,128)(2,1)} %grad_hbm.1, s32[16,512]{1,0:T(8,128)} %bitcast.12, bf16[512,256]{1,0:T(8,128)(2,1)} %agg_hbm.1, bf16[256,256]{1,0:T(8,128)(2,1)} %weight_hbm.1), custom_call_target="tpu_custom_call" | custom-call | flops 200000000 | tf_op jit(solution)/shard_map/prep/pallas_call | solution.py:262
  3.1 2.9 %collective-permute-start.1 = (bf16[2,256,128]{2,1,0:T(8,128)(2,1)}, bf16[2,256,128]{2,1,0:T(8,128)(2,1)S(1)}, u32[]{:S(2)}, u32[]{:S(2)}) collective-permute-start(bf16[2,256,128]{2,1,0:T(8,128)(2,1)} %get-tuple-element.81), channel_id=1, source_target_pairs={{0,6},{1,7},{2,0},{3,1},{4,2},{5,3},{6,4},{7,5},{8,14},{9,15},{10,... | collective-permute-start | bytes 393224 | tf_op jit(solution)/shard_map/ppermute | solution.py:241
  6.0 0.8 %collective-permute-start.2 = (bf16[2,256,128]{2,1,0:T(8,128)(2,1)}, bf16[2,256,128]{2,1,0:T(8,128)(2,1)S(1)}, u32[]{:S(2)}, u32[]{:S(2)}) collective-permute-start(bf16[2,256,128]{2,1,0:T(8,128)(2,1)} %get-tuple-element.81), channel_id=1, source_target_pairs={{0,4},{1,5},{2,6},{3,7},{4,0},{5,1},{6,2},{7,3},{8,12},{9,13},{10,... | collective-permute-start | bytes 393224 | tf_op jit(solution)/shard_map/ppermute | solution.py:241
  6.8 0.9 %collective-permute-start.3 = (bf16[2,256,128]{2,1,0:T(8,128)(2,1)}, bf16[2,256,128]{2,1,0:T(8,128)(2,1)S(1)}, u32[]{:S(2)}, u32[]{:S(2)}) collective-permute-start(bf16[2,256,128]{2,1,0:T(8,128)(2,1)} %get-tuple-element.81), channel_id=1, source_target_pairs={{0,2},{1,3},{2,4},{3,5},{4,6},{5,7},{6,0},{7,1},{8,10},{9,11},{10,... | collective-permute-start | bytes 393224 | tf_op jit(solution)/shard_map/ppermute | solution.py:241
  7.7 3.2 %collective-permute-start = (bf16[2,256,128]{2,1,0:T(8,128)(2,1)}, bf16[2,256,128]{2,1,0:T(8,128)(2,1)S(1)}, u32[]{:S(2)}, u32[]{:S(2)}) collective-permute-start(bf16[2,256,128]{2,1,0:T(8,128)(2,1)} %get-tuple-element.79), channel_id=1, source_target_pairs={{0,1},{1,0},{2,3},{3,2},{4,5},{5,4},{6,7},{7,6},{8,9},{9,8},{10,11... | collective-permute-start | bytes 393224 | tf_op jit(solution)/shard_map/ppermute | solution.py:244
  11.5 0.0 copy-start.4
  11.6 2.4 %stage.1.tiles_ref = bf16[512,128,128]{2,1,0:T(8,128)(2,1)S(1)} custom-call(s32[1]{0:T(128)} %bitcast.7.count_ref, bf16[512,128,128]{2,1,0:T(8,128)(2,1)} %bitcast.11), custom_call_target="tpu_custom_call" | custom-call | flops 1000000000 | tf_op jit(solution)/shard_map/stage/pallas_call | solution.py:283
  14.0 0.1 collective-permute-done.2
  14.1 1.4 %collective-permute-done.3 = bf16[2,256,128]{2,1,0:T(8,128)(2,1)S(1)} collective-permute-done((bf16[2,256,128]{2,1,0:T(8,128)(2,1)}, bf16[2,256,128]{2,1,0:T(8,128)(2,1)S(1)}, u32[]{:S(2)}, u32[]{:S(2)}) %collective-permute-start.3) | collective-permute-done | bytes 131104 | tf_op jit(solution)/shard_map/ppermute | solution.py:241
  15.6 3.3 %collective-permute-start.8 = (bf16[8,256,128]{2,1,0:T(8,128)(2,1)S(1)}, bf16[8,256,128]{2,1,0:T(8,128)(2,1)S(1)}, u32[]{:S(2)}, u32[]{:S(2)}) collective-permute-start(bf16[8,256,128]{2,1,0:T(8,128)(2,1)S(1)} %constant_dynamic-update-slice_fusion.2.b0), channel_id=1, source_target_pairs={{0,1},{1,0},{2,3},{3,2},{4,5},{5,4},{6,7},{7,6},{8,9},{9,8},{10,11... | collective-permute-start | bytes 1572872 | tf_op jit(solution)/shard_map/ppermute | solution.py:244
  18.9 1.3 %collective-permute-start.5 = (bf16[4,256,128]{2,1,0:T(8,128)(2,1)S(1)}, bf16[4,256,128]{2,1,0:T(8,128)(2,1)S(1)}, u32[]{:S(2)}, u32[]{:S(2)}) collective-permute-start(bf16[4,256,128]{2,1,0:T(8,128)(2,1)S(1)} %constant_dynamic-update-slice_fusion.a0), channel_id=1, source_target_pairs={{0,6},{1,7},{2,0},{3,1},{4,2},{5,3},{6,4},{7,5},{8,14},{9,15},{10,... | collective-permute-start | bytes 786440 | tf_op jit(solution)/shard_map/ppermute | solution.py:241
  20.2 1.5 %collective-permute-start.6 = (bf16[4,256,128]{2,1,0:T(8,128)(2,1)S(1)}, bf16[4,256,128]{2,1,0:T(8,128)(2,1)S(1)}, u32[]{:S(2)}, u32[]{:S(2)}) collective-permute-start(bf16[4,256,128]{2,1,0:T(8,128)(2,1)S(1)} %constant_dynamic-update-slice_fusion.a0), channel_id=1, source_target_pairs={{0,4},{1,5},{2,6},{3,7},{4,0},{5,1},{6,2},{7,3},{8,12},{9,13},{10,... | collective-permute-start | bytes 786440 | tf_op jit(solution)/shard_map/ppermute | solution.py:241
  21.7 2.0 %collective-permute-start.9 = (f32[128,256]{1,0:T(8,128)S(1)}, f32[128,256]{1,0:T(8,128)S(1)}, u32[]{:S(2)}, u32[]{:S(2)}) collective-permute-start(f32[128,256]{1,0:T(8,128)S(1)} %add_w.7.a), channel_id=1, source_target_pairs={{0,16},{8,24},{16,0},{24,8},{32,48},{40,56},{48,32},{56,40},{64,80... | collective-permute-start | bytes 393224 | tf_op jit(solution)/shard_map/ppermute | solution.py:253
  23.7 1.2 %order_slots.1.steps_ref = s32[8,512]{1,0:T(8,128)S(1)} custom-call(s32[1]{0:T(128)} %bitcast.8.count_ref, s32[2,512]{1,0:T(2,128)S(1)} %bitcast.10), custom_call_target="tpu_custom_call" | custom-call | flops 10000000 | tf_op jit(solution)/shard_map/order_slots/pallas_call | solution.py:301
  24.9 2.9 %early.1.so_far_ref = f32[65,256,128]{2,1,0:T(8,128)S(1)} custom-call(s32[8,512]{1,0:T(8,128)S(1)} %order_slots.1.steps_ref, bf16[4,256,128]{2,1,0:T(8,128)(2,1)S(1)} %constant_dynamic-update-slice_fusion.a0, bf16[8,256,128]{2,1,0:T(8,128)(2,1)S(1)} %constant_dynamic-update-slice_fusion.2.b0, bf16[512,128,128]{2,1,0:T(8,128)(2,1)S(1)} %stage.1.tiles_ref), custom_call_target="tpu_custom_call" | custom-call | flops 4000000000 | tf_op jit(solution)/shard_map/early/pallas_call | solution.py:304
  27.9 0.3 collective-permute-done.5.a1
  28.2 2.8 %collective-permute-done.6.a2 = bf16[4,256,128]{2,1,0:T(8,128)(2,1)S(1)} collective-permute-done((bf16[4,256,128]{2,1,0:T(8,128)(2,1)S(1)}, bf16[4,256,128]{2,1,0:T(8,128)(2,1)S(1)}, u32[]{:S(2)}, u32[]{:S(2)}) %collective-permute-start.6) | collective-permute-done | bytes 262176 | tf_op jit(solution)/shard_map/ppermute | solution.py:241
  31.0 3.0 %collective-permute-done.7.a3 = bf16[4,256,128]{2,1,0:T(8,128)(2,1)S(1)} collective-permute-done((bf16[4,256,128]{2,1,0:T(8,128)(2,1)S(1)}, bf16[4,256,128]{2,1,0:T(8,128)(2,1)S(1)}, u32[]{:S(2)}, u32[]{:S(2)}) %collective-permute-start.7) | collective-permute-done | bytes 262176 | tf_op jit(solution)/shard_map/ppermute | solution.py:241
  34.0 3.9 %collective-permute-start.10 = (f32[128,256]{1,0:T(8,128)S(1)}, f32[128,256]{1,0:T(8,128)S(1)}, u32[]{:S(2)}, u32[]{:S(2)}) collective-permute-start(f32[128,256]{1,0:T(8,128)S(1)} %add_w.8.a), channel_id=1, source_target_pairs={{0,32},{8,40},{16,48},{24,56},{32,0},{40,8},{48,16},{56,24},{64,96... | collective-permute-start | bytes 393224 | tf_op jit(solution)/shard_map/ppermute | solution.py:253
  37.8 3.1 %late_first.1 = (bf16[16,256,128]{2,1,0:T(8,128)(2,1)S(1)}, bf16[16,256,128]{2,1,0:T(8,128)(2,1)S(1)}, bf16[33,256,128]{2,1,0:T(8,128)(2,1)S(1)}) custom-call(s32[8,512]{1,0:T(8,128)S(1)} %order_slots.1.steps_ref, bf16[4,256,128]{2,1,0:T(8,128)(2,1)S(1)} %constant_dynamic-update-slice_fusion.a0, bf16[4,256,128]{2,1,0:T(8,128)(2,1)S(1)} %collective-permute-done.7.a3, ...), custom_call_target="tpu_custom_call" | custom-call | flops 2000000000 | tf_op jit(solution)/shard_map/late_first/pallas_call | solution.py:338
  41.0 0.2 collective-permute-done.10.b
  41.2 0.5 collective-permute-start.13
  41.7 0.8 collective-permute-start.12
  42.4 1.9 %late_2.1.acc_ref = f32[16,256,128]{2,1,0:T(8,128)S(1)} custom-call(s32[8,512]{1,0:T(8,128)S(1)} %order_slots.1.steps_ref, bf16[33,256,128]{2,1,0:T(8,128)(2,1)S(1)} %get-tuple-element.118.h_ref, bf16[512,128,128]{2,1,0:T(8,128)(2,1)S(1)} %stage.1.tiles_ref, f32[65,256,128]{2,1,0:T(8,128)S(1)} %early.1.so_far_ref), custom_call_target="tpu_custom_call" | custom-call | flops 2000000000 | tf_op jit(solution)/shard_map/late_2/pallas_call | solution.py:352
  44.3 0.2 split_p.1
  44.5 3.6 %collective-permute-start.14 = (bf16[4,256,128]{2,1,0:T(8,128)(2,1)S(1)}, bf16[4,256,128]{2,1,0:T(8,128)(2,1)S(1)}, u32[]{:S(2)}, u32[]{:S(2)}) collective-permute-start(bf16[4,256,128]{2,1,0:T(8,128)(2,1)S(1)} %get-tuple-element.111), channel_id=1, source_target_pairs={{0,16},{8,24},{16,32},{24,40},{32,48},{40,56},{48,0},{56,8},{64,80... | collective-permute-start | bytes 786440 | tf_op jit(solution)/shard_map/ppermute | solution.py:247
  48.1 3.1 %collective-permute-start.15 = (bf16[4,256,128]{2,1,0:T(8,128)(2,1)S(1)}, bf16[4,256,128]{2,1,0:T(8,128)(2,1)S(1)}, u32[]{:S(2)}, u32[]{:S(2)}) collective-permute-start(bf16[4,256,128]{2,1,0:T(8,128)(2,1)S(1)} %get-tuple-element.112), channel_id=1, source_target_pairs={{0,32},{8,40},{16,48},{24,56},{32,0},{40,8},{48,16},{56,24},{64,96... | collective-permute-start | bytes 786440 | tf_op jit(solution)/shard_map/ppermute | solution.py:247
  51.3 3.1 %collective-permute-start.17 = (f32[128,256]{1,0:T(8,128)S(1)}, f32[128,256]{1,0:T(8,128)S(1)}, u32[]{:S(2)}, u32[]{:S(2)}) collective-permute-start(f32[128,256]{1,0:T(8,128)S(1)} %add_w.10.a), channel_id=1, source_target_pairs={{0,1},{1,0},{2,3},{3,2},{4,5},{5,4},{6,7},{7,6},{8,9},{9,8},{10,11... | collective-permute-start | bytes 393224 | tf_op jit(solution)/shard_map/ppermute | solution.py:244
  54.4 0.1 collective-permute-start.16
  54.5 1.9 %late_4.1.acc_ref = f32[16,256,128]{2,1,0:T(8,128)S(1)} custom-call(s32[8,512]{1,0:T(8,128)S(1)} %order_slots.1.steps_ref, bf16[33,256,128]{2,1,0:T(8,128)(2,1)S(1)} %get-tuple-element.118.h_ref, bf16[512,128,128]{2,1,0:T(8,128)(2,1)S(1)} %stage.1.tiles_ref, f32[65,256,128]{2,1,0:T(8,128)S(1)} %early.1.so_far_ref), custom_call_target="tpu_custom_call" | custom-call | flops 2000000000 | tf_op jit(solution)/shard_map/late_4/pallas_call | solution.py:359
  56.4 0.2 split_q.1
  56.6 2.9 %collective-permute-start.20 = (bf16[4,256,128]{2,1,0:T(8,128)(2,1)S(1)}, bf16[4,256,128]{2,1,0:T(8,128)(2,1)S(1)}, u32[]{:S(2)}, u32[]{:S(2)}) collective-permute-start(bf16[4,256,128]{2,1,0:T(8,128)(2,1)S(1)} %get-tuple-element.130), channel_id=1, source_target_pairs={{0,16},{8,24},{16,32},{24,40},{32,48},{40,56},{48,0},{56,8},{64,80... | collective-permute-start | bytes 786440 | tf_op jit(solution)/shard_map/ppermute | solution.py:247
  59.4 0.4 collective-permute-start.21
  59.9 0.2 collective-permute-start.18
  60.0 4.0 %collective-permute-done.15.g2 = bf16[4,256,128]{2,1,0:T(8,128)(2,1)S(1)} collective-permute-done((bf16[4,256,128]{2,1,0:T(8,128)(2,1)S(1)}, bf16[4,256,128]{2,1,0:T(8,128)(2,1)S(1)}, u32[]{:S(2)}, u32[]{:S(2)}) %collective-permute-start.15) | collective-permute-done | bytes 262176 | tf_op jit(solution)/shard_map/ppermute | solution.py:247
  64.1 0.1 gather_p.1
  64.2 0.2 collective-permute-start.19
  64.3 0.3 in_mask.1.mask_ref
  64.6 0.3 collective-permute-done.18.b
  64.9 0.4 collective-permute-start.24
  65.3 3.9 %collective-permute-done.19.p_got = bf16[2,256,128]{2,1,0:T(8,128)(2,1)S(1)} collective-permute-done((bf16[2,256,128]{2,1,0:T(8,128)(2,1)S(1)}, bf16[2,256,128]{2,1,0:T(8,128)(2,1)S(1)}, u32[]{:S(2)}, u32[]{:S(2)}) %collective-permute-start.19) | collective-permute-done | bytes 131104 | tf_op jit(solution)/shard_map/ppermute | solution.py:256
  69.2 0.4 collective-permute-done.20.g1
  69.7 4.3 %collective-permute-done.21.g2 = bf16[4,256,128]{2,1,0:T(8,128)(2,1)S(1)} collective-permute-done((bf16[4,256,128]{2,1,0:T(8,128)(2,1)S(1)}, bf16[4,256,128]{2,1,0:T(8,128)(2,1)S(1)}, u32[]{:S(2)}, u32[]{:S(2)}) %collective-permute-start.21) | collective-permute-done | bytes 262176 | tf_op jit(solution)/shard_map/ppermute | solution.py:247
  74.0 0.1 gather_q.1
  74.1 1.1 %collective-permute-start.23 = (bf16[2,256,128]{2,1,0:T(8,128)(2,1)S(1)}, bf16[2,256,128]{2,1,0:T(8,128)(2,1)S(1)}, u32[]{:S(2)}, u32[]{:S(2)}) collective-permute-start(bf16[2,256,128]{2,1,0:T(8,128)(2,1)S(1)} %get-tuple-element.134), channel_id=1, source_target_pairs={{0,64},{8,72},{16,80},{24,88},{32,96},{40,104},{48,112},{56,120},{... | collective-permute-start | bytes 393224 | tf_op jit(solution)/shard_map/ppermute | solution.py:256
  75.3 0.1 collective-permute-start.25
  75.4 3.8 %collective-permute-done.23.q_got = bf16[2,256,128]{2,1,0:T(8,128)(2,1)S(1)} collective-permute-done((bf16[2,256,128]{2,1,0:T(8,128)(2,1)S(1)}, bf16[2,256,128]{2,1,0:T(8,128)(2,1)S(1)}, u32[]{:S(2)}, u32[]{:S(2)}) %collective-permute-start.23) | collective-permute-done | bytes 131104 | tf_op jit(solution)/shard_map/ppermute | solution.py:256
  79.2 0.9 %finish.1 = (bf16[512,256]{1,0:T(8,128)(2,1)}, f32[256,256]{1,0:T(8,128)}) custom-call(f32[2,256,128]{2,1,0:T(8,128)S(1)} %get-tuple-element.125.p_keep, bf16[2,256,128]{2,1,0:T(8,128)(2,1)S(1)} %collective-permute-done.19.p_got, f32[2,256,128]{2,1,0:T(8,128)S(1)} %get-tuple-element.133.q_keep, bf16[2,256,128]{2,1,0:T(8,128)(2,1)S(1)} %collective-permute-done.23.q_got, ...), custom_call_target="tpu_custom_call" | custom-call | flops 1000000 | tf_op jit(solution)/shard_map/finish/pallas_call | solution.py:376
  (40 shorter events, 0.3 us)
Async XLA Ops:
  3.1 10.9 %collective-permute-start.1 = (bf16[2,256,128]{2,1,0:T(8,128)(2,1)}, bf16[2,256,128]{2,1,0:T(8,128)(2,1)S(1)}, u32[]{:S(2)}, u32[]{:S(2)}) collective-permute-start(bf16[2,256,128]{2,1,0:T(8,128)(2,1)} %get-tuple-element.81), channel_id=1, source_target_pairs={{0,6},{1,7},{2,0},{3,1},{4,2},{5,3},{6,4},{7,5},{8,14},{9,15},{10,... | collective-permute-start | bytes 393224 | tf_op jit(solution)/shard_map/ppermute | solution.py:241
  6.0 8.1 %collective-permute-start.2 = (bf16[2,256,128]{2,1,0:T(8,128)(2,1)}, bf16[2,256,128]{2,1,0:T(8,128)(2,1)S(1)}, u32[]{:S(2)}, u32[]{:S(2)}) collective-permute-start(bf16[2,256,128]{2,1,0:T(8,128)(2,1)} %get-tuple-element.81), channel_id=1, source_target_pairs={{0,4},{1,5},{2,6},{3,7},{4,0},{5,1},{6,2},{7,3},{8,12},{9,13},{10,... | collective-permute-start | bytes 393224 | tf_op jit(solution)/shard_map/ppermute | solution.py:241
  6.8 8.7 %collective-permute-start.3 = (bf16[2,256,128]{2,1,0:T(8,128)(2,1)}, bf16[2,256,128]{2,1,0:T(8,128)(2,1)S(1)}, u32[]{:S(2)}, u32[]{:S(2)}) collective-permute-start(bf16[2,256,128]{2,1,0:T(8,128)(2,1)} %get-tuple-element.81), channel_id=1, source_target_pairs={{0,2},{1,3},{2,4},{3,5},{4,6},{5,7},{6,0},{7,1},{8,10},{9,11},{10,... | collective-permute-start | bytes 393224 | tf_op jit(solution)/shard_map/ppermute | solution.py:241
  7.7 7.8 %collective-permute-start = (bf16[2,256,128]{2,1,0:T(8,128)(2,1)}, bf16[2,256,128]{2,1,0:T(8,128)(2,1)S(1)}, u32[]{:S(2)}, u32[]{:S(2)}) collective-permute-start(bf16[2,256,128]{2,1,0:T(8,128)(2,1)} %get-tuple-element.79), channel_id=1, source_target_pairs={{0,1},{1,0},{2,3},{3,2},{4,5},{5,4},{6,7},{7,6},{8,9},{9,8},{10,11... | collective-permute-start | bytes 393224 | tf_op jit(solution)/shard_map/ppermute | solution.py:244
  10.9 4.6 %collective-permute-start.4 = (f32[128,256]{1,0:T(8,128)}, f32[128,256]{1,0:T(8,128)S(1)}, u32[]{:S(2)}, u32[]{:S(2)}) collective-permute-start(f32[128,256]{1,0:T(8,128)} %get-tuple-element.76), channel_id=1, source_target_pairs={{0,8},{8,0},{16,24},{24,16},{32,40},{40,32},{48,56},{56,48},{64,72... | collective-permute-start | bytes 393224 | tf_op jit(solution)/shard_map/ppermute | solution.py:259
  11.5 4.0 %copy-start.4 = (bf16[2,256,128]{2,1,0:T(8,128)(2,1)S(1)}, bf16[2,256,128]{2,1,0:T(8,128)(2,1)}, u32[]{:S(2)}) copy-start(bf16[2,256,128]{2,1,0:T(8,128)(2,1)} %get-tuple-element.81) | copy-start | bytes 393220
  11.5 7.3 %copy-start.3 = (bf16[2,256,128]{2,1,0:T(8,128)(2,1)S(1)}, bf16[2,256,128]{2,1,0:T(8,128)(2,1)}, u32[]{:S(2)}) copy-start(bf16[2,256,128]{2,1,0:T(8,128)(2,1)} %get-tuple-element.79) | copy-start | bytes 393220
  11.6 10.2 %copy-start = (f32[128,256]{1,0:T(8,128)S(1)}, f32[128,256]{1,0:T(8,128)}, u32[]{:S(2)}) copy-start(f32[128,256]{1,0:T(8,128)} %get-tuple-element.86.a) | copy-start | bytes 393220
  11.6 12.2 %copy-start.2 = (s32[1,1,512,2]{2,3,1,0:T(2,128)S(1)}, s32[1,1,512,2]{2,3,1,0:T(2,128)}, u32[]{:S(2)}) copy-start(s32[1,1,512,2]{2,3,1,0:T(2,128)} %param.13) | copy-start | bytes 12292
  15.6 18.4 %collective-permute-start.8 = (bf16[8,256,128]{2,1,0:T(8,128)(2,1)S(1)}, bf16[8,256,128]{2,1,0:T(8,128)(2,1)S(1)}, u32[]{:S(2)}, u32[]{:S(2)}) collective-permute-start(bf16[8,256,128]{2,1,0:T(8,128)(2,1)S(1)} %constant_dynamic-update-slice_fusion.2.b0), channel_id=1, source_target_pairs={{0,1},{1,0},{2,3},{3,2},{4,5},{5,4},{6,7},{7,6},{8,9},{9,8},{10,11... | collective-permute-start | bytes 1572872 | tf_op jit(solution)/shard_map/ppermute | solution.py:244
  18.9 9.3 %collective-permute-start.5 = (bf16[4,256,128]{2,1,0:T(8,128)(2,1)S(1)}, bf16[4,256,128]{2,1,0:T(8,128)(2,1)S(1)}, u32[]{:S(2)}, u32[]{:S(2)}) collective-permute-start(bf16[4,256,128]{2,1,0:T(8,128)(2,1)S(1)} %constant_dynamic-update-slice_fusion.a0), channel_id=1, source_target_pairs={{0,6},{1,7},{2,0},{3,1},{4,2},{5,3},{6,4},{7,5},{8,14},{9,15},{10,... | collective-permute-start | bytes 786440 | tf_op jit(solution)/shard_map/ppermute | solution.py:241
  20.2 10.8 %collective-permute-start.6 = (bf16[4,256,128]{2,1,0:T(8,128)(2,1)S(1)}, bf16[4,256,128]{2,1,0:T(8,128)(2,1)S(1)}, u32[]{:S(2)}, u32[]{:S(2)}) collective-permute-start(bf16[4,256,128]{2,1,0:T(8,128)(2,1)S(1)} %constant_dynamic-update-slice_fusion.a0), channel_id=1, source_target_pairs={{0,4},{1,5},{2,6},{3,7},{4,0},{5,1},{6,2},{7,3},{8,12},{9,13},{10,... | collective-permute-start | bytes 786440 | tf_op jit(solution)/shard_map/ppermute | solution.py:241
  21.7 12.2 %collective-permute-start.7 = (bf16[4,256,128]{2,1,0:T(8,128)(2,1)S(1)}, bf16[4,256,128]{2,1,0:T(8,128)(2,1)S(1)}, u32[]{:S(2)}, u32[]{:S(2)}) collective-permute-start(bf16[4,256,128]{2,1,0:T(8,128)(2,1)S(1)} %constant_dynamic-update-slice_fusion.a0), channel_id=1, source_target_pairs={{0,2},{1,3},{2,4},{3,5},{4,6},{5,7},{6,0},{7,1},{8,10},{9,11},{10,... | collective-permute-start | bytes 786440 | tf_op jit(solution)/shard_map/ppermute | solution.py:241
  21.7 6.1 %collective-permute-start.9 = (f32[128,256]{1,0:T(8,128)S(1)}, f32[128,256]{1,0:T(8,128)S(1)}, u32[]{:S(2)}, u32[]{:S(2)}) collective-permute-start(f32[128,256]{1,0:T(8,128)S(1)} %add_w.7.a), channel_id=1, source_target_pairs={{0,16},{8,24},{16,0},{24,8},{32,48},{40,56},{48,32},{56,40},{64,80... | collective-permute-start | bytes 393224 | tf_op jit(solution)/shard_map/ppermute | solution.py:253
  34.0 7.2 %collective-permute-start.10 = (f32[128,256]{1,0:T(8,128)S(1)}, f32[128,256]{1,0:T(8,128)S(1)}, u32[]{:S(2)}, u32[]{:S(2)}) collective-permute-start(f32[128,256]{1,0:T(8,128)S(1)} %add_w.8.a), channel_id=1, source_target_pairs={{0,32},{8,40},{16,48},{24,56},{32,0},{40,8},{48,16},{56,24},{64,96... | collective-permute-start | bytes 393224 | tf_op jit(solution)/shard_map/ppermute | solution.py:253
  41.2 3.2 %collective-permute-start.11 = (bf16[16,256,128]{2,1,0:T(8,128)(2,1)S(1)}, bf16[16,256,128]{2,1,0:T(8,128)(2,1)S(1)}, u32[]{:S(2)}, u32[]{:S(2)}) collective-permute-start(bf16[16,256,128]{2,1,0:T(8,128)(2,1)S(1)} %get-tuple-element.106), channel_id=1, source_target_pairs={{0,8},{8,0},{16,24},{24,16},{32,40},{40,32},{48,56},{56,48},{64,72... | collective-permute-start | bytes 3145736 | tf_op jit(solution)/shard_map/ppermute | solution.py:259
  41.2 10.1 %collective-permute-start.13 = (bf16[16,256,128]{2,1,0:T(8,128)(2,1)S(1)}, bf16[16,256,128]{2,1,0:T(8,128)(2,1)S(1)}, u32[]{:S(2)}, u32[]{:S(2)}) collective-permute-start(bf16[16,256,128]{2,1,0:T(8,128)(2,1)S(1)} %get-tuple-element.109), channel_id=1, source_target_pairs={{0,8},{8,0},{16,24},{24,16},{32,40},{40,32},{48,56},{56,48},{64,72... | collective-permute-start | bytes 3145736 | tf_op jit(solution)/shard_map/ppermute | solution.py:259
  41.7 9.6 %collective-permute-start.12 = (f32[128,256]{1,0:T(8,128)S(1)}, f32[128,256]{1,0:T(8,128)S(1)}, u32[]{:S(2)}, u32[]{:S(2)}) collective-permute-start(f32[128,256]{1,0:T(8,128)S(1)} %add_w.9.a), channel_id=1, source_target_pairs={{0,64},{8,72},{16,80},{24,88},{32,96},{40,104},{48,112},{56,120},{... | collective-permute-start | bytes 393224 | tf_op jit(solution)/shard_map/ppermute | solution.py:256
  44.5 15.3 %collective-permute-start.14 = (bf16[4,256,128]{2,1,0:T(8,128)(2,1)S(1)}, bf16[4,256,128]{2,1,0:T(8,128)(2,1)S(1)}, u32[]{:S(2)}, u32[]{:S(2)}) collective-permute-start(bf16[4,256,128]{2,1,0:T(8,128)(2,1)S(1)} %get-tuple-element.111), channel_id=1, source_target_pairs={{0,16},{8,24},{16,32},{24,40},{32,48},{40,56},{48,0},{56,8},{64,80... | collective-permute-start | bytes 786440 | tf_op jit(solution)/shard_map/ppermute | solution.py:247
  48.1 15.9 %collective-permute-start.15 = (bf16[4,256,128]{2,1,0:T(8,128)(2,1)S(1)}, bf16[4,256,128]{2,1,0:T(8,128)(2,1)S(1)}, u32[]{:S(2)}, u32[]{:S(2)}) collective-permute-start(bf16[4,256,128]{2,1,0:T(8,128)(2,1)S(1)} %get-tuple-element.112), channel_id=1, source_target_pairs={{0,32},{8,40},{16,48},{24,56},{32,0},{40,8},{48,16},{56,24},{64,96... | collective-permute-start | bytes 786440 | tf_op jit(solution)/shard_map/ppermute | solution.py:247
  51.3 8.2 %collective-permute-start.17 = (f32[128,256]{1,0:T(8,128)S(1)}, f32[128,256]{1,0:T(8,128)S(1)}, u32[]{:S(2)}, u32[]{:S(2)}) collective-permute-start(f32[128,256]{1,0:T(8,128)S(1)} %add_w.10.a), channel_id=1, source_target_pairs={{0,1},{1,0},{2,3},{3,2},{4,5},{5,4},{6,7},{7,6},{8,9},{9,8},{10,11... | collective-permute-start | bytes 393224 | tf_op jit(solution)/shard_map/ppermute | solution.py:244
  54.4 10.0 %copy-start.1 = (s32[512,16]{0,1:T(8,128)S(1)}, s32[512,16]{0,1:T(8,128)}, u32[]{:S(2)}) copy-start(s32[512,16]{0,1:T(8,128)} %param.15) | copy-start | bytes 98308
  54.4 9.7 %collective-permute-start.16 = (bf16[4,256,128]{2,1,0:T(8,128)(2,1)S(1)}, bf16[4,256,128]{2,1,0:T(8,128)(2,1)S(1)}, u32[]{:S(2)}, u32[]{:S(2)}) collective-permute-start(bf16[4,256,128]{2,1,0:T(8,128)(2,1)S(1)} %get-tuple-element.113), channel_id=1, source_target_pairs={{0,48},{8,56},{16,0},{24,8},{32,16},{40,24},{48,32},{56,40},{64,11... | collective-permute-start | bytes 786440 | tf_op jit(solution)/shard_map/ppermute | solution.py:247
  56.6 13.1 %collective-permute-start.20 = (bf16[4,256,128]{2,1,0:T(8,128)(2,1)S(1)}, bf16[4,256,128]{2,1,0:T(8,128)(2,1)S(1)}, u32[]{:S(2)}, u32[]{:S(2)}) collective-permute-start(bf16[4,256,128]{2,1,0:T(8,128)(2,1)S(1)} %get-tuple-element.130), channel_id=1, source_target_pairs={{0,16},{8,24},{16,32},{24,40},{32,48},{40,56},{48,0},{56,8},{64,80... | collective-permute-start | bytes 786440 | tf_op jit(solution)/shard_map/ppermute | solution.py:247
  59.4 14.6 %collective-permute-start.21 = (bf16[4,256,128]{2,1,0:T(8,128)(2,1)S(1)}, bf16[4,256,128]{2,1,0:T(8,128)(2,1)S(1)}, u32[]{:S(2)}, u32[]{:S(2)}) collective-permute-start(bf16[4,256,128]{2,1,0:T(8,128)(2,1)S(1)} %get-tuple-element.131), channel_id=1, source_target_pairs={{0,32},{8,40},{16,48},{24,56},{32,0},{40,8},{48,16},{56,24},{64,96... | collective-permute-start | bytes 786440 | tf_op jit(solution)/shard_map/ppermute | solution.py:247
  59.9 5.0 %collective-permute-start.18 = (f32[128,256]{1,0:T(8,128)S(1)}, f32[128,256]{1,0:T(8,128)S(1)}, u32[]{:S(2)}, u32[]{:S(2)}) collective-permute-start(f32[128,256]{1,0:T(8,128)S(1)} %add_w.11.a), channel_id=1, source_target_pairs={{0,2},{1,3},{2,0},{3,1},{4,6},{5,7},{6,4},{7,5},{8,10},{9,11},{10,... | collective-permute-start | bytes 393224 | tf_op jit(solution)/shard_map/ppermute | solution.py:250
  64.0 10.0 %collective-permute-start.22 = (bf16[4,256,128]{2,1,0:T(8,128)(2,1)S(1)}, bf16[4,256,128]{2,1,0:T(8,128)(2,1)S(1)}, u32[]{:S(2)}, u32[]{:S(2)}) collective-permute-start(bf16[4,256,128]{2,1,0:T(8,128)(2,1)S(1)} %get-tuple-element.132), channel_id=1, source_target_pairs={{0,48},{8,56},{16,0},{24,8},{32,16},{40,24},{48,32},{56,40},{64,11... | collective-permute-start | bytes 786440 | tf_op jit(solution)/shard_map/ppermute | solution.py:247
  64.2 5.0 %collective-permute-start.19 = (bf16[2,256,128]{2,1,0:T(8,128)(2,1)S(1)}, bf16[2,256,128]{2,1,0:T(8,128)(2,1)S(1)}, u32[]{:S(2)}, u32[]{:S(2)}) collective-permute-start(bf16[2,256,128]{2,1,0:T(8,128)(2,1)S(1)} %get-tuple-element.127), channel_id=1, source_target_pairs={{0,64},{8,72},{16,80},{24,88},{32,96},{40,104},{48,112},{56,120},{... | collective-permute-start | bytes 393224 | tf_op jit(solution)/shard_map/ppermute | solution.py:256
  64.9 10.3 %collective-permute-start.24 = (f32[128,256]{1,0:T(8,128)S(1)}, f32[128,256]{1,0:T(8,128)S(1)}, u32[]{:S(2)}, u32[]{:S(2)}) collective-permute-start(f32[128,256]{1,0:T(8,128)S(1)} %add_w.12.a), channel_id=1, source_target_pairs={{0,4},{1,5},{2,6},{3,7},{4,0},{5,1},{6,2},{7,3},{8,12},{9,13},{10,... | collective-permute-start | bytes 393224 | tf_op jit(solution)/shard_map/ppermute | solution.py:250
  74.1 5.0 %collective-permute-start.23 = (bf16[2,256,128]{2,1,0:T(8,128)(2,1)S(1)}, bf16[2,256,128]{2,1,0:T(8,128)(2,1)S(1)}, u32[]{:S(2)}, u32[]{:S(2)}) collective-permute-start(bf16[2,256,128]{2,1,0:T(8,128)(2,1)S(1)} %get-tuple-element.134), channel_id=1, source_target_pairs={{0,64},{8,72},{16,80},{24,88},{32,96},{40,104},{48,112},{56,120},{... | collective-permute-start | bytes 393224 | tf_op jit(solution)/shard_map/ppermute | solution.py:256
  75.3 3.9 %collective-permute-start.25 = (f32[128,256]{1,0:T(8,128)S(1)}, f32[128,256]{1,0:T(8,128)S(1)}, u32[]{:S(2)}, u32[]{:S(2)}) collective-permute-start(f32[128,256]{1,0:T(8,128)S(1)} %add_w.13.w), channel_id=1, source_target_pairs={{0,8},{8,0},{16,24},{24,16},{32,40},{40,32},{48,56},{56,48},{64,72... | collective-permute-start | bytes 393224 | tf_op jit(solution)/shard_map/ppermute | solution.py:259

commit v4 on v3

--- a/solution.py
+++ b/solution.py
@@ -14,6 +14,7 @@
 PREP_LIMIT = 61
 STAGE_LIMIT = 24
 ZERO_ROW = 32
+LOWEST = (0, 0, 32, 48)
 bf16 = jnp.bfloat16
 f32 = jnp.float32
 tie = lambda *values: lax.optimization_barrier(values)
@@ -51,7 +52,16 @@
     return ((byte >> (lane & 7)) & 1) == 1
 
 
-def prep(grad_hbm, words_hbm, agg_hbm, weight_hbm, ha_ref, hb_ref, keep_ref, send_ref, grad, words, agg, weight, part, sems):
+def both_parts(value):
+    high = value.astype(bf16)
+    return jnp.concatenate([high, (value - high.astype(f32)).astype(bf16)], 0)
+
+
+def whole(parts):
+    return parts[0:T].astype(f32) + parts[T : 2 * T].astype(f32)
+
+
+def prep(grad_hbm, words_hbm, agg_hbm, weight_hbm, ha, hb, m1, m2, m3, keep, grad, words, agg, weight, part, sems):
     copies = [
         pltpu.make_async_copy(src, dst, sems.at[i])
         for i, (src, dst) in enumerate(((words_hbm, words), (grad_hbm, grad), (weight_hbm, weight), (agg_hbm, agg)))
@@ -64,18 +74,37 @@
     masked = jnp.where(mask, grad[...], jnp.zeros((), bf16))
     copies[2].wait()
     hidden = contract(weight[...], masked, 1, 1).astype(bf16)
-    for t in range(4):
-        ref = ha_ref if t < 2 else hb_ref
-        ref[t & 1] = hidden[:, t * T : (t + 1) * T]
+    for t in range(2):
+        ha[t] = hidden[:, t * T : (t + 1) * T]
+        for ref in (hb, m1, m2, m3):
+            ref[t] = hidden[:, (t + 2) * T : (t + 3) * T]
     copies[3].wait()
     part[...] = contract(agg[...], masked, 0, 0) * (1.0 / 256.0)
-    core = lax.axis_index("row") & 1
-    keep_ref[...] = part[pl.ds(pl.multiple_of(core * T, T), T)]
-    send_ref[...] = part[pl.ds(pl.multiple_of((1 - core) * T, T), T)]
-
-
-def add_two(a, b, out):
-    out[...] = a[...] + b[...]
+    x = lax.axis_index("col") >> 1
+
+    def quarter(q):
+        rows = part[pl.ds(pl.multiple_of(q * 64, 64), 64)]
+        return jnp.concatenate([rows[:, 0:T], rows[:, T : 2 * T]], 0)
+
+    keep[...] = quarter(x)
+    for s, ref in ((1, m1), (2, m2), (3, m3)):
+        ref[2] = both_parts(quarter((x + s) & 3))
+
+
+def pack(ha, ha_y, hb, m1, m2, m3, keep, a0, b0):
+    a0[0:2], a0[2:4] = ha[...], ha_y[...]
+    b0[0:2], b0[2:4], b0[4:6], b0[6:8] = hb[...], m1[0:2], m2[0:2], m3[0:2]
+    b0[8] = both_parts((keep[...] + whole(m2[2])) + (whole(m1[2]) + whole(m3[2])))
+
+
+def sum_parts(own, got, out):
+    out[...] = whole(own[2]) + whole(got[2])
+
+
+def pair_up(own, got, out):
+    odd = (lax.axis_index("col") >> 1) & 1
+    out[odd] = own[...]
+    out[1 - odd] = got[...]
 
 
 def in_mask(words_ref, out_ref):
@@ -95,7 +124,7 @@
     late = jnp.where(jnp.where(t < 2, dx, dyh) == 0, 0, 64)
     u, q = j & 3, j >> 2
     dc, dz, dy = (q & 1) ^ core ^ 1, ((q >> 1) - z) & 3, (q >> 3) ^ y_lo
-    column = (u >> 1) * 32 + dc * 16 + dz * 4 + dy * 2 + (u & 1)
+    column = dc * 32 + (u >> 1) * 16 + dz * 4 + dy * 2 + (u & 1)
     key = jnp.where(slot < count_ref[0], column + late, T)
     both = jnp.concatenate([key, slot | (row << 9), column << 15, jnp.zeros((5, slots), jnp.int32)], 0).T
     key_c, word_c, high_c = both[:, 0:1], both[:, 1:2], both[:, 2:3]
@@ -108,11 +137,11 @@
     pairs = (held + 1) >> 1
 
     def list_of(k):
-        return jnp.where(k < 64, 0, (k >> 4) - 3)
+        return jnp.where(k < 64, 0, jnp.maximum((k >> 4) - 4, 1))
 
     start = jnp.zeros((1, 1), jnp.int32)
     starts, counts, base = (jnp.zeros((1, T), jnp.int32) for _ in range(3))
-    for number in range(5):
+    for number in range(4):
         total = jnp.sum(jnp.where(list_of(lane) == number, pairs, 0), 1, keepdims=True)
         groups = (total + UNROLL - 1) // UNROLL
         starts = jnp.where(lane == number, start, starts)
@@ -151,7 +180,7 @@
 
 
 def products(number, steps_ref, h_ref, tiles_ref, acc_ref):
-    lowest = 0 if number == 0 else (number - 1) * 16
+    lowest = LOWEST[number]
     spare = acc_ref.shape[0] - 1
 
     def some(g, carry):
@@ -172,7 +201,7 @@
 
 
 def early(steps_ref, a0, b0, tiles_ref, acc_ref, h_ref):
-    h_ref[0:4], h_ref[16:24] = a0[...], b0[...]
+    h_ref[0:4], h_ref[16:24] = a0[...], b0[0:8]
     h_ref[ZERO_ROW] = jnp.zeros((256, T), bf16)
 
     def clear(k, carry):
@@ -183,52 +212,74 @@
     products(0, steps_ref, h_ref, tiles_ref, acc_ref)
 
 
-def late(number, steps_ref, h_ref, tiles_ref, so_far_ref, out_ref, acc_ref):
-    base = (number - 1) * 16
+def late(number, steps_ref, h_ref, tiles_ref, so_far_ref, outs, acc_ref):
+    base, columns = LOWEST[number], 16 * len(outs)
 
     def take(k, carry):
         acc_ref[k] = so_far_ref[base + k]
         return carry
 
-    lax.fori_loop(0, 16, take, 0)
-    acc_ref[16] = jnp.zeros((256, T), f32)
+    lax.fori_loop(0, columns, take, 0)
+    acc_ref[columns] = jnp.zeros((256, T), f32)
     products(number, steps_ref, h_ref, tiles_ref, acc_ref)
-
-    def give(k, carry):
-        out_ref[k] = acc_ref[k].astype(out_ref.dtype)
-        return carry
-
-    lax.fori_loop(0, 16, give, 0)
-
-
-def late_first(steps_ref, a0, a3, a1, a2, b0, b1, tiles_ref, so_far_ref, p_ref, q_ref, h_ref, acc_ref):
+    for i, ref in enumerate(outs):
+
+        def give(k, carry, i=i, ref=ref):
+            ref[k] = acc_ref[16 * i + k].astype(ref.dtype)
+            return carry
+
+        lax.fori_loop(0, 16, give, 0)
+
+
+def late_partner(steps_ref, a0, a3, a1, a2, b0, b1, tiles_ref, so_far_ref, p_ref, q_ref, h_ref, acc_ref):
     h_ref[0:4], h_ref[4:8], h_ref[8:12], h_ref[12:16] = a0[...], a1[...], a2[...], a3[...]
-    h_ref[16:24], h_ref[24:32] = b0[...], b1[...]
+    h_ref[16:24], h_ref[24:32] = b0[0:8], b1[0:8]
     h_ref[ZERO_ROW] = jnp.zeros((256, T), bf16)
-    late(1, steps_ref, h_ref, tiles_ref, so_far_ref, p_ref, acc_ref)
-    late(3, steps_ref, h_ref, tiles_ref, so_far_ref, q_ref, acc_ref)
-
-
-def join_cores(acc_ref, got_ref, keep, z1, z2, z3):
+    p_ref[16] = both_parts(whole(b0[8]) + whole(b1[8]))
+    late(1, steps_ref, h_ref, tiles_ref, so_far_ref, (p_ref, q_ref), acc_ref)
+
+
+def late_own(number, steps_ref, h_ref, tiles_ref, so_far_ref, out_ref, acc_ref):
+    late(number, steps_ref, h_ref, tiles_ref, so_far_ref, (out_ref,), acc_ref)
+
+
+def split_q(acc_ref, got_ref, keep, z1, z2, z3):
     for k in range(4):
         keep[k] = acc_ref[k] + got_ref[k].astype(f32)
         for dz, ref in ((1, z1), (2, z2), (3, z3)):
-            ref[k] = (acc_ref[4 * dz + k] + got_ref[4 * dz + k].astype(f32)).astype(bf16)
-
-
-def join_z(keep_ref, g1, g2, g3, keep, y):
+            ref[k * 256 : (k + 1) * 256] = (acc_ref[4 * dz + k] + got_ref[4 * dz + k].astype(f32)).astype(bf16)
+
+
+def split_p(acc_ref, got_ref, sent_ref, keep, z1, z2, z3):
+    split_q(acc_ref, got_ref, keep, z1, z2, z3)
+    total = (whole(sent_ref[16]) + whole(got_ref[16])).astype(bf16)
+    for ref in (z1, z2, z3):
+        ref[1024 : 1024 + T] = total
+
+
+def gather_q(keep_ref, g1, g2, g3, keep, y):
     for k in range(4):
-        total = keep_ref[k] + g1[k].astype(f32) + g2[k].astype(f32) + g3[k].astype(f32)
+        rows = slice(k * 256, (k + 1) * 256)
+        total = keep_ref[k] + g1[rows].astype(f32) + g2[rows].astype(f32) + g3[rows].astype(f32)
         if k < 2:
             keep[k] = total
         else:
             y[k - 2] = total.astype(bf16)
 
 
+def gather_p(keep_ref, g1, g2, g3, sent_ref, keep, y):
+    gather_q(keep_ref, g1, g2, g3, keep, y)
+    own, left, across, right = (ref[1024 : 1024 + T].astype(f32) for ref in (sent_ref, g1, g2, g3))
+    y[2] = both_parts((own + across) + (left + right))
+
+
 def finish(p_keep, p_got, q_keep, q_got, mask_ref, w, w_got, out_ref, weight_ref):
-    core = lax.axis_index("row") & 1
-    weight_ref[pl.ds(pl.multiple_of(core * T, T), T)] = w[...]
-    weight_ref[pl.ds(pl.multiple_of((1 - core) * T, T), T)] = w_got[...]
+    upper = lax.axis_index("col") >> 2
+    for pair, ref in ((upper, w), (1 - upper, w_got)):
+        for i in range(2):
+            rows = pl.ds(pl.multiple_of(pair * T + i * 64, 64), 64)
+            weight_ref[rows, 0:T] = ref[i, 0:64]
+            weight_ref[rows, T : 2 * T] = ref[i, 64:T]
     for t in range(4):
         keep, got = (p_keep, p_got) if t < 2 else (q_keep, q_got)
         total = keep[t & 1] + got[t & 1].astype(f32)
@@ -249,19 +300,16 @@
     def swap_x(v, bit):
         return lax.ppermute(v, "col", [(c, c ^ (2 << bit)) for c in range(8)])
 
-    def swap_z(v, bit):
-        return lax.ppermute(v, "row", [(r, r ^ (2 << bit)) for r in range(16)])
-
     def over_y_lo(v):
         return lax.ppermute(v, "row", [(r, r ^ 8) for r in range(16)])
 
     def over_core(v):
         return lax.ppermute(v, "row", [(r, r ^ 1) for r in range(16)])
 
-    half, quad, part = (2, 256, T), (4, 256, T), (T, 256)
-    ha, hb, w, w_send = call(
+    half, three, quad, square = (2, 256, T), (3, 256, T), (4, 256, T), (T, T)
+    ha, hb, m1, m2, m3, w = call(
         prep,
-        [(half, bf16), (half, bf16), (part, f32), (part, f32)],
+        [(half, bf16)] * 2 + [(three, bf16)] * 3 + [(square, f32)],
         [ANY] * 4,
         "prep",
         limit=PREP_LIMIT,
@@ -276,9 +324,8 @@
         flops=2 * 10**8,
     )(out_grad, out_bits.T, agg_saved, weight)
 
-    w_got = over_core(w_send)
     ha_y = over_y_hi(ha)
-    hb_1, hb_2, hb_3 = over_x(hb, -1), over_x(hb, 2), over_x(hb, 1)
+    m3, m2, m1 = over_x(m1, 1), over_x(m2, 2), over_x(m3, 3)
     count, own_tiles, ha = tie(tile_count.reshape(1), tiles[0, 0], ha)
     (own_tiles,) = call(
         stage,
@@ -289,18 +336,16 @@
         scratch=[pltpu.SemaphoreType.DMA((8,))],
         flops=10**9,
     )(count, own_tiles)
-    ha, ha_y, hb, hb_1, hb_2, hb_3, own_tiles, w_got, coords, count = tie(
-        ha, ha_y, hb, hb_1, hb_2, hb_3, own_tiles, w_got, tile_coords[0, 0].T, count
-    )
-
-    a0 = jnp.concatenate([ha, ha_y], 0)
-    b0 = jnp.concatenate([hb, hb_1, hb_2, hb_3], 0)
+    ha, ha_y, hb, m1, m2, m3, own_tiles, coords, count = tie(
+        ha, ha_y, hb, m1, m2, m3, own_tiles, tile_coords[0, 0].T, count
+    )
+
+    a0, b0 = call(pack, [(quad, bf16), ((9, 256, T), bf16)], [VMEM] * 7, "pack", flops=10**6)(
+        ha, ha_y, hb, m1, m2, m3, w
+    )
+    b1 = over_y_hi(b0)
     a3, a1, a2 = over_x(a0, 1), over_x(a0, -1), over_x(a0, 2)
-    b1 = over_y_hi(b0)
-    add_w = call(add_two, [(part, f32)], [VMEM] * 2, "add_w", limit=2)
     (steps,) = call(order_slots, [((8, N_STEP), jnp.int32)], [SMEM, VMEM], "order_slots", flops=10**7)(count, coords)
-    (w,) = add_w(w, w_got)
-    w_got = swap_z(w, 0)
     (acc,) = call(
         early,
         [((65, 256, T), f32)],
@@ -310,69 +355,57 @@
         scratch=[pltpu.VMEM((33, 256, T), bf16)],
         flops=4 * 10**9,
     )(steps, a0, b0, own_tiles)
-    acc, w, w_got = tie(acc, w, w_got)
-    (w,) = add_w(w, w_got)
-    a0, a1, a2, a3, b0, b1, acc, w = tie(a0, a1, a2, a3, b0, b1, acc, w)
-    w_got = swap_z(w, 1)
-
-    cost = dict(flops=2 * 10**9)
-    group = [pltpu.VMEM((17, 256, T), f32)]
+    a0, a1, a2, a3, b0, b1, acc = tie(a0, a1, a2, a3, b0, b1, acc)
+
     sixteen = (16, 256, T)
-
-    def later(number, kind):
-        body = functools.partial(late, number)
-        name = "late_" + str(number)
-        outs = [(sixteen, kind)]
-        return call(body, outs, [SMEM] + [VMEM] * 3, name, limit=LIMIT, scratch=group, **cost)
-
-    def split(own, got, name):
-        outs = [(quad, f32)] + [(quad, bf16)] * 3
-        return call(join_cores, outs, [VMEM] * 2, name, flops=10**6)(own, got)
+    z_p, z_q = (1024 + T, T), (1024, T)
+
+    def own_columns(number):
+        return call(
+            functools.partial(late_own, number),
+            [(sixteen, f32)],
+            [SMEM] + [VMEM] * 3,
+            "late_" + str(number),
+            limit=LIMIT,
+            scratch=[pltpu.VMEM((17, 256, T), f32)],
+            flops=2 * 10**9,
+        )(steps, hidden, own_tiles, acc)[0]
 
     def around_z(z1, z2, z3):
-        return over_z(z1, 1), over_z(z2, 2), over_z(z3, -1)
-
-    def gather_z(keep, got, name):
-        return call(join_z, [(half, f32), (half, bf16)], [VMEM] * 4, name, flops=10**6)(keep, *got)
-
-    p_partner, q_partner, hidden = call(
-        late_first,
-        [(sixteen, bf16), (sixteen, bf16), ((33, 256, T), bf16)],
+        return over_z(z1, 1), over_z(z2, 2), over_z(z3, 3)
+
+    p_sent, q_sent, hidden = call(
+        late_partner,
+        [((17, 256, T), bf16), (sixteen, bf16), ((33, 256, T), bf16)],
         [SMEM] + [VMEM] * 8,
-        "late_first",
+        "late_1",
         limit=LIMIT,
-        scratch=group,
-        **cost,
+        scratch=[pltpu.VMEM((33, 256, T), f32)],
+        flops=4 * 10**9,
     )(steps, a0, a3, a1, a2, b0, b1, own_tiles, acc)
-    p_partner, q_partner, hidden, w, w_got = tie(p_partner, q_partner, hidden, w, w_got)
-    p_partner, q_partner = over_core(p_partner), over_core(q_partner)
-    (w,) = add_w(w, w_got)
-    hidden, w = tie(hidden, w)
-    w_got = over_y_lo(w)
-    (own,) = later(2, f32)(steps, hidden, own_tiles, acc)
-    p_keep, *p_z = split(own, p_partner, "split_p")
-    p_z = around_z(*p_z)
-    p_keep, hidden, w, w_got, q_partner = tie(p_keep, hidden, w, w_got, q_partner)
-    (w,) = add_w(w, w_got)
-    hidden, w = tie(hidden, w)
-    w_got = over_y_hi(w)
-    (own,) = later(4, f32)(steps, hidden, own_tiles, acc)
-    q_keep, *q_z = split(own, q_partner, "split_q")
-    q_z = around_z(*q_z)
-    q_keep, w, w_got, words = tie(q_keep, w, w_got, in_bits.T)
-    (w,) = add_w(w, w_got)
-    w_got = swap_x(w, 0)
+    p_got, q_got = over_core(p_sent), over_core(q_sent)
+    own = own_columns(2)
+    p_keep, *p_z = call(split_p, [(quad, f32)] + [(z_p, bf16)] * 3, [VMEM] * 3, "split_p", flops=10**6)(
+        own, p_got, p_sent
+    )
+    p_all = around_z(*p_z)
+    p_keep, hidden, q_got = tie(p_keep, hidden, q_got)
+    own = own_columns(3)
+    q_keep, *q_z = call(split_q, [(quad, f32)] + [(z_q, bf16)] * 3, [VMEM] * 2, "split_q", flops=10**6)(own, q_got)
+    q_all = around_z(*q_z)
+    p_keep, q_keep, words = tie(p_keep, q_keep, in_bits.T)
     (mask,) = call(in_mask, [((512, 256), bf16)], [VMEM], "in_mask", flops=10**7)(words)
-    p_keep, p_y = gather_z(p_keep, p_z, "gather_p")
+    p_keep, p_y = call(gather_p, [(half, f32), (three, bf16)], [VMEM] * 5, "gather_p", flops=10**6)(
+        p_keep, *p_all, p_z[0]
+    )
     p_got = over_y_lo(p_y)
-    p_keep, w, w_got, mask = tie(p_keep, w, w_got, mask)
-    (w,) = add_w(w, w_got)
+    p_keep, p_got, q_keep, mask = tie(p_keep, p_got, q_keep, mask)
+    q_keep, q_y = call(gather_q, [(half, f32), (half, bf16)], [VMEM] * 4, "gather_q", flops=10**6)(q_keep, *q_all)
+    q_got = over_y_lo(q_y)
+    p_y, p_got, q_keep = tie(p_y, p_got, q_keep)
+    (w,) = call(sum_parts, [(square, f32)], [VMEM] * 2, "sum_parts", limit=2)(p_y, p_got)
+    (w,) = call(pair_up, [((2, T, T), f32)], [VMEM] * 2, "pair_up", limit=2)(w, swap_x(w, 0))
     w_got = swap_x(w, 1)
-    (w,) = add_w(w, w_got)
-    w_got = over_core(w)
-    q_keep, p_got = tie(q_keep, p_got)
-    q_keep, q_y = gather_z(q_keep, q_z, "gather_q")
-    q_got = over_y_lo(q_y)
     prev_grad, weight_grad = call(
         finish, [((512, 256), bf16), ((256, 256), f32)], [VMEM] * 7, "finish", flops=10**6
     )(p_keep, p_got, q_keep, q_got, mask, w, w_got)

time: 81.6 us -> 86.9 us (1.065)
  Pallas kernels: 17.7 us -> 21.2 us
  waiting for transfers between devices: 24.5 us -> 27.9 us
  starting transfers between devices: 36.2 us -> 34.9 us
    ppermute x2 -> x0, starting transfers between devices: 5.88 us -> none  [swap_z(): return lax.ppermute(v, 'row', [(r, r ^ 2 << bit) for r in range(16)])]
    ppermute x2, waiting for transfers between devices: 0.28 us -> 3.76 us  [swap_x(): return lax.ppermute(v, 'col', [(c, c ^ 2 << bit) for c in range(8)])]
    ppermute x3 -> x2, starting transfers between devices: 9.57 us -> 6.46 us  [over_y_hi(): return lax.ppermute(v, 'col', [(c, c ^ 1) for c in range(8)])]
    ppermute x2, starting transfers between devices: 0.6 us -> 3.45 us  [swap_x(): return lax.ppermute(v, 'col', [(c, c ^ 2 << bit) for c in range(8)])]
    ppermute x3 -> x2, starting transfers between devices: 2.04 us -> 4.43 us  [over_y_lo(): return lax.ppermute(v, 'row', [(r, r ^ 8) for r in range(16)])]
    ppermute x6, waiting for transfers between devices: 7.55 us -> 9.5 us  [over_x(): lax.ppermute(v, 'col', [(c, ((c >> 1) + s & 3) * 2 + (c & 1)) for c in ra...]
    ppermute x6, starting transfers between devices: 10.1 us -> 11.9 us  [over_z(): lax.ppermute(v, 'row', [(r, r & 9 | ((r >> 1) + s & 3) << 1) for r in ran...]
    pallas_call x1, Pallas kernels: 2.94 us -> 4.37 us  [shards(): call(early, [((65, 256, T), f32)], [SMEM] + [VMEM] * 3, 'early', limit=LI...]
  transfers between devices with their start and end apart: 26 -> 20, of which waited for: 12 -> 12; matrix products, arithmetic and copies ran while one was open for 0% -> 0% of each run, Pallas kernels for 18% -> 17%
where the time goes in v4:
time: 86.9 us; the launch traced here: 85.5 us
  starting transfers between devices  34.9 us (40%)
  waiting for transfers between devices  27.9 us (32%)
  Pallas kernels  21.2 us (24%)
  between operations  1.47 us (2%)
    ppermute x6, starting transfers between devices, over_z(): lax.ppermute(v, 'row', [(r, r & 9 | ((r >> 1) + s & 3) << 1) for r in ran...  11.9 us
    ppermute x6, waiting for transfers between devices, over_x(): lax.ppermute(v, 'col', [(c, ((c >> 1) + s & 3) * 2 + (c & 1)) for c in ra...  9.5 us
    ppermute x6, starting transfers between devices, over_x(): lax.ppermute(v, 'col', [(c, ((c >> 1) + s & 3) * 2 + (c & 1)) for c in ra...  8.03 us
    ppermute x6, waiting for transfers between devices, over_z(): lax.ppermute(v, 'row', [(r, r & 9 | ((r >> 1) + s & 3) << 1) for r in ran...  7.93 us
    ppermute x2, starting transfers between devices, over_y_hi(): return lax.ppermute(v, 'col', [(c, c ^ 1) for c in range(8)])  6.46 us
    ppermute x2, waiting for transfers between devices, over_y_lo(): return lax.ppermute(v, 'row', [(r, r ^ 8) for r in range(16)])  6.4 us
    pallas_call x2, Pallas kernels, own_columns(): call(functools.partial(late_own, number), [(sixteen, f32)], [SMEM] + [VME...  4.48 us
    ppermute x2, starting transfers between devices, over_y_lo(): return lax.ppermute(v, 'row', [(r, r ^ 8) for r in range(16)])  4.43 us
  transfers between devices with their start and end apart: 20, of which 12 were waited for; matrix products, arithmetic and copies ran while one was open for 0% of the time, Pallas kernels for 17%

profile of v4, /device:TPU:0, one launch (start us, length us, event | category | flops | bytes accessed | tf_op | source)
XLA Modules:
  0.0 85.5 jit_solution(1467052230248224721)
XLA Ops:
  0.6 2.6 %prep.1 = (bf16[2,256,128]{2,1,0:T(8,128)(2,1)}, bf16[2,256,128]{2,1,0:T(8,128)(2,1)}, bf16[3,256,128]{2,1,0:T(8,128)(2,1)}, bf16[3,256,128]{2,1,0:T(8,128)(2,1)...) custom-call(bf16[512,256]{1,0:T(8,128)(2,1)} %grad_hbm.1, s32[16,512]{1,0:T(8,128)} %bitcast.12, ...), custom_call_target="tpu_custom_call" | custom-call | flops 200000000 | tf_op jit(solution)/shard_map/prep/pallas_call | solution.py:310
  3.2 2.9 %collective-permute-start.1 = (bf16[3,256,128]{2,1,0:T(8,128)(2,1)}, bf16[3,256,128]{2,1,0:T(8,128)(2,1)S(1)}, u32[]{:S(2)}, u32[]{:S(2)}) collective-permute-start(bf16[3,256,128]{2,1,0:T(8,128)(2,1)} %get-tuple-element.62), channel_id=1, source_target_pairs={{0,6},{1,7},{2,0},{3,1},{4,2},{5,3},{6,4},{7,5},{8,14},{9,15},{10,... | collective-permute-start | bytes 589832 | tf_op jit(solution)/shard_map/ppermute | solution.py:292
  6.1 0.8 collective-permute-start.2
  6.9 0.9 %collective-permute-start.3 = (bf16[3,256,128]{2,1,0:T(8,128)(2,1)}, bf16[3,256,128]{2,1,0:T(8,128)(2,1)S(1)}, u32[]{:S(2)}, u32[]{:S(2)}) collective-permute-start(bf16[3,256,128]{2,1,0:T(8,128)(2,1)} %get-tuple-element.64), channel_id=1, source_target_pairs={{0,2},{1,3},{2,4},{3,5},{4,6},{5,7},{6,0},{7,1},{8,10},{9,11},{10,... | collective-permute-start | bytes 589832 | tf_op jit(solution)/shard_map/ppermute | solution.py:292
  7.8 3.2 %collective-permute-start = (bf16[2,256,128]{2,1,0:T(8,128)(2,1)}, bf16[2,256,128]{2,1,0:T(8,128)(2,1)S(1)}, u32[]{:S(2)}, u32[]{:S(2)}) collective-permute-start(bf16[2,256,128]{2,1,0:T(8,128)(2,1)} %get-tuple-element.69.ha), channel_id=1, source_target_pairs={{0,1},{1,0},{2,3},{3,2},{4,5},{5,4},{6,7},{7,6},{8,9},{9,8},{10,11... | collective-permute-start | bytes 393224 | tf_op jit(solution)/shard_map/ppermute | solution.py:295
  11.7 0.0 copy-start.4
  11.7 3.6 %stage.1.tiles_ref = bf16[512,128,128]{2,1,0:T(8,128)(2,1)S(1)} custom-call(s32[1]{0:T(128)} %bitcast.7.count_ref, bf16[512,128,128]{2,1,0:T(8,128)(2,1)} %bitcast.11), custom_call_target="tpu_custom_call" | custom-call | flops 1000000000 | tf_op jit(solution)/shard_map/stage/pallas_call | solution.py:330
  15.3 0.0 collective-permute-done.ha_y
  15.3 0.4 collective-permute-done.2.m2
  15.7 2.7 %collective-permute-done.3.m3 = bf16[3,256,128]{2,1,0:T(8,128)(2,1)S(1)} collective-permute-done((bf16[3,256,128]{2,1,0:T(8,128)(2,1)}, bf16[3,256,128]{2,1,0:T(8,128)(2,1)S(1)}, u32[]{:S(2)}, u32[]{:S(2)}) %collective-permute-start.3) | collective-permute-done | bytes 196640 | tf_op jit(solution)/shard_map/ppermute | solution.py:292
  18.4 0.1 pack.1
  18.5 3.3 %collective-permute-start.7 = (bf16[9,256,128]{2,1,0:T(8,128)(2,1)S(1)}, bf16[9,256,128]{2,1,0:T(8,128)(2,1)S(1)}, u32[]{:S(2)}, u32[]{:S(2)}) collective-permute-start(bf16[9,256,128]{2,1,0:T(8,128)(2,1)S(1)} %get-tuple-element.83.b0), channel_id=1, source_target_pairs={{0,1},{1,0},{2,3},{3,2},{4,5},{5,4},{6,7},{7,6},{8,9},{9,8},{10,11... | collective-permute-start | bytes 1769480 | tf_op jit(solution)/shard_map/ppermute | solution.py:295
  21.8 2.1 %collective-permute-start.5 = (bf16[4,256,128]{2,1,0:T(8,128)(2,1)S(1)}, bf16[4,256,128]{2,1,0:T(8,128)(2,1)S(1)}, u32[]{:S(2)}, u32[]{:S(2)}) collective-permute-start(bf16[4,256,128]{2,1,0:T(8,128)(2,1)S(1)} %get-tuple-element.79.a0), channel_id=1, source_target_pairs={{0,4},{1,5},{2,6},{3,7},{4,0},{5,1},{6,2},{7,3},{8,12},{9,13},{10,... | collective-permute-start | bytes 786440 | tf_op jit(solution)/shard_map/ppermute | solution.py:292
  23.9 1.4 %collective-permute-start.4 = (bf16[4,256,128]{2,1,0:T(8,128)(2,1)S(1)}, bf16[4,256,128]{2,1,0:T(8,128)(2,1)S(1)}, u32[]{:S(2)}, u32[]{:S(2)}) collective-permute-start(bf16[4,256,128]{2,1,0:T(8,128)(2,1)S(1)} %get-tuple-element.79.a0), channel_id=1, source_target_pairs={{0,6},{1,7},{2,0},{3,1},{4,2},{5,3},{6,4},{7,5},{8,14},{9,15},{10,... | collective-permute-start | bytes 786440 | tf_op jit(solution)/shard_map/ppermute | solution.py:292
  25.2 1.2 %order_slots.1.steps_ref = s32[8,512]{1,0:T(8,128)S(1)} custom-call(s32[1]{0:T(128)} %bitcast.8.count_ref, s32[2,512]{1,0:T(2,128)S(1)} %bitcast.10), custom_call_target="tpu_custom_call" | custom-call | flops 10000000 | tf_op jit(solution)/shard_map/order_slots/pallas_call | solution.py:348
  26.4 4.4 %early.1.so_far_ref = f32[65,256,128]{2,1,0:T(8,128)S(1)} custom-call(s32[8,512]{1,0:T(8,128)S(1)} %order_slots.1.steps_ref, bf16[4,256,128]{2,1,0:T(8,128)(2,1)S(1)} %get-tuple-element.79.a0, bf16[9,256,128]{2,1,0:T(8,128)(2,1)S(1)} %get-tuple-element.83.b0, bf16[512,128,128]{2,1,0:T(8,128)(2,1)S(1)} %stage.1.tiles_ref), custom_call_target="tpu_custom_call" | custom-call | flops 4000000000 | tf_op jit(solution)/shard_map/early/pallas_call | solution.py:349
  30.8 5.8 %collective-permute-done.6.a3 = bf16[4,256,128]{2,1,0:T(8,128)(2,1)S(1)} collective-permute-done((bf16[4,256,128]{2,1,0:T(8,128)(2,1)S(1)}, bf16[4,256,128]{2,1,0:T(8,128)(2,1)S(1)}, u32[]{:S(2)}, u32[]{:S(2)}) %collective-permute-start.6) | collective-permute-done | bytes 262176 | tf_op jit(solution)/shard_map/ppermute | solution.py:292
  36.6 0.6 collective-permute-done.4.a1
  37.2 3.1 %late_1.1 = (bf16[17,256,128]{2,1,0:T(8,128)(2,1)S(1)}, bf16[16,256,128]{2,1,0:T(8,128)(2,1)S(1)}, bf16[33,256,128]{2,1,0:T(8,128)(2,1)S(1)}) custom-call(s32[8,512]{1,0:T(8,128)S(1)} %order_slots.1.steps_ref, bf16[4,256,128]{2,1,0:T(8,128)(2,1)S(1)} %get-tuple-element.79.a0, bf16[4,256,128]{2,1,0:T(8,128)(2,1)S(1)} %collective-permute-done.6.a3, ...), custom_call_target="tpu_custom_call" | custom-call | flops 4000000000 | tf_op jit(solution)/shard_map/late_1/pallas_call | solution.py:377
  40.3 0.1 collective-permute-start.8
  40.4 0.5 collective-permute-start.9
  40.9 1.9 %late_2.1.acc_ref = f32[16,256,128]{2,1,0:T(8,128)S(1)} custom-call(s32[8,512]{1,0:T(8,128)S(1)} %order_slots.1.steps_ref, bf16[33,256,128]{2,1,0:T(8,128)(2,1)S(1)} %get-tuple-element.91.h_ref, bf16[512,128,128]{2,1,0:T(8,128)(2,1)S(1)} %stage.1.tiles_ref, f32[65,256,128]{2,1,0:T(8,128)S(1)} %early.1.so_far_ref), custom_call_target="tpu_custom_call" | custom-call | flops 2000000000 | tf_op jit(solution)/shard_map/late_2/pallas_call | solution.py:364
  42.8 0.3 collective-permute-done.8.got_ref
  43.1 0.2 split_p.1
  43.3 5.0 %collective-permute-start.11 = (bf16[1152,128]{1,0:T(8,128)(2,1)S(1)}, bf16[1152,128]{1,0:T(8,128)(2,1)S(1)}, u32[]{:S(2)}, u32[]{:S(2)}) collective-permute-start(bf16[1152,128]{1,0:T(8,128)(2,1)S(1)} %get-tuple-element.96), channel_id=1, source_target_pairs={{0,32},{8,40},{16,48},{24,56},{32,0},{40,8},{48,16},{56,24},{64,96... | collective-permute-start | bytes 884744 | tf_op jit(solution)/shard_map/ppermute | solution.py:298
  48.3 1.5 %collective-permute-start.12 = (bf16[1152,128]{1,0:T(8,128)(2,1)S(1)}, bf16[1152,128]{1,0:T(8,128)(2,1)S(1)}, u32[]{:S(2)}, u32[]{:S(2)}) collective-permute-start(bf16[1152,128]{1,0:T(8,128)(2,1)S(1)} %get-tuple-element.97), channel_id=1, source_target_pairs={{0,48},{8,56},{16,0},{24,8},{32,16},{40,24},{48,32},{56,40},{64,11... | collective-permute-start | bytes 884744 | tf_op jit(solution)/shard_map/ppermute | solution.py:298
  49.8 0.6 collective-permute-start.10
  50.3 2.6 %late_3.1.acc_ref = f32[16,256,128]{2,1,0:T(8,128)S(1)} custom-call(s32[8,512]{1,0:T(8,128)S(1)} %order_slots.1.steps_ref, bf16[33,256,128]{2,1,0:T(8,128)(2,1)S(1)} %get-tuple-element.91.h_ref, bf16[512,128,128]{2,1,0:T(8,128)(2,1)S(1)} %stage.1.tiles_ref, f32[65,256,128]{2,1,0:T(8,128)S(1)} %early.1.so_far_ref), custom_call_target="tpu_custom_call" | custom-call | flops 2000000000 | tf_op jit(solution)/shard_map/late_3/pallas_call | solution.py:364
  52.9 0.0 copy-start.3
  53.0 0.2 split_q.1
  53.1 0.1 collective-permute-start.14
  53.2 3.4 %collective-permute-start.15 = (bf16[1024,128]{1,0:T(8,128)(2,1)S(1)}, bf16[1024,128]{1,0:T(8,128)(2,1)S(1)}, u32[]{:S(2)}, u32[]{:S(2)}) collective-permute-start(bf16[1024,128]{1,0:T(8,128)(2,1)S(1)} %get-tuple-element.106), channel_id=1, source_target_pairs={{0,32},{8,40},{16,48},{24,56},{32,0},{40,8},{48,16},{56,24},{64,96... | collective-permute-start | bytes 786440 | tf_op jit(solution)/shard_map/ppermute | solution.py:298
  56.6 1.4 %collective-permute-start.16 = (bf16[1024,128]{1,0:T(8,128)(2,1)S(1)}, bf16[1024,128]{1,0:T(8,128)(2,1)S(1)}, u32[]{:S(2)}, u32[]{:S(2)}) collective-permute-start(bf16[1024,128]{1,0:T(8,128)(2,1)S(1)} %get-tuple-element.107), channel_id=1, source_target_pairs={{0,48},{8,56},{16,0},{24,8},{32,16},{40,24},{48,32},{56,40},{64,11... | collective-permute-start | bytes 786440 | tf_op jit(solution)/shard_map/ppermute | solution.py:298
  58.0 3.6 %collective-permute-done.12.g3 = bf16[1152,128]{1,0:T(8,128)(2,1)S(1)} collective-permute-done((bf16[1152,128]{1,0:T(8,128)(2,1)S(1)}, bf16[1152,128]{1,0:T(8,128)(2,1)S(1)}, u32[]{:S(2)}, u32[]{:S(2)}) %collective-permute-start.12) | collective-permute-done | bytes 294944 | tf_op jit(solution)/shard_map/ppermute | solution.py:298
  61.7 0.9 %collective-permute-done.10.g1 = bf16[1152,128]{1,0:T(8,128)(2,1)S(1)} collective-permute-done((bf16[1152,128]{1,0:T(8,128)(2,1)S(1)}, bf16[1152,128]{1,0:T(8,128)(2,1)S(1)}, u32[]{:S(2)}, u32[]{:S(2)}) %collective-permute-start.10) | collective-permute-done | bytes 294944 | tf_op jit(solution)/shard_map/ppermute | solution.py:298
  62.6 0.1 gather_p.1
  62.7 0.9 %collective-permute-start.13 = (bf16[3,256,128]{2,1,0:T(8,128)(2,1)S(1)}, bf16[3,256,128]{2,1,0:T(8,128)(2,1)S(1)}, u32[]{:S(2)}, u32[]{:S(2)}) collective-permute-start(bf16[3,256,128]{2,1,0:T(8,128)(2,1)S(1)} %get-tuple-element.113.own), channel_id=1, source_target_pairs={{0,64},{8,72},{16,80},{24,88},{32,96},{40,104},{48,112},{56,120},{... | collective-permute-start | bytes 589832 | tf_op jit(solution)/shard_map/ppermute | solution.py:304
  63.7 0.3 in_mask.1.mask_ref
  64.0 5.7 %collective-permute-done.13.got.p_got = bf16[3,256,128]{2,1,0:T(8,128)(2,1)S(1)} collective-permute-done((bf16[3,256,128]{2,1,0:T(8,128)(2,1)S(1)}, bf16[3,256,128]{2,1,0:T(8,128)(2,1)S(1)}, u32[]{:S(2)}, u32[]{:S(2)}) %collective-permute-start.13) | collective-permute-done | bytes 196640 | tf_op jit(solution)/shard_map/ppermute | solution.py:304
  69.6 3.4 %collective-permute-done.15.g2 = bf16[1024,128]{1,0:T(8,128)(2,1)S(1)} collective-permute-done((bf16[1024,128]{1,0:T(8,128)(2,1)S(1)}, bf16[1024,128]{1,0:T(8,128)(2,1)S(1)}, u32[]{:S(2)}, u32[]{:S(2)}) %collective-permute-start.15) | collective-permute-done | bytes 262176 | tf_op jit(solution)/shard_map/ppermute | solution.py:298
  73.0 0.1 gather_q.1
  73.2 0.9 %collective-permute-start.18 = (f32[128,128]{1,0:T(8,128)S(1)}, f32[128,128]{1,0:T(8,128)S(1)}, u32[]{:S(2)}, u32[]{:S(2)}) collective-permute-start(f32[128,128]{1,0:T(8,128)S(1)} %sum_parts.1.own), channel_id=1, source_target_pairs={{0,2},{1,3},{2,0},{3,1},{4,6},{5,7},{6,4},{7,5},{8,10},{9,11},{10,... | collective-permute-start | bytes 196616 | tf_op jit(solution)/shard_map/ppermute | solution.py:301
  74.1 3.5 %collective-permute-start.17 = (bf16[2,256,128]{2,1,0:T(8,128)(2,1)S(1)}, bf16[2,256,128]{2,1,0:T(8,128)(2,1)S(1)}, u32[]{:S(2)}, u32[]{:S(2)}) collective-permute-start(bf16[2,256,128]{2,1,0:T(8,128)(2,1)S(1)} %get-tuple-element.111), channel_id=1, source_target_pairs={{0,64},{8,72},{16,80},{24,88},{32,96},{40,104},{48,112},{56,120},{... | collective-permute-start | bytes 393224 | tf_op jit(solution)/shard_map/ppermute | solution.py:304
  77.6 0.2 collective-permute-done.18.got
  77.8 2.5 %collective-permute-start.19 = (f32[2,128,128]{2,1,0:T(8,128)S(1)}, f32[2,128,128]{2,1,0:T(8,128)S(1)}, u32[]{:S(2)}, u32[]{:S(2)}) collective-permute-start(f32[2,128,128]{2,1,0:T(8,128)S(1)} %pair_up.1.w), channel_id=1, source_target_pairs={{0,4},{1,5},{2,6},{3,7},{4,0},{5,1},{6,2},{7,3},{8,12},{9,13},{10,... | collective-permute-start | bytes 393224 | tf_op jit(solution)/shard_map/ppermute | solution.py:301
  80.3 0.7 collective-permute-done.17.q_got
  81.1 3.5 %collective-permute-done.19.w_got = f32[2,128,128]{2,1,0:T(8,128)S(1)} collective-permute-done((f32[2,128,128]{2,1,0:T(8,128)S(1)}, f32[2,128,128]{2,1,0:T(8,128)S(1)}, u32[]{:S(2)}, u32[]{:S(2)}) %collective-permute-start.19) | collective-permute-done | bytes 131104 | tf_op jit(solution)/shard_map/ppermute | solution.py:301
  84.6 0.9 %finish.1 = (bf16[512,256]{1,0:T(8,128)(2,1)}, f32[256,256]{1,0:T(8,128)}) custom-call(f32[2,256,128]{2,1,0:T(8,128)S(1)} %get-tuple-element.102.p_keep, bf16[3,256,128]{2,1,0:T(8,128)(2,1)S(1)} %collective-permute-done.13.got.p_got, f32[2,256,128]{2,1,0:T(8,128)S(1)} %get-tuple-element.110.q_keep, bf16[2,256,128]{2,1,0:T(8,128)(2,1)S(1)} %collective-permute-done.17.q_got, ...), custom_call_target="tpu_custom_call" | custom-call | flops 1000000 | tf_op jit(solution)/shard_map/finish/pallas_call | solution.py:409
  (18 shorter events, 0.1 us)
Async XLA Ops:
  3.2 12.1 %collective-permute-start.1 = (bf16[3,256,128]{2,1,0:T(8,128)(2,1)}, bf16[3,256,128]{2,1,0:T(8,128)(2,1)S(1)}, u32[]{:S(2)}, u32[]{:S(2)}) collective-permute-start(bf16[3,256,128]{2,1,0:T(8,128)(2,1)} %get-tuple-element.62), channel_id=1, source_target_pairs={{0,6},{1,7},{2,0},{3,1},{4,2},{5,3},{6,4},{7,5},{8,14},{9,15},{10,... | collective-permute-start | bytes 589832 | tf_op jit(solution)/shard_map/ppermute | solution.py:292
  6.1 9.6 %collective-permute-start.2 = (bf16[3,256,128]{2,1,0:T(8,128)(2,1)}, bf16[3,256,128]{2,1,0:T(8,128)(2,1)S(1)}, u32[]{:S(2)}, u32[]{:S(2)}) collective-permute-start(bf16[3,256,128]{2,1,0:T(8,128)(2,1)} %get-tuple-element.63), channel_id=1, source_target_pairs={{0,4},{1,5},{2,6},{3,7},{4,0},{5,1},{6,2},{7,3},{8,12},{9,13},{10,... | collective-permute-start | bytes 589832 | tf_op jit(solution)/shard_map/ppermute | solution.py:292
  6.9 11.5 %collective-permute-start.3 = (bf16[3,256,128]{2,1,0:T(8,128)(2,1)}, bf16[3,256,128]{2,1,0:T(8,128)(2,1)S(1)}, u32[]{:S(2)}, u32[]{:S(2)}) collective-permute-start(bf16[3,256,128]{2,1,0:T(8,128)(2,1)} %get-tuple-element.64), channel_id=1, source_target_pairs={{0,2},{1,3},{2,4},{3,5},{4,6},{5,7},{6,0},{7,1},{8,10},{9,11},{10,... | collective-permute-start | bytes 589832 | tf_op jit(solution)/shard_map/ppermute | solution.py:292
  7.8 7.5 %collective-permute-start = (bf16[2,256,128]{2,1,0:T(8,128)(2,1)}, bf16[2,256,128]{2,1,0:T(8,128)(2,1)S(1)}, u32[]{:S(2)}, u32[]{:S(2)}) collective-permute-start(bf16[2,256,128]{2,1,0:T(8,128)(2,1)} %get-tuple-element.69.ha), channel_id=1, source_target_pairs={{0,1},{1,0},{2,3},{3,2},{4,5},{5,4},{6,7},{7,6},{8,9},{9,8},{10,11... | collective-permute-start | bytes 393224 | tf_op jit(solution)/shard_map/ppermute | solution.py:295
  11.6 6.8 %copy-start = (bf16[2,256,128]{2,1,0:T(8,128)(2,1)S(1)}, bf16[2,256,128]{2,1,0:T(8,128)(2,1)}, u32[]{:S(2)}) copy-start(bf16[2,256,128]{2,1,0:T(8,128)(2,1)} %get-tuple-element.69.ha) | copy-start | bytes 393220
  11.7 6.8 %copy-start.1 = (bf16[2,256,128]{2,1,0:T(8,128)(2,1)S(1)}, bf16[2,256,128]{2,1,0:T(8,128)(2,1)}, u32[]{:S(2)}) copy-start(bf16[2,256,128]{2,1,0:T(8,128)(2,1)} %get-tuple-element.71.hb) | copy-start | bytes 393220
  11.7 6.8 %copy-start.2 = (f32[128,128]{1,0:T(8,128)S(1)}, f32[128,128]{1,0:T(8,128)}, u32[]{:S(2)}) copy-start(f32[128,128]{1,0:T(8,128)} %get-tuple-element.75.keep) | copy-start | bytes 196612
  11.7 13.5 %copy-start.4 = (s32[1,1,512,2]{2,3,1,0:T(2,128)S(1)}, s32[1,1,512,2]{2,3,1,0:T(2,128)}, u32[]{:S(2)}) copy-start(s32[1,1,512,2]{2,3,1,0:T(2,128)} %param.13) | copy-start | bytes 12292
  18.5 18.7 %collective-permute-start.7 = (bf16[9,256,128]{2,1,0:T(8,128)(2,1)S(1)}, bf16[9,256,128]{2,1,0:T(8,128)(2,1)S(1)}, u32[]{:S(2)}, u32[]{:S(2)}) collective-permute-start(bf16[9,256,128]{2,1,0:T(8,128)(2,1)S(1)} %get-tuple-element.83.b0), channel_id=1, source_target_pairs={{0,1},{1,0},{2,3},{3,2},{4,5},{5,4},{6,7},{7,6},{8,9},{9,8},{10,11... | collective-permute-start | bytes 1769480 | tf_op jit(solution)/shard_map/ppermute | solution.py:295
  21.8 14.8 %collective-permute-start.6 = (bf16[4,256,128]{2,1,0:T(8,128)(2,1)S(1)}, bf16[4,256,128]{2,1,0:T(8,128)(2,1)S(1)}, u32[]{:S(2)}, u32[]{:S(2)}) collective-permute-start(bf16[4,256,128]{2,1,0:T(8,128)(2,1)S(1)} %get-tuple-element.79.a0), channel_id=1, source_target_pairs={{0,2},{1,3},{2,4},{3,5},{4,6},{5,7},{6,0},{7,1},{8,10},{9,11},{10,... | collective-permute-start | bytes 786440 | tf_op jit(solution)/shard_map/ppermute | solution.py:292
  21.8 14.8 %collective-permute-start.5 = (bf16[4,256,128]{2,1,0:T(8,128)(2,1)S(1)}, bf16[4,256,128]{2,1,0:T(8,128)(2,1)S(1)}, u32[]{:S(2)}, u32[]{:S(2)}) collective-permute-start(bf16[4,256,128]{2,1,0:T(8,128)(2,1)S(1)} %get-tuple-element.79.a0), channel_id=1, source_target_pairs={{0,4},{1,5},{2,6},{3,7},{4,0},{5,1},{6,2},{7,3},{8,12},{9,13},{10,... | collective-permute-start | bytes 786440 | tf_op jit(solution)/shard_map/ppermute | solution.py:292
  23.9 13.3 %collective-permute-start.4 = (bf16[4,256,128]{2,1,0:T(8,128)(2,1)S(1)}, bf16[4,256,128]{2,1,0:T(8,128)(2,1)S(1)}, u32[]{:S(2)}, u32[]{:S(2)}) collective-permute-start(bf16[4,256,128]{2,1,0:T(8,128)(2,1)S(1)} %get-tuple-element.79.a0), channel_id=1, source_target_pairs={{0,6},{1,7},{2,0},{3,1},{4,2},{5,3},{6,4},{7,5},{8,14},{9,15},{10,... | collective-permute-start | bytes 786440 | tf_op jit(solution)/shard_map/ppermute | solution.py:292
  40.3 2.8 %collective-permute-start.8 = (bf16[17,256,128]{2,1,0:T(8,128)(2,1)S(1)}, bf16[17,256,128]{2,1,0:T(8,128)(2,1)S(1)}, u32[]{:S(2)}, u32[]{:S(2)}) collective-permute-start(bf16[17,256,128]{2,1,0:T(8,128)(2,1)S(1)} %get-tuple-element.87.sent_ref), channel_id=1, source_target_pairs={{0,8},{8,0},{16,24},{24,16},{32,40},{40,32},{48,56},{56,48},{64,72... | collective-permute-start | bytes 3342344 | tf_op jit(solution)/shard_map/ppermute | solution.py:307
  40.4 10.0 %collective-permute-start.9 = (bf16[16,256,128]{2,1,0:T(8,128)(2,1)S(1)}, bf16[16,256,128]{2,1,0:T(8,128)(2,1)S(1)}, u32[]{:S(2)}, u32[]{:S(2)}) collective-permute-start(bf16[16,256,128]{2,1,0:T(8,128)(2,1)S(1)} %get-tuple-element.89), channel_id=1, source_target_pairs={{0,8},{8,0},{16,24},{24,16},{32,40},{40,32},{48,56},{56,48},{64,72... | collective-permute-start | bytes 3145736 | tf_op jit(solution)/shard_map/ppermute | solution.py:307
  43.3 13.3 %collective-permute-start.11 = (bf16[1152,128]{1,0:T(8,128)(2,1)S(1)}, bf16[1152,128]{1,0:T(8,128)(2,1)S(1)}, u32[]{:S(2)}, u32[]{:S(2)}) collective-permute-start(bf16[1152,128]{1,0:T(8,128)(2,1)S(1)} %get-tuple-element.96), channel_id=1, source_target_pairs={{0,32},{8,40},{16,48},{24,56},{32,0},{40,8},{48,16},{56,24},{64,96... | collective-permute-start | bytes 884744 | tf_op jit(solution)/shard_map/ppermute | solution.py:298
  48.3 13.4 %collective-permute-start.12 = (bf16[1152,128]{1,0:T(8,128)(2,1)S(1)}, bf16[1152,128]{1,0:T(8,128)(2,1)S(1)}, u32[]{:S(2)}, u32[]{:S(2)}) collective-permute-start(bf16[1152,128]{1,0:T(8,128)(2,1)S(1)} %get-tuple-element.97), channel_id=1, source_target_pairs={{0,48},{8,56},{16,0},{24,8},{32,16},{40,24},{48,32},{56,40},{64,11... | collective-permute-start | bytes 884744 | tf_op jit(solution)/shard_map/ppermute | solution.py:298
  49.8 12.8 %collective-permute-start.10 = (bf16[1152,128]{1,0:T(8,128)(2,1)S(1)}, bf16[1152,128]{1,0:T(8,128)(2,1)S(1)}, u32[]{:S(2)}, u32[]{:S(2)}) collective-permute-start(bf16[1152,128]{1,0:T(8,128)(2,1)S(1)} %get-tuple-element.95.sent_ref), channel_id=1, source_target_pairs={{0,16},{8,24},{16,32},{24,40},{32,48},{40,56},{48,0},{56,8},{64,80... | collective-permute-start | bytes 884744 | tf_op jit(solution)/shard_map/ppermute | solution.py:298
  52.9 10.7 %copy-start.3 = (s32[512,16]{0,1:T(8,128)S(1)}, s32[512,16]{0,1:T(8,128)}, u32[]{:S(2)}) copy-start(s32[512,16]{0,1:T(8,128)} %param.15) | copy-start | bytes 98308
  53.1 16.5 %collective-permute-start.14 = (bf16[1024,128]{1,0:T(8,128)(2,1)S(1)}, bf16[1024,128]{1,0:T(8,128)(2,1)S(1)}, u32[]{:S(2)}, u32[]{:S(2)}) collective-permute-start(bf16[1024,128]{1,0:T(8,128)(2,1)S(1)} %get-tuple-element.105), channel_id=1, source_target_pairs={{0,16},{8,24},{16,32},{24,40},{32,48},{40,56},{48,0},{56,8},{64,80... | collective-permute-start | bytes 786440 | tf_op jit(solution)/shard_map/ppermute | solution.py:298
  53.2 19.8 %collective-permute-start.15 = (bf16[1024,128]{1,0:T(8,128)(2,1)S(1)}, bf16[1024,128]{1,0:T(8,128)(2,1)S(1)}, u32[]{:S(2)}, u32[]{:S(2)}) collective-permute-start(bf16[1024,128]{1,0:T(8,128)(2,1)S(1)} %get-tuple-element.106), channel_id=1, source_target_pairs={{0,32},{8,40},{16,48},{24,56},{32,0},{40,8},{48,16},{56,24},{64,96... | collective-permute-start | bytes 786440 | tf_op jit(solution)/shard_map/ppermute | solution.py:298
  56.6 16.4 %collective-permute-start.16 = (bf16[1024,128]{1,0:T(8,128)(2,1)S(1)}, bf16[1024,128]{1,0:T(8,128)(2,1)S(1)}, u32[]{:S(2)}, u32[]{:S(2)}) collective-permute-start(bf16[1024,128]{1,0:T(8,128)(2,1)S(1)} %get-tuple-element.107), channel_id=1, source_target_pairs={{0,48},{8,56},{16,0},{24,8},{32,16},{40,24},{48,32},{56,40},{64,11... | collective-permute-start | bytes 786440 | tf_op jit(solution)/shard_map/ppermute | solution.py:298
  62.7 6.9 %collective-permute-start.13 = (bf16[3,256,128]{2,1,0:T(8,128)(2,1)S(1)}, bf16[3,256,128]{2,1,0:T(8,128)(2,1)S(1)}, u32[]{:S(2)}, u32[]{:S(2)}) collective-permute-start(bf16[3,256,128]{2,1,0:T(8,128)(2,1)S(1)} %get-tuple-element.113.own), channel_id=1, source_target_pairs={{0,64},{8,72},{16,80},{24,88},{32,96},{40,104},{48,112},{56,120},{... | collective-permute-start | bytes 589832 | tf_op jit(solution)/shard_map/ppermute | solution.py:304
  73.2 4.6 %collective-permute-start.18 = (f32[128,128]{1,0:T(8,128)S(1)}, f32[128,128]{1,0:T(8,128)S(1)}, u32[]{:S(2)}, u32[]{:S(2)}) collective-permute-start(f32[128,128]{1,0:T(8,128)S(1)} %sum_parts.1.own), channel_id=1, source_target_pairs={{0,2},{1,3},{2,0},{3,1},{4,6},{5,7},{6,4},{7,5},{8,10},{9,11},{10,... | collective-permute-start | bytes 196616 | tf_op jit(solution)/shard_map/ppermute | solution.py:301
  74.1 7.0 %collective-permute-start.17 = (bf16[2,256,128]{2,1,0:T(8,128)(2,1)S(1)}, bf16[2,256,128]{2,1,0:T(8,128)(2,1)S(1)}, u32[]{:S(2)}, u32[]{:S(2)}) collective-permute-start(bf16[2,256,128]{2,1,0:T(8,128)(2,1)S(1)} %get-tuple-element.111), channel_id=1, source_target_pairs={{0,64},{8,72},{16,80},{24,88},{32,96},{40,104},{48,112},{56,120},{... | collective-permute-start | bytes 393224 | tf_op jit(solution)/shard_map/ppermute | solution.py:304
  77.8 6.8 %collective-permute-start.19 = (f32[2,128,128]{2,1,0:T(8,128)S(1)}, f32[2,128,128]{2,1,0:T(8,128)S(1)}, u32[]{:S(2)}, u32[]{:S(2)}) collective-permute-start(f32[2,128,128]{2,1,0:T(8,128)S(1)} %pair_up.1.w), channel_id=1, source_target_pairs={{0,4},{1,5},{2,6},{3,7},{4,0},{5,1},{6,2},{7,3},{8,12},{9,13},{10,... | collective-permute-start | bytes 393224 | tf_op jit(solution)/shard_map/ppermute | solution.py:301

commit v5 on v4

--- a/solution.py
+++ b/solution.py
@@ -76,8 +76,9 @@
     hidden = contract(weight[...], masked, 1, 1).astype(bf16)
     for t in range(2):
         ha[t] = hidden[:, t * T : (t + 1) * T]
-        for ref in (hb, m1, m2, m3):
-            ref[t] = hidden[:, (t + 2) * T : (t + 3) * T]
+        hb[t] = hidden[:, (t + 2) * T : (t + 3) * T]
+        for ref in (m1, m2, m3):
+            ref[t * 256 : (t + 1) * 256] = hidden[:, (t + 2) * T : (t + 3) * T]
     copies[3].wait()
     part[...] = contract(agg[...], masked, 0, 0) * (1.0 / 256.0)
     x = lax.axis_index("col") >> 1
@@ -88,17 +89,21 @@
 
     keep[...] = quarter(x)
     for s, ref in ((1, m1), (2, m2), (3, m3)):
-        ref[2] = both_parts(quarter((x + s) & 3))
+        ref[512 : 512 + T] = quarter((x + s) & 3).astype(bf16)
 
 
 def pack(ha, ha_y, hb, m1, m2, m3, keep, a0, b0):
     a0[0:2], a0[2:4] = ha[...], ha_y[...]
-    b0[0:2], b0[2:4], b0[4:6], b0[6:8] = hb[...], m1[0:2], m2[0:2], m3[0:2]
-    b0[8] = both_parts((keep[...] + whole(m2[2])) + (whole(m1[2]) + whole(m3[2])))
-
-
-def sum_parts(own, got, out):
-    out[...] = whole(own[2]) + whole(got[2])
+    b0[0:2] = hb[...]
+    total = keep[...]
+    for s, ref in ((1, m1), (2, m2), (3, m3)):
+        b0[2 * s], b0[2 * s + 1] = ref[0:256], ref[256:512]
+        total += ref[512 : 512 + T].astype(f32)
+    b0[8] = both_parts(total)
+
+
+def add_two(a, b, out):
+    out[...] = a[...] + b[...]
 
 
 def pair_up(own, got, out):
@@ -243,21 +248,17 @@
     late(number, steps_ref, h_ref, tiles_ref, so_far_ref, (out_ref,), acc_ref)
 
 
-def split_q(acc_ref, got_ref, keep, z1, z2, z3):
+def split_p(acc_ref, got_ref, sent_ref, keep, z1, z2, z3):
     for k in range(4):
         keep[k] = acc_ref[k] + got_ref[k].astype(f32)
         for dz, ref in ((1, z1), (2, z2), (3, z3)):
             ref[k * 256 : (k + 1) * 256] = (acc_ref[4 * dz + k] + got_ref[4 * dz + k].astype(f32)).astype(bf16)
-
-
-def split_p(acc_ref, got_ref, sent_ref, keep, z1, z2, z3):
-    split_q(acc_ref, got_ref, keep, z1, z2, z3)
     total = (whole(sent_ref[16]) + whole(got_ref[16])).astype(bf16)
     for ref in (z1, z2, z3):
         ref[1024 : 1024 + T] = total
 
 
-def gather_q(keep_ref, g1, g2, g3, keep, y):
+def gather_p(keep_ref, g1, g2, g3, sent_ref, keep, y, w):
     for k in range(4):
         rows = slice(k * 256, (k + 1) * 256)
         total = keep_ref[k] + g1[rows].astype(f32) + g2[rows].astype(f32) + g3[rows].astype(f32)
@@ -265,15 +266,26 @@
             keep[k] = total
         else:
             y[k - 2] = total.astype(bf16)
-
-
-def gather_p(keep_ref, g1, g2, g3, sent_ref, keep, y):
-    gather_q(keep_ref, g1, g2, g3, keep, y)
     own, left, across, right = (ref[1024 : 1024 + T].astype(f32) for ref in (sent_ref, g1, g2, g3))
-    y[2] = both_parts((own + across) + (left + right))
-
-
-def finish(p_keep, p_got, q_keep, q_got, mask_ref, w, w_got, out_ref, weight_ref):
+    w[...] = (own + across) + (left + right)
+
+
+def split_q(acc_ref, got_ref, keep, y):
+    for dz in range(4):
+        for u in range(2):
+            k = 4 * dz + u
+            keep[2 * dz + u] = acc_ref[k] + got_ref[k].astype(f32)
+            y[2 * dz + u] = (acc_ref[k + 2] + got_ref[k + 2].astype(f32)).astype(bf16)
+
+
+def gather_q(keep_ref, got_ref, keep, z1, z2, z3):
+    for u in range(2):
+        keep[u] = keep_ref[u] + got_ref[u].astype(f32)
+        for dz, ref in ((1, z1), (2, z2), (3, z3)):
+            ref[u] = (keep_ref[2 * dz + u] + got_ref[2 * dz + u].astype(f32)).astype(bf16)
+
+
+def finish(p_keep, p_got, q_keep, g1, g2, g3, mask_ref, w, w_got, out_ref, weight_ref):
     upper = lax.axis_index("col") >> 2
     for pair, ref in ((upper, w), (1 - upper, w_got)):
         for i in range(2):
@@ -281,8 +293,10 @@
             weight_ref[rows, 0:T] = ref[i, 0:64]
             weight_ref[rows, T : 2 * T] = ref[i, 64:T]
     for t in range(4):
-        keep, got = (p_keep, p_got) if t < 2 else (q_keep, q_got)
-        total = keep[t & 1] + got[t & 1].astype(f32)
+        keep, *parts = (p_keep, p_got) if t < 2 else (q_keep, g1, g2, g3)
+        total = keep[t & 1]
+        for got in parts:
+            total += got[t & 1].astype(f32)
         rows = slice(t * T, (t + 1) * T)
         out_ref[rows] = jnp.where(mask_ref[rows] == 1, total.T, 0.0).astype(bf16)
 
@@ -306,10 +320,10 @@
     def over_core(v):
         return lax.ppermute(v, "row", [(r, r ^ 1) for r in range(16)])
 
-    half, three, quad, square = (2, 256, T), (3, 256, T), (4, 256, T), (T, T)
+    half, quad, square, message = (2, 256, T), (4, 256, T), (T, T), (512 + T, T)
     ha, hb, m1, m2, m3, w = call(
         prep,
-        [(half, bf16)] * 2 + [(three, bf16)] * 3 + [(square, f32)],
+        [(half, bf16)] * 2 + [(message, bf16)] * 3 + [(square, f32)],
         [ANY] * 4,
         "prep",
         limit=PREP_LIMIT,
@@ -358,7 +372,7 @@
     a0, a1, a2, a3, b0, b1, acc = tie(a0, a1, a2, a3, b0, b1, acc)
 
     sixteen = (16, 256, T)
-    z_p, z_q = (1024 + T, T), (1024, T)
+    z_p, eight = (1024 + T, T), (8, 256, T)
 
     def own_columns(number):
         return call(
@@ -391,24 +405,25 @@
     p_all = around_z(*p_z)
     p_keep, hidden, q_got = tie(p_keep, hidden, q_got)
     own = own_columns(3)
-    q_keep, *q_z = call(split_q, [(quad, f32)] + [(z_q, bf16)] * 3, [VMEM] * 2, "split_q", flops=10**6)(own, q_got)
-    q_all = around_z(*q_z)
+    q_keep, q_y = call(split_q, [(eight, f32), (eight, bf16)], [VMEM] * 2, "split_q", flops=10**6)(own, q_got)
+    q_got = over_y_lo(q_y)
     p_keep, q_keep, words = tie(p_keep, q_keep, in_bits.T)
     (mask,) = call(in_mask, [((512, 256), bf16)], [VMEM], "in_mask", flops=10**7)(words)
-    p_keep, p_y = call(gather_p, [(half, f32), (three, bf16)], [VMEM] * 5, "gather_p", flops=10**6)(
-        p_keep, *p_all, p_z[0]
-    )
-    p_got = over_y_lo(p_y)
-    p_keep, p_got, q_keep, mask = tie(p_keep, p_got, q_keep, mask)
-    q_keep, q_y = call(gather_q, [(half, f32), (half, bf16)], [VMEM] * 4, "gather_q", flops=10**6)(q_keep, *q_all)
-    q_got = over_y_lo(q_y)
-    p_y, p_got, q_keep = tie(p_y, p_got, q_keep)
-    (w,) = call(sum_parts, [(square, f32)], [VMEM] * 2, "sum_parts", limit=2)(p_y, p_got)
+    p_keep, p_y, w = call(
+        gather_p, [(half, f32), (half, bf16), (square, f32)], [VMEM] * 5, "gather_p", flops=10**10, touched=2**25
+    )(p_keep, *p_all, p_z[0])
+    p_got, w_got = over_y_lo(p_y), over_y_lo(w)
+    q_keep, p_keep, mask = tie(q_keep, p_keep, mask)
+    q_keep, *q_z = call(gather_q, [(half, f32)] + [(half, bf16)] * 3, [VMEM] * 2, "gather_q", flops=10**6)(
+        q_keep, q_got
+    )
+    q_all = around_z(*q_z)
+    (w,) = call(add_two, [(square, f32)], [VMEM] * 2, "add_two", limit=2)(w, w_got)
     (w,) = call(pair_up, [((2, T, T), f32)], [VMEM] * 2, "pair_up", limit=2)(w, swap_x(w, 0))
     w_got = swap_x(w, 1)
     prev_grad, weight_grad = call(
-        finish, [((512, 256), bf16), ((256, 256), f32)], [VMEM] * 7, "finish", flops=10**6
-    )(p_keep, p_got, q_keep, q_got, mask, w, w_got)
+        finish, [((512, 256), bf16), ((256, 256), f32)], [VMEM] * 9, "finish", flops=10**6
+    )(p_keep, p_got, q_keep, *q_all, mask, w, w_got)
     return weight_grad, prev_grad
 
 

time: 86.9 us -> 83.5 us (0.961); the launches traced: 85.5 us -> 83.7 us
  starting transfers between devices: 34.9 us -> 33.2 us
    ppermute x6, waiting for transfers between devices: 7.93 us -> 11.4 us  [over_z(): lax.ppermute(v, 'row', [(r, r & 9 | ((r >> 1) + s & 3) << 1) for r in ran...]
    ppermute x2 -> x3, starting transfers between devices: 4.43 us -> 1.59 us  [over_y_lo(): return lax.ppermute(v, 'row', [(r, r ^ 8) for r in range(16)])]
    ppermute x2, waiting for transfers between devices: 3.76 us -> 2.02 us  [swap_x(): return lax.ppermute(v, 'col', [(c, c ^ 2 << bit) for c in range(8)])]
    ppermute x2, starting transfers between devices: 3.45 us -> 5.11 us  [swap_x(): return lax.ppermute(v, 'col', [(c, c ^ 2 << bit) for c in range(8)])]
    ppermute x2 -> x3, waiting for transfers between devices: 6.4 us -> 4.89 us  [over_y_lo(): return lax.ppermute(v, 'row', [(r, r ^ 8) for r in range(16)])]
  transfers between devices with their start and end apart: 20 -> 21, of which waited for: 12 -> 10; matrix products, arithmetic and copies ran while one was open for 0% -> 0% of each run, Pallas kernels for 17% -> 17%
where the time goes in v5:
time: 83.5 us; the launch traced here: 83.7 us
  starting transfers between devices  33.2 us (40%)
  waiting for transfers between devices  27.1 us (32%)
  Pallas kernels  21.9 us (26%)
  between operations  1.48 us (2%)
    ppermute x6, waiting for transfers between devices, over_z(): lax.ppermute(v, 'row', [(r, r & 9 | ((r >> 1) + s & 3) << 1) for r in ran...  11.4 us
    ppermute x6, starting transfers between devices, over_z(): lax.ppermute(v, 'row', [(r, r & 9 | ((r >> 1) + s & 3) << 1) for r in ran...  11.4 us
    ppermute x6, waiting for transfers between devices, over_x(): lax.ppermute(v, 'col', [(c, ((c >> 1) + s & 3) * 2 + (c & 1)) for c in ra...  8.7 us
    ppermute x6, starting transfers between devices, over_x(): lax.ppermute(v, 'col', [(c, ((c >> 1) + s & 3) * 2 + (c & 1)) for c in ra...  8.03 us
    ppermute x2, starting transfers between devices, over_y_hi(): return lax.ppermute(v, 'col', [(c, c ^ 1) for c in range(8)])  6.46 us
    pallas_call x2, Pallas kernels, own_columns(): call(functools.partial(late_own, number), [(sixteen, f32)], [SMEM] + [VME...  5.2 us
    ppermute x2, starting transfers between devices, swap_x(): return lax.ppermute(v, 'col', [(c, c ^ 2 << bit) for c in range(8)])  5.11 us
    ppermute x3, waiting for transfers between devices, over_y_lo(): return lax.ppermute(v, 'row', [(r, r ^ 8) for r in range(16)])  4.89 us
  transfers between devices with their start and end apart: 21, of which 10 were waited for; matrix products, arithmetic and copies ran while one was open for 0% of the time, Pallas kernels for 17%

profile of v5, /device:TPU:0, one launch (start us, length us, event | category | flops | bytes accessed | tf_op | source)
XLA Modules:
  0.0 83.7 jit_solution(5601854181663066477)
XLA Ops:
  0.6 2.5 %prep.1 = (bf16[2,256,128]{2,1,0:T(8,128)(2,1)}, bf16[2,256,128]{2,1,0:T(8,128)(2,1)}, bf16[640,128]{1,0:T(8,128)(2,1)}, bf16[640,128]{1,0:T(8,128)(2,1)}, bf16[640,128]{1,0:T(8,128)(2,1)}, /*index=5*/f32[128,128]{1,0:T(8,128)}) custom-call(bf16[512,256]{1,0:T(8,128)(2,1)} %grad_hbm.1, s32[16,512]{1,0:T(8,128)} %bitcast.12, bf16[512,256]{1,0:T(8,128)(2,1)} %agg_hbm.1, ...), custom_call_target="tpu_custom_call" | custom-call | flops 200000000 | tf_op jit(solution)/shard_map/prep/pallas_call | solution.py:324
  3.2 2.9 %collective-permute-start.1 = (bf16[640,128]{1,0:T(8,128)(2,1)}, bf16[640,128]{1,0:T(8,128)(2,1)S(1)}, u32[]{:S(2)}, u32[]{:S(2)}) collective-permute-start(bf16[640,128]{1,0:T(8,128)(2,1)} %get-tuple-element.59), channel_id=1, source_target_pairs={{0,6},{1,7},{2,0},{3,1},{4,2},{5,3},{6,4},{7,5},{8,14},{9,15},{10,... | collective-permute-start | bytes 491528 | tf_op jit(solution)/shard_map/ppermute | solution.py:306
  6.1 0.8 collective-permute-start.2
  6.9 0.9 %collective-permute-start.3 = (bf16[640,128]{1,0:T(8,128)(2,1)}, bf16[640,128]{1,0:T(8,128)(2,1)S(1)}, u32[]{:S(2)}, u32[]{:S(2)}) collective-permute-start(bf16[640,128]{1,0:T(8,128)(2,1)} %get-tuple-element.61), channel_id=1, source_target_pairs={{0,2},{1,3},{2,4},{3,5},{4,6},{5,7},{6,0},{7,1},{8,10},{9,11},{10,... | collective-permute-start | bytes 491528 | tf_op jit(solution)/shard_map/ppermute | solution.py:306
  7.8 3.2 %collective-permute-start = (bf16[2,256,128]{2,1,0:T(8,128)(2,1)}, bf16[2,256,128]{2,1,0:T(8,128)(2,1)S(1)}, u32[]{:S(2)}, u32[]{:S(2)}) collective-permute-start(bf16[2,256,128]{2,1,0:T(8,128)(2,1)} %get-tuple-element.66.ha), channel_id=1, source_target_pairs={{0,1},{1,0},{2,3},{3,2},{4,5},{5,4},{6,7},{7,6},{8,9},{9,8},{10,11... | collective-permute-start | bytes 393224 | tf_op jit(solution)/shard_map/ppermute | solution.py:309
  11.6 0.0 copy-start.4
  11.7 3.0 %stage.1.tiles_ref = bf16[512,128,128]{2,1,0:T(8,128)(2,1)S(1)} custom-call(s32[1]{0:T(128)} %bitcast.7.count_ref, bf16[512,128,128]{2,1,0:T(8,128)(2,1)} %bitcast.11), custom_call_target="tpu_custom_call" | custom-call | flops 1000000000 | tf_op jit(solution)/shard_map/stage/pallas_call | solution.py:344
  14.7 0.0 collective-permute-done.ha_y
  14.7 0.3 collective-permute-done.2.m2
  15.0 2.0 %collective-permute-done.3.m3 = bf16[640,128]{1,0:T(8,128)(2,1)S(1)} collective-permute-done((bf16[640,128]{1,0:T(8,128)(2,1)}, bf16[640,128]{1,0:T(8,128)(2,1)S(1)}, u32[]{:S(2)}, u32[]{:S(2)}) %collective-permute-start.3) | collective-permute-done | bytes 163872 | tf_op jit(solution)/shard_map/ppermute | solution.py:306
  17.0 0.1 pack.1
  17.1 3.3 %collective-permute-start.7 = (bf16[9,256,128]{2,1,0:T(8,128)(2,1)S(1)}, bf16[9,256,128]{2,1,0:T(8,128)(2,1)S(1)}, u32[]{:S(2)}, u32[]{:S(2)}) collective-permute-start(bf16[9,256,128]{2,1,0:T(8,128)(2,1)S(1)} %get-tuple-element.80.b0), channel_id=1, source_target_pairs={{0,1},{1,0},{2,3},{3,2},{4,5},{5,4},{6,7},{7,6},{8,9},{9,8},{10,11... | collective-permute-start | bytes 1769480 | tf_op jit(solution)/shard_map/ppermute | solution.py:309
  20.3 0.0 collective-permute-start.6
  20.3 2.1 %collective-permute-start.5 = (bf16[4,256,128]{2,1,0:T(8,128)(2,1)S(1)}, bf16[4,256,128]{2,1,0:T(8,128)(2,1)S(1)}, u32[]{:S(2)}, u32[]{:S(2)}) collective-permute-start(bf16[4,256,128]{2,1,0:T(8,128)(2,1)S(1)} %get-tuple-element.76.a0), channel_id=1, source_target_pairs={{0,4},{1,5},{2,6},{3,7},{4,0},{5,1},{6,2},{7,3},{8,12},{9,13},{10,... | collective-permute-start | bytes 786440 | tf_op jit(solution)/shard_map/ppermute | solution.py:306
  22.4 1.4 %collective-permute-start.4 = (bf16[4,256,128]{2,1,0:T(8,128)(2,1)S(1)}, bf16[4,256,128]{2,1,0:T(8,128)(2,1)S(1)}, u32[]{:S(2)}, u32[]{:S(2)}) collective-permute-start(bf16[4,256,128]{2,1,0:T(8,128)(2,1)S(1)} %get-tuple-element.76.a0), channel_id=1, source_target_pairs={{0,6},{1,7},{2,0},{3,1},{4,2},{5,3},{6,4},{7,5},{8,14},{9,15},{10,... | collective-permute-start | bytes 786440 | tf_op jit(solution)/shard_map/ppermute | solution.py:306
  23.8 1.2 %order_slots.1.steps_ref = s32[8,512]{1,0:T(8,128)S(1)} custom-call(s32[1]{0:T(128)} %bitcast.8.count_ref, s32[2,512]{1,0:T(2,128)S(1)} %bitcast.10), custom_call_target="tpu_custom_call" | custom-call | flops 10000000 | tf_op jit(solution)/shard_map/order_slots/pallas_call | solution.py:362
  24.9 4.4 %early.1.so_far_ref = f32[65,256,128]{2,1,0:T(8,128)S(1)} custom-call(s32[8,512]{1,0:T(8,128)S(1)} %order_slots.1.steps_ref, bf16[4,256,128]{2,1,0:T(8,128)(2,1)S(1)} %get-tuple-element.76.a0, bf16[9,256,128]{2,1,0:T(8,128)(2,1)S(1)} %get-tuple-element.80.b0, bf16[512,128,128]{2,1,0:T(8,128)(2,1)S(1)} %stage.1.tiles_ref), custom_call_target="tpu_custom_call" | custom-call | flops 4000000000 | tf_op jit(solution)/shard_map/early/pallas_call | solution.py:363
  29.3 5.8 %collective-permute-done.6.a3 = bf16[4,256,128]{2,1,0:T(8,128)(2,1)S(1)} collective-permute-done((bf16[4,256,128]{2,1,0:T(8,128)(2,1)S(1)}, bf16[4,256,128]{2,1,0:T(8,128)(2,1)S(1)}, u32[]{:S(2)}, u32[]{:S(2)}) %collective-permute-start.6) | collective-permute-done | bytes 262176 | tf_op jit(solution)/shard_map/ppermute | solution.py:306
  35.1 0.0 collective-permute-done.5.a2
  35.1 0.6 collective-permute-done.4.a1
  35.7 3.8 %late_1.1 = (bf16[17,256,128]{2,1,0:T(8,128)(2,1)S(1)}, bf16[16,256,128]{2,1,0:T(8,128)(2,1)S(1)}, bf16[33,256,128]{2,1,0:T(8,128)(2,1)S(1)}) custom-call(s32[8,512]{1,0:T(8,128)S(1)} %order_slots.1.steps_ref, bf16[4,256,128]{2,1,0:T(8,128)(2,1)S(1)} %get-tuple-element.76.a0, bf16[4,256,128]{2,1,0:T(8,128)(2,1)S(1)} %collective-permute-done.6.a3, ...), custom_call_target="tpu_custom_call" | custom-call | flops 4000000000 | tf_op jit(solution)/shard_map/late_1/pallas_call | solution.py:391
  39.5 0.1 collective-permute-start.8
  39.6 0.5 collective-permute-start.9
  40.1 2.6 %late_2.1.acc_ref = f32[16,256,128]{2,1,0:T(8,128)S(1)} custom-call(s32[8,512]{1,0:T(8,128)S(1)} %order_slots.1.steps_ref, bf16[33,256,128]{2,1,0:T(8,128)(2,1)S(1)} %get-tuple-element.88.h_ref, bf16[512,128,128]{2,1,0:T(8,128)(2,1)S(1)} %stage.1.tiles_ref, f32[65,256,128]{2,1,0:T(8,128)S(1)} %early.1.so_far_ref), custom_call_target="tpu_custom_call" | custom-call | flops 2000000000 | tf_op jit(solution)/shard_map/late_2/pallas_call | solution.py:378
  42.7 0.2 split_p.1
  42.9 2.9 %collective-permute-start.11 = (bf16[1152,128]{1,0:T(8,128)(2,1)S(1)}, bf16[1152,128]{1,0:T(8,128)(2,1)S(1)}, u32[]{:S(2)}, u32[]{:S(2)}) collective-permute-start(bf16[1152,128]{1,0:T(8,128)(2,1)S(1)} %get-tuple-element.94), channel_id=1, source_target_pairs={{0,32},{8,40},{16,48},{24,56},{32,0},{40,8},{48,16},{56,24},{64,96... | collective-permute-start | bytes 884744 | tf_op jit(solution)/shard_map/ppermute | solution.py:312
  45.8 4.0 %collective-permute-start.12 = (bf16[1152,128]{1,0:T(8,128)(2,1)S(1)}, bf16[1152,128]{1,0:T(8,128)(2,1)S(1)}, u32[]{:S(2)}, u32[]{:S(2)}) collective-permute-start(bf16[1152,128]{1,0:T(8,128)(2,1)S(1)} %get-tuple-element.95), channel_id=1, source_target_pairs={{0,48},{8,56},{16,0},{24,8},{32,16},{40,24},{48,32},{56,40},{64,11... | collective-permute-start | bytes 884744 | tf_op jit(solution)/shard_map/ppermute | solution.py:312
  49.8 2.6 %late_3.1.acc_ref = f32[16,256,128]{2,1,0:T(8,128)S(1)} custom-call(s32[8,512]{1,0:T(8,128)S(1)} %order_slots.1.steps_ref, bf16[33,256,128]{2,1,0:T(8,128)(2,1)S(1)} %get-tuple-element.88.h_ref, bf16[512,128,128]{2,1,0:T(8,128)(2,1)S(1)} %stage.1.tiles_ref, f32[65,256,128]{2,1,0:T(8,128)S(1)} %early.1.so_far_ref), custom_call_target="tpu_custom_call" | custom-call | flops 2000000000 | tf_op jit(solution)/shard_map/late_3/pallas_call | solution.py:378
  52.4 0.2 split_q.1
  52.5 0.0 copy-start.3
  52.5 0.1 collective-permute-start.14
  52.6 1.8 %collective-permute-done.11.g2 = bf16[1152,128]{1,0:T(8,128)(2,1)S(1)} collective-permute-done((bf16[1152,128]{1,0:T(8,128)(2,1)S(1)}, bf16[1152,128]{1,0:T(8,128)(2,1)S(1)}, u32[]{:S(2)}, u32[]{:S(2)}) %collective-permute-start.11) | collective-permute-done | bytes 294944 | tf_op jit(solution)/shard_map/ppermute | solution.py:312
  54.4 5.8 %collective-permute-done.12.g3 = bf16[1152,128]{1,0:T(8,128)(2,1)S(1)} collective-permute-done((bf16[1152,128]{1,0:T(8,128)(2,1)S(1)}, bf16[1152,128]{1,0:T(8,128)(2,1)S(1)}, u32[]{:S(2)}, u32[]{:S(2)}) %collective-permute-start.12) | collective-permute-done | bytes 294944 | tf_op jit(solution)/shard_map/ppermute | solution.py:312
  60.2 0.1 gather_p.1
  60.3 0.8 collective-permute-start.18
  61.1 4.9 %collective-permute-done.18.b = f32[128,128]{1,0:T(8,128)S(1)} collective-permute-done((f32[128,128]{1,0:T(8,128)S(1)}, f32[128,128]{1,0:T(8,128)S(1)}, u32[]{:S(2)}, u32[]{:S(2)}) %collective-permute-start.18) | collective-permute-done | bytes 65568 | tf_op jit(solution)/shard_map/ppermute | solution.py:318
  66.0 1.3 %collective-permute-start.19 = (f32[128,128]{1,0:T(8,128)S(1)}, f32[128,128]{1,0:T(8,128)S(1)}, u32[]{:S(2)}, u32[]{:S(2)}) collective-permute-start(f32[128,128]{1,0:T(8,128)S(1)} %add_two.1.own), channel_id=1, source_target_pairs={{0,2},{1,3},{2,0},{3,1},{4,6},{5,7},{6,4},{7,5},{8,10},{9,11},{10,... | collective-permute-start | bytes 196616 | tf_op jit(solution)/shard_map/ppermute | solution.py:315
  67.3 0.3 in_mask.1.mask_ref
  67.6 0.7 collective-permute-start.13
  68.3 2.0 %collective-permute-done.19.got = f32[128,128]{1,0:T(8,128)S(1)} collective-permute-done((f32[128,128]{1,0:T(8,128)S(1)}, f32[128,128]{1,0:T(8,128)S(1)}, u32[]{:S(2)}, u32[]{:S(2)}) %collective-permute-start.19) | collective-permute-done | bytes 65568 | tf_op jit(solution)/shard_map/ppermute | solution.py:315
  70.3 3.8 %collective-permute-start.20 = (f32[2,128,128]{2,1,0:T(8,128)S(1)}, f32[2,128,128]{2,1,0:T(8,128)S(1)}, u32[]{:S(2)}, u32[]{:S(2)}) collective-permute-start(f32[2,128,128]{2,1,0:T(8,128)S(1)} %pair_up.1.w), channel_id=1, source_target_pairs={{0,4},{1,5},{2,6},{3,7},{4,0},{5,1},{6,2},{7,3},{8,12},{9,13},{10,... | collective-permute-start | bytes 393224 | tf_op jit(solution)/shard_map/ppermute | solution.py:315
  74.2 0.1 gather_q.1
  74.3 0.4 collective-permute-start.15
  74.7 2.4 %collective-permute-start.16 = (bf16[2,256,128]{2,1,0:T(8,128)(2,1)S(1)}, bf16[2,256,128]{2,1,0:T(8,128)(2,1)S(1)}, u32[]{:S(2)}, u32[]{:S(2)}) collective-permute-start(bf16[2,256,128]{2,1,0:T(8,128)(2,1)S(1)} %get-tuple-element.104), channel_id=1, source_target_pairs={{0,32},{8,40},{16,48},{24,56},{32,0},{40,8},{48,16},{56,24},{64,96... | collective-permute-start | bytes 393224 | tf_op jit(solution)/shard_map/ppermute | solution.py:312
  77.1 1.8 %collective-permute-start.17 = (bf16[2,256,128]{2,1,0:T(8,128)(2,1)S(1)}, bf16[2,256,128]{2,1,0:T(8,128)(2,1)S(1)}, u32[]{:S(2)}, u32[]{:S(2)}) collective-permute-start(bf16[2,256,128]{2,1,0:T(8,128)(2,1)S(1)} %get-tuple-element.105), channel_id=1, source_target_pairs={{0,48},{8,56},{16,0},{24,8},{32,16},{40,24},{48,32},{56,40},{64,11... | collective-permute-start | bytes 393224 | tf_op jit(solution)/shard_map/ppermute | solution.py:312
  78.9 3.0 %collective-permute-done.15.g1 = bf16[2,256,128]{2,1,0:T(8,128)(2,1)S(1)} collective-permute-done((bf16[2,256,128]{2,1,0:T(8,128)(2,1)S(1)}, bf16[2,256,128]{2,1,0:T(8,128)(2,1)S(1)}, u32[]{:S(2)}, u32[]{:S(2)}) %collective-permute-start.15) | collective-permute-done | bytes 131104 | tf_op jit(solution)/shard_map/ppermute | solution.py:312
  81.9 0.9 %collective-permute-done.17.g3 = bf16[2,256,128]{2,1,0:T(8,128)(2,1)S(1)} collective-permute-done((bf16[2,256,128]{2,1,0:T(8,128)(2,1)S(1)}, bf16[2,256,128]{2,1,0:T(8,128)(2,1)S(1)}, u32[]{:S(2)}, u32[]{:S(2)}) %collective-permute-start.17) | collective-permute-done | bytes 131104 | tf_op jit(solution)/shard_map/ppermute | solution.py:312
  82.8 0.9 %finish.1 = (bf16[512,256]{1,0:T(8,128)(2,1)}, f32[256,256]{1,0:T(8,128)}) custom-call(f32[2,256,128]{2,1,0:T(8,128)S(1)} %get-tuple-element.98.p_keep, bf16[2,256,128]{2,1,0:T(8,128)(2,1)S(1)} %collective-permute-done.13.p_got, f32[2,256,128]{2,1,0:T(8,128)S(1)} %get-tuple-element.102.q_keep, bf16[2,256,128]{2,1,0:T(8,128)(2,1)S(1)} %collective-permute-done.15.g1, ...), custom_call_target="tpu_custom_call" | custom-call | flops 1000000 | tf_op jit(solution)/shard_map/finish/pallas_call | solution.py:424
  (20 shorter events, 0.1 us)
Async XLA Ops:
  3.2 11.5 %collective-permute-start.1 = (bf16[640,128]{1,0:T(8,128)(2,1)}, bf16[640,128]{1,0:T(8,128)(2,1)S(1)}, u32[]{:S(2)}, u32[]{:S(2)}) collective-permute-start(bf16[640,128]{1,0:T(8,128)(2,1)} %get-tuple-element.59), channel_id=1, source_target_pairs={{0,6},{1,7},{2,0},{3,1},{4,2},{5,3},{6,4},{7,5},{8,14},{9,15},{10,... | collective-permute-start | bytes 491528 | tf_op jit(solution)/shard_map/ppermute | solution.py:306
  6.1 8.9 %collective-permute-start.2 = (bf16[640,128]{1,0:T(8,128)(2,1)}, bf16[640,128]{1,0:T(8,128)(2,1)S(1)}, u32[]{:S(2)}, u32[]{:S(2)}) collective-permute-start(bf16[640,128]{1,0:T(8,128)(2,1)} %get-tuple-element.60), channel_id=1, source_target_pairs={{0,4},{1,5},{2,6},{3,7},{4,0},{5,1},{6,2},{7,3},{8,12},{9,13},{10,... | collective-permute-start | bytes 491528 | tf_op jit(solution)/shard_map/ppermute | solution.py:306
  6.9 10.1 %collective-permute-start.3 = (bf16[640,128]{1,0:T(8,128)(2,1)}, bf16[640,128]{1,0:T(8,128)(2,1)S(1)}, u32[]{:S(2)}, u32[]{:S(2)}) collective-permute-start(bf16[640,128]{1,0:T(8,128)(2,1)} %get-tuple-element.61), channel_id=1, source_target_pairs={{0,2},{1,3},{2,4},{3,5},{4,6},{5,7},{6,0},{7,1},{8,10},{9,11},{10,... | collective-permute-start | bytes 491528 | tf_op jit(solution)/shard_map/ppermute | solution.py:306
  7.8 6.9 %collective-permute-start = (bf16[2,256,128]{2,1,0:T(8,128)(2,1)}, bf16[2,256,128]{2,1,0:T(8,128)(2,1)S(1)}, u32[]{:S(2)}, u32[]{:S(2)}) collective-permute-start(bf16[2,256,128]{2,1,0:T(8,128)(2,1)} %get-tuple-element.66.ha), channel_id=1, source_target_pairs={{0,1},{1,0},{2,3},{3,2},{4,5},{5,4},{6,7},{7,6},{8,9},{9,8},{10,11... | collective-permute-start | bytes 393224 | tf_op jit(solution)/shard_map/ppermute | solution.py:309
  11.6 5.4 %copy-start = (bf16[2,256,128]{2,1,0:T(8,128)(2,1)S(1)}, bf16[2,256,128]{2,1,0:T(8,128)(2,1)}, u32[]{:S(2)}) copy-start(bf16[2,256,128]{2,1,0:T(8,128)(2,1)} %get-tuple-element.66.ha) | copy-start | bytes 393220
  11.6 5.4 %copy-start.1 = (bf16[2,256,128]{2,1,0:T(8,128)(2,1)S(1)}, bf16[2,256,128]{2,1,0:T(8,128)(2,1)}, u32[]{:S(2)}) copy-start(bf16[2,256,128]{2,1,0:T(8,128)(2,1)} %get-tuple-element.68.hb) | copy-start | bytes 393220
  11.6 5.3 %copy-start.2 = (f32[128,128]{1,0:T(8,128)S(1)}, f32[128,128]{1,0:T(8,128)}, u32[]{:S(2)}) copy-start(f32[128,128]{1,0:T(8,128)} %get-tuple-element.72.keep) | copy-start | bytes 196612
  11.6 12.1 %copy-start.4 = (s32[1,1,512,2]{2,3,1,0:T(2,128)S(1)}, s32[1,1,512,2]{2,3,1,0:T(2,128)}, u32[]{:S(2)}) copy-start(s32[1,1,512,2]{2,3,1,0:T(2,128)} %param.13) | copy-start | bytes 12292
  17.1 18.7 %collective-permute-start.7 = (bf16[9,256,128]{2,1,0:T(8,128)(2,1)S(1)}, bf16[9,256,128]{2,1,0:T(8,128)(2,1)S(1)}, u32[]{:S(2)}, u32[]{:S(2)}) collective-permute-start(bf16[9,256,128]{2,1,0:T(8,128)(2,1)S(1)} %get-tuple-element.80.b0), channel_id=1, source_target_pairs={{0,1},{1,0},{2,3},{3,2},{4,5},{5,4},{6,7},{7,6},{8,9},{9,8},{10,11... | collective-permute-start | bytes 1769480 | tf_op jit(solution)/shard_map/ppermute | solution.py:309
  20.3 14.8 %collective-permute-start.6 = (bf16[4,256,128]{2,1,0:T(8,128)(2,1)S(1)}, bf16[4,256,128]{2,1,0:T(8,128)(2,1)S(1)}, u32[]{:S(2)}, u32[]{:S(2)}) collective-permute-start(bf16[4,256,128]{2,1,0:T(8,128)(2,1)S(1)} %get-tuple-element.76.a0), channel_id=1, source_target_pairs={{0,2},{1,3},{2,4},{3,5},{4,6},{5,7},{6,0},{7,1},{8,10},{9,11},{10,... | collective-permute-start | bytes 786440 | tf_op jit(solution)/shard_map/ppermute | solution.py:306
  20.3 14.8 %collective-permute-start.5 = (bf16[4,256,128]{2,1,0:T(8,128)(2,1)S(1)}, bf16[4,256,128]{2,1,0:T(8,128)(2,1)S(1)}, u32[]{:S(2)}, u32[]{:S(2)}) collective-permute-start(bf16[4,256,128]{2,1,0:T(8,128)(2,1)S(1)} %get-tuple-element.76.a0), channel_id=1, source_target_pairs={{0,4},{1,5},{2,6},{3,7},{4,0},{5,1},{6,2},{7,3},{8,12},{9,13},{10,... | collective-permute-start | bytes 786440 | tf_op jit(solution)/shard_map/ppermute | solution.py:306
  22.4 13.3 %collective-permute-start.4 = (bf16[4,256,128]{2,1,0:T(8,128)(2,1)S(1)}, bf16[4,256,128]{2,1,0:T(8,128)(2,1)S(1)}, u32[]{:S(2)}, u32[]{:S(2)}) collective-permute-start(bf16[4,256,128]{2,1,0:T(8,128)(2,1)S(1)} %get-tuple-element.76.a0), channel_id=1, source_target_pairs={{0,6},{1,7},{2,0},{3,1},{4,2},{5,3},{6,4},{7,5},{8,14},{9,15},{10,... | collective-permute-start | bytes 786440 | tf_op jit(solution)/shard_map/ppermute | solution.py:306
  39.5 3.2 %collective-permute-start.8 = (bf16[17,256,128]{2,1,0:T(8,128)(2,1)S(1)}, bf16[17,256,128]{2,1,0:T(8,128)(2,1)S(1)}, u32[]{:S(2)}, u32[]{:S(2)}) collective-permute-start(bf16[17,256,128]{2,1,0:T(8,128)(2,1)S(1)} %get-tuple-element.84.sent_ref), channel_id=1, source_target_pairs={{0,8},{8,0},{16,24},{24,16},{32,40},{40,32},{48,56},{56,48},{64,72... | collective-permute-start | bytes 3342344 | tf_op jit(solution)/shard_map/ppermute | solution.py:321
  39.6 10.1 %collective-permute-start.9 = (bf16[16,256,128]{2,1,0:T(8,128)(2,1)S(1)}, bf16[16,256,128]{2,1,0:T(8,128)(2,1)S(1)}, u32[]{:S(2)}, u32[]{:S(2)}) collective-permute-start(bf16[16,256,128]{2,1,0:T(8,128)(2,1)S(1)} %get-tuple-element.86), channel_id=1, source_target_pairs={{0,8},{8,0},{16,24},{24,16},{32,40},{40,32},{48,56},{56,48},{64,72... | collective-permute-start | bytes 3145736 | tf_op jit(solution)/shard_map/ppermute | solution.py:321
  42.9 11.5 %collective-permute-start.11 = (bf16[1152,128]{1,0:T(8,128)(2,1)S(1)}, bf16[1152,128]{1,0:T(8,128)(2,1)S(1)}, u32[]{:S(2)}, u32[]{:S(2)}) collective-permute-start(bf16[1152,128]{1,0:T(8,128)(2,1)S(1)} %get-tuple-element.94), channel_id=1, source_target_pairs={{0,32},{8,40},{16,48},{24,56},{32,0},{40,8},{48,16},{56,24},{64,96... | collective-permute-start | bytes 884744 | tf_op jit(solution)/shard_map/ppermute | solution.py:312
  45.8 14.4 %collective-permute-start.12 = (bf16[1152,128]{1,0:T(8,128)(2,1)S(1)}, bf16[1152,128]{1,0:T(8,128)(2,1)S(1)}, u32[]{:S(2)}, u32[]{:S(2)}) collective-permute-start(bf16[1152,128]{1,0:T(8,128)(2,1)S(1)} %get-tuple-element.95), channel_id=1, source_target_pairs={{0,48},{8,56},{16,0},{24,8},{32,16},{40,24},{48,32},{56,40},{64,11... | collective-permute-start | bytes 884744 | tf_op jit(solution)/shard_map/ppermute | solution.py:312
  49.7 10.5 %collective-permute-start.10 = (bf16[1152,128]{1,0:T(8,128)(2,1)S(1)}, bf16[1152,128]{1,0:T(8,128)(2,1)S(1)}, u32[]{:S(2)}, u32[]{:S(2)}) collective-permute-start(bf16[1152,128]{1,0:T(8,128)(2,1)S(1)} %get-tuple-element.93.sent_ref), channel_id=1, source_target_pairs={{0,16},{8,24},{16,32},{24,40},{32,48},{40,56},{48,0},{56,8},{64,80... | collective-permute-start | bytes 884744 | tf_op jit(solution)/shard_map/ppermute | solution.py:312
  52.5 14.7 %copy-start.3 = (s32[512,16]{0,1:T(8,128)S(1)}, s32[512,16]{0,1:T(8,128)}, u32[]{:S(2)}) copy-start(s32[512,16]{0,1:T(8,128)} %param.15) | copy-start | bytes 98308
  52.5 21.6 %collective-permute-start.14 = (bf16[8,256,128]{2,1,0:T(8,128)(2,1)S(1)}, bf16[8,256,128]{2,1,0:T(8,128)(2,1)S(1)}, u32[]{:S(2)}, u32[]{:S(2)}) collective-permute-start(bf16[8,256,128]{2,1,0:T(8,128)(2,1)S(1)} %get-tuple-element.101), channel_id=1, source_target_pairs={{0,64},{8,72},{16,80},{24,88},{32,96},{40,104},{48,112},{56,120},{... | collective-permute-start | bytes 1572872 | tf_op jit(solution)/shard_map/ppermute | solution.py:318
  60.3 5.6 %collective-permute-start.18 = (f32[128,128]{1,0:T(8,128)S(1)}, f32[128,128]{1,0:T(8,128)S(1)}, u32[]{:S(2)}, u32[]{:S(2)}) collective-permute-start(f32[128,128]{1,0:T(8,128)S(1)} %get-tuple-element.107.a), channel_id=1, source_target_pairs={{0,64},{8,72},{16,80},{24,88},{32,96},{40,104},{48,112},{56,120},{... | collective-permute-start | bytes 196616 | tf_op jit(solution)/shard_map/ppermute | solution.py:318
  66.0 4.3 %collective-permute-start.19 = (f32[128,128]{1,0:T(8,128)S(1)}, f32[128,128]{1,0:T(8,128)S(1)}, u32[]{:S(2)}, u32[]{:S(2)}) collective-permute-start(f32[128,128]{1,0:T(8,128)S(1)} %add_two.1.own), channel_id=1, source_target_pairs={{0,2},{1,3},{2,0},{3,1},{4,6},{5,7},{6,4},{7,5},{8,10},{9,11},{10,... | collective-permute-start | bytes 196616 | tf_op jit(solution)/shard_map/ppermute | solution.py:315
  67.6 11.3 %collective-permute-start.13 = (bf16[2,256,128]{2,1,0:T(8,128)(2,1)S(1)}, bf16[2,256,128]{2,1,0:T(8,128)(2,1)S(1)}, u32[]{:S(2)}, u32[]{:S(2)}) collective-permute-start(bf16[2,256,128]{2,1,0:T(8,128)(2,1)S(1)} %get-tuple-element.99), channel_id=1, source_target_pairs={{0,64},{8,72},{16,80},{24,88},{32,96},{40,104},{48,112},{56,120},{... | collective-permute-start | bytes 393224 | tf_op jit(solution)/shard_map/ppermute | solution.py:318
  70.3 8.6 %collective-permute-start.20 = (f32[2,128,128]{2,1,0:T(8,128)S(1)}, f32[2,128,128]{2,1,0:T(8,128)S(1)}, u32[]{:S(2)}, u32[]{:S(2)}) collective-permute-start(f32[2,128,128]{2,1,0:T(8,128)S(1)} %pair_up.1.w), channel_id=1, source_target_pairs={{0,4},{1,5},{2,6},{3,7},{4,0},{5,1},{6,2},{7,3},{8,12},{9,13},{10,... | collective-permute-start | bytes 393224 | tf_op jit(solution)/shard_map/ppermute | solution.py:315
  74.3 7.7 %collective-permute-start.15 = (bf16[2,256,128]{2,1,0:T(8,128)(2,1)S(1)}, bf16[2,256,128]{2,1,0:T(8,128)(2,1)S(1)}, u32[]{:S(2)}, u32[]{:S(2)}) collective-permute-start(bf16[2,256,128]{2,1,0:T(8,128)(2,1)S(1)} %get-tuple-element.103), channel_id=1, source_target_pairs={{0,16},{8,24},{16,32},{24,40},{32,48},{40,56},{48,0},{56,8},{64,80... | collective-permute-start | bytes 393224 | tf_op jit(solution)/shard_map/ppermute | solution.py:312
  74.7 7.2 %collective-permute-start.16 = (bf16[2,256,128]{2,1,0:T(8,128)(2,1)S(1)}, bf16[2,256,128]{2,1,0:T(8,128)(2,1)S(1)}, u32[]{:S(2)}, u32[]{:S(2)}) collective-permute-start(bf16[2,256,128]{2,1,0:T(8,128)(2,1)S(1)} %get-tuple-element.104), channel_id=1, source_target_pairs={{0,32},{8,40},{16,48},{24,56},{32,0},{40,8},{48,16},{56,24},{64,96... | collective-permute-start | bytes 393224 | tf_op jit(solution)/shard_map/ppermute | solution.py:312
  77.1 5.7 %collective-permute-start.17 = (bf16[2,256,128]{2,1,0:T(8,128)(2,1)S(1)}, bf16[2,256,128]{2,1,0:T(8,128)(2,1)S(1)}, u32[]{:S(2)}, u32[]{:S(2)}) collective-permute-start(bf16[2,256,128]{2,1,0:T(8,128)(2,1)S(1)} %get-tuple-element.105), channel_id=1, source_target_pairs={{0,48},{8,56},{16,0},{24,8},{32,16},{40,24},{48,32},{56,40},{64,11... | collective-permute-start | bytes 393224 | tf_op jit(solution)/shard_map/ppermute | solution.py:312

commit v6 on v5

--- a/solution.py
+++ b/solution.py
@@ -11,6 +11,9 @@
 N_STEP = 512
 UNROLL = 16
 LIMIT = 16
+MASK_COST = 10**6
+Q_COST = 10**6
+P_COST = 10**10
 PREP_LIMIT = 61
 STAGE_LIMIT = 24
 ZERO_ROW = 32
@@ -92,7 +95,7 @@
         ref[512 : 512 + T] = quarter((x + s) & 3).astype(bf16)
 
 
-def pack(ha, ha_y, hb, m1, m2, m3, keep, a0, b0):
+def pack(ha, ha_y, hb, m1, m2, m3, keep, a0, b0, w):
     a0[0:2], a0[2:4] = ha[...], ha_y[...]
     b0[0:2] = hb[...]
     total = keep[...]
@@ -100,10 +103,7 @@
         b0[2 * s], b0[2 * s + 1] = ref[0:256], ref[256:512]
         total += ref[512 : 512 + T].astype(f32)
     b0[8] = both_parts(total)
-
-
-def add_two(a, b, out):
-    out[...] = a[...] + b[...]
+    w[...] = b0[8]
 
 
 def pair_up(own, got, out):
@@ -236,11 +236,11 @@
         lax.fori_loop(0, 16, give, 0)
 
 
-def late_partner(steps_ref, a0, a3, a1, a2, b0, b1, tiles_ref, so_far_ref, p_ref, q_ref, h_ref, acc_ref):
+def late_partner(steps_ref, a0, a3, a1, a2, b0, b1, w_y, w_diagonal, tiles_ref, so_far_ref, p_ref, q_ref, h_ref, acc_ref):
     h_ref[0:4], h_ref[4:8], h_ref[8:12], h_ref[12:16] = a0[...], a1[...], a2[...], a3[...]
     h_ref[16:24], h_ref[24:32] = b0[0:8], b1[0:8]
     h_ref[ZERO_ROW] = jnp.zeros((256, T), bf16)
-    p_ref[16] = both_parts(whole(b0[8]) + whole(b1[8]))
+    p_ref[16] = both_parts((whole(b0[8]) + whole(b1[8])) + (whole(w_y[...]) + whole(w_diagonal[...])))
     late(1, steps_ref, h_ref, tiles_ref, so_far_ref, (p_ref, q_ref), acc_ref)
 
 
@@ -316,6 +316,10 @@
 
     def over_y_lo(v):
         return lax.ppermute(v, "row", [(r, r ^ 8) for r in range(16)])
+
+    def over_both_y(v):
+        pairs = [(r * 8 + c, (r ^ 8) * 8 + (c ^ 1)) for r in range(16) for c in range(8)]
+        return lax.ppermute(v, ("row", "col"), pairs)
 
     def over_core(v):
         return lax.ppermute(v, "row", [(r, r ^ 1) for r in range(16)])
@@ -354,12 +358,15 @@
         ha, ha_y, hb, m1, m2, m3, own_tiles, tile_coords[0, 0].T, count
     )
 
-    a0, b0 = call(pack, [(quad, bf16), ((9, 256, T), bf16)], [VMEM] * 7, "pack", flops=10**6)(
+    a0, b0, w = call(pack, [(quad, bf16), ((9, 256, T), bf16), ((256, T), bf16)], [VMEM] * 7, "pack", flops=10**6)(
         ha, ha_y, hb, m1, m2, m3, w
     )
     b1 = over_y_hi(b0)
     a3, a1, a2 = over_x(a0, 1), over_x(a0, -1), over_x(a0, 2)
+    w_y = over_y_lo(w)
     (steps,) = call(order_slots, [((8, N_STEP), jnp.int32)], [SMEM, VMEM], "order_slots", flops=10**7)(count, coords)
+    steps, w_y, w = tie(steps, w_y, w)
+    w_diagonal = over_both_y(w)
     (acc,) = call(
         early,
         [((65, 256, T), f32)],
@@ -369,7 +376,7 @@
         scratch=[pltpu.VMEM((33, 256, T), bf16)],
         flops=4 * 10**9,
     )(steps, a0, b0, own_tiles)
-    a0, a1, a2, a3, b0, b1, acc = tie(a0, a1, a2, a3, b0, b1, acc)
+    a0, a1, a2, a3, b0, b1, w_y, w_diagonal, acc = tie(a0, a1, a2, a3, b0, b1, w_y, w_diagonal, acc)
 
     sixteen = (16, 256, T)
     z_p, eight = (1024 + T, T), (8, 256, T)
@@ -391,34 +398,33 @@
     p_sent, q_sent, hidden = call(
         late_partner,
         [((17, 256, T), bf16), (sixteen, bf16), ((33, 256, T), bf16)],
-        [SMEM] + [VMEM] * 8,
+        [SMEM] + [VMEM] * 10,
         "late_1",
         limit=LIMIT,
         scratch=[pltpu.VMEM((33, 256, T), f32)],
         flops=4 * 10**9,
-    )(steps, a0, a3, a1, a2, b0, b1, own_tiles, acc)
+    )(steps, a0, a3, a1, a2, b0, b1, w_y, w_diagonal, own_tiles, acc)
     p_got, q_got = over_core(p_sent), over_core(q_sent)
+    own = own_columns(3)
+    q_keep, q_y = call(split_q, [(eight, f32), (eight, bf16)], [VMEM] * 2, "split_q", flops=10**6)(own, q_got)
+    q_got = over_y_lo(q_y)
+    q_keep, hidden, p_got = tie(q_keep, hidden, p_got)
     own = own_columns(2)
     p_keep, *p_z = call(split_p, [(quad, f32)] + [(z_p, bf16)] * 3, [VMEM] * 3, "split_p", flops=10**6)(
         own, p_got, p_sent
     )
     p_all = around_z(*p_z)
-    p_keep, hidden, q_got = tie(p_keep, hidden, q_got)
-    own = own_columns(3)
-    q_keep, q_y = call(split_q, [(eight, f32), (eight, bf16)], [VMEM] * 2, "split_q", flops=10**6)(own, q_got)
-    q_got = over_y_lo(q_y)
     p_keep, q_keep, words = tie(p_keep, q_keep, in_bits.T)
-    (mask,) = call(in_mask, [((512, 256), bf16)], [VMEM], "in_mask", flops=10**7)(words)
+    (mask,) = call(in_mask, [((512, 256), bf16)], [VMEM], "in_mask", flops=MASK_COST)(words)
+    q_keep, *q_z = call(gather_q, [(half, f32)] + [(half, bf16)] * 3, [VMEM] * 2, "gather_q", flops=Q_COST)(
+        q_keep, q_got
+    )
+    q_all = list(around_z(*q_z))
+    p_keep, q_keep, mask, q_all[0], q_all[2] = tie(p_keep, q_keep, mask, q_all[0], q_all[2])
     p_keep, p_y, w = call(
-        gather_p, [(half, f32), (half, bf16), (square, f32)], [VMEM] * 5, "gather_p", flops=10**10, touched=2**25
+        gather_p, [(half, f32), (half, bf16), (square, f32)], [VMEM] * 5, "gather_p", flops=P_COST
     )(p_keep, *p_all, p_z[0])
-    p_got, w_got = over_y_lo(p_y), over_y_lo(w)
-    q_keep, p_keep, mask = tie(q_keep, p_keep, mask)
-    q_keep, *q_z = call(gather_q, [(half, f32)] + [(half, bf16)] * 3, [VMEM] * 2, "gather_q", flops=10**6)(
-        q_keep, q_got
-    )
-    q_all = around_z(*q_z)
-    (w,) = call(add_two, [(square, f32)], [VMEM] * 2, "add_two", limit=2)(w, w_got)
+    p_got = over_y_lo(p_y)
     (w,) = call(pair_up, [((2, T, T), f32)], [VMEM] * 2, "pair_up", limit=2)(w, swap_x(w, 0))
     w_got = swap_x(w, 1)
     prev_grad, weight_grad = call(

time: 83.5 us -> 88 us (1.054); the launches traced: 83.7 us -> 86.3 us
  Pallas kernels: 21.9 us -> 25.3 us
  starting transfers between devices: 33.2 us -> 30.2 us
  waiting for transfers between devices: 27.1 us -> 29.3 us
    ppermute x3, waiting for transfers between devices: 4.89 us -> 16.8 us  [over_y_lo(): return lax.ppermute(v, 'row', [(r, r ^ 8) for r in range(16)])]
    ppermute x6, waiting for transfers between devices: 8.7 us -> 1.08 us  [over_x(): lax.ppermute(v, 'col', [(c, ((c >> 1) + s & 3) * 2 + (c & 1)) for c in ra...]
    ppermute x6, waiting for transfers between devices: 11.4 us -> 7.99 us  [over_z(): lax.ppermute(v, 'row', [(r, r & 9 | ((r >> 1) + s & 3) << 1) for r in ran...]
    ppermute x2, starting transfers between devices: 5.11 us -> 1.8 us  [swap_x(): return lax.ppermute(v, 'col', [(c, c ^ 2 << bit) for c in range(8)])]
    pallas_call x1, Pallas kernels: 3.78 us -> 5.24 us  [shards(): call(late_partner, [((17, 256, T), bf16), (sixteen, bf16), ((33, 256, T),...]
    ppermute x6, starting transfers between devices: 11.4 us -> 12.7 us  [over_z(): lax.ppermute(v, 'row', [(r, r & 9 | ((r >> 1) + s & 3) << 1) for r in ran...]
    ppermute x6, starting transfers between devices: 8.03 us -> 6.82 us  [over_x(): lax.ppermute(v, 'col', [(c, ((c >> 1) + s & 3) * 2 + (c & 1)) for c in ra...]
    pallas_call x1, Pallas kernels: 3.01 us -> 4.21 us  [shards(): call(stage, [(own_tiles.shape, bf16)], [SMEM, ANY], 'stage', limit=STAGE_...]
  transfers between devices with their start and end apart: 21 -> 22, of which waited for: 10 -> 9; matrix products, arithmetic and copies ran while one was open for 0% -> 0% of each run, Pallas kernels for 17% -> 19%
where the time goes in v6:
time: 88 us; the launch traced here: 86.3 us
  starting transfers between devices  30.2 us (34%)
  waiting for transfers between devices  29.3 us (33%)
  Pallas kernels  25.3 us (29%)
  between operations  1.52 us (2%)
    ppermute x3, waiting for transfers between devices, over_y_lo(): return lax.ppermute(v, 'row', [(r, r ^ 8) for r in range(16)])  16.8 us
    ppermute x6, starting transfers between devices, over_z(): lax.ppermute(v, 'row', [(r, r & 9 | ((r >> 1) + s & 3) << 1) for r in ran...  12.7 us
    ppermute x6, waiting for transfers between devices, over_z(): lax.ppermute(v, 'row', [(r, r & 9 | ((r >> 1) + s & 3) << 1) for r in ran...  7.99 us
    ppermute x6, starting transfers between devices, over_x(): lax.ppermute(v, 'col', [(c, ((c >> 1) + s & 3) * 2 + (c & 1)) for c in ra...  6.82 us
    ppermute x2, starting transfers between devices, over_y_hi(): return lax.ppermute(v, 'col', [(c, c ^ 1) for c in range(8)])  6.46 us
    pallas_call x1, Pallas kernels, shards(): call(late_partner, [((17, 256, T), bf16), (sixteen, bf16), ((33, 256, T),...  5.24 us
    pallas_call x2, Pallas kernels, own_columns(): call(functools.partial(late_own, number), [(sixteen, f32)], [SMEM] + [VME...  5.2 us
    pallas_call x1, Pallas kernels, shards(): call(early, [((65, 256, T), f32)], [SMEM] + [VMEM] * 3, 'early', limit=LI...  5.08 us
  transfers between devices with their start and end apart: 22, of which 9 were waited for; matrix products, arithmetic and copies ran while one was open for 0% of the time, Pallas kernels for 19%

profile of v6, /device:TPU:0, one launch (start us, length us, event | category | flops | bytes accessed | tf_op | source)
XLA Modules:
  0.0 86.3 jit_solution(2677367124530985127)
XLA Ops:
  0.6 2.5 %prep.1 = (bf16[2,256,128]{2,1,0:T(8,128)(2,1)}, bf16[2,256,128]{2,1,0:T(8,128)(2,1)}, bf16[640,128]{1,0:T(8,128)(2,1)}, bf16[640,128]{1,0:T(8,128)(2,1)}, bf16[640,128]{1,0:T(8,128)(2,1)}, /*index=5*/f32[128,128]{1,0:T(8,128)}) custom-call(bf16[512,256]{1,0:T(8,128)(2,1)} %grad_hbm.1, s32[16,512]{1,0:T(8,128)} %bitcast.12, bf16[512,256]{1,0:T(8,128)(2,1)} %agg_hbm.1, ...), custom_call_target="tpu_custom_call" | custom-call | flops 200000000 | tf_op jit(solution)/shard_map/prep/pallas_call | solution.py:328
  3.2 2.9 %collective-permute-start.1 = (bf16[640,128]{1,0:T(8,128)(2,1)}, bf16[640,128]{1,0:T(8,128)(2,1)S(1)}, u32[]{:S(2)}, u32[]{:S(2)}) collective-permute-start(bf16[640,128]{1,0:T(8,128)(2,1)} %get-tuple-element.67), channel_id=1, source_target_pairs={{0,6},{1,7},{2,0},{3,1},{4,2},{5,3},{6,4},{7,5},{8,14},{9,15},{10,... | collective-permute-start | bytes 491528 | tf_op jit(solution)/shard_map/ppermute | solution.py:306
  6.1 0.8 collective-permute-start.2
  6.9 0.9 %collective-permute-start.3 = (bf16[640,128]{1,0:T(8,128)(2,1)}, bf16[640,128]{1,0:T(8,128)(2,1)S(1)}, u32[]{:S(2)}, u32[]{:S(2)}) collective-permute-start(bf16[640,128]{1,0:T(8,128)(2,1)} %get-tuple-element.69), channel_id=1, source_target_pairs={{0,2},{1,3},{2,4},{3,5},{4,6},{5,7},{6,0},{7,1},{8,10},{9,11},{10,... | collective-permute-start | bytes 491528 | tf_op jit(solution)/shard_map/ppermute | solution.py:306
  7.8 3.2 %collective-permute-start = (bf16[2,256,128]{2,1,0:T(8,128)(2,1)}, bf16[2,256,128]{2,1,0:T(8,128)(2,1)S(1)}, u32[]{:S(2)}, u32[]{:S(2)}) collective-permute-start(bf16[2,256,128]{2,1,0:T(8,128)(2,1)} %get-tuple-element.74.ha), channel_id=1, source_target_pairs={{0,1},{1,0},{2,3},{3,2},{4,5},{5,4},{6,7},{7,6},{8,9},{9,8},{10,11... | collective-permute-start | bytes 393224 | tf_op jit(solution)/shard_map/ppermute | solution.py:309
  11.6 0.0 copy-start.4
  11.7 4.2 %stage.1.tiles_ref = bf16[512,128,128]{2,1,0:T(8,128)(2,1)S(1)} custom-call(s32[1]{0:T(128)} %bitcast.7.count_ref, bf16[512,128,128]{2,1,0:T(8,128)(2,1)} %bitcast.11), custom_call_target="tpu_custom_call" | custom-call | flops 1000000000 | tf_op jit(solution)/shard_map/stage/pallas_call | solution.py:348
  15.9 0.0 collective-permute-done.ha_y
  15.9 1.1 %collective-permute-done.3.m3 = bf16[640,128]{1,0:T(8,128)(2,1)S(1)} collective-permute-done((bf16[640,128]{1,0:T(8,128)(2,1)}, bf16[640,128]{1,0:T(8,128)(2,1)S(1)}, u32[]{:S(2)}, u32[]{:S(2)}) %collective-permute-start.3) | collective-permute-done | bytes 163872 | tf_op jit(solution)/shard_map/ppermute | solution.py:306
  17.0 0.1 pack.1
  17.1 3.3 %collective-permute-start.8 = (bf16[9,256,128]{2,1,0:T(8,128)(2,1)S(1)}, bf16[9,256,128]{2,1,0:T(8,128)(2,1)S(1)}, u32[]{:S(2)}, u32[]{:S(2)}) collective-permute-start(bf16[9,256,128]{2,1,0:T(8,128)(2,1)S(1)} %get-tuple-element.92.b0), channel_id=1, source_target_pairs={{0,1},{1,0},{2,3},{3,2},{4,5},{5,4},{6,7},{7,6},{8,9},{9,8},{10,11... | collective-permute-start | bytes 1769480 | tf_op jit(solution)/shard_map/ppermute | solution.py:309
  20.3 0.7 collective-permute-start.4
  21.0 0.6 collective-permute-start.5
  21.6 0.8 collective-permute-start.6
  22.4 0.8 collective-permute-start.7
  23.2 1.2 %order_slots.1.steps_ref = s32[8,512]{1,0:T(8,128)S(1)} custom-call(s32[1]{0:T(128)} %bitcast.8.count_ref, s32[2,512]{1,0:T(2,128)S(1)} %bitcast.10), custom_call_target="tpu_custom_call" | custom-call | flops 10000000 | tf_op jit(solution)/shard_map/order_slots/pallas_call | solution.py:367
  24.4 11.2 %collective-permute-done.4.w_y = bf16[256,128]{1,0:T(8,128)(2,1)S(1)} collective-permute-done((bf16[256,128]{1,0:T(8,128)(2,1)S(1)}, bf16[256,128]{1,0:T(8,128)(2,1)S(1)}, u32[]{:S(2)}, u32[]{:S(2)}) %collective-permute-start.4) | collective-permute-done | bytes 65568 | tf_op jit(solution)/shard_map/ppermute | solution.py:318
  35.6 0.2 collective-permute-start.9
  35.9 5.1 %early.1.so_far_ref = f32[65,256,128]{2,1,0:T(8,128)S(1)} custom-call(s32[8,512]{1,0:T(8,128)S(1)} %order_slots.1.steps_ref, bf16[4,256,128]{2,1,0:T(8,128)(2,1)S(1)} %get-tuple-element.88.a0, bf16[9,256,128]{2,1,0:T(8,128)(2,1)S(1)} %get-tuple-element.92.b0, bf16[512,128,128]{2,1,0:T(8,128)(2,1)S(1)} %stage.1.tiles_ref), custom_call_target="tpu_custom_call" | custom-call | flops 4000000000 | tf_op jit(solution)/shard_map/early/pallas_call | solution.py:370
  41.0 0.2 collective-permute-done.9.w_diagonal
  41.1 5.2 %late_1.1 = (bf16[17,256,128]{2,1,0:T(8,128)(2,1)S(1)}, bf16[16,256,128]{2,1,0:T(8,128)(2,1)S(1)}, bf16[33,256,128]{2,1,0:T(8,128)(2,1)S(1)}) custom-call(s32[8,512]{1,0:T(8,128)S(1)} %order_slots.1.steps_ref, bf16[4,256,128]{2,1,0:T(8,128)(2,1)S(1)} %get-tuple-element.88.a0, bf16[4,256,128]{2,1,0:T(8,128)(2,1)S(1)} %collective-permute-done.7.a3, ...), custom_call_target="tpu_custom_call" | custom-call | flops 4000000000 | tf_op jit(solution)/shard_map/late_1/pallas_call | solution.py:398
  46.4 0.1 collective-permute-start.10
  46.5 0.5 collective-permute-start.11
  47.0 2.6 %late_3.1.acc_ref = f32[16,256,128]{2,1,0:T(8,128)S(1)} custom-call(s32[8,512]{1,0:T(8,128)S(1)} %order_slots.1.steps_ref, bf16[33,256,128]{2,1,0:T(8,128)(2,1)S(1)} %get-tuple-element.101.h_ref, bf16[512,128,128]{2,1,0:T(8,128)(2,1)S(1)} %stage.1.tiles_ref, f32[65,256,128]{2,1,0:T(8,128)S(1)} %early.1.so_far_ref), custom_call_target="tpu_custom_call" | custom-call | flops 2000000000 | tf_op jit(solution)/shard_map/late_3/pallas_call | solution.py:385
  49.6 0.2 split_q.1
  49.8 0.1 collective-permute-start.12
  49.9 0.9 collective-permute-done.11.got_ref
  50.7 2.6 %late_2.1.acc_ref = f32[16,256,128]{2,1,0:T(8,128)S(1)} custom-call(s32[8,512]{1,0:T(8,128)S(1)} %order_slots.1.steps_ref, bf16[33,256,128]{2,1,0:T(8,128)(2,1)S(1)} %get-tuple-element.101.h_ref, bf16[512,128,128]{2,1,0:T(8,128)(2,1)S(1)} %stage.1.tiles_ref, f32[65,256,128]{2,1,0:T(8,128)S(1)} %early.1.so_far_ref), custom_call_target="tpu_custom_call" | custom-call | flops 2000000000 | tf_op jit(solution)/shard_map/late_2/pallas_call | solution.py:385
  53.3 0.0 copy-start.3
  53.3 0.2 split_p.1
  53.5 2.5 %collective-permute-start.15 = (bf16[1152,128]{1,0:T(8,128)(2,1)S(1)}, bf16[1152,128]{1,0:T(8,128)(2,1)S(1)}, u32[]{:S(2)}, u32[]{:S(2)}) collective-permute-start(bf16[1152,128]{1,0:T(8,128)(2,1)S(1)} %get-tuple-element.113.sent_ref), channel_id=1, source_target_pairs={{0,16},{8,24},{16,32},{24,40},{32,48},{40,56},{48,0},{56,8},{64,80... | collective-permute-start | bytes 884744 | tf_op jit(solution)/shard_map/ppermute | solution.py:312
  56.1 1.4 %collective-permute-start.16 = (bf16[1152,128]{1,0:T(8,128)(2,1)S(1)}, bf16[1152,128]{1,0:T(8,128)(2,1)S(1)}, u32[]{:S(2)}, u32[]{:S(2)}) collective-permute-start(bf16[1152,128]{1,0:T(8,128)(2,1)S(1)} %get-tuple-element.114), channel_id=1, source_target_pairs={{0,32},{8,40},{16,48},{24,56},{32,0},{40,8},{48,16},{56,24},{64,96... | collective-permute-start | bytes 884744 | tf_op jit(solution)/shard_map/ppermute | solution.py:312
  57.5 1.8 %collective-permute-start.17 = (bf16[1152,128]{1,0:T(8,128)(2,1)S(1)}, bf16[1152,128]{1,0:T(8,128)(2,1)S(1)}, u32[]{:S(2)}, u32[]{:S(2)}) collective-permute-start(bf16[1152,128]{1,0:T(8,128)(2,1)S(1)} %get-tuple-element.115), channel_id=1, source_target_pairs={{0,48},{8,56},{16,0},{24,8},{32,16},{40,24},{48,32},{56,40},{64,11... | collective-permute-start | bytes 884744 | tf_op jit(solution)/shard_map/ppermute | solution.py:312
  59.3 4.1 %collective-permute-done.12.got_ref = bf16[8,256,128]{2,1,0:T(8,128)(2,1)S(1)} collective-permute-done((bf16[8,256,128]{2,1,0:T(8,128)(2,1)S(1)}, bf16[8,256,128]{2,1,0:T(8,128)(2,1)S(1)}, u32[]{:S(2)}, u32[]{:S(2)}) %collective-permute-start.12) | collective-permute-done | bytes 524320 | tf_op jit(solution)/shard_map/ppermute | solution.py:318
  63.3 0.1 gather_q.1
  63.4 2.3 %collective-permute-start.13 = (bf16[2,256,128]{2,1,0:T(8,128)(2,1)S(1)}, bf16[2,256,128]{2,1,0:T(8,128)(2,1)S(1)}, u32[]{:S(2)}, u32[]{:S(2)}) collective-permute-start(bf16[2,256,128]{2,1,0:T(8,128)(2,1)S(1)} %get-tuple-element.110), channel_id=1, source_target_pairs={{0,16},{8,24},{16,32},{24,40},{32,48},{40,56},{48,0},{56,8},{64,80... | collective-permute-start | bytes 393224 | tf_op jit(solution)/shard_map/ppermute | solution.py:312
  65.7 1.0 %collective-permute-start.14 = (bf16[2,256,128]{2,1,0:T(8,128)(2,1)S(1)}, bf16[2,256,128]{2,1,0:T(8,128)(2,1)S(1)}, u32[]{:S(2)}, u32[]{:S(2)}) collective-permute-start(bf16[2,256,128]{2,1,0:T(8,128)(2,1)S(1)} %get-tuple-element.111), channel_id=1, source_target_pairs={{0,48},{8,56},{16,0},{24,8},{32,16},{40,24},{48,32},{56,40},{64,11... | collective-permute-start | bytes 393224 | tf_op jit(solution)/shard_map/ppermute | solution.py:312
  66.7 0.3 in_mask.1.mask_ref
  67.0 7.0 %collective-permute-done.13.g1 = bf16[2,256,128]{2,1,0:T(8,128)(2,1)S(1)} collective-permute-done((bf16[2,256,128]{2,1,0:T(8,128)(2,1)S(1)}, bf16[2,256,128]{2,1,0:T(8,128)(2,1)S(1)}, u32[]{:S(2)}, u32[]{:S(2)}) %collective-permute-start.13) | collective-permute-done | bytes 131104 | tf_op jit(solution)/shard_map/ppermute | solution.py:312
  74.0 0.1 gather_p.1
  74.2 0.1 collective-permute-start.20
  74.3 3.6 %collective-permute-start.19 = (bf16[2,256,128]{2,1,0:T(8,128)(2,1)S(1)}, bf16[2,256,128]{2,1,0:T(8,128)(2,1)S(1)}, u32[]{:S(2)}, u32[]{:S(2)}) collective-permute-start(bf16[2,256,128]{2,1,0:T(8,128)(2,1)S(1)} %get-tuple-element.120), channel_id=1, source_target_pairs={{0,32},{8,40},{16,48},{24,56},{32,0},{40,8},{48,16},{56,24},{64,96... | collective-permute-start | bytes 393224 | tf_op jit(solution)/shard_map/ppermute | solution.py:312
  77.9 0.9 %collective-permute-start.18 = (bf16[2,256,128]{2,1,0:T(8,128)(2,1)S(1)}, bf16[2,256,128]{2,1,0:T(8,128)(2,1)S(1)}, u32[]{:S(2)}, u32[]{:S(2)}) collective-permute-start(bf16[2,256,128]{2,1,0:T(8,128)(2,1)S(1)} %get-tuple-element.117), channel_id=1, source_target_pairs={{0,64},{8,72},{16,80},{24,88},{32,96},{40,104},{48,112},{56,120},{... | collective-permute-start | bytes 393224 | tf_op jit(solution)/shard_map/ppermute | solution.py:318
  78.8 1.7 %collective-permute-start.21 = (f32[2,128,128]{2,1,0:T(8,128)S(1)}, f32[2,128,128]{2,1,0:T(8,128)S(1)}, u32[]{:S(2)}, u32[]{:S(2)}) collective-permute-start(f32[2,128,128]{2,1,0:T(8,128)S(1)} %pair_up.1.w), channel_id=1, source_target_pairs={{0,4},{1,5},{2,6},{3,7},{4,0},{5,1},{6,2},{7,3},{8,12},{9,13},{10,... | collective-permute-start | bytes 393224 | tf_op jit(solution)/shard_map/ppermute | solution.py:315
  80.5 1.0 %collective-permute-done.19.g2 = bf16[2,256,128]{2,1,0:T(8,128)(2,1)S(1)} collective-permute-done((bf16[2,256,128]{2,1,0:T(8,128)(2,1)S(1)}, bf16[2,256,128]{2,1,0:T(8,128)(2,1)S(1)}, u32[]{:S(2)}, u32[]{:S(2)}) %collective-permute-start.19) | collective-permute-done | bytes 131104 | tf_op jit(solution)/shard_map/ppermute | solution.py:312
  81.5 1.5 %collective-permute-done.18.p_got = bf16[2,256,128]{2,1,0:T(8,128)(2,1)S(1)} collective-permute-done((bf16[2,256,128]{2,1,0:T(8,128)(2,1)S(1)}, bf16[2,256,128]{2,1,0:T(8,128)(2,1)S(1)}, u32[]{:S(2)}, u32[]{:S(2)}) %collective-permute-start.18) | collective-permute-done | bytes 131104 | tf_op jit(solution)/shard_map/ppermute | solution.py:318
  83.0 2.4 %collective-permute-done.21.w_got = f32[2,128,128]{2,1,0:T(8,128)S(1)} collective-permute-done((f32[2,128,128]{2,1,0:T(8,128)S(1)}, f32[2,128,128]{2,1,0:T(8,128)S(1)}, u32[]{:S(2)}, u32[]{:S(2)}) %collective-permute-start.21) | collective-permute-done | bytes 131104 | tf_op jit(solution)/shard_map/ppermute | solution.py:315
  85.4 0.9 %finish.1 = (bf16[512,256]{1,0:T(8,128)(2,1)}, f32[256,256]{1,0:T(8,128)}) custom-call(f32[2,256,128]{2,1,0:T(8,128)S(1)} %get-tuple-element.116.p_keep, bf16[2,256,128]{2,1,0:T(8,128)(2,1)S(1)} %collective-permute-done.18.p_got, f32[2,256,128]{2,1,0:T(8,128)S(1)} %get-tuple-element.118.q_keep, bf16[2,256,128]{2,1,0:T(8,128)(2,1)S(1)} %collective-permute-done.13.g1, ...), custom_call_target="tpu_custom_call" | custom-call | flops 1000000 | tf_op jit(solution)/shard_map/finish/pallas_call | solution.py:430
  (21 shorter events, 0.1 us)
Async XLA Ops:
  3.2 12.7 %collective-permute-start.1 = (bf16[640,128]{1,0:T(8,128)(2,1)}, bf16[640,128]{1,0:T(8,128)(2,1)S(1)}, u32[]{:S(2)}, u32[]{:S(2)}) collective-permute-start(bf16[640,128]{1,0:T(8,128)(2,1)} %get-tuple-element.67), channel_id=1, source_target_pairs={{0,6},{1,7},{2,0},{3,1},{4,2},{5,3},{6,4},{7,5},{8,14},{9,15},{10,... | collective-permute-start | bytes 491528 | tf_op jit(solution)/shard_map/ppermute | solution.py:306
  6.1 9.8 %collective-permute-start.2 = (bf16[640,128]{1,0:T(8,128)(2,1)}, bf16[640,128]{1,0:T(8,128)(2,1)S(1)}, u32[]{:S(2)}, u32[]{:S(2)}) collective-permute-start(bf16[640,128]{1,0:T(8,128)(2,1)} %get-tuple-element.68), channel_id=1, source_target_pairs={{0,4},{1,5},{2,6},{3,7},{4,0},{5,1},{6,2},{7,3},{8,12},{9,13},{10,... | collective-permute-start | bytes 491528 | tf_op jit(solution)/shard_map/ppermute | solution.py:306
  6.9 10.1 %collective-permute-start.3 = (bf16[640,128]{1,0:T(8,128)(2,1)}, bf16[640,128]{1,0:T(8,128)(2,1)S(1)}, u32[]{:S(2)}, u32[]{:S(2)}) collective-permute-start(bf16[640,128]{1,0:T(8,128)(2,1)} %get-tuple-element.69), channel_id=1, source_target_pairs={{0,2},{1,3},{2,4},{3,5},{4,6},{5,7},{6,0},{7,1},{8,10},{9,11},{10,... | collective-permute-start | bytes 491528 | tf_op jit(solution)/shard_map/ppermute | solution.py:306
  7.8 8.1 %collective-permute-start = (bf16[2,256,128]{2,1,0:T(8,128)(2,1)}, bf16[2,256,128]{2,1,0:T(8,128)(2,1)S(1)}, u32[]{:S(2)}, u32[]{:S(2)}) collective-permute-start(bf16[2,256,128]{2,1,0:T(8,128)(2,1)} %get-tuple-element.74.ha), channel_id=1, source_target_pairs={{0,1},{1,0},{2,3},{3,2},{4,5},{5,4},{6,7},{7,6},{8,9},{9,8},{10,11... | collective-permute-start | bytes 393224 | tf_op jit(solution)/shard_map/ppermute | solution.py:309
  11.6 5.4 %copy-start = (bf16[2,256,128]{2,1,0:T(8,128)(2,1)S(1)}, bf16[2,256,128]{2,1,0:T(8,128)(2,1)}, u32[]{:S(2)}) copy-start(bf16[2,256,128]{2,1,0:T(8,128)(2,1)} %get-tuple-element.74.ha) | copy-start | bytes 393220
  11.6 5.4 %copy-start.1 = (bf16[2,256,128]{2,1,0:T(8,128)(2,1)S(1)}, bf16[2,256,128]{2,1,0:T(8,128)(2,1)}, u32[]{:S(2)}) copy-start(bf16[2,256,128]{2,1,0:T(8,128)(2,1)} %get-tuple-element.76.hb) | copy-start | bytes 393220
  11.6 5.3 %copy-start.2 = (f32[128,128]{1,0:T(8,128)S(1)}, f32[128,128]{1,0:T(8,128)}, u32[]{:S(2)}) copy-start(f32[128,128]{1,0:T(8,128)} %get-tuple-element.80.keep) | copy-start | bytes 196612
  11.6 11.6 %copy-start.4 = (s32[1,1,512,2]{2,3,1,0:T(2,128)S(1)}, s32[1,1,512,2]{2,3,1,0:T(2,128)}, u32[]{:S(2)}) copy-start(s32[1,1,512,2]{2,3,1,0:T(2,128)} %param.13) | copy-start | bytes 12292
  17.1 24.1 %collective-permute-start.8 = (bf16[9,256,128]{2,1,0:T(8,128)(2,1)S(1)}, bf16[9,256,128]{2,1,0:T(8,128)(2,1)S(1)}, u32[]{:S(2)}, u32[]{:S(2)}) collective-permute-start(bf16[9,256,128]{2,1,0:T(8,128)(2,1)S(1)} %get-tuple-element.92.b0), channel_id=1, source_target_pairs={{0,1},{1,0},{2,3},{3,2},{4,5},{5,4},{6,7},{7,6},{8,9},{9,8},{10,11... | collective-permute-start | bytes 1769480 | tf_op jit(solution)/shard_map/ppermute | solution.py:309
  20.3 15.3 %collective-permute-start.4 = (bf16[256,128]{1,0:T(8,128)(2,1)S(1)}, bf16[256,128]{1,0:T(8,128)(2,1)S(1)}, u32[]{:S(2)}, u32[]{:S(2)}) collective-permute-start(bf16[256,128]{1,0:T(8,128)(2,1)S(1)} %get-tuple-element.86), channel_id=1, source_target_pairs={{0,64},{8,72},{16,80},{24,88},{32,96},{40,104},{48,112},{56,120},{... | collective-permute-start | bytes 196616 | tf_op jit(solution)/shard_map/ppermute | solution.py:318
  21.0 20.1 %collective-permute-start.5 = (bf16[4,256,128]{2,1,0:T(8,128)(2,1)S(1)}, bf16[4,256,128]{2,1,0:T(8,128)(2,1)S(1)}, u32[]{:S(2)}, u32[]{:S(2)}) collective-permute-start(bf16[4,256,128]{2,1,0:T(8,128)(2,1)S(1)} %get-tuple-element.88.a0), channel_id=1, source_target_pairs={{0,6},{1,7},{2,0},{3,1},{4,2},{5,3},{6,4},{7,5},{8,14},{9,15},{10,... | collective-permute-start | bytes 786440 | tf_op jit(solution)/shard_map/ppermute | solution.py:306
  21.6 19.5 %collective-permute-start.6 = (bf16[4,256,128]{2,1,0:T(8,128)(2,1)S(1)}, bf16[4,256,128]{2,1,0:T(8,128)(2,1)S(1)}, u32[]{:S(2)}, u32[]{:S(2)}) collective-permute-start(bf16[4,256,128]{2,1,0:T(8,128)(2,1)S(1)} %get-tuple-element.88.a0), channel_id=1, source_target_pairs={{0,4},{1,5},{2,6},{3,7},{4,0},{5,1},{6,2},{7,3},{8,12},{9,13},{10,... | collective-permute-start | bytes 786440 | tf_op jit(solution)/shard_map/ppermute | solution.py:306
  22.4 18.7 %collective-permute-start.7 = (bf16[4,256,128]{2,1,0:T(8,128)(2,1)S(1)}, bf16[4,256,128]{2,1,0:T(8,128)(2,1)S(1)}, u32[]{:S(2)}, u32[]{:S(2)}) collective-permute-start(bf16[4,256,128]{2,1,0:T(8,128)(2,1)S(1)} %get-tuple-element.88.a0), channel_id=1, source_target_pairs={{0,2},{1,3},{2,4},{3,5},{4,6},{5,7},{6,0},{7,1},{8,10},{9,11},{10,... | collective-permute-start | bytes 786440 | tf_op jit(solution)/shard_map/ppermute | solution.py:306
  35.6 5.5 %collective-permute-start.9 = (bf16[256,128]{1,0:T(8,128)(2,1)S(1)}, bf16[256,128]{1,0:T(8,128)(2,1)S(1)}, u32[]{:S(2)}, u32[]{:S(2)}) collective-permute-start(bf16[256,128]{1,0:T(8,128)(2,1)S(1)} %get-tuple-element.86), channel_id=1, source_target_pairs={{0,65},{1,64},{2,67},{3,66},{4,69},{5,68},{6,71},{7,70},{8,73},{9,... | collective-permute-start | bytes 196616 | tf_op jit(solution)/shard_map/ppermute | solution.py:322
  46.4 3.2 %collective-permute-start.10 = (bf16[16,256,128]{2,1,0:T(8,128)(2,1)S(1)}, bf16[16,256,128]{2,1,0:T(8,128)(2,1)S(1)}, u32[]{:S(2)}, u32[]{:S(2)}) collective-permute-start(bf16[16,256,128]{2,1,0:T(8,128)(2,1)S(1)} %get-tuple-element.98), channel_id=1, source_target_pairs={{0,8},{8,0},{16,24},{24,16},{32,40},{40,32},{48,56},{56,48},{64,72... | collective-permute-start | bytes 3145736 | tf_op jit(solution)/shard_map/ppermute | solution.py:325
  46.5 4.2 %collective-permute-start.11 = (bf16[17,256,128]{2,1,0:T(8,128)(2,1)S(1)}, bf16[17,256,128]{2,1,0:T(8,128)(2,1)S(1)}, u32[]{:S(2)}, u32[]{:S(2)}) collective-permute-start(bf16[17,256,128]{2,1,0:T(8,128)(2,1)S(1)} %get-tuple-element.100.sent_ref), channel_id=1, source_target_pairs={{0,8},{8,0},{16,24},{24,16},{32,40},{40,32},{48,56},{56,48},{64,72... | collective-permute-start | bytes 3342344 | tf_op jit(solution)/shard_map/ppermute | solution.py:325
  49.8 13.6 %collective-permute-start.12 = (bf16[8,256,128]{2,1,0:T(8,128)(2,1)S(1)}, bf16[8,256,128]{2,1,0:T(8,128)(2,1)S(1)}, u32[]{:S(2)}, u32[]{:S(2)}) collective-permute-start(bf16[8,256,128]{2,1,0:T(8,128)(2,1)S(1)} %get-tuple-element.107), channel_id=1, source_target_pairs={{0,64},{8,72},{16,80},{24,88},{32,96},{40,104},{48,112},{56,120},{... | collective-permute-start | bytes 1572872 | tf_op jit(solution)/shard_map/ppermute | solution.py:318
  53.3 13.4 %copy-start.3 = (s32[512,16]{0,1:T(8,128)S(1)}, s32[512,16]{0,1:T(8,128)}, u32[]{:S(2)}) copy-start(s32[512,16]{0,1:T(8,128)} %param.15) | copy-start | bytes 98308
  53.5 20.5 %collective-permute-start.15 = (bf16[1152,128]{1,0:T(8,128)(2,1)S(1)}, bf16[1152,128]{1,0:T(8,128)(2,1)S(1)}, u32[]{:S(2)}, u32[]{:S(2)}) collective-permute-start(bf16[1152,128]{1,0:T(8,128)(2,1)S(1)} %get-tuple-element.113.sent_ref), channel_id=1, source_target_pairs={{0,16},{8,24},{16,32},{24,40},{32,48},{40,56},{48,0},{56,8},{64,80... | collective-permute-start | bytes 884744 | tf_op jit(solution)/shard_map/ppermute | solution.py:312
  56.1 17.9 %collective-permute-start.16 = (bf16[1152,128]{1,0:T(8,128)(2,1)S(1)}, bf16[1152,128]{1,0:T(8,128)(2,1)S(1)}, u32[]{:S(2)}, u32[]{:S(2)}) collective-permute-start(bf16[1152,128]{1,0:T(8,128)(2,1)S(1)} %get-tuple-element.114), channel_id=1, source_target_pairs={{0,32},{8,40},{16,48},{24,56},{32,0},{40,8},{48,16},{56,24},{64,96... | collective-permute-start | bytes 884744 | tf_op jit(solution)/shard_map/ppermute | solution.py:312
  57.5 16.6 %collective-permute-start.17 = (bf16[1152,128]{1,0:T(8,128)(2,1)S(1)}, bf16[1152,128]{1,0:T(8,128)(2,1)S(1)}, u32[]{:S(2)}, u32[]{:S(2)}) collective-permute-start(bf16[1152,128]{1,0:T(8,128)(2,1)S(1)} %get-tuple-element.115), channel_id=1, source_target_pairs={{0,48},{8,56},{16,0},{24,8},{32,16},{40,24},{48,32},{56,40},{64,11... | collective-permute-start | bytes 884744 | tf_op jit(solution)/shard_map/ppermute | solution.py:312
  63.4 10.6 %collective-permute-start.13 = (bf16[2,256,128]{2,1,0:T(8,128)(2,1)S(1)}, bf16[2,256,128]{2,1,0:T(8,128)(2,1)S(1)}, u32[]{:S(2)}, u32[]{:S(2)}) collective-permute-start(bf16[2,256,128]{2,1,0:T(8,128)(2,1)S(1)} %get-tuple-element.110), channel_id=1, source_target_pairs={{0,16},{8,24},{16,32},{24,40},{32,48},{40,56},{48,0},{56,8},{64,80... | collective-permute-start | bytes 393224 | tf_op jit(solution)/shard_map/ppermute | solution.py:312
  65.7 8.3 %collective-permute-start.14 = (bf16[2,256,128]{2,1,0:T(8,128)(2,1)S(1)}, bf16[2,256,128]{2,1,0:T(8,128)(2,1)S(1)}, u32[]{:S(2)}, u32[]{:S(2)}) collective-permute-start(bf16[2,256,128]{2,1,0:T(8,128)(2,1)S(1)} %get-tuple-element.111), channel_id=1, source_target_pairs={{0,48},{8,56},{16,0},{24,8},{32,16},{40,24},{48,32},{56,40},{64,11... | collective-permute-start | bytes 393224 | tf_op jit(solution)/shard_map/ppermute | solution.py:312
  74.2 4.6 %collective-permute-start.20 = (f32[128,128]{1,0:T(8,128)S(1)}, f32[128,128]{1,0:T(8,128)S(1)}, u32[]{:S(2)}, u32[]{:S(2)}) collective-permute-start(f32[128,128]{1,0:T(8,128)S(1)} %get-tuple-element.123.own), channel_id=1, source_target_pairs={{0,2},{1,3},{2,0},{3,1},{4,6},{5,7},{6,4},{7,5},{8,10},{9,11},{10,... | collective-permute-start | bytes 196616 | tf_op jit(solution)/shard_map/ppermute | solution.py:315
  74.3 7.3 %collective-permute-start.19 = (bf16[2,256,128]{2,1,0:T(8,128)(2,1)S(1)}, bf16[2,256,128]{2,1,0:T(8,128)(2,1)S(1)}, u32[]{:S(2)}, u32[]{:S(2)}) collective-permute-start(bf16[2,256,128]{2,1,0:T(8,128)(2,1)S(1)} %get-tuple-element.120), channel_id=1, source_target_pairs={{0,32},{8,40},{16,48},{24,56},{32,0},{40,8},{48,16},{56,24},{64,96... | collective-permute-start | bytes 393224 | tf_op jit(solution)/shard_map/ppermute | solution.py:312
  77.9 5.1 %collective-permute-start.18 = (bf16[2,256,128]{2,1,0:T(8,128)(2,1)S(1)}, bf16[2,256,128]{2,1,0:T(8,128)(2,1)S(1)}, u32[]{:S(2)}, u32[]{:S(2)}) collective-permute-start(bf16[2,256,128]{2,1,0:T(8,128)(2,1)S(1)} %get-tuple-element.117), channel_id=1, source_target_pairs={{0,64},{8,72},{16,80},{24,88},{32,96},{40,104},{48,112},{56,120},{... | collective-permute-start | bytes 393224 | tf_op jit(solution)/shard_map/ppermute | solution.py:318
  78.8 6.6 %collective-permute-start.21 = (f32[2,128,128]{2,1,0:T(8,128)S(1)}, f32[2,128,128]{2,1,0:T(8,128)S(1)}, u32[]{:S(2)}, u32[]{:S(2)}) collective-permute-start(f32[2,128,128]{2,1,0:T(8,128)S(1)} %pair_up.1.w), channel_id=1, source_target_pairs={{0,4},{1,5},{2,6},{3,7},{4,0},{5,1},{6,2},{7,3},{8,12},{9,13},{10,... | collective-permute-start | bytes 393224 | tf_op jit(solution)/shard_map/ppermute | solution.py:315

commit v7 on v5

--- a/solution.py
+++ b/solution.py
@@ -417,6 +417,7 @@
     q_keep, *q_z = call(gather_q, [(half, f32)] + [(half, bf16)] * 3, [VMEM] * 2, "gather_q", flops=10**6)(
         q_keep, q_got
     )
+    q_keep, w, w_got = tie(q_keep, w, w_got)
     q_all = around_z(*q_z)
     (w,) = call(add_two, [(square, f32)], [VMEM] * 2, "add_two", limit=2)(w, w_got)
     (w,) = call(pair_up, [((2, T, T), f32)], [VMEM] * 2, "pair_up", limit=2)(w, swap_x(w, 0))

time: 83.5 us -> 81.1 us (0.971)
  Pallas kernels: 21.9 us -> 17.7 us
  starting transfers between devices: 33.2 us -> 35.8 us
    ppermute x3, starting transfers between devices: 1.59 us -> 4.68 us  [over_y_lo(): return lax.ppermute(v, 'row', [(r, r ^ 8) for r in range(16)])]
    ppermute x3, waiting for transfers between devices: 4.89 us -> 2.56 us  [over_y_lo(): return lax.ppermute(v, 'row', [(r, r ^ 8) for r in range(16)])]
    ppermute x6, waiting for transfers between devices: 8.7 us -> 10.4 us  [over_x(): lax.ppermute(v, 'col', [(c, ((c >> 1) + s & 3) * 2 + (c & 1)) for c in ra...]
    pallas_call x1, Pallas kernels: 4.37 us -> 2.94 us  [shards(): call(early, [((65, 256, T), f32)], [SMEM] + [VMEM] * 3, 'early', limit=LI...]
    pallas_call x2, Pallas kernels: 5.2 us -> 3.78 us  [own_columns(): call(functools.partial(late_own, number), [(sixteen, f32)], [SMEM] + [VME...]
  transfers between devices with their start and end apart: 21 -> 21, of which waited for: 10 -> 13; matrix products, arithmetic and copies ran while one was open for 0% -> 0% of each run, Pallas kernels for 17% -> 14%
where the time goes in v7:
time: 81.1 us; the launch traced here: 81.6 us
  starting transfers between devices  35.8 us (44%)
  waiting for transfers between devices  26.6 us (33%)
  Pallas kernels  17.7 us (22%)
  between operations  1.45 us (2%)
    ppermute x6, starting transfers between devices, over_z(): lax.ppermute(v, 'row', [(r, r & 9 | ((r >> 1) + s & 3) << 1) for r in ran...  11.5 us
    ppermute x6, waiting for transfers between devices, over_z(): lax.ppermute(v, 'row', [(r, r & 9 | ((r >> 1) + s & 3) << 1) for r in ran...  10.8 us
    ppermute x6, waiting for transfers between devices, over_x(): lax.ppermute(v, 'col', [(c, ((c >> 1) + s & 3) * 2 + (c & 1)) for c in ra...  10.4 us
    ppermute x6, starting transfers between devices, over_x(): lax.ppermute(v, 'col', [(c, ((c >> 1) + s & 3) * 2 + (c & 1)) for c in ra...  8.03 us
    ppermute x2, starting transfers between devices, over_y_hi(): return lax.ppermute(v, 'col', [(c, c ^ 1) for c in range(8)])  6.46 us
    ppermute x3, starting transfers between devices, over_y_lo(): return lax.ppermute(v, 'row', [(r, r ^ 8) for r in range(16)])  4.68 us
    ppermute x2, starting transfers between devices, swap_x(): return lax.ppermute(v, 'col', [(c, c ^ 2 << bit) for c in range(8)])  4.5 us
    pallas_call x2, Pallas kernels, own_columns(): call(functools.partial(late_own, number), [(sixteen, f32)], [SMEM] + [VME...  3.78 us
  transfers between devices with their start and end apart: 21, of which 13 were waited for; matrix products, arithmetic and copies ran while one was open for 0% of the time, Pallas kernels for 14%

profile of v7, /device:TPU:0, one launch (start us, length us, event | category | flops | bytes accessed | tf_op | source)
XLA Modules:
  0.0 81.6 jit_solution(18145146087937401043)
XLA Ops:
  0.6 2.5 %prep.1 = (bf16[2,256,128]{2,1,0:T(8,128)(2,1)}, bf16[2,256,128]{2,1,0:T(8,128)(2,1)}, bf16[640,128]{1,0:T(8,128)(2,1)}, bf16[640,128]{1,0:T(8,128)(2,1)}, bf16[640,128]{1,0:T(8,128)(2,1)}, /*index=5*/f32[128,128]{1,0:T(8,128)}) custom-call(bf16[512,256]{1,0:T(8,128)(2,1)} %grad_hbm.1, s32[16,512]{1,0:T(8,128)} %bitcast.12, bf16[512,256]{1,0:T(8,128)(2,1)} %agg_hbm.1, ...), custom_call_target="tpu_custom_call" | custom-call | flops 200000000 | tf_op jit(solution)/shard_map/prep/pallas_call | solution.py:324
  3.2 2.9 %collective-permute-start.1 = (bf16[640,128]{1,0:T(8,128)(2,1)}, bf16[640,128]{1,0:T(8,128)(2,1)S(1)}, u32[]{:S(2)}, u32[]{:S(2)}) collective-permute-start(bf16[640,128]{1,0:T(8,128)(2,1)} %get-tuple-element.62), channel_id=1, source_target_pairs={{0,6},{1,7},{2,0},{3,1},{4,2},{5,3},{6,4},{7,5},{8,14},{9,15},{10,... | collective-permute-start | bytes 491528 | tf_op jit(solution)/shard_map/ppermute | solution.py:306
  6.1 0.8 collective-permute-start.2
  6.9 0.9 %collective-permute-start.3 = (bf16[640,128]{1,0:T(8,128)(2,1)}, bf16[640,128]{1,0:T(8,128)(2,1)S(1)}, u32[]{:S(2)}, u32[]{:S(2)}) collective-permute-start(bf16[640,128]{1,0:T(8,128)(2,1)} %get-tuple-element.64), channel_id=1, source_target_pairs={{0,2},{1,3},{2,4},{3,5},{4,6},{5,7},{6,0},{7,1},{8,10},{9,11},{10,... | collective-permute-start | bytes 491528 | tf_op jit(solution)/shard_map/ppermute | solution.py:306
  7.8 3.2 %collective-permute-start = (bf16[2,256,128]{2,1,0:T(8,128)(2,1)}, bf16[2,256,128]{2,1,0:T(8,128)(2,1)S(1)}, u32[]{:S(2)}, u32[]{:S(2)}) collective-permute-start(bf16[2,256,128]{2,1,0:T(8,128)(2,1)} %get-tuple-element.69.ha), channel_id=1, source_target_pairs={{0,1},{1,0},{2,3},{3,2},{4,5},{5,4},{6,7},{7,6},{8,9},{9,8},{10,11... | collective-permute-start | bytes 393224 | tf_op jit(solution)/shard_map/ppermute | solution.py:309
  11.6 0.0 copy-start.4
  11.7 2.4 %stage.1.tiles_ref = bf16[512,128,128]{2,1,0:T(8,128)(2,1)S(1)} custom-call(s32[1]{0:T(128)} %bitcast.7.count_ref, bf16[512,128,128]{2,1,0:T(8,128)(2,1)} %bitcast.11), custom_call_target="tpu_custom_call" | custom-call | flops 1000000000 | tf_op jit(solution)/shard_map/stage/pallas_call | solution.py:344
  14.0 0.4 collective-permute-done.ha_y
  14.5 0.5 collective-permute-done.2.m2
  15.0 2.0 %collective-permute-done.3.m3 = bf16[640,128]{1,0:T(8,128)(2,1)S(1)} collective-permute-done((bf16[640,128]{1,0:T(8,128)(2,1)}, bf16[640,128]{1,0:T(8,128)(2,1)S(1)}, u32[]{:S(2)}, u32[]{:S(2)}) %collective-permute-start.3) | collective-permute-done | bytes 163872 | tf_op jit(solution)/shard_map/ppermute | solution.py:306
  17.0 0.1 pack.1
  17.1 3.3 %collective-permute-start.7 = (bf16[9,256,128]{2,1,0:T(8,128)(2,1)S(1)}, bf16[9,256,128]{2,1,0:T(8,128)(2,1)S(1)}, u32[]{:S(2)}, u32[]{:S(2)}) collective-permute-start(bf16[9,256,128]{2,1,0:T(8,128)(2,1)S(1)} %get-tuple-element.83.b0), channel_id=1, source_target_pairs={{0,1},{1,0},{2,3},{3,2},{4,5},{5,4},{6,7},{7,6},{8,9},{9,8},{10,11... | collective-permute-start | bytes 1769480 | tf_op jit(solution)/shard_map/ppermute | solution.py:309
  20.3 2.1 %collective-permute-start.5 = (bf16[4,256,128]{2,1,0:T(8,128)(2,1)S(1)}, bf16[4,256,128]{2,1,0:T(8,128)(2,1)S(1)}, u32[]{:S(2)}, u32[]{:S(2)}) collective-permute-start(bf16[4,256,128]{2,1,0:T(8,128)(2,1)S(1)} %get-tuple-element.79.a0), channel_id=1, source_target_pairs={{0,4},{1,5},{2,6},{3,7},{4,0},{5,1},{6,2},{7,3},{8,12},{9,13},{10,... | collective-permute-start | bytes 786440 | tf_op jit(solution)/shard_map/ppermute | solution.py:306
  22.4 1.4 %collective-permute-start.4 = (bf16[4,256,128]{2,1,0:T(8,128)(2,1)S(1)}, bf16[4,256,128]{2,1,0:T(8,128)(2,1)S(1)}, u32[]{:S(2)}, u32[]{:S(2)}) collective-permute-start(bf16[4,256,128]{2,1,0:T(8,128)(2,1)S(1)} %get-tuple-element.79.a0), channel_id=1, source_target_pairs={{0,6},{1,7},{2,0},{3,1},{4,2},{5,3},{6,4},{7,5},{8,14},{9,15},{10,... | collective-permute-start | bytes 786440 | tf_op jit(solution)/shard_map/ppermute | solution.py:306
  23.8 1.2 %order_slots.1.steps_ref = s32[8,512]{1,0:T(8,128)S(1)} custom-call(s32[1]{0:T(128)} %bitcast.8.count_ref, s32[2,512]{1,0:T(2,128)S(1)} %bitcast.10), custom_call_target="tpu_custom_call" | custom-call | flops 10000000 | tf_op jit(solution)/shard_map/order_slots/pallas_call | solution.py:362
  24.9 2.9 %early.1.so_far_ref = f32[65,256,128]{2,1,0:T(8,128)S(1)} custom-call(s32[8,512]{1,0:T(8,128)S(1)} %order_slots.1.steps_ref, bf16[4,256,128]{2,1,0:T(8,128)(2,1)S(1)} %get-tuple-element.79.a0, bf16[9,256,128]{2,1,0:T(8,128)(2,1)S(1)} %get-tuple-element.83.b0, bf16[512,128,128]{2,1,0:T(8,128)(2,1)S(1)} %stage.1.tiles_ref), custom_call_target="tpu_custom_call" | custom-call | flops 4000000000 | tf_op jit(solution)/shard_map/early/pallas_call | solution.py:363
  27.9 7.2 %collective-permute-done.6.a3 = bf16[4,256,128]{2,1,0:T(8,128)(2,1)S(1)} collective-permute-done((bf16[4,256,128]{2,1,0:T(8,128)(2,1)S(1)}, bf16[4,256,128]{2,1,0:T(8,128)(2,1)S(1)}, u32[]{:S(2)}, u32[]{:S(2)}) %collective-permute-start.6) | collective-permute-done | bytes 262176 | tf_op jit(solution)/shard_map/ppermute | solution.py:306
  35.1 0.6 collective-permute-done.4.a1
  35.7 3.1 %late_1.1 = (bf16[17,256,128]{2,1,0:T(8,128)(2,1)S(1)}, bf16[16,256,128]{2,1,0:T(8,128)(2,1)S(1)}, bf16[33,256,128]{2,1,0:T(8,128)(2,1)S(1)}) custom-call(s32[8,512]{1,0:T(8,128)S(1)} %order_slots.1.steps_ref, bf16[4,256,128]{2,1,0:T(8,128)(2,1)S(1)} %get-tuple-element.79.a0, bf16[4,256,128]{2,1,0:T(8,128)(2,1)S(1)} %collective-permute-done.6.a3, ...), custom_call_target="tpu_custom_call" | custom-call | flops 4000000000 | tf_op jit(solution)/shard_map/late_1/pallas_call | solution.py:391
  38.8 0.1 collective-permute-start.8
  38.9 0.5 collective-permute-start.9
  39.4 1.9 %late_2.1.acc_ref = f32[16,256,128]{2,1,0:T(8,128)S(1)} custom-call(s32[8,512]{1,0:T(8,128)S(1)} %order_slots.1.steps_ref, bf16[33,256,128]{2,1,0:T(8,128)(2,1)S(1)} %get-tuple-element.91.h_ref, bf16[512,128,128]{2,1,0:T(8,128)(2,1)S(1)} %stage.1.tiles_ref, f32[65,256,128]{2,1,0:T(8,128)S(1)} %early.1.so_far_ref), custom_call_target="tpu_custom_call" | custom-call | flops 2000000000 | tf_op jit(solution)/shard_map/late_2/pallas_call | solution.py:378
  41.3 0.3 collective-permute-done.8.got_ref
  41.6 0.2 split_p.1
  41.8 4.3 %collective-permute-start.11 = (bf16[1152,128]{1,0:T(8,128)(2,1)S(1)}, bf16[1152,128]{1,0:T(8,128)(2,1)S(1)}, u32[]{:S(2)}, u32[]{:S(2)}) collective-permute-start(bf16[1152,128]{1,0:T(8,128)(2,1)S(1)} %get-tuple-element.97), channel_id=1, source_target_pairs={{0,32},{8,40},{16,48},{24,56},{32,0},{40,8},{48,16},{56,24},{64,96... | collective-permute-start | bytes 884744 | tf_op jit(solution)/shard_map/ppermute | solution.py:312
  46.1 1.7 %collective-permute-start.12 = (bf16[1152,128]{1,0:T(8,128)(2,1)S(1)}, bf16[1152,128]{1,0:T(8,128)(2,1)S(1)}, u32[]{:S(2)}, u32[]{:S(2)}) collective-permute-start(bf16[1152,128]{1,0:T(8,128)(2,1)S(1)} %get-tuple-element.98), channel_id=1, source_target_pairs={{0,48},{8,56},{16,0},{24,8},{32,16},{40,24},{48,32},{56,40},{64,11... | collective-permute-start | bytes 884744 | tf_op jit(solution)/shard_map/ppermute | solution.py:312
  47.8 0.8 collective-permute-start.10
  48.6 1.9 %late_3.1.acc_ref = f32[16,256,128]{2,1,0:T(8,128)S(1)} custom-call(s32[8,512]{1,0:T(8,128)S(1)} %order_slots.1.steps_ref, bf16[33,256,128]{2,1,0:T(8,128)(2,1)S(1)} %get-tuple-element.91.h_ref, bf16[512,128,128]{2,1,0:T(8,128)(2,1)S(1)} %stage.1.tiles_ref, f32[65,256,128]{2,1,0:T(8,128)S(1)} %early.1.so_far_ref), custom_call_target="tpu_custom_call" | custom-call | flops 2000000000 | tf_op jit(solution)/shard_map/late_3/pallas_call | solution.py:378
  50.5 0.2 split_q.1
  50.7 1.5 %collective-permute-start.14 = (bf16[8,256,128]{2,1,0:T(8,128)(2,1)S(1)}, bf16[8,256,128]{2,1,0:T(8,128)(2,1)S(1)}, u32[]{:S(2)}, u32[]{:S(2)}) collective-permute-start(bf16[8,256,128]{2,1,0:T(8,128)(2,1)S(1)} %get-tuple-element.104), channel_id=1, source_target_pairs={{0,64},{8,72},{16,80},{24,88},{32,96},{40,104},{48,112},{56,120},{... | collective-permute-start | bytes 1572872 | tf_op jit(solution)/shard_map/ppermute | solution.py:318
  52.2 1.2 %collective-permute-done.11.g2 = bf16[1152,128]{1,0:T(8,128)(2,1)S(1)} collective-permute-done((bf16[1152,128]{1,0:T(8,128)(2,1)S(1)}, bf16[1152,128]{1,0:T(8,128)(2,1)S(1)}, u32[]{:S(2)}, u32[]{:S(2)}) %collective-permute-start.11) | collective-permute-done | bytes 294944 | tf_op jit(solution)/shard_map/ppermute | solution.py:312
  53.3 8.3 %collective-permute-done.12.g3 = bf16[1152,128]{1,0:T(8,128)(2,1)S(1)} collective-permute-done((bf16[1152,128]{1,0:T(8,128)(2,1)S(1)}, bf16[1152,128]{1,0:T(8,128)(2,1)S(1)}, u32[]{:S(2)}, u32[]{:S(2)}) %collective-permute-start.12) | collective-permute-done | bytes 294944 | tf_op jit(solution)/shard_map/ppermute | solution.py:312
  61.6 0.1 gather_p.1
  61.8 1.5 %collective-permute-start.15 = (f32[128,128]{1,0:T(8,128)S(1)}, f32[128,128]{1,0:T(8,128)S(1)}, u32[]{:S(2)}, u32[]{:S(2)}) collective-permute-start(f32[128,128]{1,0:T(8,128)S(1)} %get-tuple-element.112.a), channel_id=1, source_target_pairs={{0,64},{8,72},{16,80},{24,88},{32,96},{40,104},{48,112},{56,120},{... | collective-permute-start | bytes 196616 | tf_op jit(solution)/shard_map/ppermute | solution.py:318
  63.2 0.3 in_mask.1.mask_ref
  63.5 1.9 %collective-permute-done.14.got_ref = bf16[8,256,128]{2,1,0:T(8,128)(2,1)S(1)} collective-permute-done((bf16[8,256,128]{2,1,0:T(8,128)(2,1)S(1)}, bf16[8,256,128]{2,1,0:T(8,128)(2,1)S(1)}, u32[]{:S(2)}, u32[]{:S(2)}) %collective-permute-start.14) | collective-permute-done | bytes 524320 | tf_op jit(solution)/shard_map/ppermute | solution.py:318
  65.5 0.1 gather_q.1
  65.6 0.6 collective-permute-done.15.b
  66.2 1.4 %collective-permute-start.19 = (f32[128,128]{1,0:T(8,128)S(1)}, f32[128,128]{1,0:T(8,128)S(1)}, u32[]{:S(2)}, u32[]{:S(2)}) collective-permute-start(f32[128,128]{1,0:T(8,128)S(1)} %add_two.1.own), channel_id=1, source_target_pairs={{0,2},{1,3},{2,0},{3,1},{4,6},{5,7},{6,4},{7,5},{8,10},{9,11},{10,... | collective-permute-start | bytes 196616 | tf_op jit(solution)/shard_map/ppermute | solution.py:315
  67.6 1.7 %collective-permute-start.13 = (bf16[2,256,128]{2,1,0:T(8,128)(2,1)S(1)}, bf16[2,256,128]{2,1,0:T(8,128)(2,1)S(1)}, u32[]{:S(2)}, u32[]{:S(2)}) collective-permute-start(bf16[2,256,128]{2,1,0:T(8,128)(2,1)S(1)} %get-tuple-element.102), channel_id=1, source_target_pairs={{0,64},{8,72},{16,80},{24,88},{32,96},{40,104},{48,112},{56,120},{... | collective-permute-start | bytes 393224 | tf_op jit(solution)/shard_map/ppermute | solution.py:318
  69.4 0.5 collective-permute-start.16
  69.9 2.4 %collective-permute-start.17 = (bf16[2,256,128]{2,1,0:T(8,128)(2,1)S(1)}, bf16[2,256,128]{2,1,0:T(8,128)(2,1)S(1)}, u32[]{:S(2)}, u32[]{:S(2)}) collective-permute-start(bf16[2,256,128]{2,1,0:T(8,128)(2,1)S(1)} %get-tuple-element.109), channel_id=1, source_target_pairs={{0,32},{8,40},{16,48},{24,56},{32,0},{40,8},{48,16},{56,24},{64,96... | collective-permute-start | bytes 393224 | tf_op jit(solution)/shard_map/ppermute | solution.py:312
  72.3 1.8 %collective-permute-start.18 = (bf16[2,256,128]{2,1,0:T(8,128)(2,1)S(1)}, bf16[2,256,128]{2,1,0:T(8,128)(2,1)S(1)}, u32[]{:S(2)}, u32[]{:S(2)}) collective-permute-start(bf16[2,256,128]{2,1,0:T(8,128)(2,1)S(1)} %get-tuple-element.110), channel_id=1, source_target_pairs={{0,48},{8,56},{16,0},{24,8},{32,16},{40,24},{48,32},{56,40},{64,11... | collective-permute-start | bytes 393224 | tf_op jit(solution)/shard_map/ppermute | solution.py:312
  74.1 3.1 %collective-permute-start.20 = (f32[2,128,128]{2,1,0:T(8,128)S(1)}, f32[2,128,128]{2,1,0:T(8,128)S(1)}, u32[]{:S(2)}, u32[]{:S(2)}) collective-permute-start(f32[2,128,128]{2,1,0:T(8,128)S(1)} %pair_up.1.w), channel_id=1, source_target_pairs={{0,4},{1,5},{2,6},{3,7},{4,0},{5,1},{6,2},{7,3},{8,12},{9,13},{10,... | collective-permute-start | bytes 393224 | tf_op jit(solution)/shard_map/ppermute | solution.py:315
  77.2 0.9 %collective-permute-done.16.g1 = bf16[2,256,128]{2,1,0:T(8,128)(2,1)S(1)} collective-permute-done((bf16[2,256,128]{2,1,0:T(8,128)(2,1)S(1)}, bf16[2,256,128]{2,1,0:T(8,128)(2,1)S(1)}, u32[]{:S(2)}, u32[]{:S(2)}) %collective-permute-start.16) | collective-permute-done | bytes 131104 | tf_op jit(solution)/shard_map/ppermute | solution.py:312
  78.1 0.5 collective-permute-done.18.g3
  78.6 2.1 %collective-permute-done.20.w_got = f32[2,128,128]{2,1,0:T(8,128)S(1)} collective-permute-done((f32[2,128,128]{2,1,0:T(8,128)S(1)}, f32[2,128,128]{2,1,0:T(8,128)S(1)}, u32[]{:S(2)}, u32[]{:S(2)}) %collective-permute-start.20) | collective-permute-done | bytes 131104 | tf_op jit(solution)/shard_map/ppermute | solution.py:315
  80.7 0.9 %finish.1 = (bf16[512,256]{1,0:T(8,128)(2,1)}, f32[256,256]{1,0:T(8,128)}) custom-call(f32[2,256,128]{2,1,0:T(8,128)S(1)} %get-tuple-element.101.p_keep, bf16[2,256,128]{2,1,0:T(8,128)(2,1)S(1)} %collective-permute-done.13.p_got, f32[2,256,128]{2,1,0:T(8,128)S(1)} %get-tuple-element.107.q_keep, bf16[2,256,128]{2,1,0:T(8,128)(2,1)S(1)} %collective-permute-done.16.g1, ...), custom_call_target="tpu_custom_call" | custom-call | flops 1000000 | tf_op jit(solution)/shard_map/finish/pallas_call | solution.py:425
  (20 shorter events, 0.1 us)
Async XLA Ops:
  3.2 11.3 %collective-permute-start.1 = (bf16[640,128]{1,0:T(8,128)(2,1)}, bf16[640,128]{1,0:T(8,128)(2,1)S(1)}, u32[]{:S(2)}, u32[]{:S(2)}) collective-permute-start(bf16[640,128]{1,0:T(8,128)(2,1)} %get-tuple-element.62), channel_id=1, source_target_pairs={{0,6},{1,7},{2,0},{3,1},{4,2},{5,3},{6,4},{7,5},{8,14},{9,15},{10,... | collective-permute-start | bytes 491528 | tf_op jit(solution)/shard_map/ppermute | solution.py:306
  6.1 8.9 %collective-permute-start.2 = (bf16[640,128]{1,0:T(8,128)(2,1)}, bf16[640,128]{1,0:T(8,128)(2,1)S(1)}, u32[]{:S(2)}, u32[]{:S(2)}) collective-permute-start(bf16[640,128]{1,0:T(8,128)(2,1)} %get-tuple-element.63), channel_id=1, source_target_pairs={{0,4},{1,5},{2,6},{3,7},{4,0},{5,1},{6,2},{7,3},{8,12},{9,13},{10,... | collective-permute-start | bytes 491528 | tf_op jit(solution)/shard_map/ppermute | solution.py:306
  6.9 10.1 %collective-permute-start.3 = (bf16[640,128]{1,0:T(8,128)(2,1)}, bf16[640,128]{1,0:T(8,128)(2,1)S(1)}, u32[]{:S(2)}, u32[]{:S(2)}) collective-permute-start(bf16[640,128]{1,0:T(8,128)(2,1)} %get-tuple-element.64), channel_id=1, source_target_pairs={{0,2},{1,3},{2,4},{3,5},{4,6},{5,7},{6,0},{7,1},{8,10},{9,11},{10,... | collective-permute-start | bytes 491528 | tf_op jit(solution)/shard_map/ppermute | solution.py:306
  7.8 6.7 %collective-permute-start = (bf16[2,256,128]{2,1,0:T(8,128)(2,1)}, bf16[2,256,128]{2,1,0:T(8,128)(2,1)S(1)}, u32[]{:S(2)}, u32[]{:S(2)}) collective-permute-start(bf16[2,256,128]{2,1,0:T(8,128)(2,1)} %get-tuple-element.69.ha), channel_id=1, source_target_pairs={{0,1},{1,0},{2,3},{3,2},{4,5},{5,4},{6,7},{7,6},{8,9},{9,8},{10,11... | collective-permute-start | bytes 393224 | tf_op jit(solution)/shard_map/ppermute | solution.py:309
  11.6 5.4 %copy-start = (bf16[2,256,128]{2,1,0:T(8,128)(2,1)S(1)}, bf16[2,256,128]{2,1,0:T(8,128)(2,1)}, u32[]{:S(2)}) copy-start(bf16[2,256,128]{2,1,0:T(8,128)(2,1)} %get-tuple-element.69.ha) | copy-start | bytes 393220
  11.6 5.4 %copy-start.1 = (bf16[2,256,128]{2,1,0:T(8,128)(2,1)S(1)}, bf16[2,256,128]{2,1,0:T(8,128)(2,1)}, u32[]{:S(2)}) copy-start(bf16[2,256,128]{2,1,0:T(8,128)(2,1)} %get-tuple-element.71.hb) | copy-start | bytes 393220
  11.6 5.3 %copy-start.2 = (f32[128,128]{1,0:T(8,128)S(1)}, f32[128,128]{1,0:T(8,128)}, u32[]{:S(2)}) copy-start(f32[128,128]{1,0:T(8,128)} %get-tuple-element.75.keep) | copy-start | bytes 196612
  11.6 12.1 %copy-start.4 = (s32[1,1,512,2]{2,3,1,0:T(2,128)S(1)}, s32[1,1,512,2]{2,3,1,0:T(2,128)}, u32[]{:S(2)}) copy-start(s32[1,1,512,2]{2,3,1,0:T(2,128)} %param.13) | copy-start | bytes 12292
  17.1 18.7 %collective-permute-start.7 = (bf16[9,256,128]{2,1,0:T(8,128)(2,1)S(1)}, bf16[9,256,128]{2,1,0:T(8,128)(2,1)S(1)}, u32[]{:S(2)}, u32[]{:S(2)}) collective-permute-start(bf16[9,256,128]{2,1,0:T(8,128)(2,1)S(1)} %get-tuple-element.83.b0), channel_id=1, source_target_pairs={{0,1},{1,0},{2,3},{3,2},{4,5},{5,4},{6,7},{7,6},{8,9},{9,8},{10,11... | collective-permute-start | bytes 1769480 | tf_op jit(solution)/shard_map/ppermute | solution.py:309
  20.3 14.8 %collective-permute-start.6 = (bf16[4,256,128]{2,1,0:T(8,128)(2,1)S(1)}, bf16[4,256,128]{2,1,0:T(8,128)(2,1)S(1)}, u32[]{:S(2)}, u32[]{:S(2)}) collective-permute-start(bf16[4,256,128]{2,1,0:T(8,128)(2,1)S(1)} %get-tuple-element.79.a0), channel_id=1, source_target_pairs={{0,2},{1,3},{2,4},{3,5},{4,6},{5,7},{6,0},{7,1},{8,10},{9,11},{10,... | collective-permute-start | bytes 786440 | tf_op jit(solution)/shard_map/ppermute | solution.py:306
  20.3 14.8 %collective-permute-start.5 = (bf16[4,256,128]{2,1,0:T(8,128)(2,1)S(1)}, bf16[4,256,128]{2,1,0:T(8,128)(2,1)S(1)}, u32[]{:S(2)}, u32[]{:S(2)}) collective-permute-start(bf16[4,256,128]{2,1,0:T(8,128)(2,1)S(1)} %get-tuple-element.79.a0), channel_id=1, source_target_pairs={{0,4},{1,5},{2,6},{3,7},{4,0},{5,1},{6,2},{7,3},{8,12},{9,13},{10,... | collective-permute-start | bytes 786440 | tf_op jit(solution)/shard_map/ppermute | solution.py:306
  22.4 13.3 %collective-permute-start.4 = (bf16[4,256,128]{2,1,0:T(8,128)(2,1)S(1)}, bf16[4,256,128]{2,1,0:T(8,128)(2,1)S(1)}, u32[]{:S(2)}, u32[]{:S(2)}) collective-permute-start(bf16[4,256,128]{2,1,0:T(8,128)(2,1)S(1)} %get-tuple-element.79.a0), channel_id=1, source_target_pairs={{0,6},{1,7},{2,0},{3,1},{4,2},{5,3},{6,4},{7,5},{8,14},{9,15},{10,... | collective-permute-start | bytes 786440 | tf_op jit(solution)/shard_map/ppermute | solution.py:306
  38.8 2.8 %collective-permute-start.8 = (bf16[17,256,128]{2,1,0:T(8,128)(2,1)S(1)}, bf16[17,256,128]{2,1,0:T(8,128)(2,1)S(1)}, u32[]{:S(2)}, u32[]{:S(2)}) collective-permute-start(bf16[17,256,128]{2,1,0:T(8,128)(2,1)S(1)} %get-tuple-element.87.sent_ref), channel_id=1, source_target_pairs={{0,8},{8,0},{16,24},{24,16},{32,40},{40,32},{48,56},{56,48},{64,72... | collective-permute-start | bytes 3342344 | tf_op jit(solution)/shard_map/ppermute | solution.py:321
  38.9 9.7 %collective-permute-start.9 = (bf16[16,256,128]{2,1,0:T(8,128)(2,1)S(1)}, bf16[16,256,128]{2,1,0:T(8,128)(2,1)S(1)}, u32[]{:S(2)}, u32[]{:S(2)}) collective-permute-start(bf16[16,256,128]{2,1,0:T(8,128)(2,1)S(1)} %get-tuple-element.89), channel_id=1, source_target_pairs={{0,8},{8,0},{16,24},{24,16},{32,40},{40,32},{48,56},{56,48},{64,72... | collective-permute-start | bytes 3145736 | tf_op jit(solution)/shard_map/ppermute | solution.py:321
  41.8 11.5 %collective-permute-start.11 = (bf16[1152,128]{1,0:T(8,128)(2,1)S(1)}, bf16[1152,128]{1,0:T(8,128)(2,1)S(1)}, u32[]{:S(2)}, u32[]{:S(2)}) collective-permute-start(bf16[1152,128]{1,0:T(8,128)(2,1)S(1)} %get-tuple-element.97), channel_id=1, source_target_pairs={{0,32},{8,40},{16,48},{24,56},{32,0},{40,8},{48,16},{56,24},{64,96... | collective-permute-start | bytes 884744 | tf_op jit(solution)/shard_map/ppermute | solution.py:312
  46.1 15.5 %collective-permute-start.12 = (bf16[1152,128]{1,0:T(8,128)(2,1)S(1)}, bf16[1152,128]{1,0:T(8,128)(2,1)S(1)}, u32[]{:S(2)}, u32[]{:S(2)}) collective-permute-start(bf16[1152,128]{1,0:T(8,128)(2,1)S(1)} %get-tuple-element.98), channel_id=1, source_target_pairs={{0,48},{8,56},{16,0},{24,8},{32,16},{40,24},{48,32},{56,40},{64,11... | collective-permute-start | bytes 884744 | tf_op jit(solution)/shard_map/ppermute | solution.py:312
  47.8 13.8 %collective-permute-start.10 = (bf16[1152,128]{1,0:T(8,128)(2,1)S(1)}, bf16[1152,128]{1,0:T(8,128)(2,1)S(1)}, u32[]{:S(2)}, u32[]{:S(2)}) collective-permute-start(bf16[1152,128]{1,0:T(8,128)(2,1)S(1)} %get-tuple-element.96.sent_ref), channel_id=1, source_target_pairs={{0,16},{8,24},{16,32},{24,40},{32,48},{40,56},{48,0},{56,8},{64,80... | collective-permute-start | bytes 884744 | tf_op jit(solution)/shard_map/ppermute | solution.py:312
  50.7 12.5 %copy-start.3 = (s32[512,16]{0,1:T(8,128)S(1)}, s32[512,16]{0,1:T(8,128)}, u32[]{:S(2)}) copy-start(s32[512,16]{0,1:T(8,128)} %param.15) | copy-start | bytes 98308
  50.7 14.8 %collective-permute-start.14 = (bf16[8,256,128]{2,1,0:T(8,128)(2,1)S(1)}, bf16[8,256,128]{2,1,0:T(8,128)(2,1)S(1)}, u32[]{:S(2)}, u32[]{:S(2)}) collective-permute-start(bf16[8,256,128]{2,1,0:T(8,128)(2,1)S(1)} %get-tuple-element.104), channel_id=1, source_target_pairs={{0,64},{8,72},{16,80},{24,88},{32,96},{40,104},{48,112},{56,120},{... | collective-permute-start | bytes 1572872 | tf_op jit(solution)/shard_map/ppermute | solution.py:318
  61.8 4.4 %collective-permute-start.15 = (f32[128,128]{1,0:T(8,128)S(1)}, f32[128,128]{1,0:T(8,128)S(1)}, u32[]{:S(2)}, u32[]{:S(2)}) collective-permute-start(f32[128,128]{1,0:T(8,128)S(1)} %get-tuple-element.112.a), channel_id=1, source_target_pairs={{0,64},{8,72},{16,80},{24,88},{32,96},{40,104},{48,112},{56,120},{... | collective-permute-start | bytes 196616 | tf_op jit(solution)/shard_map/ppermute | solution.py:318
  66.2 7.9 %collective-permute-start.19 = (f32[128,128]{1,0:T(8,128)S(1)}, f32[128,128]{1,0:T(8,128)S(1)}, u32[]{:S(2)}, u32[]{:S(2)}) collective-permute-start(f32[128,128]{1,0:T(8,128)S(1)} %add_two.1.own), channel_id=1, source_target_pairs={{0,2},{1,3},{2,0},{3,1},{4,6},{5,7},{6,4},{7,5},{8,10},{9,11},{10,... | collective-permute-start | bytes 196616 | tf_op jit(solution)/shard_map/ppermute | solution.py:315
  67.6 9.6 %collective-permute-start.13 = (bf16[2,256,128]{2,1,0:T(8,128)(2,1)S(1)}, bf16[2,256,128]{2,1,0:T(8,128)(2,1)S(1)}, u32[]{:S(2)}, u32[]{:S(2)}) collective-permute-start(bf16[2,256,128]{2,1,0:T(8,128)(2,1)S(1)} %get-tuple-element.102), channel_id=1, source_target_pairs={{0,64},{8,72},{16,80},{24,88},{32,96},{40,104},{48,112},{56,120},{... | collective-permute-start | bytes 393224 | tf_op jit(solution)/shard_map/ppermute | solution.py:318
  69.4 8.7 %collective-permute-start.16 = (bf16[2,256,128]{2,1,0:T(8,128)(2,1)S(1)}, bf16[2,256,128]{2,1,0:T(8,128)(2,1)S(1)}, u32[]{:S(2)}, u32[]{:S(2)}) collective-permute-start(bf16[2,256,128]{2,1,0:T(8,128)(2,1)S(1)} %get-tuple-element.108), channel_id=1, source_target_pairs={{0,16},{8,24},{16,32},{24,40},{32,48},{40,56},{48,0},{56,8},{64,80... | collective-permute-start | bytes 393224 | tf_op jit(solution)/shard_map/ppermute | solution.py:312
  69.9 8.2 %collective-permute-start.17 = (bf16[2,256,128]{2,1,0:T(8,128)(2,1)S(1)}, bf16[2,256,128]{2,1,0:T(8,128)(2,1)S(1)}, u32[]{:S(2)}, u32[]{:S(2)}) collective-permute-start(bf16[2,256,128]{2,1,0:T(8,128)(2,1)S(1)} %get-tuple-element.109), channel_id=1, source_target_pairs={{0,32},{8,40},{16,48},{24,56},{32,0},{40,8},{48,16},{56,24},{64,96... | collective-permute-start | bytes 393224 | tf_op jit(solution)/shard_map/ppermute | solution.py:312
  72.3 6.3 %collective-permute-start.18 = (bf16[2,256,128]{2,1,0:T(8,128)(2,1)S(1)}, bf16[2,256,128]{2,1,0:T(8,128)(2,1)S(1)}, u32[]{:S(2)}, u32[]{:S(2)}) collective-permute-start(bf16[2,256,128]{2,1,0:T(8,128)(2,1)S(1)} %get-tuple-element.110), channel_id=1, source_target_pairs={{0,48},{8,56},{16,0},{24,8},{32,16},{40,24},{48,32},{56,40},{64,11... | collective-permute-start | bytes 393224 | tf_op jit(solution)/shard_map/ppermute | solution.py:312
  74.1 6.6 %collective-permute-start.20 = (f32[2,128,128]{2,1,0:T(8,128)S(1)}, f32[2,128,128]{2,1,0:T(8,128)S(1)}, u32[]{:S(2)}, u32[]{:S(2)}) collective-permute-start(f32[2,128,128]{2,1,0:T(8,128)S(1)} %pair_up.1.w), channel_id=1, source_target_pairs={{0,4},{1,5},{2,6},{3,7},{4,0},{5,1},{6,2},{7,3},{8,12},{9,13},{10,... | collective-permute-start | bytes 393224 | tf_op jit(solution)/shard_map/ppermute | solution.py:315

commit v8 on v5

--- a/solution.py
+++ b/solution.py
@@ -102,14 +102,17 @@
     b0[8] = both_parts(total)
 
 
-def add_two(a, b, out):
-    out[...] = a[...] + b[...]
-
-
-def pair_up(own, got, out):
+def pair_up(y, own, got, message):
     odd = (lax.axis_index("col") >> 1) & 1
-    out[odd] = own[...]
-    out[1 - odd] = got[...]
+    message[0:2] = y[...]
+    message[2, pl.ds(pl.multiple_of(odd * T, T), T)] = own[...].astype(bf16)
+    message[2, pl.ds(pl.multiple_of((1 - odd) * T, T), T)] = got[...].astype(bf16)
+
+
+def sum_pair(own, got, out):
+    for i in range(2):
+        rows = slice(i * T, (i + 1) * T)
+        out[i] = own[2, rows].astype(f32) + got[2, rows].astype(f32)
 
 
 def in_mask(words_ref, out_ref):
@@ -412,14 +415,15 @@
     p_keep, p_y, w = call(
         gather_p, [(half, f32), (half, bf16), (square, f32)], [VMEM] * 5, "gather_p", flops=10**10, touched=2**25
     )(p_keep, *p_all, p_z[0])
-    p_got, w_got = over_y_lo(p_y), over_y_lo(w)
+    w_got = swap_x(w, 0)
     q_keep, p_keep, mask = tie(q_keep, p_keep, mask)
     q_keep, *q_z = call(gather_q, [(half, f32)] + [(half, bf16)] * 3, [VMEM] * 2, "gather_q", flops=10**6)(
         q_keep, q_got
     )
+    (p_y,) = call(pair_up, [((3, 256, T), bf16)], [VMEM] * 3, "pair_up", limit=4)(p_y, w, w_got)
+    p_got = over_y_lo(p_y)
     q_all = around_z(*q_z)
-    (w,) = call(add_two, [(square, f32)], [VMEM] * 2, "add_two", limit=2)(w, w_got)
-    (w,) = call(pair_up, [((2, T, T), f32)], [VMEM] * 2, "pair_up", limit=2)(w, swap_x(w, 0))
+    (w,) = call(sum_pair, [((2, T, T), f32)], [VMEM] * 2, "sum_pair", limit=4)(p_y, p_got)
     w_got = swap_x(w, 1)
     prev_grad, weight_grad = call(
         finish, [((512, 256), bf16), ((256, 256), f32)], [VMEM] * 9, "finish", flops=10**6

time: 83.5 us -> 80.7 us (0.966)
  Pallas kernels: 21.9 us -> 28.6 us
  starting transfers between devices: 33.2 us -> 27.3 us
  waiting for transfers between devices: 27.1 us -> 23.2 us
    ppermute x2, waiting for transfers between devices: 2.02 us -> 7.62 us  [swap_x(): return lax.ppermute(v, 'col', [(c, c ^ 2 << bit) for c in range(8)])]
    ppermute x3 -> x2, waiting for transfers between devices: 4.89 us -> 0.01 us  [over_y_lo(): return lax.ppermute(v, 'row', [(r, r ^ 8) for r in range(16)])]
    ppermute x2, starting transfers between devices: 5.11 us -> 0.84 us  [swap_x(): return lax.ppermute(v, 'col', [(c, c ^ 2 << bit) for c in range(8)])]
    ppermute x6, waiting for transfers between devices: 8.7 us -> 5 us  [over_x(): lax.ppermute(v, 'col', [(c, ((c >> 1) + s & 3) * 2 + (c & 1)) for c in ra...]
    pallas_call x1, Pallas kernels: 3.01 us -> 5.4 us  [shards(): call(stage, [(own_tiles.shape, bf16)], [SMEM, ANY], 'stage', limit=STAGE_...]
    pallas_call x1, Pallas kernels: 3.78 us -> 5.21 us  [shards(): call(late_partner, [((17, 256, T), bf16), (sixteen, bf16), ((33, 256, T),...]
    pallas_call x2, Pallas kernels: 5.2 us -> 6.63 us  [own_columns(): call(functools.partial(late_own, number), [(sixteen, f32)], [SMEM] + [VME...]
    pallas_call x1, Pallas kernels: 4.37 us -> 5.79 us  [shards(): call(early, [((65, 256, T), f32)], [SMEM] + [VMEM] * 3, 'early', limit=LI...]
  transfers between devices with their start and end apart: 21 -> 20, of which waited for: 10 -> 9; matrix products, arithmetic and copies ran while one was open for 0% -> 0% of each run, Pallas kernels for 17% -> 25%
where the time goes in v8:
time: 80.7 us
  Pallas kernels  28.6 us (35%)
  starting transfers between devices  27.3 us (34%)
  waiting for transfers between devices  23.2 us (29%)
  between operations  1.52 us (2%)
    ppermute x6, waiting for transfers between devices, over_z(): lax.ppermute(v, 'row', [(r, r & 9 | ((r >> 1) + s & 3) << 1) for r in ran...  10.5 us
    ppermute x6, starting transfers between devices, over_z(): lax.ppermute(v, 'row', [(r, r & 9 | ((r >> 1) + s & 3) << 1) for r in ran...  10.5 us
    ppermute x6, starting transfers between devices, over_x(): lax.ppermute(v, 'col', [(c, ((c >> 1) + s & 3) * 2 + (c & 1)) for c in ra...  8.03 us
    ppermute x2, waiting for transfers between devices, swap_x(): return lax.ppermute(v, 'col', [(c, c ^ 2 << bit) for c in range(8)])  7.62 us
    pallas_call x2, Pallas kernels, own_columns(): call(functools.partial(late_own, number), [(sixteen, f32)], [SMEM] + [VME...  6.63 us
    ppermute x2, starting transfers between devices, over_y_hi(): return lax.ppermute(v, 'col', [(c, c ^ 1) for c in range(8)])  6.31 us
    pallas_call x1, Pallas kernels, shards(): call(early, [((65, 256, T), f32)], [SMEM] + [VMEM] * 3, 'early', limit=LI...  5.79 us
    pallas_call x1, Pallas kernels, shards(): call(stage, [(own_tiles.shape, bf16)], [SMEM, ANY], 'stage', limit=STAGE_...  5.4 us
  transfers between devices with their start and end apart: 20, of which 9 were waited for; matrix products, arithmetic and copies ran while one was open for 0% of the time, Pallas kernels for 25%

profile of v8, /device:TPU:0, one launch (start us, length us, event | category | flops | bytes accessed | tf_op | source)
XLA Modules:
  0.0 80.7 jit_solution(9049446405582466280)
XLA Ops:
  0.6 2.5 %prep.1 = (bf16[2,256,128]{2,1,0:T(8,128)(2,1)}, bf16[2,256,128]{2,1,0:T(8,128)(2,1)}, bf16[640,128]{1,0:T(8,128)(2,1)}, bf16[640,128]{1,0:T(8,128)(2,1)}, bf16[640,128]{1,0:T(8,128)(2,1)}, /*index=5*/f32[128,128]{1,0:T(8,128)}) custom-call(bf16[512,256]{1,0:T(8,128)(2,1)} %grad_hbm.1, s32[16,512]{1,0:T(8,128)} %bitcast.12, bf16[512,256]{1,0:T(8,128)(2,1)} %agg_hbm.1, ...), custom_call_target="tpu_custom_call" | custom-call | flops 200000000 | tf_op jit(solution)/shard_map/prep/pallas_call | solution.py:327
  3.2 2.9 %collective-permute-start.1 = (bf16[640,128]{1,0:T(8,128)(2,1)}, bf16[640,128]{1,0:T(8,128)(2,1)S(1)}, u32[]{:S(2)}, u32[]{:S(2)}) collective-permute-start(bf16[640,128]{1,0:T(8,128)(2,1)} %get-tuple-element.59), channel_id=1, source_target_pairs={{0,6},{1,7},{2,0},{3,1},{4,2},{5,3},{6,4},{7,5},{8,14},{9,15},{10,... | collective-permute-start | bytes 491528 | tf_op jit(solution)/shard_map/ppermute | solution.py:309
  6.1 0.8 collective-permute-start.2
  6.9 0.9 %collective-permute-start.3 = (bf16[640,128]{1,0:T(8,128)(2,1)}, bf16[640,128]{1,0:T(8,128)(2,1)S(1)}, u32[]{:S(2)}, u32[]{:S(2)}) collective-permute-start(bf16[640,128]{1,0:T(8,128)(2,1)} %get-tuple-element.61), channel_id=1, source_target_pairs={{0,2},{1,3},{2,4},{3,5},{4,6},{5,7},{6,0},{7,1},{8,10},{9,11},{10,... | collective-permute-start | bytes 491528 | tf_op jit(solution)/shard_map/ppermute | solution.py:309
  7.8 3.2 %collective-permute-start = (bf16[2,256,128]{2,1,0:T(8,128)(2,1)}, bf16[2,256,128]{2,1,0:T(8,128)(2,1)S(1)}, u32[]{:S(2)}, u32[]{:S(2)}) collective-permute-start(bf16[2,256,128]{2,1,0:T(8,128)(2,1)} %get-tuple-element.66.ha), channel_id=1, source_target_pairs={{0,1},{1,0},{2,3},{3,2},{4,5},{5,4},{6,7},{7,6},{8,9},{9,8},{10,11... | collective-permute-start | bytes 393224 | tf_op jit(solution)/shard_map/ppermute | solution.py:312
  11.7 0.0 copy-start.4
  11.7 5.4 %stage.1.tiles_ref = bf16[512,128,128]{2,1,0:T(8,128)(2,1)S(1)} custom-call(s32[1]{0:T(128)} %bitcast.7.count_ref, bf16[512,128,128]{2,1,0:T(8,128)(2,1)} %bitcast.11), custom_call_target="tpu_custom_call" | custom-call | flops 1000000000 | tf_op jit(solution)/shard_map/stage/pallas_call | solution.py:347
  17.1 0.0 collective-permute-done.ha_y
  17.1 0.0 collective-permute-done.2.m2
  17.1 0.0 collective-permute-done.3.m3
  17.1 0.1 pack.1
  17.2 3.1 %collective-permute-start.7 = (bf16[9,256,128]{2,1,0:T(8,128)(2,1)S(1)}, bf16[9,256,128]{2,1,0:T(8,128)(2,1)S(1)}, u32[]{:S(2)}, u32[]{:S(2)}) collective-permute-start(bf16[9,256,128]{2,1,0:T(8,128)(2,1)S(1)} %get-tuple-element.80.b0), channel_id=1, source_target_pairs={{0,1},{1,0},{2,3},{3,2},{4,5},{5,4},{6,7},{7,6},{8,9},{9,8},{10,11... | collective-permute-start | bytes 1769480 | tf_op jit(solution)/shard_map/ppermute | solution.py:312
  20.4 0.0 collective-permute-start.6
  20.4 2.1 %collective-permute-start.5 = (bf16[4,256,128]{2,1,0:T(8,128)(2,1)S(1)}, bf16[4,256,128]{2,1,0:T(8,128)(2,1)S(1)}, u32[]{:S(2)}, u32[]{:S(2)}) collective-permute-start(bf16[4,256,128]{2,1,0:T(8,128)(2,1)S(1)} %get-tuple-element.76.a0), channel_id=1, source_target_pairs={{0,4},{1,5},{2,6},{3,7},{4,0},{5,1},{6,2},{7,3},{8,12},{9,13},{10,... | collective-permute-start | bytes 786440 | tf_op jit(solution)/shard_map/ppermute | solution.py:309
  22.4 1.4 %collective-permute-start.4 = (bf16[4,256,128]{2,1,0:T(8,128)(2,1)S(1)}, bf16[4,256,128]{2,1,0:T(8,128)(2,1)S(1)}, u32[]{:S(2)}, u32[]{:S(2)}) collective-permute-start(bf16[4,256,128]{2,1,0:T(8,128)(2,1)S(1)} %get-tuple-element.76.a0), channel_id=1, source_target_pairs={{0,6},{1,7},{2,0},{3,1},{4,2},{5,3},{6,4},{7,5},{8,14},{9,15},{10,... | collective-permute-start | bytes 786440 | tf_op jit(solution)/shard_map/ppermute | solution.py:309
  23.8 1.2 %order_slots.1.steps_ref = s32[8,512]{1,0:T(8,128)S(1)} custom-call(s32[1]{0:T(128)} %bitcast.8.count_ref, s32[2,512]{1,0:T(2,128)S(1)} %bitcast.10), custom_call_target="tpu_custom_call" | custom-call | flops 10000000 | tf_op jit(solution)/shard_map/order_slots/pallas_call | solution.py:365
  25.0 5.8 %early.1.so_far_ref = f32[65,256,128]{2,1,0:T(8,128)S(1)} custom-call(s32[8,512]{1,0:T(8,128)S(1)} %order_slots.1.steps_ref, bf16[4,256,128]{2,1,0:T(8,128)(2,1)S(1)} %get-tuple-element.76.a0, bf16[9,256,128]{2,1,0:T(8,128)(2,1)S(1)} %get-tuple-element.80.b0, bf16[512,128,128]{2,1,0:T(8,128)(2,1)S(1)} %stage.1.tiles_ref), custom_call_target="tpu_custom_call" | custom-call | flops 4000000000 | tf_op jit(solution)/shard_map/early/pallas_call | solution.py:366
  30.8 4.4 %collective-permute-done.6.a3 = bf16[4,256,128]{2,1,0:T(8,128)(2,1)S(1)} collective-permute-done((bf16[4,256,128]{2,1,0:T(8,128)(2,1)S(1)}, bf16[4,256,128]{2,1,0:T(8,128)(2,1)S(1)}, u32[]{:S(2)}, u32[]{:S(2)}) %collective-permute-start.6) | collective-permute-done | bytes 262176 | tf_op jit(solution)/shard_map/ppermute | solution.py:309
  35.1 0.6 collective-permute-done.4.a1
  35.8 5.2 %late_1.1 = (bf16[17,256,128]{2,1,0:T(8,128)(2,1)S(1)}, bf16[16,256,128]{2,1,0:T(8,128)(2,1)S(1)}, bf16[33,256,128]{2,1,0:T(8,128)(2,1)S(1)}) custom-call(s32[8,512]{1,0:T(8,128)S(1)} %order_slots.1.steps_ref, bf16[4,256,128]{2,1,0:T(8,128)(2,1)S(1)} %get-tuple-element.76.a0, bf16[4,256,128]{2,1,0:T(8,128)(2,1)S(1)} %collective-permute-done.6.a3, ...), custom_call_target="tpu_custom_call" | custom-call | flops 4000000000 | tf_op jit(solution)/shard_map/late_1/pallas_call | solution.py:394
  41.0 0.1 collective-permute-start.8
  41.1 0.5 collective-permute-start.9
  41.6 3.3 %late_2.1.acc_ref = f32[16,256,128]{2,1,0:T(8,128)S(1)} custom-call(s32[8,512]{1,0:T(8,128)S(1)} %order_slots.1.steps_ref, bf16[33,256,128]{2,1,0:T(8,128)(2,1)S(1)} %get-tuple-element.88.h_ref, bf16[512,128,128]{2,1,0:T(8,128)(2,1)S(1)} %stage.1.tiles_ref, f32[65,256,128]{2,1,0:T(8,128)S(1)} %early.1.so_far_ref), custom_call_target="tpu_custom_call" | custom-call | flops 2000000000 | tf_op jit(solution)/shard_map/late_2/pallas_call | solution.py:381
  44.9 0.2 split_p.1
  45.1 2.5 %collective-permute-start.11 = (bf16[1152,128]{1,0:T(8,128)(2,1)S(1)}, bf16[1152,128]{1,0:T(8,128)(2,1)S(1)}, u32[]{:S(2)}, u32[]{:S(2)}) collective-permute-start(bf16[1152,128]{1,0:T(8,128)(2,1)S(1)} %get-tuple-element.94), channel_id=1, source_target_pairs={{0,32},{8,40},{16,48},{24,56},{32,0},{40,8},{48,16},{56,24},{64,96... | collective-permute-start | bytes 884744 | tf_op jit(solution)/shard_map/ppermute | solution.py:315
  47.6 0.2 collective-permute-start.12
  47.9 1.8 %collective-permute-start.10 = (bf16[1152,128]{1,0:T(8,128)(2,1)S(1)}, bf16[1152,128]{1,0:T(8,128)(2,1)S(1)}, u32[]{:S(2)}, u32[]{:S(2)}) collective-permute-start(bf16[1152,128]{1,0:T(8,128)(2,1)S(1)} %get-tuple-element.93.sent_ref), channel_id=1, source_target_pairs={{0,16},{8,24},{16,32},{24,40},{32,48},{40,56},{48,0},{56,8},{64,80... | collective-permute-start | bytes 884744 | tf_op jit(solution)/shard_map/ppermute | solution.py:315
  49.6 3.3 %late_3.1.acc_ref = f32[16,256,128]{2,1,0:T(8,128)S(1)} custom-call(s32[8,512]{1,0:T(8,128)S(1)} %order_slots.1.steps_ref, bf16[33,256,128]{2,1,0:T(8,128)(2,1)S(1)} %get-tuple-element.88.h_ref, bf16[512,128,128]{2,1,0:T(8,128)(2,1)S(1)} %stage.1.tiles_ref, f32[65,256,128]{2,1,0:T(8,128)S(1)} %early.1.so_far_ref), custom_call_target="tpu_custom_call" | custom-call | flops 2000000000 | tf_op jit(solution)/shard_map/late_3/pallas_call | solution.py:381
  53.0 0.2 split_q.1
  53.1 0.0 copy-start.3
  53.1 0.8 collective-permute-start.15
  53.9 2.7 %collective-permute-done.11.g2 = bf16[1152,128]{1,0:T(8,128)(2,1)S(1)} collective-permute-done((bf16[1152,128]{1,0:T(8,128)(2,1)S(1)}, bf16[1152,128]{1,0:T(8,128)(2,1)S(1)}, u32[]{:S(2)}, u32[]{:S(2)}) %collective-permute-start.11) | collective-permute-done | bytes 294944 | tf_op jit(solution)/shard_map/ppermute | solution.py:315
  56.6 5.3 %collective-permute-done.12.g3 = bf16[1152,128]{1,0:T(8,128)(2,1)S(1)} collective-permute-done((bf16[1152,128]{1,0:T(8,128)(2,1)S(1)}, bf16[1152,128]{1,0:T(8,128)(2,1)S(1)}, u32[]{:S(2)}, u32[]{:S(2)}) %collective-permute-start.12) | collective-permute-done | bytes 294944 | tf_op jit(solution)/shard_map/ppermute | solution.py:315
  62.0 0.1 gather_p.1
  62.1 0.3 collective-permute-start.13
  62.4 4.0 %collective-permute-done.13.got = f32[128,128]{1,0:T(8,128)S(1)} collective-permute-done((f32[128,128]{1,0:T(8,128)S(1)}, f32[128,128]{1,0:T(8,128)S(1)}, u32[]{:S(2)}, u32[]{:S(2)}) %collective-permute-start.13) | collective-permute-done | bytes 65568 | tf_op jit(solution)/shard_map/ppermute | solution.py:318
  66.5 0.3 collective-permute-start.14
  66.8 0.3 in_mask.1.mask_ref
  67.1 0.1 gather_q.1
  67.2 1.8 %collective-permute-start.16 = (bf16[2,256,128]{2,1,0:T(8,128)(2,1)S(1)}, bf16[2,256,128]{2,1,0:T(8,128)(2,1)S(1)}, u32[]{:S(2)}, u32[]{:S(2)}) collective-permute-start(bf16[2,256,128]{2,1,0:T(8,128)(2,1)S(1)} %get-tuple-element.104), channel_id=1, source_target_pairs={{0,16},{8,24},{16,32},{24,40},{32,48},{40,56},{48,0},{56,8},{64,80... | collective-permute-start | bytes 393224 | tf_op jit(solution)/shard_map/ppermute | solution.py:315
  69.1 1.8 %collective-permute-start.17 = (bf16[2,256,128]{2,1,0:T(8,128)(2,1)S(1)}, bf16[2,256,128]{2,1,0:T(8,128)(2,1)S(1)}, u32[]{:S(2)}, u32[]{:S(2)}) collective-permute-start(bf16[2,256,128]{2,1,0:T(8,128)(2,1)S(1)} %get-tuple-element.105), channel_id=1, source_target_pairs={{0,32},{8,40},{16,48},{24,56},{32,0},{40,8},{48,16},{56,24},{64,96... | collective-permute-start | bytes 393224 | tf_op jit(solution)/shard_map/ppermute | solution.py:315
  70.9 2.2 %collective-permute-start.18 = (bf16[2,256,128]{2,1,0:T(8,128)(2,1)S(1)}, bf16[2,256,128]{2,1,0:T(8,128)(2,1)S(1)}, u32[]{:S(2)}, u32[]{:S(2)}) collective-permute-start(bf16[2,256,128]{2,1,0:T(8,128)(2,1)S(1)} %get-tuple-element.106), channel_id=1, source_target_pairs={{0,48},{8,56},{16,0},{24,8},{32,16},{40,24},{48,32},{56,40},{64,11... | collective-permute-start | bytes 393224 | tf_op jit(solution)/shard_map/ppermute | solution.py:315
  73.2 0.5 collective-permute-start.19
  73.7 0.7 collective-permute-done.16.g1
  74.4 1.4 %collective-permute-done.17.g2 = bf16[2,256,128]{2,1,0:T(8,128)(2,1)S(1)} collective-permute-done((bf16[2,256,128]{2,1,0:T(8,128)(2,1)S(1)}, bf16[2,256,128]{2,1,0:T(8,128)(2,1)S(1)}, u32[]{:S(2)}, u32[]{:S(2)}) %collective-permute-start.17) | collective-permute-done | bytes 131104 | tf_op jit(solution)/shard_map/ppermute | solution.py:315
  75.8 0.4 collective-permute-done.18.g3
  76.2 3.6 %collective-permute-done.19.w_got = f32[2,128,128]{2,1,0:T(8,128)S(1)} collective-permute-done((f32[2,128,128]{2,1,0:T(8,128)S(1)}, f32[2,128,128]{2,1,0:T(8,128)S(1)}, u32[]{:S(2)}, u32[]{:S(2)}) %collective-permute-start.19) | collective-permute-done | bytes 131104 | tf_op jit(solution)/shard_map/ppermute | solution.py:318
  79.8 0.9 %finish.1 = (bf16[512,256]{1,0:T(8,128)(2,1)}, f32[256,256]{1,0:T(8,128)}) custom-call(f32[2,256,128]{2,1,0:T(8,128)S(1)} %get-tuple-element.98.p_keep, bf16[3,256,128]{2,1,0:T(8,128)(2,1)S(1)} %collective-permute-done.14.got.p_got, f32[2,256,128]{2,1,0:T(8,128)S(1)} %get-tuple-element.103.q_keep, bf16[2,256,128]{2,1,0:T(8,128)(2,1)S(1)} %collective-permute-done.16.g1, ...), custom_call_target="tpu_custom_call" | custom-call | flops 1000000 | tf_op jit(solution)/shard_map/finish/pallas_call | solution.py:428
  (18 shorter events, 0.1 us)
Async XLA Ops:
  3.2 13.9 %collective-permute-start.1 = (bf16[640,128]{1,0:T(8,128)(2,1)}, bf16[640,128]{1,0:T(8,128)(2,1)S(1)}, u32[]{:S(2)}, u32[]{:S(2)}) collective-permute-start(bf16[640,128]{1,0:T(8,128)(2,1)} %get-tuple-element.59), channel_id=1, source_target_pairs={{0,6},{1,7},{2,0},{3,1},{4,2},{5,3},{6,4},{7,5},{8,14},{9,15},{10,... | collective-permute-start | bytes 491528 | tf_op jit(solution)/shard_map/ppermute | solution.py:309
  6.1 11.0 %collective-permute-start.2 = (bf16[640,128]{1,0:T(8,128)(2,1)}, bf16[640,128]{1,0:T(8,128)(2,1)S(1)}, u32[]{:S(2)}, u32[]{:S(2)}) collective-permute-start(bf16[640,128]{1,0:T(8,128)(2,1)} %get-tuple-element.60), channel_id=1, source_target_pairs={{0,4},{1,5},{2,6},{3,7},{4,0},{5,1},{6,2},{7,3},{8,12},{9,13},{10,... | collective-permute-start | bytes 491528 | tf_op jit(solution)/shard_map/ppermute | solution.py:309
  6.9 10.2 %collective-permute-start.3 = (bf16[640,128]{1,0:T(8,128)(2,1)}, bf16[640,128]{1,0:T(8,128)(2,1)S(1)}, u32[]{:S(2)}, u32[]{:S(2)}) collective-permute-start(bf16[640,128]{1,0:T(8,128)(2,1)} %get-tuple-element.61), channel_id=1, source_target_pairs={{0,2},{1,3},{2,4},{3,5},{4,6},{5,7},{6,0},{7,1},{8,10},{9,11},{10,... | collective-permute-start | bytes 491528 | tf_op jit(solution)/shard_map/ppermute | solution.py:309
  7.8 9.3 %collective-permute-start = (bf16[2,256,128]{2,1,0:T(8,128)(2,1)}, bf16[2,256,128]{2,1,0:T(8,128)(2,1)S(1)}, u32[]{:S(2)}, u32[]{:S(2)}) collective-permute-start(bf16[2,256,128]{2,1,0:T(8,128)(2,1)} %get-tuple-element.66.ha), channel_id=1, source_target_pairs={{0,1},{1,0},{2,3},{3,2},{4,5},{5,4},{6,7},{7,6},{8,9},{9,8},{10,11... | collective-permute-start | bytes 393224 | tf_op jit(solution)/shard_map/ppermute | solution.py:312
  11.6 5.5 %copy-start = (bf16[2,256,128]{2,1,0:T(8,128)(2,1)S(1)}, bf16[2,256,128]{2,1,0:T(8,128)(2,1)}, u32[]{:S(2)}) copy-start(bf16[2,256,128]{2,1,0:T(8,128)(2,1)} %get-tuple-element.66.ha) | copy-start | bytes 393220
  11.6 5.5 %copy-start.1 = (bf16[2,256,128]{2,1,0:T(8,128)(2,1)S(1)}, bf16[2,256,128]{2,1,0:T(8,128)(2,1)}, u32[]{:S(2)}) copy-start(bf16[2,256,128]{2,1,0:T(8,128)(2,1)} %get-tuple-element.68.hb) | copy-start | bytes 393220
  11.6 5.5 %copy-start.2 = (f32[128,128]{1,0:T(8,128)S(1)}, f32[128,128]{1,0:T(8,128)}, u32[]{:S(2)}) copy-start(f32[128,128]{1,0:T(8,128)} %get-tuple-element.72.keep) | copy-start | bytes 196612
  11.7 12.1 %copy-start.4 = (s32[1,1,512,2]{2,3,1,0:T(2,128)S(1)}, s32[1,1,512,2]{2,3,1,0:T(2,128)}, u32[]{:S(2)}) copy-start(s32[1,1,512,2]{2,3,1,0:T(2,128)} %param.13) | copy-start | bytes 12292
  17.2 18.5 %collective-permute-start.7 = (bf16[9,256,128]{2,1,0:T(8,128)(2,1)S(1)}, bf16[9,256,128]{2,1,0:T(8,128)(2,1)S(1)}, u32[]{:S(2)}, u32[]{:S(2)}) collective-permute-start(bf16[9,256,128]{2,1,0:T(8,128)(2,1)S(1)} %get-tuple-element.80.b0), channel_id=1, source_target_pairs={{0,1},{1,0},{2,3},{3,2},{4,5},{5,4},{6,7},{7,6},{8,9},{9,8},{10,11... | collective-permute-start | bytes 1769480 | tf_op jit(solution)/shard_map/ppermute | solution.py:312
  20.4 14.8 %collective-permute-start.6 = (bf16[4,256,128]{2,1,0:T(8,128)(2,1)S(1)}, bf16[4,256,128]{2,1,0:T(8,128)(2,1)S(1)}, u32[]{:S(2)}, u32[]{:S(2)}) collective-permute-start(bf16[4,256,128]{2,1,0:T(8,128)(2,1)S(1)} %get-tuple-element.76.a0), channel_id=1, source_target_pairs={{0,2},{1,3},{2,4},{3,5},{4,6},{5,7},{6,0},{7,1},{8,10},{9,11},{10,... | collective-permute-start | bytes 786440 | tf_op jit(solution)/shard_map/ppermute | solution.py:309
  20.4 14.8 %collective-permute-start.5 = (bf16[4,256,128]{2,1,0:T(8,128)(2,1)S(1)}, bf16[4,256,128]{2,1,0:T(8,128)(2,1)S(1)}, u32[]{:S(2)}, u32[]{:S(2)}) collective-permute-start(bf16[4,256,128]{2,1,0:T(8,128)(2,1)S(1)} %get-tuple-element.76.a0), channel_id=1, source_target_pairs={{0,4},{1,5},{2,6},{3,7},{4,0},{5,1},{6,2},{7,3},{8,12},{9,13},{10,... | collective-permute-start | bytes 786440 | tf_op jit(solution)/shard_map/ppermute | solution.py:309
  22.4 13.3 %collective-permute-start.4 = (bf16[4,256,128]{2,1,0:T(8,128)(2,1)S(1)}, bf16[4,256,128]{2,1,0:T(8,128)(2,1)S(1)}, u32[]{:S(2)}, u32[]{:S(2)}) collective-permute-start(bf16[4,256,128]{2,1,0:T(8,128)(2,1)S(1)} %get-tuple-element.76.a0), channel_id=1, source_target_pairs={{0,6},{1,7},{2,0},{3,1},{4,2},{5,3},{6,4},{7,5},{8,14},{9,15},{10,... | collective-permute-start | bytes 786440 | tf_op jit(solution)/shard_map/ppermute | solution.py:309
  41.0 3.9 %collective-permute-start.8 = (bf16[17,256,128]{2,1,0:T(8,128)(2,1)S(1)}, bf16[17,256,128]{2,1,0:T(8,128)(2,1)S(1)}, u32[]{:S(2)}, u32[]{:S(2)}) collective-permute-start(bf16[17,256,128]{2,1,0:T(8,128)(2,1)S(1)} %get-tuple-element.84.sent_ref), channel_id=1, source_target_pairs={{0,8},{8,0},{16,24},{24,16},{32,40},{40,32},{48,56},{56,48},{64,72... | collective-permute-start | bytes 3342344 | tf_op jit(solution)/shard_map/ppermute | solution.py:324
  41.1 8.6 %collective-permute-start.9 = (bf16[16,256,128]{2,1,0:T(8,128)(2,1)S(1)}, bf16[16,256,128]{2,1,0:T(8,128)(2,1)S(1)}, u32[]{:S(2)}, u32[]{:S(2)}) collective-permute-start(bf16[16,256,128]{2,1,0:T(8,128)(2,1)S(1)} %get-tuple-element.86), channel_id=1, source_target_pairs={{0,8},{8,0},{16,24},{24,16},{32,40},{40,32},{48,56},{56,48},{64,72... | collective-permute-start | bytes 3145736 | tf_op jit(solution)/shard_map/ppermute | solution.py:324
  45.1 11.6 %collective-permute-start.11 = (bf16[1152,128]{1,0:T(8,128)(2,1)S(1)}, bf16[1152,128]{1,0:T(8,128)(2,1)S(1)}, u32[]{:S(2)}, u32[]{:S(2)}) collective-permute-start(bf16[1152,128]{1,0:T(8,128)(2,1)S(1)} %get-tuple-element.94), channel_id=1, source_target_pairs={{0,32},{8,40},{16,48},{24,56},{32,0},{40,8},{48,16},{56,24},{64,96... | collective-permute-start | bytes 884744 | tf_op jit(solution)/shard_map/ppermute | solution.py:315
  47.6 14.4 %collective-permute-start.12 = (bf16[1152,128]{1,0:T(8,128)(2,1)S(1)}, bf16[1152,128]{1,0:T(8,128)(2,1)S(1)}, u32[]{:S(2)}, u32[]{:S(2)}) collective-permute-start(bf16[1152,128]{1,0:T(8,128)(2,1)S(1)} %get-tuple-element.95), channel_id=1, source_target_pairs={{0,48},{8,56},{16,0},{24,8},{32,16},{40,24},{48,32},{56,40},{64,11... | collective-permute-start | bytes 884744 | tf_op jit(solution)/shard_map/ppermute | solution.py:315
  47.9 14.1 %collective-permute-start.10 = (bf16[1152,128]{1,0:T(8,128)(2,1)S(1)}, bf16[1152,128]{1,0:T(8,128)(2,1)S(1)}, u32[]{:S(2)}, u32[]{:S(2)}) collective-permute-start(bf16[1152,128]{1,0:T(8,128)(2,1)S(1)} %get-tuple-element.93.sent_ref), channel_id=1, source_target_pairs={{0,16},{8,24},{16,32},{24,40},{32,48},{40,56},{48,0},{56,8},{64,80... | collective-permute-start | bytes 884744 | tf_op jit(solution)/shard_map/ppermute | solution.py:315
  53.1 13.7 %copy-start.3 = (s32[512,16]{0,1:T(8,128)S(1)}, s32[512,16]{0,1:T(8,128)}, u32[]{:S(2)}) copy-start(s32[512,16]{0,1:T(8,128)} %param.15) | copy-start | bytes 98308
  53.1 14.0 %collective-permute-start.15 = (bf16[8,256,128]{2,1,0:T(8,128)(2,1)S(1)}, bf16[8,256,128]{2,1,0:T(8,128)(2,1)S(1)}, u32[]{:S(2)}, u32[]{:S(2)}) collective-permute-start(bf16[8,256,128]{2,1,0:T(8,128)(2,1)S(1)} %get-tuple-element.102), channel_id=1, source_target_pairs={{0,64},{8,72},{16,80},{24,88},{32,96},{40,104},{48,112},{56,120},{... | collective-permute-start | bytes 1572872 | tf_op jit(solution)/shard_map/ppermute | solution.py:321
  62.1 4.3 %collective-permute-start.13 = (f32[128,128]{1,0:T(8,128)S(1)}, f32[128,128]{1,0:T(8,128)S(1)}, u32[]{:S(2)}, u32[]{:S(2)}) collective-permute-start(f32[128,128]{1,0:T(8,128)S(1)} %get-tuple-element.100.own), channel_id=1, source_target_pairs={{0,2},{1,3},{2,0},{3,1},{4,6},{5,7},{6,4},{7,5},{8,10},{9,11},{10,... | collective-permute-start | bytes 196616 | tf_op jit(solution)/shard_map/ppermute | solution.py:318
  66.5 6.7 %collective-permute-start.14 = (bf16[3,256,128]{2,1,0:T(8,128)(2,1)S(1)}, bf16[3,256,128]{2,1,0:T(8,128)(2,1)S(1)}, u32[]{:S(2)}, u32[]{:S(2)}) collective-permute-start(bf16[3,256,128]{2,1,0:T(8,128)(2,1)S(1)} %pair_up.1.own), channel_id=1, source_target_pairs={{0,64},{8,72},{16,80},{24,88},{32,96},{40,104},{48,112},{56,120},{... | collective-permute-start | bytes 589832 | tf_op jit(solution)/shard_map/ppermute | solution.py:321
  67.2 7.1 %collective-permute-start.16 = (bf16[2,256,128]{2,1,0:T(8,128)(2,1)S(1)}, bf16[2,256,128]{2,1,0:T(8,128)(2,1)S(1)}, u32[]{:S(2)}, u32[]{:S(2)}) collective-permute-start(bf16[2,256,128]{2,1,0:T(8,128)(2,1)S(1)} %get-tuple-element.104), channel_id=1, source_target_pairs={{0,16},{8,24},{16,32},{24,40},{32,48},{40,56},{48,0},{56,8},{64,80... | collective-permute-start | bytes 393224 | tf_op jit(solution)/shard_map/ppermute | solution.py:315
  69.1 6.7 %collective-permute-start.17 = (bf16[2,256,128]{2,1,0:T(8,128)(2,1)S(1)}, bf16[2,256,128]{2,1,0:T(8,128)(2,1)S(1)}, u32[]{:S(2)}, u32[]{:S(2)}) collective-permute-start(bf16[2,256,128]{2,1,0:T(8,128)(2,1)S(1)} %get-tuple-element.105), channel_id=1, source_target_pairs={{0,32},{8,40},{16,48},{24,56},{32,0},{40,8},{48,16},{56,24},{64,96... | collective-permute-start | bytes 393224 | tf_op jit(solution)/shard_map/ppermute | solution.py:315
  70.9 5.2 %collective-permute-start.18 = (bf16[2,256,128]{2,1,0:T(8,128)(2,1)S(1)}, bf16[2,256,128]{2,1,0:T(8,128)(2,1)S(1)}, u32[]{:S(2)}, u32[]{:S(2)}) collective-permute-start(bf16[2,256,128]{2,1,0:T(8,128)(2,1)S(1)} %get-tuple-element.106), channel_id=1, source_target_pairs={{0,48},{8,56},{16,0},{24,8},{32,16},{40,24},{48,32},{56,40},{64,11... | collective-permute-start | bytes 393224 | tf_op jit(solution)/shard_map/ppermute | solution.py:315
  73.2 6.6 %collective-permute-start.19 = (f32[2,128,128]{2,1,0:T(8,128)S(1)}, f32[2,128,128]{2,1,0:T(8,128)S(1)}, u32[]{:S(2)}, u32[]{:S(2)}) collective-permute-start(f32[2,128,128]{2,1,0:T(8,128)S(1)} %sum_pair.1.w), channel_id=1, source_target_pairs={{0,4},{1,5},{2,6},{3,7},{4,0},{5,1},{6,2},{7,3},{8,12},{9,13},{10,... | collective-permute-start | bytes 393224 | tf_op jit(solution)/shard_map/ppermute | solution.py:318

commit v9 on v7

--- a/solution.py
+++ b/solution.py
@@ -420,7 +420,10 @@
     q_keep, w, w_got = tie(q_keep, w, w_got)
     q_all = around_z(*q_z)
     (w,) = call(add_two, [(square, f32)], [VMEM] * 2, "add_two", limit=2)(w, w_got)
-    (w,) = call(pair_up, [((2, T, T), f32)], [VMEM] * 2, "pair_up", limit=2)(w, swap_x(w, 0))
+    w_got = swap_x(w, 0)
+    q_all = list(q_all)
+    w, w_got, q_all[0], q_all[1] = tie(w, w_got, q_all[0], q_all[1])
+    (w,) = call(pair_up, [((2, T, T), f32)], [VMEM] * 2, "pair_up", limit=2)(w, w_got)
     w_got = swap_x(w, 1)
     prev_grad, weight_grad = call(
         finish, [((512, 256), bf16), ((256, 256), f32)], [VMEM] * 9, "finish", flops=10**6

time: 81.1 us -> 82.9 us (1.022)
  starting transfers between devices: 35.8 us -> 29 us
  Pallas kernels: 17.7 us -> 23.3 us
  waiting for transfers between devices: 26.6 us -> 29.1 us
    ppermute x2, waiting for transfers between devices: 2.11 us -> 8.28 us  [swap_x(): return lax.ppermute(v, 'col', [(c, c ^ 2 << bit) for c in range(8)])]
    ppermute x3, starting transfers between devices: 4.68 us -> 0.54 us  [over_y_lo(): return lax.ppermute(v, 'row', [(r, r ^ 8) for r in range(16)])]
    ppermute x2, starting transfers between devices: 4.5 us -> 1.24 us  [swap_x(): return lax.ppermute(v, 'col', [(c, c ^ 2 << bit) for c in range(8)])]
    ppermute x6, waiting for transfers between devices: 10.8 us -> 7.81 us  [over_z(): lax.ppermute(v, 'row', [(r, r & 9 | ((r >> 1) + s & 3) << 1) for r in ran...]
    ppermute x3, waiting for transfers between devices: 2.56 us -> 4.88 us  [over_y_lo(): return lax.ppermute(v, 'row', [(r, r ^ 8) for r in range(16)])]
    ppermute x6, waiting for transfers between devices: 10.4 us -> 8.09 us  [over_x(): lax.ppermute(v, 'col', [(c, ((c >> 1) + s & 3) * 2 + (c & 1)) for c in ra...]
    pallas_call x1, Pallas kernels: 3.06 us -> 4.49 us  [shards(): call(late_partner, [((17, 256, T), bf16), (sixteen, bf16), ((33, 256, T),...]
    pallas_call x1, Pallas kernels: 2.94 us -> 4.37 us  [shards(): call(early, [((65, 256, T), f32)], [SMEM] + [VMEM] * 3, 'early', limit=LI...]
  transfers between devices with their start and end apart: 21 -> 21, of which waited for: 13 -> 10; matrix products, arithmetic and copies ran while one was open for 0% -> 0% of each run, Pallas kernels for 14% -> 18%
where the time goes in v9:
time: 82.9 us; the launch traced here: 83.3 us
  waiting for transfers between devices  29.1 us (35%)
  starting transfers between devices  29 us (35%)
  Pallas kernels  23.3 us (28%)
  between operations  1.52 us (2%)
    ppermute x6, starting transfers between devices, over_z(): lax.ppermute(v, 'row', [(r, r & 9 | ((r >> 1) + s & 3) << 1) for r in ran...  12.1 us
    ppermute x2, waiting for transfers between devices, swap_x(): return lax.ppermute(v, 'col', [(c, c ^ 2 << bit) for c in range(8)])  8.28 us
    ppermute x6, waiting for transfers between devices, over_x(): lax.ppermute(v, 'col', [(c, ((c >> 1) + s & 3) * 2 + (c & 1)) for c in ra...  8.09 us
    ppermute x6, starting transfers between devices, over_x(): lax.ppermute(v, 'col', [(c, ((c >> 1) + s & 3) * 2 + (c & 1)) for c in ra...  8.03 us
    ppermute x6, waiting for transfers between devices, over_z(): lax.ppermute(v, 'row', [(r, r & 9 | ((r >> 1) + s & 3) << 1) for r in ran...  7.81 us
    ppermute x2, starting transfers between devices, over_y_hi(): return lax.ppermute(v, 'col', [(c, c ^ 1) for c in range(8)])  6.46 us
    pallas_call x2, Pallas kernels, own_columns(): call(functools.partial(late_own, number), [(sixteen, f32)], [SMEM] + [VME...  5.2 us
    ppermute x3, waiting for transfers between devices, over_y_lo(): return lax.ppermute(v, 'row', [(r, r ^ 8) for r in range(16)])  4.88 us
  transfers between devices with their start and end apart: 21, of which 10 were waited for; matrix products, arithmetic and copies ran while one was open for 0% of the time, Pallas kernels for 18%

profile of v9, /device:TPU:0, one launch (start us, length us, event | category | flops | bytes accessed | tf_op | source)
XLA Modules:
  0.0 83.3 jit_solution(9985962509856644905)
XLA Ops:
  0.6 2.5 %prep.1 = (bf16[2,256,128]{2,1,0:T(8,128)(2,1)}, bf16[2,256,128]{2,1,0:T(8,128)(2,1)}, bf16[640,128]{1,0:T(8,128)(2,1)}, bf16[640,128]{1,0:T(8,128)(2,1)}, bf16[640,128]{1,0:T(8,128)(2,1)}, /*index=5*/f32[128,128]{1,0:T(8,128)}) custom-call(bf16[512,256]{1,0:T(8,128)(2,1)} %grad_hbm.1, s32[16,512]{1,0:T(8,128)} %bitcast.12, bf16[512,256]{1,0:T(8,128)(2,1)} %agg_hbm.1, ...), custom_call_target="tpu_custom_call" | custom-call | flops 200000000 | tf_op jit(solution)/shard_map/prep/pallas_call | solution.py:324
  3.2 2.9 %collective-permute-start.1 = (bf16[640,128]{1,0:T(8,128)(2,1)}, bf16[640,128]{1,0:T(8,128)(2,1)S(1)}, u32[]{:S(2)}, u32[]{:S(2)}) collective-permute-start(bf16[640,128]{1,0:T(8,128)(2,1)} %get-tuple-element.66), channel_id=1, source_target_pairs={{0,6},{1,7},{2,0},{3,1},{4,2},{5,3},{6,4},{7,5},{8,14},{9,15},{10,... | collective-permute-start | bytes 491528 | tf_op jit(solution)/shard_map/ppermute | solution.py:306
  6.1 0.8 collective-permute-start.2
  6.9 0.9 %collective-permute-start.3 = (bf16[640,128]{1,0:T(8,128)(2,1)}, bf16[640,128]{1,0:T(8,128)(2,1)S(1)}, u32[]{:S(2)}, u32[]{:S(2)}) collective-permute-start(bf16[640,128]{1,0:T(8,128)(2,1)} %get-tuple-element.68), channel_id=1, source_target_pairs={{0,2},{1,3},{2,4},{3,5},{4,6},{5,7},{6,0},{7,1},{8,10},{9,11},{10,... | collective-permute-start | bytes 491528 | tf_op jit(solution)/shard_map/ppermute | solution.py:306
  7.8 3.2 %collective-permute-start = (bf16[2,256,128]{2,1,0:T(8,128)(2,1)}, bf16[2,256,128]{2,1,0:T(8,128)(2,1)S(1)}, u32[]{:S(2)}, u32[]{:S(2)}) collective-permute-start(bf16[2,256,128]{2,1,0:T(8,128)(2,1)} %get-tuple-element.73.ha), channel_id=1, source_target_pairs={{0,1},{1,0},{2,3},{3,2},{4,5},{5,4},{6,7},{7,6},{8,9},{9,8},{10,11... | collective-permute-start | bytes 393224 | tf_op jit(solution)/shard_map/ppermute | solution.py:309
  11.6 0.0 copy-start.4
  11.7 3.6 %stage.1.tiles_ref = bf16[512,128,128]{2,1,0:T(8,128)(2,1)S(1)} custom-call(s32[1]{0:T(128)} %bitcast.7.count_ref, bf16[512,128,128]{2,1,0:T(8,128)(2,1)} %bitcast.11), custom_call_target="tpu_custom_call" | custom-call | flops 1000000000 | tf_op jit(solution)/shard_map/stage/pallas_call | solution.py:344
  15.3 0.0 collective-permute-done.2.m2
  15.3 1.7 %collective-permute-done.3.m3 = bf16[640,128]{1,0:T(8,128)(2,1)S(1)} collective-permute-done((bf16[640,128]{1,0:T(8,128)(2,1)}, bf16[640,128]{1,0:T(8,128)(2,1)S(1)}, u32[]{:S(2)}, u32[]{:S(2)}) %collective-permute-start.3) | collective-permute-done | bytes 163872 | tf_op jit(solution)/shard_map/ppermute | solution.py:306
  17.0 0.1 pack.1
  17.1 3.3 %collective-permute-start.7 = (bf16[9,256,128]{2,1,0:T(8,128)(2,1)S(1)}, bf16[9,256,128]{2,1,0:T(8,128)(2,1)S(1)}, u32[]{:S(2)}, u32[]{:S(2)}) collective-permute-start(bf16[9,256,128]{2,1,0:T(8,128)(2,1)S(1)} %get-tuple-element.87.b0), channel_id=1, source_target_pairs={{0,1},{1,0},{2,3},{3,2},{4,5},{5,4},{6,7},{7,6},{8,9},{9,8},{10,11... | collective-permute-start | bytes 1769480 | tf_op jit(solution)/shard_map/ppermute | solution.py:309
  20.3 2.1 %collective-permute-start.5 = (bf16[4,256,128]{2,1,0:T(8,128)(2,1)S(1)}, bf16[4,256,128]{2,1,0:T(8,128)(2,1)S(1)}, u32[]{:S(2)}, u32[]{:S(2)}) collective-permute-start(bf16[4,256,128]{2,1,0:T(8,128)(2,1)S(1)} %get-tuple-element.83.a0), channel_id=1, source_target_pairs={{0,4},{1,5},{2,6},{3,7},{4,0},{5,1},{6,2},{7,3},{8,12},{9,13},{10,... | collective-permute-start | bytes 786440 | tf_op jit(solution)/shard_map/ppermute | solution.py:306
  22.4 1.4 %collective-permute-start.4 = (bf16[4,256,128]{2,1,0:T(8,128)(2,1)S(1)}, bf16[4,256,128]{2,1,0:T(8,128)(2,1)S(1)}, u32[]{:S(2)}, u32[]{:S(2)}) collective-permute-start(bf16[4,256,128]{2,1,0:T(8,128)(2,1)S(1)} %get-tuple-element.83.a0), channel_id=1, source_target_pairs={{0,6},{1,7},{2,0},{3,1},{4,2},{5,3},{6,4},{7,5},{8,14},{9,15},{10,... | collective-permute-start | bytes 786440 | tf_op jit(solution)/shard_map/ppermute | solution.py:306
  23.8 1.2 %order_slots.1.steps_ref = s32[8,512]{1,0:T(8,128)S(1)} custom-call(s32[1]{0:T(128)} %bitcast.8.count_ref, s32[2,512]{1,0:T(2,128)S(1)} %bitcast.10), custom_call_target="tpu_custom_call" | custom-call | flops 10000000 | tf_op jit(solution)/shard_map/order_slots/pallas_call | solution.py:362
  24.9 4.4 %early.1.so_far_ref = f32[65,256,128]{2,1,0:T(8,128)S(1)} custom-call(s32[8,512]{1,0:T(8,128)S(1)} %order_slots.1.steps_ref, bf16[4,256,128]{2,1,0:T(8,128)(2,1)S(1)} %get-tuple-element.83.a0, bf16[9,256,128]{2,1,0:T(8,128)(2,1)S(1)} %get-tuple-element.87.b0, bf16[512,128,128]{2,1,0:T(8,128)(2,1)S(1)} %stage.1.tiles_ref), custom_call_target="tpu_custom_call" | custom-call | flops 4000000000 | tf_op jit(solution)/shard_map/early/pallas_call | solution.py:363
  29.3 5.8 %collective-permute-done.6.a3 = bf16[4,256,128]{2,1,0:T(8,128)(2,1)S(1)} collective-permute-done((bf16[4,256,128]{2,1,0:T(8,128)(2,1)S(1)}, bf16[4,256,128]{2,1,0:T(8,128)(2,1)S(1)}, u32[]{:S(2)}, u32[]{:S(2)}) %collective-permute-start.6) | collective-permute-done | bytes 262176 | tf_op jit(solution)/shard_map/ppermute | solution.py:306
  35.1 0.0 collective-permute-done.5.a2
  35.1 0.6 collective-permute-done.4.a1
  35.7 4.5 %late_1.1 = (bf16[17,256,128]{2,1,0:T(8,128)(2,1)S(1)}, bf16[16,256,128]{2,1,0:T(8,128)(2,1)S(1)}, bf16[33,256,128]{2,1,0:T(8,128)(2,1)S(1)}) custom-call(s32[8,512]{1,0:T(8,128)S(1)} %order_slots.1.steps_ref, bf16[4,256,128]{2,1,0:T(8,128)(2,1)S(1)} %get-tuple-element.83.a0, bf16[4,256,128]{2,1,0:T(8,128)(2,1)S(1)} %collective-permute-done.6.a3, ...), custom_call_target="tpu_custom_call" | custom-call | flops 4000000000 | tf_op jit(solution)/shard_map/late_1/pallas_call | solution.py:391
  40.2 0.1 collective-permute-start.8
  40.3 0.5 collective-permute-start.9
  40.8 2.6 %late_2.1.acc_ref = f32[16,256,128]{2,1,0:T(8,128)S(1)} custom-call(s32[8,512]{1,0:T(8,128)S(1)} %order_slots.1.steps_ref, bf16[33,256,128]{2,1,0:T(8,128)(2,1)S(1)} %get-tuple-element.95.h_ref, bf16[512,128,128]{2,1,0:T(8,128)(2,1)S(1)} %stage.1.tiles_ref, f32[65,256,128]{2,1,0:T(8,128)S(1)} %early.1.so_far_ref), custom_call_target="tpu_custom_call" | custom-call | flops 2000000000 | tf_op jit(solution)/shard_map/late_2/pallas_call | solution.py:378
  43.5 0.2 split_p.1
  43.6 6.8 %collective-permute-start.11 = (bf16[1152,128]{1,0:T(8,128)(2,1)S(1)}, bf16[1152,128]{1,0:T(8,128)(2,1)S(1)}, u32[]{:S(2)}, u32[]{:S(2)}) collective-permute-start(bf16[1152,128]{1,0:T(8,128)(2,1)S(1)} %get-tuple-element.101), channel_id=1, source_target_pairs={{0,32},{8,40},{16,48},{24,56},{32,0},{40,8},{48,16},{56,24},{64,96... | collective-permute-start | bytes 884744 | tf_op jit(solution)/shard_map/ppermute | solution.py:312
  50.5 2.0 %collective-permute-start.10 = (bf16[1152,128]{1,0:T(8,128)(2,1)S(1)}, bf16[1152,128]{1,0:T(8,128)(2,1)S(1)}, u32[]{:S(2)}, u32[]{:S(2)}) collective-permute-start(bf16[1152,128]{1,0:T(8,128)(2,1)S(1)} %get-tuple-element.100.sent_ref), channel_id=1, source_target_pairs={{0,16},{8,24},{16,32},{24,40},{32,48},{40,56},{48,0},{56,8},{64,80... | collective-permute-start | bytes 884744 | tf_op jit(solution)/shard_map/ppermute | solution.py:312
  52.5 2.6 %late_3.1.acc_ref = f32[16,256,128]{2,1,0:T(8,128)S(1)} custom-call(s32[8,512]{1,0:T(8,128)S(1)} %order_slots.1.steps_ref, bf16[33,256,128]{2,1,0:T(8,128)(2,1)S(1)} %get-tuple-element.95.h_ref, bf16[512,128,128]{2,1,0:T(8,128)(2,1)S(1)} %stage.1.tiles_ref, f32[65,256,128]{2,1,0:T(8,128)S(1)} %early.1.so_far_ref), custom_call_target="tpu_custom_call" | custom-call | flops 2000000000 | tf_op jit(solution)/shard_map/late_3/pallas_call | solution.py:378
  55.1 0.0 copy-start.3
  55.1 0.2 split_q.1
  55.3 0.1 collective-permute-start.14
  55.4 0.5 copy-done.3
  55.9 0.3 in_mask.1.mask_ref
  56.2 2.3 %collective-permute-done.11.g2 = bf16[1152,128]{1,0:T(8,128)(2,1)S(1)} collective-permute-done((bf16[1152,128]{1,0:T(8,128)(2,1)S(1)}, bf16[1152,128]{1,0:T(8,128)(2,1)S(1)}, u32[]{:S(2)}, u32[]{:S(2)}) %collective-permute-start.11) | collective-permute-done | bytes 294944 | tf_op jit(solution)/shard_map/ppermute | solution.py:312
  58.4 2.5 %collective-permute-done.12.g3 = bf16[1152,128]{1,0:T(8,128)(2,1)S(1)} collective-permute-done((bf16[1152,128]{1,0:T(8,128)(2,1)S(1)}, bf16[1152,128]{1,0:T(8,128)(2,1)S(1)}, u32[]{:S(2)}, u32[]{:S(2)}) %collective-permute-start.12) | collective-permute-done | bytes 294944 | tf_op jit(solution)/shard_map/ppermute | solution.py:312
  60.9 2.1 %collective-permute-done.10.g1 = bf16[1152,128]{1,0:T(8,128)(2,1)S(1)} collective-permute-done((bf16[1152,128]{1,0:T(8,128)(2,1)S(1)}, bf16[1152,128]{1,0:T(8,128)(2,1)S(1)}, u32[]{:S(2)}, u32[]{:S(2)}) %collective-permute-start.10) | collective-permute-done | bytes 294944 | tf_op jit(solution)/shard_map/ppermute | solution.py:312
  63.0 0.1 gather_p.1
  63.1 0.1 collective-permute-start.15
  63.2 4.9 %collective-permute-done.14.got_ref = bf16[8,256,128]{2,1,0:T(8,128)(2,1)S(1)} collective-permute-done((bf16[8,256,128]{2,1,0:T(8,128)(2,1)S(1)}, bf16[8,256,128]{2,1,0:T(8,128)(2,1)S(1)}, u32[]{:S(2)}, u32[]{:S(2)}) %collective-permute-start.14) | collective-permute-done | bytes 524320 | tf_op jit(solution)/shard_map/ppermute | solution.py:318
  68.1 0.1 gather_q.1
  68.2 0.1 collective-permute-start.17
  68.3 2.2 %collective-permute-start.18 = (bf16[2,256,128]{2,1,0:T(8,128)(2,1)S(1)}, bf16[2,256,128]{2,1,0:T(8,128)(2,1)S(1)}, u32[]{:S(2)}, u32[]{:S(2)}) collective-permute-start(bf16[2,256,128]{2,1,0:T(8,128)(2,1)S(1)} %get-tuple-element.115), channel_id=1, source_target_pairs={{0,32},{8,40},{16,48},{24,56},{32,0},{40,8},{48,16},{56,24},{64,96... | collective-permute-start | bytes 393224 | tf_op jit(solution)/shard_map/ppermute | solution.py:312
  70.5 0.1 collective-permute-start.16
  70.6 0.4 collective-permute-start.13
  71.0 1.0 %collective-permute-start.19 = (bf16[2,256,128]{2,1,0:T(8,128)(2,1)S(1)}, bf16[2,256,128]{2,1,0:T(8,128)(2,1)S(1)}, u32[]{:S(2)}, u32[]{:S(2)}) collective-permute-start(bf16[2,256,128]{2,1,0:T(8,128)(2,1)S(1)} %get-tuple-element.118), channel_id=1, source_target_pairs={{0,48},{8,56},{16,0},{24,8},{32,16},{40,24},{48,32},{56,40},{64,11... | collective-permute-start | bytes 393224 | tf_op jit(solution)/shard_map/ppermute | solution.py:312
  72.0 2.9 %collective-permute-done.16.got = f32[128,128]{1,0:T(8,128)S(1)} collective-permute-done((f32[128,128]{1,0:T(8,128)S(1)}, f32[128,128]{1,0:T(8,128)S(1)}, u32[]{:S(2)}, u32[]{:S(2)}) %collective-permute-start.16) | collective-permute-done | bytes 65568 | tf_op jit(solution)/shard_map/ppermute | solution.py:315
  74.9 1.0 %collective-permute-done.17.g1 = bf16[2,256,128]{2,1,0:T(8,128)(2,1)S(1)} collective-permute-done((bf16[2,256,128]{2,1,0:T(8,128)(2,1)S(1)}, bf16[2,256,128]{2,1,0:T(8,128)(2,1)S(1)}, u32[]{:S(2)}, u32[]{:S(2)}) %collective-permute-start.17) | collective-permute-done | bytes 131104 | tf_op jit(solution)/shard_map/ppermute | solution.py:312
  75.9 1.1 %collective-permute-start.20 = (f32[2,128,128]{2,1,0:T(8,128)S(1)}, f32[2,128,128]{2,1,0:T(8,128)S(1)}, u32[]{:S(2)}, u32[]{:S(2)}) collective-permute-start(f32[2,128,128]{2,1,0:T(8,128)S(1)} %pair_up.1.w), channel_id=1, source_target_pairs={{0,4},{1,5},{2,6},{3,7},{4,0},{5,1},{6,2},{7,3},{8,12},{9,13},{10,... | collective-permute-start | bytes 393224 | tf_op jit(solution)/shard_map/ppermute | solution.py:315
  77.0 5.4 %collective-permute-done.20.w_got = f32[2,128,128]{2,1,0:T(8,128)S(1)} collective-permute-done((f32[2,128,128]{2,1,0:T(8,128)S(1)}, f32[2,128,128]{2,1,0:T(8,128)S(1)}, u32[]{:S(2)}, u32[]{:S(2)}) %collective-permute-start.20) | collective-permute-done | bytes 131104 | tf_op jit(solution)/shard_map/ppermute | solution.py:315
  82.4 0.9 %finish.1 = (bf16[512,256]{1,0:T(8,128)(2,1)}, f32[256,256]{1,0:T(8,128)}) custom-call(f32[2,256,128]{2,1,0:T(8,128)S(1)} %get-tuple-element.105.p_keep, bf16[2,256,128]{2,1,0:T(8,128)(2,1)S(1)} %collective-permute-done.13.p_got, f32[2,256,128]{2,1,0:T(8,128)S(1)} %get-tuple-element.111.q_keep, bf16[2,256,128]{2,1,0:T(8,128)(2,1)S(1)} %collective-permute-done.17.g1, ...), custom_call_target="tpu_custom_call" | custom-call | flops 1000000 | tf_op jit(solution)/shard_map/finish/pallas_call | solution.py:428
  (20 shorter events, 0.1 us)
Async XLA Ops:
  3.2 12.1 %collective-permute-start.1 = (bf16[640,128]{1,0:T(8,128)(2,1)}, bf16[640,128]{1,0:T(8,128)(2,1)S(1)}, u32[]{:S(2)}, u32[]{:S(2)}) collective-permute-start(bf16[640,128]{1,0:T(8,128)(2,1)} %get-tuple-element.66), channel_id=1, source_target_pairs={{0,6},{1,7},{2,0},{3,1},{4,2},{5,3},{6,4},{7,5},{8,14},{9,15},{10,... | collective-permute-start | bytes 491528 | tf_op jit(solution)/shard_map/ppermute | solution.py:306
  6.1 9.2 %collective-permute-start.2 = (bf16[640,128]{1,0:T(8,128)(2,1)}, bf16[640,128]{1,0:T(8,128)(2,1)S(1)}, u32[]{:S(2)}, u32[]{:S(2)}) collective-permute-start(bf16[640,128]{1,0:T(8,128)(2,1)} %get-tuple-element.67), channel_id=1, source_target_pairs={{0,4},{1,5},{2,6},{3,7},{4,0},{5,1},{6,2},{7,3},{8,12},{9,13},{10,... | collective-permute-start | bytes 491528 | tf_op jit(solution)/shard_map/ppermute | solution.py:306
  6.9 10.1 %collective-permute-start.3 = (bf16[640,128]{1,0:T(8,128)(2,1)}, bf16[640,128]{1,0:T(8,128)(2,1)S(1)}, u32[]{:S(2)}, u32[]{:S(2)}) collective-permute-start(bf16[640,128]{1,0:T(8,128)(2,1)} %get-tuple-element.68), channel_id=1, source_target_pairs={{0,2},{1,3},{2,4},{3,5},{4,6},{5,7},{6,0},{7,1},{8,10},{9,11},{10,... | collective-permute-start | bytes 491528 | tf_op jit(solution)/shard_map/ppermute | solution.py:306
  7.8 7.5 %collective-permute-start = (bf16[2,256,128]{2,1,0:T(8,128)(2,1)}, bf16[2,256,128]{2,1,0:T(8,128)(2,1)S(1)}, u32[]{:S(2)}, u32[]{:S(2)}) collective-permute-start(bf16[2,256,128]{2,1,0:T(8,128)(2,1)} %get-tuple-element.73.ha), channel_id=1, source_target_pairs={{0,1},{1,0},{2,3},{3,2},{4,5},{5,4},{6,7},{7,6},{8,9},{9,8},{10,11... | collective-permute-start | bytes 393224 | tf_op jit(solution)/shard_map/ppermute | solution.py:309
  11.6 5.4 %copy-start = (bf16[2,256,128]{2,1,0:T(8,128)(2,1)S(1)}, bf16[2,256,128]{2,1,0:T(8,128)(2,1)}, u32[]{:S(2)}) copy-start(bf16[2,256,128]{2,1,0:T(8,128)(2,1)} %get-tuple-element.73.ha) | copy-start | bytes 393220
  11.6 5.4 %copy-start.1 = (bf16[2,256,128]{2,1,0:T(8,128)(2,1)S(1)}, bf16[2,256,128]{2,1,0:T(8,128)(2,1)}, u32[]{:S(2)}) copy-start(bf16[2,256,128]{2,1,0:T(8,128)(2,1)} %get-tuple-element.75.hb) | copy-start | bytes 393220
  11.6 5.3 %copy-start.2 = (f32[128,128]{1,0:T(8,128)S(1)}, f32[128,128]{1,0:T(8,128)}, u32[]{:S(2)}) copy-start(f32[128,128]{1,0:T(8,128)} %get-tuple-element.79.keep) | copy-start | bytes 196612
  11.6 12.1 %copy-start.4 = (s32[1,1,512,2]{2,3,1,0:T(2,128)S(1)}, s32[1,1,512,2]{2,3,1,0:T(2,128)}, u32[]{:S(2)}) copy-start(s32[1,1,512,2]{2,3,1,0:T(2,128)} %param.13) | copy-start | bytes 12292
  17.1 18.7 %collective-permute-start.7 = (bf16[9,256,128]{2,1,0:T(8,128)(2,1)S(1)}, bf16[9,256,128]{2,1,0:T(8,128)(2,1)S(1)}, u32[]{:S(2)}, u32[]{:S(2)}) collective-permute-start(bf16[9,256,128]{2,1,0:T(8,128)(2,1)S(1)} %get-tuple-element.87.b0), channel_id=1, source_target_pairs={{0,1},{1,0},{2,3},{3,2},{4,5},{5,4},{6,7},{7,6},{8,9},{9,8},{10,11... | collective-permute-start | bytes 1769480 | tf_op jit(solution)/shard_map/ppermute | solution.py:309
  20.3 14.8 %collective-permute-start.6 = (bf16[4,256,128]{2,1,0:T(8,128)(2,1)S(1)}, bf16[4,256,128]{2,1,0:T(8,128)(2,1)S(1)}, u32[]{:S(2)}, u32[]{:S(2)}) collective-permute-start(bf16[4,256,128]{2,1,0:T(8,128)(2,1)S(1)} %get-tuple-element.83.a0), channel_id=1, source_target_pairs={{0,2},{1,3},{2,4},{3,5},{4,6},{5,7},{6,0},{7,1},{8,10},{9,11},{10,... | collective-permute-start | bytes 786440 | tf_op jit(solution)/shard_map/ppermute | solution.py:306
  20.3 14.8 %collective-permute-start.5 = (bf16[4,256,128]{2,1,0:T(8,128)(2,1)S(1)}, bf16[4,256,128]{2,1,0:T(8,128)(2,1)S(1)}, u32[]{:S(2)}, u32[]{:S(2)}) collective-permute-start(bf16[4,256,128]{2,1,0:T(8,128)(2,1)S(1)} %get-tuple-element.83.a0), channel_id=1, source_target_pairs={{0,4},{1,5},{2,6},{3,7},{4,0},{5,1},{6,2},{7,3},{8,12},{9,13},{10,... | collective-permute-start | bytes 786440 | tf_op jit(solution)/shard_map/ppermute | solution.py:306
  22.4 13.3 %collective-permute-start.4 = (bf16[4,256,128]{2,1,0:T(8,128)(2,1)S(1)}, bf16[4,256,128]{2,1,0:T(8,128)(2,1)S(1)}, u32[]{:S(2)}, u32[]{:S(2)}) collective-permute-start(bf16[4,256,128]{2,1,0:T(8,128)(2,1)S(1)} %get-tuple-element.83.a0), channel_id=1, source_target_pairs={{0,6},{1,7},{2,0},{3,1},{4,2},{5,3},{6,4},{7,5},{8,14},{9,15},{10,... | collective-permute-start | bytes 786440 | tf_op jit(solution)/shard_map/ppermute | solution.py:306
  40.2 3.2 %collective-permute-start.8 = (bf16[17,256,128]{2,1,0:T(8,128)(2,1)S(1)}, bf16[17,256,128]{2,1,0:T(8,128)(2,1)S(1)}, u32[]{:S(2)}, u32[]{:S(2)}) collective-permute-start(bf16[17,256,128]{2,1,0:T(8,128)(2,1)S(1)} %get-tuple-element.91.sent_ref), channel_id=1, source_target_pairs={{0,8},{8,0},{16,24},{24,16},{32,40},{40,32},{48,56},{56,48},{64,72... | collective-permute-start | bytes 3342344 | tf_op jit(solution)/shard_map/ppermute | solution.py:321
  40.3 12.2 %collective-permute-start.9 = (bf16[16,256,128]{2,1,0:T(8,128)(2,1)S(1)}, bf16[16,256,128]{2,1,0:T(8,128)(2,1)S(1)}, u32[]{:S(2)}, u32[]{:S(2)}) collective-permute-start(bf16[16,256,128]{2,1,0:T(8,128)(2,1)S(1)} %get-tuple-element.93), channel_id=1, source_target_pairs={{0,8},{8,0},{16,24},{24,16},{32,40},{40,32},{48,56},{56,48},{64,72... | collective-permute-start | bytes 3145736 | tf_op jit(solution)/shard_map/ppermute | solution.py:321
  43.6 14.8 %collective-permute-start.11 = (bf16[1152,128]{1,0:T(8,128)(2,1)S(1)}, bf16[1152,128]{1,0:T(8,128)(2,1)S(1)}, u32[]{:S(2)}, u32[]{:S(2)}) collective-permute-start(bf16[1152,128]{1,0:T(8,128)(2,1)S(1)} %get-tuple-element.101), channel_id=1, source_target_pairs={{0,32},{8,40},{16,48},{24,56},{32,0},{40,8},{48,16},{56,24},{64,96... | collective-permute-start | bytes 884744 | tf_op jit(solution)/shard_map/ppermute | solution.py:312
  50.5 10.4 %collective-permute-start.12 = (bf16[1152,128]{1,0:T(8,128)(2,1)S(1)}, bf16[1152,128]{1,0:T(8,128)(2,1)S(1)}, u32[]{:S(2)}, u32[]{:S(2)}) collective-permute-start(bf16[1152,128]{1,0:T(8,128)(2,1)S(1)} %get-tuple-element.102), channel_id=1, source_target_pairs={{0,48},{8,56},{16,0},{24,8},{32,16},{40,24},{48,32},{56,40},{64,11... | collective-permute-start | bytes 884744 | tf_op jit(solution)/shard_map/ppermute | solution.py:312
  50.5 12.5 %collective-permute-start.10 = (bf16[1152,128]{1,0:T(8,128)(2,1)S(1)}, bf16[1152,128]{1,0:T(8,128)(2,1)S(1)}, u32[]{:S(2)}, u32[]{:S(2)}) collective-permute-start(bf16[1152,128]{1,0:T(8,128)(2,1)S(1)} %get-tuple-element.100.sent_ref), channel_id=1, source_target_pairs={{0,16},{8,24},{16,32},{24,40},{32,48},{40,56},{48,0},{56,8},{64,80... | collective-permute-start | bytes 884744 | tf_op jit(solution)/shard_map/ppermute | solution.py:312
  55.1 0.8 copy-start.3
  55.3 12.8 %collective-permute-start.14 = (bf16[8,256,128]{2,1,0:T(8,128)(2,1)S(1)}, bf16[8,256,128]{2,1,0:T(8,128)(2,1)S(1)}, u32[]{:S(2)}, u32[]{:S(2)}) collective-permute-start(bf16[8,256,128]{2,1,0:T(8,128)(2,1)S(1)} %get-tuple-element.108), channel_id=1, source_target_pairs={{0,64},{8,72},{16,80},{24,88},{32,96},{40,104},{48,112},{56,120},{... | collective-permute-start | bytes 1572872 | tf_op jit(solution)/shard_map/ppermute | solution.py:318
  63.1 7.4 %collective-permute-start.15 = (f32[128,128]{1,0:T(8,128)S(1)}, f32[128,128]{1,0:T(8,128)S(1)}, u32[]{:S(2)}, u32[]{:S(2)}) collective-permute-start(f32[128,128]{1,0:T(8,128)S(1)} %get-tuple-element.112.a), channel_id=1, source_target_pairs={{0,64},{8,72},{16,80},{24,88},{32,96},{40,104},{48,112},{56,120},{... | collective-permute-start | bytes 196616 | tf_op jit(solution)/shard_map/ppermute | solution.py:318
  68.2 7.7 %collective-permute-start.17 = (bf16[2,256,128]{2,1,0:T(8,128)(2,1)S(1)}, bf16[2,256,128]{2,1,0:T(8,128)(2,1)S(1)}, u32[]{:S(2)}, u32[]{:S(2)}) collective-permute-start(bf16[2,256,128]{2,1,0:T(8,128)(2,1)S(1)} %get-tuple-element.114), channel_id=1, source_target_pairs={{0,16},{8,24},{16,32},{24,40},{32,48},{40,56},{48,0},{56,8},{64,80... | collective-permute-start | bytes 393224 | tf_op jit(solution)/shard_map/ppermute | solution.py:312
  68.3 7.6 %collective-permute-start.18 = (bf16[2,256,128]{2,1,0:T(8,128)(2,1)S(1)}, bf16[2,256,128]{2,1,0:T(8,128)(2,1)S(1)}, u32[]{:S(2)}, u32[]{:S(2)}) collective-permute-start(bf16[2,256,128]{2,1,0:T(8,128)(2,1)S(1)} %get-tuple-element.115), channel_id=1, source_target_pairs={{0,32},{8,40},{16,48},{24,56},{32,0},{40,8},{48,16},{56,24},{64,96... | collective-permute-start | bytes 393224 | tf_op jit(solution)/shard_map/ppermute | solution.py:312
  70.5 4.3 %collective-permute-start.16 = (f32[128,128]{1,0:T(8,128)S(1)}, f32[128,128]{1,0:T(8,128)S(1)}, u32[]{:S(2)}, u32[]{:S(2)}) collective-permute-start(f32[128,128]{1,0:T(8,128)S(1)} %add_two.1.own), channel_id=1, source_target_pairs={{0,2},{1,3},{2,0},{3,1},{4,6},{5,7},{6,4},{7,5},{8,10},{9,11},{10,... | collective-permute-start | bytes 196616 | tf_op jit(solution)/shard_map/ppermute | solution.py:315
  70.6 6.4 %collective-permute-start.13 = (bf16[2,256,128]{2,1,0:T(8,128)(2,1)S(1)}, bf16[2,256,128]{2,1,0:T(8,128)(2,1)S(1)}, u32[]{:S(2)}, u32[]{:S(2)}) collective-permute-start(bf16[2,256,128]{2,1,0:T(8,128)(2,1)S(1)} %get-tuple-element.106), channel_id=1, source_target_pairs={{0,64},{8,72},{16,80},{24,88},{32,96},{40,104},{48,112},{56,120},{... | collective-permute-start | bytes 393224 | tf_op jit(solution)/shard_map/ppermute | solution.py:318
  71.0 6.0 %collective-permute-start.19 = (bf16[2,256,128]{2,1,0:T(8,128)(2,1)S(1)}, bf16[2,256,128]{2,1,0:T(8,128)(2,1)S(1)}, u32[]{:S(2)}, u32[]{:S(2)}) collective-permute-start(bf16[2,256,128]{2,1,0:T(8,128)(2,1)S(1)} %get-tuple-element.118), channel_id=1, source_target_pairs={{0,48},{8,56},{16,0},{24,8},{32,16},{40,24},{48,32},{56,40},{64,11... | collective-permute-start | bytes 393224 | tf_op jit(solution)/shard_map/ppermute | solution.py:312
  75.9 6.6 %collective-permute-start.20 = (f32[2,128,128]{2,1,0:T(8,128)S(1)}, f32[2,128,128]{2,1,0:T(8,128)S(1)}, u32[]{:S(2)}, u32[]{:S(2)}) collective-permute-start(f32[2,128,128]{2,1,0:T(8,128)S(1)} %pair_up.1.w), channel_id=1, source_target_pairs={{0,4},{1,5},{2,6},{3,7},{4,0},{5,1},{6,2},{7,3},{8,12},{9,13},{10,... | collective-permute-start | bytes 393224 | tf_op jit(solution)/shard_map/ppermute | solution.py:315
